TPU v7x, 32 devices: a whole 2x2x4 slice. The times are simulated.
32 devices in a mesh: lat: 4 (over z), lon: 8 (over y, x, core).
Axes of the slice: x: 2, y: 2, z: 4, core: 2. Of those that a mesh axis runs over, the one named last changes fastest.
Arguments:
- patches: bfloat16 [6144, 1536], P(('lat', 'lon')), may hold values from -6 to 6
- requests: int32 [4, 4096], P('lat', 'lon'), may hold values from 0 to 191, as said below
- footprint: int32 [256, 64], P('lat', 'lon'), may hold values from -1 to 511, as said below
- weight_index: int32 [256, 64], P('lat', 'lon'), may hold values from 0 to 15
- composite_weights: float32 [16], replicated, may hold values from 0.1 to 1
- labels: int32 [256, 1024], P('lat', 'lon'), may hold values from 0 to 10
- conv1_weight: bfloat16 [9, 64, 12], replicated, may hold values from -0.625 to 0.625
- conv2_weight: bfloat16 [9, 64, 64], replicated, may hold values from -0.25 to 0.25
- head_weight: bfloat16 [11, 64], replicated, may hold values from -0.75 to 0.75
Outputs:
- skip_features: bfloat16 [64, 256, 1024], P(None, 'lat', 'lon')
- grad_conv1: float32 [9, 64, 12], replicated
- grad_conv2: float32 [9, 64, 64], replicated
- grad_head: float32 [11, 64], replicated
- loss: float32 [], replicated
Inputs may be any that keep to these rules, and one draw needn't show every extreme that they name: `requests`: every entry is a row offset into the store of the device at the same lat index and lon index b. `footprint`: an entry that is not -1 is b*64 + p, position p of the bucket that the tile takes from lon index b. Slot 0 is never -1. In one tile no two entries are equal, and in some tiles every position of every bucket is named.
All inputs are finite; a program needn't handle non-finite values.
Results may differ from a plain program's by a relative error of at most 0.0055.
Values may be sent and summed in bfloat16 or wider, within the bound.
No kernel may reach another device: no remote copies, remote signals or barrier semaphores. Data moves between devices by JAX's collectives and lax.ppermute only.
A program may use at most 64 MiB of HBM per device.

v0:
```python
import functools

import jax
import jax.numpy as jnp
from jax import lax
from jax.experimental import pallas as pl
from jax.experimental.pallas import tpu as pltpu
from jax.sharding import PartitionSpec as P

BF16 = jnp.bfloat16
F32 = jnp.float32
GROUP = 16
VMEM_LIMIT = 40 * 1024 * 1024


def dot(left, right):
    return lax.dot_general(left, right, (((1,), (0,)), ((), ())), preferred_element_type=F32)


def dot_nt(left, right):
    return lax.dot_general(left, right, (((1,), (1,)), ((), ())), preferred_element_type=F32)


def iota(shape, dim):
    return lax.broadcasted_iota(jnp.int32, shape, dim)


def call(kernel, out_shape, scratch=(), **kwargs):
    return pl.pallas_call(
        kernel,
        out_shape=out_shape,
        scratch_shapes=list(scratch),
        compiler_params=pltpu.CompilerParams(vmem_limit_bytes=VMEM_LIMIT),
        **kwargs,
    )


def struct(shape, dtype):
    return jax.ShapeDtypeStruct(shape, dtype)


def plan_kernel(requests, footprint, weight_index, levels, labels, out):
    rows, slots = footprint.shape
    patch_cols = labels.shape[1]
    foot = footprint[...]
    level_of = weight_index[...]
    weight = jnp.zeros((rows, slots), F32)
    for level in range(levels.shape[0]):
        weight = jnp.where(level_of == level, levels[level], weight)
    weight = jnp.where(foot >= 0, weight, 0.0)
    weight = weight / jnp.sum(weight, axis=1, keepdims=True)
    foot = foot.astype(F32)
    out[...] = jnp.zeros_like(out)
    for group in range(rows // 8):
        base = group * 2 * slots
        out[0:8, base : base + slots] = foot[group * 8 : group * 8 + 8]
        out[0:8, base + slots : base + 2 * slots] = weight[group * 8 : group * 8 + 8]
    asked = requests[...].astype(F32)
    for part in range(requests.shape[1] // 128):
        out[8 + part : 9 + part, :] = asked[:, part * 128 : (part + 1) * 128]
    lane = iota((8, patch_cols), 1)
    side = iota((8, patch_cols), 0)
    pick = ((side == 0) & (lane == 0)) | ((side == 1) & (lane == patch_cols - 1))
    edges = dot_nt(jnp.where(pick, 1.0, 0.0).astype(BF16), labels[...].astype(F32).astype(BF16))
    out[12:13, 0:rows] = edges[0:1]
    out[12:13, rows : 2 * rows] = edges[1:2]


def partial_kernel(tile_rows, slots, bucket, bands, me_ref, plans, own, mate, *refs):
    count = plans.shape[0]
    store, row_width = own.shape
    patch_cols = row_width // bands
    chips = count // 2
    outs, (stored, edge, spread) = refs[:chips], refs[chips:]
    me = me_ref[0]
    chip, core = me // 2, me % 2
    stored[pl.ds(pl.multiple_of(core * store, 64), store), :] = own[...]
    stored[pl.ds(pl.multiple_of((1 - core) * store, 64), store), :] = mate[...]

    wanted = [patch_cols - 3, patch_cols - 2, patch_cols - 1, 0, 1, 2]
    row_id = iota((6 * GROUP, row_width), 0)
    lane_id = iota((6 * GROUP, row_width), 1)
    column = row_id // GROUP
    column_lane = jnp.where(column < 3, column + (patch_cols - 3), column - 3)
    band = row_id % GROUP
    pick = (lane_id == band * patch_cols + column_lane) & (band < bands)
    edge[...] = dot_nt(jnp.where(pick, 1.0, 0.0).astype(BF16), stored[...]).astype(BF16)

    zero_tile = jnp.zeros(spread.shape[1:], spread.dtype)
    spread[0] = zero_tile
    spread[count + 1] = zero_tile
    pair = 2 * bucket
    place = iota((8, pair), 1) + chip * pair
    target = place.astype(F32)
    store_row = iota((2 * store, pair), 0)
    store_base = jnp.where(iota((2 * store, pair), 1) >= bucket, store, 0)

    def one_tile(tile, carry):
        groups = []
        for group in range(tile_rows // 8):
            base = group * 2 * slots
            total = jnp.zeros((8, pair), F32)
            for slot in range(slots):
                entry = plans[tile, 0:8, base + slot : base + slot + 1]
                weight = plans[tile, 0:8, base + slots + slot : base + slots + slot + 1]
                total = total + jnp.where(entry == target, weight, 0.0)
            groups.append(total)
        at_place = jnp.concatenate(groups, axis=0)
        if pair == 128:
            asked = plans[tile, pl.ds(8 + chip, 1), :]
        else:
            start = chip * pair
            asked = plans[tile, pl.ds(8 + start // 128, 1), :]
            asked = pltpu.roll(jnp.broadcast_to(asked, (8, 128)), (128 - start % 128) % 128, 1)[0:1, 0:pair]
        hit = store_row == asked.astype(jnp.int32) + store_base
        hit = jnp.where(hit, 1.0, 0.0).astype(BF16)
        high = at_place.astype(BF16)
        low = (at_place - high.astype(F32)).astype(BF16)
        both = dot_nt(jnp.concatenate([high, low], axis=0), hit)
        over_rows = both[:tile_rows] + both[tile_rows:]
        high = over_rows.astype(BF16)
        low = (over_rows - high.astype(F32)).astype(BF16)
        spread[tile + 1, 0:tile_rows] = high
        spread[tile + 1, tile_rows : 2 * tile_rows] = low
        return carry

    lax.fori_loop(0, count, one_tile, 0, unroll=2)

    for move in range(chips):
        tile = 2 * jnp.bitwise_xor(chip, move) + core
        weights = spread[tile + 1]
        for start in range(0, row_width, 512):
            stop = min(start + 512, row_width)
            both = dot(weights, stored[:, start:stop])
            outs[move][:, start:stop] = (both[:tile_rows] + both[tile_rows:]).astype(BF16)
        left = dot_nt(edge[0 : 3 * GROUP], spread[tile])
        right = dot_nt(edge[3 * GROUP : 6 * GROUP], spread[tile + 2])
        tail = outs[move]
        tail[:, row_width:] = jnp.zeros((tile_rows, tail.shape[1] - row_width), BF16)
        tail[0 : 3 * GROUP, row_width : row_width + tile_rows] = (
            left[:, :tile_rows] + left[:, tile_rows:]
        ).astype(BF16)
        tail[0 : 3 * GROUP, row_width + tile_rows : row_width + 2 * tile_rows] = (
            right[:, :tile_rows] + right[:, tile_rows:]
        ).astype(BF16)


def composite_kernel(bands, me_ref, plans, labels, *refs):
    count = plans.shape[0]
    tile_rows, patch_cols = labels.shape
    chips = count // 2
    parts = refs[:chips]
    main, strips, upper, lower, bank, side, bundle = refs[chips:]
    row_width = bands * patch_cols
    me = me_ref[0]
    for band in range(bands):
        columns = slice(band * patch_cols, (band + 1) * patch_cols)
        total = parts[0][:, columns].astype(F32)
        for part in parts[1:]:
            total = total + part[:, columns].astype(F32)
        bank[band * tile_rows : (band + 1) * tile_rows, :] = total
    bank[bands * tile_rows : (bands + 1) * tile_rows, :] = labels[...].astype(F32)
    bank[(bands + 1) * tile_rows : GROUP * tile_rows, :] = jnp.zeros(
        ((GROUP - bands - 1) * tile_rows, patch_cols), F32
    )
    for row in range(tile_rows):
        main[:, row * patch_cols : (row + 1) * patch_cols] = bank[
            pl.ds(row, GROUP, stride=tile_rows), :
        ].astype(BF16)

    far = parts[0][0 : 3 * GROUP, row_width : row_width + 2 * tile_rows].astype(F32)
    for part in parts[1:]:
        far = far + part[0 : 3 * GROUP, row_width : row_width + 2 * tile_rows].astype(F32)
    side[...] = jnp.zeros_like(side)
    side[0 : 3 * GROUP, 3 : 3 + tile_rows] = far[:, :tile_rows]
    side[7 * GROUP : 10 * GROUP, 3 : 3 + tile_rows] = far[:, tile_rows:]
    before = plans[jnp.maximum(me - 1, 0), 12:13, tile_rows : 2 * tile_rows]
    after = plans[jnp.minimum(me + 1, count - 1), 12:13, 0:tile_rows]
    side[2 * GROUP + bands : 2 * GROUP + bands + 1, 3 : 3 + tile_rows] = before
    side[7 * GROUP + bands : 7 * GROUP + bands + 1, 3 : 3 + tile_rows] = after
    row_id = iota((4 * GROUP, patch_cols), 0)
    lane_id = iota((4 * GROUP, patch_cols), 1)
    near = jnp.zeros((4 * GROUP, tile_rows), F32)
    column = row_id // GROUP
    column_lane = jnp.where(column < 2, column, column + (patch_cols - 4))
    for band in range(bands):
        pick = (row_id % GROUP == band) & (lane_id == column_lane)
        tile = bank[band * tile_rows : (band + 1) * tile_rows, :].astype(BF16)
        near = near + dot_nt(jnp.where(pick, 1.0, 0.0).astype(BF16), tile)
    side[3 * GROUP : 7 * GROUP, 3 : 3 + tile_rows] = near
    strips[...] = side[...].astype(BF16)

    for target, start in ((upper, 0), (lower, tile_rows - 3)):
        target[:, 0 : 3 * patch_cols] = main[:, start * patch_cols : (start + 3) * patch_cols]
        bundle[...] = jnp.zeros_like(bundle)
        for column in range(10):
            bundle[:, column * 3 : column * 3 + 3] = side[
                column * GROUP : (column + 1) * GROUP, 3 + start : 6 + start
            ]
        target[:, 3 * patch_cols :] = bundle[...].astype(BF16)


def weights_kernel(conv1, conv2, head, one_main, one_strip, two_main, two_strip, two_back, head_pad, head_turn, wide, tall):
    bands = conv1.shape[2]
    feat = conv2.shape[1]
    classes = head.shape[0]
    for target, order in ((one_main, False), (one_strip, True)):
        wide[...] = jnp.zeros_like(wide)
        for tap in range(9):
            source = (tap % 3) * 3 + tap // 3 if order else tap
            wide[:, tap * GROUP : tap * GROUP + bands] = conv1[source].astype(F32)
        target[...] = wide[:, 0 : 9 * GROUP].astype(BF16)
    for target, order in ((two_main, 0), (two_strip, 1), (two_back, 2)):
        for tap in range(9):
            source = ((tap % 3) * 3 + tap // 3) if order == 1 else (8 - tap if order == 2 else tap)
            block = conv2[source].astype(F32)
            wide[:, tap * feat : (tap + 1) * feat] = jnp.transpose(block) if order == 2 else block
        target[...] = wide[...].astype(BF16)
    tall[...] = jnp.zeros_like(tall)
    tall[0:classes, 0:feat] = head[...].astype(F32)
    padded = tall[...]
    head_pad[...] = padded[0:GROUP, 0:feat].astype(BF16)
    head_turn[...] = jnp.transpose(padded)[0:feat, 0:GROUP].astype(BF16)


def sigmoid(value):
    return 0.5 * jnp.tanh(0.5 * value) + 0.5


def head_stage(pre, label, mask, head_pad, head_turn, classes):
    gate = sigmoid(pre)
    soft = pre * gate
    skip = soft.astype(BF16)
    logits = dot(head_pad, skip)
    rank = iota(logits.shape, 0)
    real = rank < classes
    total = jnp.sum(jnp.where(real, jnp.exp(logits), 0.0), axis=0, keepdims=True)
    log_total = jnp.log(total)
    chosen = rank == label
    error = jnp.where(real, jnp.exp(logits - log_total) - jnp.where(chosen, 1.0, 0.0), 0.0)
    error = error.astype(BF16)
    loss = log_total - jnp.sum(jnp.where(chosen, logits, 0.0), axis=0, keepdims=True)
    back = dot(head_turn, error)
    slope = back * (gate + soft * (1.0 - gate))
    if mask is not None:
        slope = jnp.where(mask, slope, 0.0)
    return skip, error, slope, loss


def network_kernel(
    bands, classes, rows, cols, lat_count, lon_count, step,
    place, main, strips, above, below,
    one_main, one_strip, two_main, two_strip, two_back, head_pad, head_turn,
    skip_out, keep_out, send_out,
    band_rows, band_side, hidden_rows, slope_one_rate, slope_rows, sums,
):
    feat = two_main.shape[0]
    lat, lon = place[0], place[1]
    ext = rows + 6

    def span(row, count=1):
        return pl.ds(pl.multiple_of(row * cols, 128), count * cols)

    band_side[...] = strips[...].astype(F32)
    up_tail = above[:, 3 * cols :].astype(F32)
    down_tail = below[:, 3 * cols :].astype(F32)
    for column in range(10):
        at = slice(column * GROUP, (column + 1) * GROUP)
        band_side[at, 0:3] = up_tail[:, column * 3 : column * 3 + 3]
        band_side[at, 3 + rows : 6 + rows] = down_tail[:, column * 3 : column * 3 + 3]

    def turned(value):
        return jnp.concatenate(
            [pltpu.roll(value, 1, 1), value, pltpu.roll(value, value.shape[1] - 1, 1)], axis=0
        ).astype(BF16)

    lane_row = iota((1, 128), 1) - 3
    row_inside = (lat * rows + lane_row >= 0) & (lat * rows + lane_row < lat_count * rows)
    row_inside = row_inside & (lane_row >= -3) & (lane_row < rows + 3)
    has_left, has_right = lon > 0, lon < lon_count - 1
    side_taps = [turned(band_side[c * GROUP : (c + 1) * GROUP, :]) for c in range(10)]
    hidden_side = []
    for first in (0, 1, 2, 5, 6, 7):
        pre = dot(one_strip[...], jnp.concatenate(side_taps[first : first + 3], axis=0))
        inside = row_inside
        if first in (0, 1):
            inside = inside & has_left
        if first in (6, 7):
            inside = inside & has_right
        hidden_side.append(jnp.where(inside, pre * sigmoid(pre), 0.0).astype(BF16).astype(F32))
    hidden_taps = [turned(value) for value in hidden_side]
    slope_side = []
    for first, label_column, has in ((0, 2, has_left), (3, 7, has_right)):
        pre = dot(two_strip[...], jnp.concatenate(hidden_taps[first : first + 3], axis=0))
        at = label_column * GROUP + bands
        label = band_side[at : at + 1, :].astype(jnp.int32)
        slope = head_stage(pre, label, row_inside & has, head_pad[...], head_turn[...], classes)[2]
        slope_side.append(slope.astype(BF16).astype(F32))

    lane = iota((1, cols), 1)

    def put_shifted(target, value, row, count, left_side, right_side, size):
        target[size : 2 * size, span(row, count)] = value.astype(BF16)
        for i in range(count):
            tile = value[:, i * cols : (i + 1) * cols]
            turn = lax.rem(128 - (row + i), 128)
            left = pltpu.roll(left_side, turn, 1)
            right = pltpu.roll(right_side, lax.rem(turn + cols - 1, 128), 1)
            at_left = jnp.where(lane == 0, left, pltpu.roll(tile, 1, 1))
            at_right = jnp.where(lane == cols - 1, right, pltpu.roll(tile, cols - 1, 1))
            target[0:size, span(row + i)] = at_left.astype(BF16)
            target[2 * size : 3 * size, span(row + i)] = at_right.astype(BF16)

    def around(ref, row, count):
        return jnp.concatenate([ref[:, span(row + u, count)] for u in (-1, 0, 1)], axis=0)

    band_left = band_side[2 * GROUP : 3 * GROUP, :]
    band_right = band_side[7 * GROUP : 8 * GROUP, :]
    put_shifted(band_rows, above[:, 0 : 3 * cols].astype(F32), 0, 3, band_left, band_right, GROUP)
    put_shifted(band_rows, below[:, 0 : 3 * cols].astype(F32), rows + 3, 3, band_left, band_right, GROUP)

    def band_step(i, carry):
        row = i * step
        put_shifted(band_rows, main[:, span(row, step)].astype(F32), row + 3, step, band_left, band_right, GROUP)
        return carry

    lax.fori_loop(0, rows // step, band_step, 0)

    hidden_left, hidden_right = hidden_side[1], hidden_side[4]

    def hidden_chunk(row, count, mask, keep):
        pre = dot(one_main[...], around(band_rows, row, count))
        gate = sigmoid(pre)
        soft = pre * gate
        if keep:
            slope_one_rate[:, span(row, count)] = gate + soft * (1.0 - gate)
        if mask is not None:
            soft = jnp.where(mask, soft, 0.0)
        put_shifted(hidden_rows, soft.astype(BF16).astype(F32), row, count, hidden_left, hidden_right, feat)

    top_inside, bottom_inside = lat > 0, lat < lat_count - 1
    hidden_chunk(1, 2, top_inside, False)
    hidden_chunk(rows + 3, 2, bottom_inside, False)

    def hidden_step(i, carry):
        hidden_chunk(i * step + 3, step, None, True)
        return carry

    lax.fori_loop(0, rows // step, hidden_step, 0)

    slope_left, slope_right = slope_side

    def label_of(row, count):
        return band_rows[GROUP + bands : GROUP + bands + 1, span(row, count)].astype(F32).astype(jnp.int32)

    for row, mask in ((2, top_inside), (rows + 3, bottom_inside)):
        pre = dot(two_main[...], around(hidden_rows, row, 1))
        slope = head_stage(pre, label_of(row, 1), mask, head_pad[...], head_turn[...], classes)[2]
        put_shifted(slope_rows, slope.astype(BF16).astype(F32), row, 1, slope_left, slope_right, feat)

    def slope_step(i, carry):
        grad_two, grad_head, loss_sum = carry
        row = i * step + 3
        near = around(hidden_rows, row, step)
        pre = dot(two_main[...], near)
        skip, error, slope, loss = head_stage(
            pre, label_of(row, step), None, head_pad[...], head_turn[...], classes
        )
        skip_out[:, span(row - 3, step)] = skip
        slope = slope.astype(BF16)
        grad_two = grad_two + dot_nt(slope, near)
        grad_head = grad_head + dot_nt(skip, error)
        put_shifted(slope_rows, slope.astype(F32), row, step, slope_left, slope_right, feat)
        return grad_two, grad_head, loss_sum + loss

    grad_two, grad_head, loss_sum = lax.fori_loop(
        0,
        rows // step,
        slope_step,
        (
            jnp.zeros((feat, 9 * feat), F32),
            jnp.zeros((feat, GROUP), F32),
            jnp.zeros((1, step * cols), F32),
        ),
    )

    def back_step(i, grad_one):
        row = i * step + 3
        back = dot(two_back[...], around(slope_rows, row, step))
        slope = (back * slope_one_rate[:, span(row, step)]).astype(BF16)
        return grad_one + dot_nt(slope, around(band_rows, row, step))

    grad_one = lax.fori_loop(0, rows // step, back_step, jnp.zeros((feat, 9 * GROUP), F32))

    sums[...] = jnp.zeros_like(sums)
    sums[:, 0 : 9 * feat] = grad_two
    sums[:, 9 * feat : 9 * feat + 9 * GROUP] = grad_one
    at = 9 * feat + 9 * GROUP
    sums[:, at : at + GROUP] = grad_head
    sums[0:1, at + GROUP : at + GROUP + 1] = jnp.sum(loss_sum, axis=1, keepdims=True)
    half = feat // 2
    core = lon % 2
    keep_out[...] = sums[pl.ds(pl.multiple_of(core * half, 8), half), :]
    send_out[...] = sums[pl.ds(pl.multiple_of((1 - core) * half, 8), half), :]


def finish_kernel(pixels, me_ref, own, mate, grad_one, grad_two, grad_head, loss, sums):
    half = own.shape[0]
    feat = 2 * half
    bands = grad_one.shape[2]
    classes = grad_head.shape[0]
    core = me_ref[0] % 2
    scale = 1.0 / pixels
    sums[pl.ds(pl.multiple_of(core * half, 8), half), :] = own[...]
    sums[pl.ds(pl.multiple_of((1 - core) * half, 8), half), :] = mate[...]
    for tap in range(9):
        grad_two[tap] = sums[:, tap * feat : (tap + 1) * feat] * scale
        at = 9 * feat + tap * GROUP
        grad_one[tap] = sums[:, at : at + bands] * scale
    at = 9 * feat + 9 * GROUP
    turned = jnp.transpose(sums[:, at : at + GROUP])
    grad_head[...] = turned[0:classes] * scale
    loss[...] = sums[0:1, at + GROUP : at + GROUP + 1] * scale


def tree_sum(values):
    values = list(values)
    while len(values) > 1:
        values = [values[i] + values[i + 1] for i in range(0, len(values), 2)]
    return values[0]


def body(
    patches,
    requests,
    footprint,
    weight_index,
    composite_weights,
    labels,
    conv1_weight,
    conv2_weight,
    head_weight,
):
    lon_count = lax.axis_size("lon")
    lat_count = lax.axis_size("lat")
    chips = lon_count // 2
    rows, slots = footprint.shape
    cols = labels.shape[1]
    store, row_width = patches.shape
    bands = row_width // cols
    bucket = requests.shape[1] // lon_count
    feat = conv2_weight.shape[1]
    classes = head_weight.shape[0]
    vmem = pl.BlockSpec(memory_space=pltpu.VMEM)
    smem = pl.BlockSpec(memory_space=pltpu.SMEM)

    lon = lax.axis_index("lon")
    place = jnp.stack([lax.axis_index("lat"), lon]).astype(jnp.int32)
    me = lon.astype(jnp.int32).reshape(1)

    def by_lon(value, move):
        return lax.ppermute(value, "lon", [(i, i ^ move) for i in range(lon_count)])

    mate_patches = by_lon(patches, 1)
    plan = call(
        plan_kernel,
        struct((16, 128), F32),
        in_specs=[vmem, vmem, vmem, smem, vmem],
    )(requests, footprint, weight_index, composite_weights, labels)
    plans = lax.all_to_all(
        jnp.broadcast_to(plan[None], (lon_count,) + plan.shape), "lon", split_axis=0, concat_axis=0, tiled=True
    )
    wide = row_width + 2 * rows
    parts = call(
        functools.partial(partial_kernel, rows, slots, bucket, bands),
        [struct((rows, wide), BF16)] * chips,
        [
            pltpu.VMEM((2 * store, row_width), BF16),
            pltpu.VMEM((6 * GROUP, 2 * store), BF16),
            pltpu.VMEM((lon_count + 2, 2 * rows, 2 * store), BF16),
        ],
        in_specs=[smem, vmem, vmem, vmem],
    )(me, plans, patches, mate_patches)
    parts = [parts[0]] + [by_lon(parts[move], 2 * move) for move in range(1, chips)]
    main, strips, upper, lower = call(
        functools.partial(composite_kernel, bands),
        [
            struct((GROUP, rows * cols), BF16),
            struct((10 * GROUP, 128), BF16),
            struct((GROUP, 3 * cols + 128), BF16),
            struct((GROUP, 3 * cols + 128), BF16),
        ],
        [
            pltpu.VMEM((GROUP * rows, cols), F32),
            pltpu.VMEM((10 * GROUP, 128), F32),
            pltpu.VMEM((GROUP, 128), F32),
        ],
        in_specs=[smem] + [vmem] * (2 + chips),
    )(me, plans, labels, *parts)
    below = lax.ppermute(upper, "lat", [(i + 1, i) for i in range(lat_count - 1)])
    above = lax.ppermute(lower, "lat", [(i, i + 1) for i in range(lat_count - 1)])

    weights = call(
        weights_kernel,
        [
            struct((feat, 9 * GROUP), BF16),
            struct((feat, 9 * GROUP), BF16),
            struct((feat, 9 * feat), BF16),
            struct((feat, 9 * feat), BF16),
            struct((feat, 9 * feat), BF16),
            struct((GROUP, feat), BF16),
            struct((feat, GROUP), BF16),
        ],
        [pltpu.VMEM((feat, 9 * feat), F32), pltpu.VMEM((128, 128), F32)],
    )(conv1_weight, conv2_weight, head_weight)

    sum_width = -(-(9 * feat + 9 * GROUP + GROUP + 1) // 128) * 128
    ext = rows + 6
    half = feat // 2
    skip, keep, send = call(
        functools.partial(network_kernel, bands, classes, rows, cols, lat_count, lon_count, 4),
        [
            struct((feat, rows * cols), BF16),
            struct((half, sum_width), F32),
            struct((half, sum_width), F32),
        ],
        [
            pltpu.VMEM((3 * GROUP, ext * cols), BF16),
            pltpu.VMEM((10 * GROUP, 128), F32),
            pltpu.VMEM((3 * feat, ext * cols), BF16),
            pltpu.VMEM((feat, ext * cols), F32),
            pltpu.VMEM((3 * feat, ext * cols), BF16),
            pltpu.VMEM((feat, sum_width), F32),
        ],
        in_specs=[smem] + [vmem] * 11,
    )(place, main, strips, above, below, *weights)

    total = keep + by_lon(send, 1)
    total = tree_sum([total] + [by_lon(total, 2 * move) for move in range(1, chips)])
    total = tree_sum(
        [total]
        + [
            lax.ppermute(total, "lat", [(i, i ^ move) for i in range(lat_count)])
            for move in range(1, lat_count)
        ]
    )
    other = by_lon(total, 1)
    pixels = rows * cols * lat_count * lon_count
    grad_one, grad_two, grad_head, loss = call(
        functools.partial(finish_kernel, pixels),
        [
            struct((9, feat, bands), F32),
            struct((9, feat, feat), F32),
            struct((classes, feat), F32),
            struct((1, 1), F32),
        ],
        [pltpu.VMEM((feat, sum_width), F32)],
        in_specs=[smem, vmem, vmem],
    )(me, total, other)
    return skip.reshape(feat, rows, cols), grad_one, grad_two, grad_head, loss.reshape(())


def solution(mesh):
    placed = (
        P(("lat", "lon"), None),
        P("lat", "lon"),
        P("lat", "lon"),
        P("lat", "lon"),
        P(),
        P("lat", "lon"),
        P(),
        P(),
        P(),
    )
    return jax.shard_map(
        body,
        mesh=mesh,
        in_specs=placed,
        out_specs=(P(None, "lat", "lon"), P(), P(), P(), P()),
        check_vma=False,
    )
```

profile of v0, /device:TPU:1, one launch (start us, length us, event | category | flops | bytes accessed | tf_op | source)
XLA Modules:
  0.0 94.0 jit_solution(4626648625931683176)
XLA Ops:
  0.7 0.1 collective-permute-start
  0.8 0.8 copy.14.footprint
  1.6 0.0 copy-start.5
  1.6 0.1 copy.15.weight_index
  1.7 0.6 copy-done.4
  2.2 0.7 shard_map.128
  3.0 0.7 broadcast_in_dim.2
  3.6 5.3 %all-to-all-start = ((f32[8,16,128]{2,1,0:T(8,128)}), f32[8,16,128]{2,1,0:T(8,128)S(1)}, u32[]{:S(2)}, u32[]{:S(2)}) async-start(f32[8,16,128]{2,1,0:T(8,128)} %broadcast_in_dim.2), calls=%async_computation | async-start | bytes 131072 | tf_op jit(solution)/shard_map/all_to_all | solution.py:470
  8.9 4.2 %all-to-all-done.plans = f32[8,16,128]{2,1,0:T(8,128)S(1)} async-done(((f32[8,16,128]{2,1,0:T(8,128)}), f32[8,16,128]{2,1,0:T(8,128)S(1)}, u32[]{:S(2)}, u32[]{:S(2)}) %all-to-all-start) | async-done | bytes 65568 | tf_op jit(solution)/shard_map/all_to_all | solution.py:470
  13.0 0.0 collective-permute-done.mate
  13.1 1.1 %copy-done = bf16[192,1536]{1,0:T(8,128)(2,1)S(1)} copy-done((bf16[192,1536]{1,0:T(8,128)(2,1)S(1)}, bf16[192,1536]{1,0:T(8,128)(2,1)}, u32[]{:S(2)}) %copy-start) | copy-done | bytes 589848
  14.1 4.8 %shard_map.129 = (bf16[64,1664]{1,0:T(8,128)(2,1)S(1)}, bf16[64,1664]{1,0:T(8,128)(2,1)S(1)}, bf16[64,1664]{1,0:T(8,128)(2,1)S(1)}, bf16[64,1664]{1,0:T(8,128)(2,1)S(1)}) custom-call(s32[1]{0:T(128)} %bitcast.1.me_ref, f32[8,16,128]{2,1,0:T(8,128)S(1)} %all-to-all-done.plans, bf16[192,1536]{1,0:T(8,128)(2,1)S(1)} %copy-done, ...), custom_call_target="tpu_custom_call" | custom-call | tf_op jit(solution)/shard_map/pallas_call | solution.py:474
  18.9 0.6 collective-permute-start.1
  19.5 0.3 collective-permute-start.2
  19.8 1.8 %collective-permute-start.3 = (bf16[64,1664]{1,0:T(8,128)(2,1)S(1)}, bf16[64,1664]{1,0:T(8,128)(2,1)S(1)}, u32[]{:S(2)}, u32[]{:S(2)}) collective-permute-start(bf16[64,1664]{1,0:T(8,128)(2,1)S(1)} %get-tuple-element.30), channel_id=1, source_target_pairs={{0,6},{1,7},{2,4},{3,5},{4,2},{5,3},{6,0},{7,1},{8,14},{9,15},{10,... | collective-permute-start | bytes 638984 | tf_op jit(solution)/shard_map/ppermute | solution.py:462
  21.6 3.3 %collective-permute-done.1.refs_1_ = bf16[64,1664]{1,0:T(8,128)(2,1)S(1)} collective-permute-done((bf16[64,1664]{1,0:T(8,128)(2,1)S(1)}, bf16[64,1664]{1,0:T(8,128)(2,1)S(1)}, u32[]{:S(2)}, u32[]{:S(2)}) %collective-permute-start.1) | collective-permute-done | bytes 213024 | tf_op jit(solution)/shard_map/ppermute | solution.py:462
  24.8 0.8 collective-permute-done.2.refs_2_
  25.6 4.3 %collective-permute-done.3.refs_3_ = bf16[64,1664]{1,0:T(8,128)(2,1)S(1)} collective-permute-done((bf16[64,1664]{1,0:T(8,128)(2,1)S(1)}, bf16[64,1664]{1,0:T(8,128)(2,1)S(1)}, u32[]{:S(2)}, u32[]{:S(2)}) %collective-permute-start.3) | collective-permute-done | bytes 213024 | tf_op jit(solution)/shard_map/ppermute | solution.py:462
  29.9 0.8 shard_map.130
  30.6 0.0 copy-start.1
  30.7 3.4 %collective-permute-start.4 = (bf16[16,512]{1,0:T(8,128)(2,1)S(1)}, bf16[16,512]{1,0:T(8,128)(2,1)S(1)}, u32[]{:S(2)}, u32[]{:S(2)}) collective-permute-start(bf16[16,512]{1,0:T(8,128)(2,1)S(1)} %get-tuple-element.33), channel_id=1, source_target_pairs={{0,8},{8,16},{16,24},{1,9},{9,17},{17,25},{2,10},{10,18},{18,26},{... | collective-permute-start | bytes 49160 | tf_op jit(solution)/shard_map/ppermute | solution.py:501
  34.0 1.3 %collective-permute-start.5 = (bf16[16,512]{1,0:T(8,128)(2,1)S(1)}, bf16[16,512]{1,0:T(8,128)(2,1)S(1)}, u32[]{:S(2)}, u32[]{:S(2)}) collective-permute-start(bf16[16,512]{1,0:T(8,128)(2,1)S(1)} %get-tuple-element.34), channel_id=1, source_target_pairs={{8,0},{16,8},{24,16},{9,1},{17,9},{25,17},{10,2},{18,10},{26,18},{... | collective-permute-start | bytes 49160 | tf_op jit(solution)/shard_map/ppermute | solution.py:500
  35.3 0.1 pad_add_fusion.place
  35.4 0.2 copy.16.conv1
  35.6 0.5 copy-done.3
  36.1 0.3 shard_map.131
  36.4 0.0 collective-permute-done.4.above
  36.4 2.1 %collective-permute-done.5.below = bf16[16,512]{1,0:T(8,128)(2,1)S(1)} collective-permute-done((bf16[16,512]{1,0:T(8,128)(2,1)S(1)}, bf16[16,512]{1,0:T(8,128)(2,1)S(1)}, u32[]{:S(2)}, u32[]{:S(2)}) %collective-permute-start.5) | collective-permute-done | bytes 16416 | tf_op jit(solution)/shard_map/ppermute | solution.py:500
  38.5 27.7 %shard_map.132 = (bf16[64,8192]{1,0:T(8,128)(2,1)S(1)}, f32[32,768]{1,0:T(8,128)S(1)}, f32[32,768]{1,0:T(8,128)S(1)}) custom-call(s32[2]{0:T(128)S(1)} %pad_add_fusion.place, bf16[16,8192]{1,0:T(8,128)(2,1)S(1)} %get-tuple-element.31.main, bf16[160,128]{1,0:T(8,128)(2,1)S(1)} %get-tuple-element.32.strips, bf16[16,512]{1,0:T(8,128)(2,1)S(1)} %collective-permute-done.4.above, ...), custom_call_target="tpu_custom_call" | custom-call | tf_op jit(solution)/shard_map/pallas_call | solution.py:520
  66.2 3.3 %collective-permute-start.6 = (f32[32,768]{1,0:T(8,128)S(1)}, f32[32,768]{1,0:T(8,128)S(1)}, u32[]{:S(2)}, u32[]{:S(2)}) collective-permute-start(f32[32,768]{1,0:T(8,128)S(1)} %get-tuple-element.44), channel_id=1, source_target_pairs={{0,1},{1,0},{2,3},{3,2},{4,5},{5,4},{6,7},{7,6},{8,9},{9,8},{10,11... | collective-permute-start | bytes 294920 | tf_op jit(solution)/shard_map/ppermute | solution.py:462
  69.6 0.9 %collective-permute-done.6 = f32[32,768]{1,0:T(8,128)S(1)} collective-permute-done((f32[32,768]{1,0:T(8,128)S(1)}, f32[32,768]{1,0:T(8,128)S(1)}, u32[]{:S(2)}, u32[]{:S(2)}) %collective-permute-start.6) | collective-permute-done | bytes 98336 | tf_op jit(solution)/shard_map/ppermute | solution.py:462
  70.5 1.2 %collective-permute-start.9 = (f32[32,768]{1,0:T(8,128)S(1)}, f32[32,768]{1,0:T(8,128)S(1)}, u32[]{:S(2)}, u32[]{:S(2)}) collective-permute-start(f32[32,768]{1,0:T(8,128)S(1)} %add.21), channel_id=1, source_target_pairs={{0,6},{1,7},{2,4},{3,5},{4,2},{5,3},{6,0},{7,1},{8,14},{9,15},{10,... | collective-permute-start | bytes 294920 | tf_op jit(solution)/shard_map/ppermute | solution.py:462
  71.7 1.0 %collective-permute-start.8 = (f32[32,768]{1,0:T(8,128)S(1)}, f32[32,768]{1,0:T(8,128)S(1)}, u32[]{:S(2)}, u32[]{:S(2)}) collective-permute-start(f32[32,768]{1,0:T(8,128)S(1)} %add.21), channel_id=1, source_target_pairs={{0,4},{1,5},{2,6},{3,7},{4,0},{5,1},{6,2},{7,3},{8,12},{9,13},{10,... | collective-permute-start | bytes 294920 | tf_op jit(solution)/shard_map/ppermute | solution.py:462
  72.7 0.6 collective-permute-start.7
  73.2 2.3 %collective-permute-done.9 = f32[32,768]{1,0:T(8,128)S(1)} collective-permute-done((f32[32,768]{1,0:T(8,128)S(1)}, f32[32,768]{1,0:T(8,128)S(1)}, u32[]{:S(2)}, u32[]{:S(2)}) %collective-permute-start.9) | collective-permute-done | bytes 98336 | tf_op jit(solution)/shard_map/ppermute | solution.py:462
  75.5 2.8 %collective-permute-done.8 = f32[32,768]{1,0:T(8,128)S(1)} collective-permute-done((f32[32,768]{1,0:T(8,128)S(1)}, f32[32,768]{1,0:T(8,128)S(1)}, u32[]{:S(2)}, u32[]{:S(2)}) %collective-permute-start.8) | collective-permute-done | bytes 98336 | tf_op jit(solution)/shard_map/ppermute | solution.py:462
  78.3 0.0 collective-permute-done.7
  78.3 1.6 %collective-permute-start.12 = (f32[32,768]{1,0:T(8,128)S(1)}, f32[32,768]{1,0:T(8,128)S(1)}, u32[]{:S(2)}, u32[]{:S(2)}) collective-permute-start(f32[32,768]{1,0:T(8,128)S(1)} %add_add_fusion.1), channel_id=1, source_target_pairs={{0,24},{8,16},{16,8},{24,0},{1,25},{9,17},{17,9},{25,1},{2,26},{10... | collective-permute-start | bytes 294920 | tf_op jit(solution)/shard_map/ppermute | solution.py:543
  79.9 1.0 %collective-permute-start.11 = (f32[32,768]{1,0:T(8,128)S(1)}, f32[32,768]{1,0:T(8,128)S(1)}, u32[]{:S(2)}, u32[]{:S(2)}) collective-permute-start(f32[32,768]{1,0:T(8,128)S(1)} %add_add_fusion.1), channel_id=1, source_target_pairs={{0,16},{8,24},{16,0},{24,8},{1,17},{9,25},{17,1},{25,9},{2,18},{10... | collective-permute-start | bytes 294920 | tf_op jit(solution)/shard_map/ppermute | solution.py:543
  80.9 1.1 %collective-permute-start.10 = (f32[32,768]{1,0:T(8,128)S(1)}, f32[32,768]{1,0:T(8,128)S(1)}, u32[]{:S(2)}, u32[]{:S(2)}) collective-permute-start(f32[32,768]{1,0:T(8,128)S(1)} %add_add_fusion.1), channel_id=1, source_target_pairs={{0,8},{8,0},{16,24},{24,16},{1,9},{9,1},{17,25},{25,17},{2,10},{10... | collective-permute-start | bytes 294920 | tf_op jit(solution)/shard_map/ppermute | solution.py:543
  81.9 2.2 %collective-permute-done.12 = f32[32,768]{1,0:T(8,128)S(1)} collective-permute-done((f32[32,768]{1,0:T(8,128)S(1)}, f32[32,768]{1,0:T(8,128)S(1)}, u32[]{:S(2)}, u32[]{:S(2)}) %collective-permute-start.12) | collective-permute-done | bytes 98336 | tf_op jit(solution)/shard_map/ppermute | solution.py:543
  84.1 5.6 %collective-permute-done.11 = f32[32,768]{1,0:T(8,128)S(1)} collective-permute-done((f32[32,768]{1,0:T(8,128)S(1)}, f32[32,768]{1,0:T(8,128)S(1)}, u32[]{:S(2)}, u32[]{:S(2)}) %collective-permute-start.11) | collective-permute-done | bytes 98336 | tf_op jit(solution)/shard_map/ppermute | solution.py:543
  89.7 0.0 collective-permute-done.10
  89.7 1.3 %collective-permute-start.13 = (f32[32,768]{1,0:T(8,128)S(1)}, f32[32,768]{1,0:T(8,128)S(1)}, u32[]{:S(2)}, u32[]{:S(2)}) collective-permute-start(f32[32,768]{1,0:T(8,128)S(1)} %add_add_fusion.own), channel_id=1, source_target_pairs={{0,1},{1,0},{2,3},{3,2},{4,5},{5,4},{6,7},{7,6},{8,9},{9,8},{10,11... | collective-permute-start | bytes 294920 | tf_op jit(solution)/shard_map/ppermute | solution.py:462
  91.0 1.3 %copy.18 = bf16[8,8,64,128]{3,2,1,0:T(8,128)(2,1)} copy(bf16[8,8,64,128]{3,1,2,0:T(8,128)(2,1)S(1)} %bitcast.5) | data formatting | bytes 2097152
  92.3 0.0 collective-permute-done.13.mate
  92.3 0.9 shard_map.133
  93.2 0.8 copy.17
  (14 shorter events, 0.1 us)
Async XLA Ops:
  0.6 0.9 copy-start.7
  0.6 1.0 %copy-start.2 = (s32[64,128]{1,0:T(8,128)S(1)}, s32[64,128]{1,0:T(8,128)}, u32[]{:S(2)}) copy-start(s32[64,128]{1,0:T(8,128)} %labels.3) | copy-start | bytes 98308
  0.7 12.4 %collective-permute-start = (bf16[192,1536]{1,0:T(8,128)(2,1)}, bf16[192,1536]{1,0:T(8,128)(2,1)S(1)}, u32[]{:S(2)}, u32[]{:S(2)}) collective-permute-start(bf16[192,1536]{1,0:T(8,128)(2,1)} %own.1), channel_id=1, source_target_pairs={{0,1},{1,0},{2,3},{3,2},{4,5},{5,4},{6,7},{7,6},{8,9},{9,8},{10,11... | collective-permute-start | bytes 1769480 | tf_op jit(solution)/shard_map/ppermute | solution.py:462
  1.5 0.7 copy-start.4
  1.6 0.7 copy-start.5
  3.6 9.4 %all-to-all-start = ((f32[8,16,128]{2,1,0:T(8,128)}), f32[8,16,128]{2,1,0:T(8,128)S(1)}, u32[]{:S(2)}, u32[]{:S(2)}) async-start(f32[8,16,128]{2,1,0:T(8,128)} %broadcast_in_dim.2), calls=%async_computation | async-start | bytes 131072 | tf_op jit(solution)/shard_map/all_to_all | solution.py:470
  13.1 1.1 %copy-start = (bf16[192,1536]{1,0:T(8,128)(2,1)S(1)}, bf16[192,1536]{1,0:T(8,128)(2,1)}, u32[]{:S(2)}) copy-start(bf16[192,1536]{1,0:T(8,128)(2,1)} %own.1) | copy-start | bytes 1769476
  18.9 6.0 %collective-permute-start.1 = (bf16[64,1664]{1,0:T(8,128)(2,1)S(1)}, bf16[64,1664]{1,0:T(8,128)(2,1)S(1)}, u32[]{:S(2)}, u32[]{:S(2)}) collective-permute-start(bf16[64,1664]{1,0:T(8,128)(2,1)S(1)} %get-tuple-element.28), channel_id=1, source_target_pairs={{0,2},{1,3},{2,0},{3,1},{4,6},{5,7},{6,4},{7,5},{8,10},{9,11},{10,... | collective-permute-start | bytes 638984 | tf_op jit(solution)/shard_map/ppermute | solution.py:462
  19.5 6.1 %collective-permute-start.2 = (bf16[64,1664]{1,0:T(8,128)(2,1)S(1)}, bf16[64,1664]{1,0:T(8,128)(2,1)S(1)}, u32[]{:S(2)}, u32[]{:S(2)}) collective-permute-start(bf16[64,1664]{1,0:T(8,128)(2,1)S(1)} %get-tuple-element.29), channel_id=1, source_target_pairs={{0,4},{1,5},{2,6},{3,7},{4,0},{5,1},{6,2},{7,3},{8,12},{9,13},{10,... | collective-permute-start | bytes 638984 | tf_op jit(solution)/shard_map/ppermute | solution.py:462
  19.8 10.1 %collective-permute-start.3 = (bf16[64,1664]{1,0:T(8,128)(2,1)S(1)}, bf16[64,1664]{1,0:T(8,128)(2,1)S(1)}, u32[]{:S(2)}, u32[]{:S(2)}) collective-permute-start(bf16[64,1664]{1,0:T(8,128)(2,1)S(1)} %get-tuple-element.30), channel_id=1, source_target_pairs={{0,6},{1,7},{2,4},{3,5},{4,2},{5,3},{6,0},{7,1},{8,14},{9,15},{10,... | collective-permute-start | bytes 638984 | tf_op jit(solution)/shard_map/ppermute | solution.py:462
  29.9 5.5 %copy-start.6 = (bf16[9,64,12]{1,2,0:T(8,128)(2,1)S(1)}, bf16[9,64,12]{1,2,0:T(8,128)(2,1)}, u32[]{:S(2)}) copy-start(bf16[9,64,12]{1,2,0:T(8,128)(2,1)} %param.15) | copy-start | bytes 41476
  30.6 4.9 %copy-start.1 = (bf16[9,64,64]{2,1,0:T(8,128)(2,1)S(1)}, bf16[9,64,64]{2,1,0:T(8,128)(2,1)}, u32[]{:S(2)}) copy-start(bf16[9,64,64]{2,1,0:T(8,128)(2,1)} %conv2.1) | copy-start | bytes 221188
  30.7 5.8 %collective-permute-start.4 = (bf16[16,512]{1,0:T(8,128)(2,1)S(1)}, bf16[16,512]{1,0:T(8,128)(2,1)S(1)}, u32[]{:S(2)}, u32[]{:S(2)}) collective-permute-start(bf16[16,512]{1,0:T(8,128)(2,1)S(1)} %get-tuple-element.33), channel_id=1, source_target_pairs={{0,8},{8,16},{16,24},{1,9},{9,17},{17,25},{2,10},{10,18},{18,26},{... | collective-permute-start | bytes 49160 | tf_op jit(solution)/shard_map/ppermute | solution.py:501
  34.0 4.5 %collective-permute-start.5 = (bf16[16,512]{1,0:T(8,128)(2,1)S(1)}, bf16[16,512]{1,0:T(8,128)(2,1)S(1)}, u32[]{:S(2)}, u32[]{:S(2)}) collective-permute-start(bf16[16,512]{1,0:T(8,128)(2,1)S(1)} %get-tuple-element.34), channel_id=1, source_target_pairs={{8,0},{16,8},{24,16},{9,1},{17,9},{25,17},{10,2},{18,10},{26,18},{... | collective-permute-start | bytes 49160 | tf_op jit(solution)/shard_map/ppermute | solution.py:500
  35.4 0.7 copy-start.3
  66.2 4.3 %collective-permute-start.6 = (f32[32,768]{1,0:T(8,128)S(1)}, f32[32,768]{1,0:T(8,128)S(1)}, u32[]{:S(2)}, u32[]{:S(2)}) collective-permute-start(f32[32,768]{1,0:T(8,128)S(1)} %get-tuple-element.44), channel_id=1, source_target_pairs={{0,1},{1,0},{2,3},{3,2},{4,5},{5,4},{6,7},{7,6},{8,9},{9,8},{10,11... | collective-permute-start | bytes 294920 | tf_op jit(solution)/shard_map/ppermute | solution.py:462
  70.5 5.0 %collective-permute-start.9 = (f32[32,768]{1,0:T(8,128)S(1)}, f32[32,768]{1,0:T(8,128)S(1)}, u32[]{:S(2)}, u32[]{:S(2)}) collective-permute-start(f32[32,768]{1,0:T(8,128)S(1)} %add.21), channel_id=1, source_target_pairs={{0,6},{1,7},{2,4},{3,5},{4,2},{5,3},{6,0},{7,1},{8,14},{9,15},{10,... | collective-permute-start | bytes 294920 | tf_op jit(solution)/shard_map/ppermute | solution.py:462
  71.7 6.6 %collective-permute-start.8 = (f32[32,768]{1,0:T(8,128)S(1)}, f32[32,768]{1,0:T(8,128)S(1)}, u32[]{:S(2)}, u32[]{:S(2)}) collective-permute-start(f32[32,768]{1,0:T(8,128)S(1)} %add.21), channel_id=1, source_target_pairs={{0,4},{1,5},{2,6},{3,7},{4,0},{5,1},{6,2},{7,3},{8,12},{9,13},{10,... | collective-permute-start | bytes 294920 | tf_op jit(solution)/shard_map/ppermute | solution.py:462
  72.7 5.7 %collective-permute-start.7 = (f32[32,768]{1,0:T(8,128)S(1)}, f32[32,768]{1,0:T(8,128)S(1)}, u32[]{:S(2)}, u32[]{:S(2)}) collective-permute-start(f32[32,768]{1,0:T(8,128)S(1)} %add.21), channel_id=1, source_target_pairs={{0,2},{1,3},{2,0},{3,1},{4,6},{5,7},{6,4},{7,5},{8,10},{9,11},{10,... | collective-permute-start | bytes 294920 | tf_op jit(solution)/shard_map/ppermute | solution.py:462
  78.3 5.8 %collective-permute-start.12 = (f32[32,768]{1,0:T(8,128)S(1)}, f32[32,768]{1,0:T(8,128)S(1)}, u32[]{:S(2)}, u32[]{:S(2)}) collective-permute-start(f32[32,768]{1,0:T(8,128)S(1)} %add_add_fusion.1), channel_id=1, source_target_pairs={{0,24},{8,16},{16,8},{24,0},{1,25},{9,17},{17,9},{25,1},{2,26},{10... | collective-permute-start | bytes 294920 | tf_op jit(solution)/shard_map/ppermute | solution.py:543
  79.9 9.8 %collective-permute-start.11 = (f32[32,768]{1,0:T(8,128)S(1)}, f32[32,768]{1,0:T(8,128)S(1)}, u32[]{:S(2)}, u32[]{:S(2)}) collective-permute-start(f32[32,768]{1,0:T(8,128)S(1)} %add_add_fusion.1), channel_id=1, source_target_pairs={{0,16},{8,24},{16,0},{24,8},{1,17},{9,25},{17,1},{25,9},{2,18},{10... | collective-permute-start | bytes 294920 | tf_op jit(solution)/shard_map/ppermute | solution.py:543
  80.9 8.8 %collective-permute-start.10 = (f32[32,768]{1,0:T(8,128)S(1)}, f32[32,768]{1,0:T(8,128)S(1)}, u32[]{:S(2)}, u32[]{:S(2)}) collective-permute-start(f32[32,768]{1,0:T(8,128)S(1)} %add_add_fusion.1), channel_id=1, source_target_pairs={{0,8},{8,0},{16,24},{24,16},{1,9},{9,1},{17,25},{25,17},{2,10},{10... | collective-permute-start | bytes 294920 | tf_op jit(solution)/shard_map/ppermute | solution.py:543
  89.7 2.6 %collective-permute-start.13 = (f32[32,768]{1,0:T(8,128)S(1)}, f32[32,768]{1,0:T(8,128)S(1)}, u32[]{:S(2)}, u32[]{:S(2)}) collective-permute-start(f32[32,768]{1,0:T(8,128)S(1)} %add_add_fusion.own), channel_id=1, source_target_pairs={{0,1},{1,0},{2,3},{3,2},{4,5},{5,4},{6,7},{7,6},{8,9},{9,8},{10,11... | collective-permute-start | bytes 294920 | tf_op jit(solution)/shard_map/ppermute | solution.py:462
where the time goes:
time: 94.4 us; the launch traced here: 94 us
  Pallas kernels  35.2 us (37%)
  waiting for transfers between devices  28.3 us (30%)
  starting transfers between devices  23.7 us (25%)
  local copies, waits for them, and re-layouts  5.88 us (6%)
    pallas_call x1, Pallas kernels, body(): call(functools.partial(network_kernel, bands, classes, rows, cols, lat_co...  27.7 us
    ppermute x9, waiting for transfers between devices, by_lon(): return lax.ppermute(value, 'lon', [(i, i ^ move) for i in range(lon_count)])  14.3 us
    ppermute x9, starting transfers between devices, by_lon(): return lax.ppermute(value, 'lon', [(i, i ^ move) for i in range(lon_count)])  10.2 us
    ppermute x3, waiting for transfers between devices, body(): lax.ppermute(total, 'lat', [(i, i ^ move) for i in range(lat_count)])  7.74 us
    all_to_all x1, starting transfers between devices, body(): lax.all_to_all(jnp.broadcast_to(plan[None], (lon_count,) + plan.shape), '...  5.28 us
    unnamed x21, local copies, waits for them, and re-layouts  5.23 us
    pallas_call x1, Pallas kernels, body(): call(functools.partial(partial_kernel, rows, slots, bucket, bands), [stru...  4.76 us
    all_to_all x1, waiting for transfers between devices, body(): lax.all_to_all(jnp.broadcast_to(plan[None], (lon_count,) + plan.shape), '...  4.16 us
  transfers between devices with their start and end apart: 15, of which 10 were waited for; matrix products, arithmetic and copies ran while one was open for 3% of the time, Pallas kernels for 1%

commit v1 on v0

v1 whole, which is shorter than its diff:
```python
import functools

import jax
import jax.numpy as jnp
from jax import lax
from jax.experimental import pallas as pl
from jax.experimental.pallas import tpu as pltpu
from jax.sharding import PartitionSpec as P

BF16 = jnp.bfloat16
F32 = jnp.float32
GROUP = 16
VMEM_LIMIT = 40 * 1024 * 1024


def dot(left, right):
    return lax.dot_general(left, right, (((1,), (0,)), ((), ())), preferred_element_type=F32)


def dot_nt(left, right):
    return lax.dot_general(left, right, (((1,), (1,)), ((), ())), preferred_element_type=F32)


def iota(shape, dim):
    return lax.broadcasted_iota(jnp.int32, shape, dim)


def call(kernel, out_shape, scratch=(), **kwargs):
    return pl.pallas_call(
        kernel,
        out_shape=out_shape,
        scratch_shapes=list(scratch),
        compiler_params=pltpu.CompilerParams(vmem_limit_bytes=VMEM_LIMIT),
        **kwargs,
    )


def struct(shape, dtype):
    return jax.ShapeDtypeStruct(shape, dtype)


def plan_kernel(requests, footprint, weight_index, levels, labels, out):
    slots, rows = footprint.shape
    patch_cols = labels.shape[1]
    foot = footprint[...]
    level_of = weight_index[...]
    weight = jnp.zeros((slots, rows), F32)
    for level in range(levels.shape[0]):
        weight = jnp.where(level_of == level, levels[level], weight)
    weight = jnp.where(foot >= 0, weight, 0.0)
    weight = weight / jnp.sum(weight, axis=0, keepdims=True)
    turned = jnp.transpose(jnp.concatenate([foot.astype(F32), weight], axis=0))
    groups = [turned[group * 8 : group * 8 + 8] for group in range(rows // 8)]
    asked = requests[...].astype(F32)
    asked = [asked[:, part * 128 : (part + 1) * 128] for part in range(requests.shape[1] // 128)]
    lane = iota((8, patch_cols), 1)
    side = iota((8, patch_cols), 0)
    pick = ((side == 0) & (lane == 0)) | ((side == 1) & (lane == patch_cols - 1))
    edges = dot_nt(jnp.where(pick, 1.0, 0.0).astype(BF16), labels[...].astype(F32).astype(BF16))
    edges = jnp.concatenate([edges[0:1], edges[1:2]], axis=1)
    lower = jnp.concatenate(asked + [edges, jnp.zeros((7 - len(asked), 128), F32)], axis=0)
    whole = jnp.concatenate([jnp.concatenate(groups, axis=1), lower], axis=0)
    for target in range(out.shape[0]):
        out[target] = whole


def store_kernel(bands, me_ref, own, mate, stored, edge):
    store, row_width = own.shape
    patch_cols = row_width // bands
    core = me_ref[0] % 2
    stored[pl.ds(pl.multiple_of(core * store, 64), store), :] = own[...]
    stored[pl.ds(pl.multiple_of((1 - core) * store, 64), store), :] = mate[...]
    row_id = iota((6 * GROUP, patch_cols), 0)
    lane_id = iota((6 * GROUP, patch_cols), 1)
    column = row_id // GROUP
    column_lane = jnp.where(column < 3, column + (patch_cols - 3), column - 3)
    at_column = lane_id == column_lane
    total = jnp.zeros(edge.shape, F32)
    for band in range(bands):
        pick = jnp.where(at_column & (row_id % GROUP == band), 1.0, 0.0).astype(BF16)
        total = total + dot_nt(pick, stored[:, band * patch_cols : (band + 1) * patch_cols])
    edge[...] = total.astype(BF16)


def spread_kernel(tile_rows, slots, bucket, store, me_ref, plans, spread):
    count = plans.shape[0]
    chip = me_ref[0] // 2
    zero_tile = jnp.zeros(spread.shape[1:], spread.dtype)
    spread[0] = zero_tile
    spread[count + 1] = zero_tile
    pair = 2 * bucket
    target = (iota((8, pair), 1) + chip * pair).astype(F32)
    store_row = iota((2 * store, pair), 0)
    store_base = jnp.where(iota((2 * store, pair), 1) >= bucket, store, 0)
    relative = (store_row - store_base).astype(F32)
    for tile in range(count):
        groups = []
        for group in range(tile_rows // 8):
            base = group * 2 * slots
            total = jnp.zeros((8, pair), F32)
            for slot in range(slots):
                entry = plans[tile, 0:8, base + slot : base + slot + 1]
                weight = plans[tile, 0:8, base + slots + slot : base + slots + slot + 1]
                total = total + jnp.where(entry == target, weight, 0.0)
            groups.append(total)
        at_place = jnp.concatenate(groups, axis=0)
        if pair == 128:
            asked = plans[tile, pl.ds(8 + chip, 1), :]
        else:
            start = chip * pair
            asked = plans[tile, pl.ds(8 + start // 128, 1), :]
            asked = pltpu.roll(jnp.broadcast_to(asked, (8, 128)), (128 - start % 128) % 128, 1)[0:1, 0:pair]
        hit = jnp.where(relative == asked, 1.0, 0.0).astype(BF16)
        high = at_place.astype(BF16)
        low = (at_place - high.astype(F32)).astype(BF16)
        both = dot_nt(jnp.concatenate([high, low], axis=0), hit)
        over_rows = both[:tile_rows] + both[tile_rows:]
        high = over_rows.astype(BF16)
        low = (over_rows - high.astype(F32)).astype(BF16)
        spread[tile + 1, 0:tile_rows] = high
        spread[tile + 1, tile_rows : 2 * tile_rows] = low


def part_kernel(move, me_ref, spread, stored, edge, out):
    tile_rows = out.shape[0]
    row_width = stored.shape[1]
    me = me_ref[0]
    tile = 2 * jnp.bitwise_xor(me // 2, move) + me % 2
    weights = spread[tile + 1]
    for start in range(0, row_width, 512):
        stop = min(start + 512, row_width)
        both = dot(weights, stored[:, start:stop])
        out[:, start:stop] = (both[:tile_rows] + both[tile_rows:]).astype(BF16)
    left = dot_nt(edge[0 : 3 * GROUP], spread[tile])
    right = dot_nt(edge[3 * GROUP : 6 * GROUP], spread[tile + 2])
    sides = jnp.concatenate(
        [left[:, :tile_rows] + left[:, tile_rows:], right[:, :tile_rows] + right[:, tile_rows:]], axis=1
    )
    out[0 : 3 * GROUP, row_width:] = sides.astype(BF16)
    out[3 * GROUP :, row_width:] = jnp.zeros((tile_rows - 3 * GROUP, 2 * tile_rows), BF16)


def composite_kernel(bands, me_ref, plans, labels, *refs):
    count = plans.shape[0]
    tile_rows, patch_cols = labels.shape
    chips = count // 2
    parts = refs[:chips]
    main, strips, upper, lower, bank, side, bundle = refs[chips:]
    row_width = bands * patch_cols
    me = me_ref[0]
    for band in range(bands):
        columns = slice(band * patch_cols, (band + 1) * patch_cols)
        total = parts[0][:, columns].astype(F32)
        for part in parts[1:]:
            total = total + part[:, columns].astype(F32)
        bank[band * tile_rows : (band + 1) * tile_rows, :] = total
    bank[bands * tile_rows : (bands + 1) * tile_rows, :] = labels[...].astype(F32)
    bank[(bands + 1) * tile_rows : GROUP * tile_rows, :] = jnp.zeros(
        ((GROUP - bands - 1) * tile_rows, patch_cols), F32
    )
    for row in range(tile_rows):
        main[:, row * patch_cols : (row + 1) * patch_cols] = bank[
            pl.ds(row, GROUP, stride=tile_rows), :
        ].astype(BF16)

    far = parts[0][0 : 3 * GROUP, row_width : row_width + 2 * tile_rows].astype(F32)
    for part in parts[1:]:
        far = far + part[0 : 3 * GROUP, row_width : row_width + 2 * tile_rows].astype(F32)
    side[...] = jnp.zeros_like(side)
    side[0 : 3 * GROUP, 3 : 3 + tile_rows] = far[:, :tile_rows]
    side[7 * GROUP : 10 * GROUP, 3 : 3 + tile_rows] = far[:, tile_rows:]
    before = plans[jnp.maximum(me - 1, 0), 12:13, tile_rows : 2 * tile_rows]
    after = plans[jnp.minimum(me + 1, count - 1), 12:13, 0:tile_rows]
    side[2 * GROUP + bands : 2 * GROUP + bands + 1, 3 : 3 + tile_rows] = before
    side[7 * GROUP + bands : 7 * GROUP + bands + 1, 3 : 3 + tile_rows] = after
    row_id = iota((4 * GROUP, patch_cols), 0)
    lane_id = iota((4 * GROUP, patch_cols), 1)
    near = jnp.zeros((4 * GROUP, tile_rows), F32)
    column = row_id // GROUP
    column_lane = jnp.where(column < 2, column, column + (patch_cols - 4))
    for band in range(bands):
        pick = (row_id % GROUP == band) & (lane_id == column_lane)
        tile = bank[band * tile_rows : (band + 1) * tile_rows, :].astype(BF16)
        near = near + dot_nt(jnp.where(pick, 1.0, 0.0).astype(BF16), tile)
    side[3 * GROUP : 7 * GROUP, 3 : 3 + tile_rows] = near
    strips[...] = side[...].astype(BF16)

    for target, start in ((upper, 0), (lower, tile_rows - 3)):
        target[:, 0 : 3 * patch_cols] = main[:, start * patch_cols : (start + 3) * patch_cols]
        bundle[...] = jnp.zeros_like(bundle)
        for column in range(10):
            bundle[:, column * 3 : column * 3 + 3] = side[
                column * GROUP : (column + 1) * GROUP, 3 + start : 6 + start
            ]
        target[:, 3 * patch_cols :] = bundle[...].astype(BF16)


def weights_kernel(conv1, conv2, head, one_main, one_strip, two_main, two_back, head_pad, head_turn, wide, tall):
    bands = conv1.shape[1]
    feat = conv2.shape[1]
    classes = head.shape[0]
    wide[...] = jnp.zeros_like(wide)
    for tap in range(9):
        wide[tap * GROUP : tap * GROUP + bands, :] = conv1[tap].astype(F32)
    one_main[...] = jnp.transpose(wide[...]).astype(BF16)
    for tap in range(9):
        wide[tap * GROUP : tap * GROUP + bands, :] = conv1[(tap % 3) * 3 + tap // 3].astype(F32)
    one_strip[...] = jnp.transpose(wide[...]).astype(BF16)
    for row in range(3):
        at = slice(row * feat, (row + 1) * feat)
        two_main[at, :] = jnp.concatenate([conv2[row * 3 + col] for col in range(3)], axis=1)
        turned = jnp.concatenate([conv2[8 - (row * 3 + col)].astype(F32) for col in range(3)], axis=0)
        two_back[at, :] = jnp.transpose(turned).astype(BF16)
    tall[...] = jnp.zeros_like(tall)
    tall[0:classes, 0:feat] = head[...].astype(F32)
    padded = tall[...]
    head_pad[...] = padded[0:GROUP, 0:feat].astype(BF16)
    head_turn[...] = jnp.transpose(padded)[0:feat, 0:GROUP].astype(BF16)


def sigmoid(value):
    return 0.5 * jnp.tanh(0.5 * value) + 0.5


def head_stage(pre, label, mask, head_pad, head_turn, classes):
    gate = sigmoid(pre)
    soft = pre * gate
    skip = soft.astype(BF16)
    logits = dot(head_pad, skip)
    rank = iota(logits.shape, 0)
    real = rank < classes
    total = jnp.sum(jnp.where(real, jnp.exp(logits), 0.0), axis=0, keepdims=True)
    log_total = jnp.log(total)
    chosen = rank == label
    error = jnp.where(real, jnp.exp(logits - log_total) - jnp.where(chosen, 1.0, 0.0), 0.0)
    error = error.astype(BF16)
    loss = log_total - jnp.sum(jnp.where(chosen, logits, 0.0), axis=0, keepdims=True)
    back = dot(head_turn, error)
    slope = back * (gate + soft * (1.0 - gate))
    if mask is not None:
        slope = jnp.where(mask, slope, 0.0)
    return skip, error, slope.astype(BF16), loss


def span(row, count, cols):
    return slice(row * cols, (row + count) * cols)


def put_shifted(target, value, row, count, left_side, right_side, size, cols):
    lane = iota((1, cols), 1)
    target[size : 2 * size, span(row, count, cols)] = value
    for i in range(count):
        tile = value[:, i * cols : (i + 1) * cols]
        turn = (128 - (row + i)) % 128
        left = pltpu.roll(left_side, turn, 1)
        right = pltpu.roll(right_side, (turn + cols - 1) % 128, 1)
        target[0:size, span(row + i, 1, cols)] = jnp.where(lane == 0, left, pltpu.roll(tile, 1, 1))
        target[2 * size : 3 * size, span(row + i, 1, cols)] = jnp.where(
            lane == cols - 1, right, pltpu.roll(tile, cols - 1, 1)
        )


def above_below(ref, row, count, cols):
    return jnp.concatenate([ref[:, span(row + u, count, cols)] for u in (-1, 0, 1)], axis=0)


def below_above(ref, row, count, cols):
    return jnp.concatenate([ref[:, span(row - u, count, cols)] for u in (-1, 0, 1)], axis=0)


def conv_rows(weight, ref, row, count, cols):
    feat = weight.shape[0] // 3
    near = dot(weight[...], ref[:, span(row - 1, count + 2, cols)])
    return (
        near[0:feat, span(0, count, cols)]
        + near[feat : 2 * feat, span(1, count, cols)]
        + near[2 * feat :, span(2, count, cols)]
    )


def turned_rows(value):
    return jnp.concatenate(
        [pltpu.roll(value, 1, 1), value, pltpu.roll(value, value.shape[1] - 1, 1)], axis=0
    ).astype(BF16)


def strip_inside(place, rows, lat_count, lon_count):
    lat, lon = place[0], place[1]
    lane_row = iota((1, 128), 1) - 3
    inside = (lat * rows + lane_row >= 0) & (lat * rows + lane_row < lat_count * rows)
    inside = inside & (lane_row < rows + 3)
    return inside, inside & (lon > 0), inside & (lon < lon_count - 1)


def strip_hidden(side, one_strip, insides, firsts):
    inside, left_inside, right_inside = insides
    taps = {}
    hidden = []
    for first in firsts:
        for column in range(first, first + 3):
            if column not in taps:
                taps[column] = turned_rows(side[column * GROUP : (column + 1) * GROUP, :])
        pre = dot(one_strip[...], jnp.concatenate([taps[first + i] for i in range(3)], axis=0))
        mask = left_inside if first in (0, 1) else right_inside if first in (6, 7) else inside
        hidden.append(jnp.where(mask, pre * sigmoid(pre), 0.0).astype(BF16))
    return hidden


def hidden_chunk(one_main, band_rows, hidden_rows, rate, row, count, mask, sides, cols):
    pre = dot(one_main[...], above_below(band_rows, row, count, cols))
    gate = sigmoid(pre)
    soft = pre * gate
    if rate is not None:
        rate[:, span(row - 3, count, cols)] = gate + soft * (1.0 - gate)
    if mask is not None:
        soft = jnp.where(mask, soft, 0.0)
    put_shifted(hidden_rows, soft.astype(BF16), row, count, *sides, pre.shape[0], cols)


def inner_kernel(rows, cols, lat_count, lon_count, step, place, main, strips, one_main, one_strip, band_rows, hidden_rows, rate, side):
    side[...] = strips[...].astype(F32)
    hidden_left, hidden_right = strip_hidden(
        side, one_strip, strip_inside(place, rows, lat_count, lon_count), (1, 6)
    )
    band_sides = (strips[2 * GROUP : 3 * GROUP, :], strips[7 * GROUP : 8 * GROUP, :])
    for row in range(0, rows, step):
        put_shifted(band_rows, main[:, span(row, step, cols)], row + 3, step, *band_sides, GROUP, cols)
    for row in range(4, rows + 2, step):
        count = min(step, rows + 2 - row)
        hidden_chunk(one_main, band_rows, hidden_rows, rate, row, count, None, (hidden_left, hidden_right), cols)


def outer_kernel(
    bands, classes, rows, cols, lat_count, lon_count, step,
    place, strips, above, below, band_in, hidden_in, rate_in,
    one_main, one_strip, two_main, two_back, head_pad, head_turn,
    skip_out, keep_out, send_out,
    band_rows, side, hidden_rows, rate, slope_rows, slope_own, sums,
):
    feat = head_turn.shape[0]
    lat, lon = place[0], place[1]
    band_rows[:, span(3, rows, cols)] = band_in[:, span(3, rows, cols)]
    hidden_rows[:, span(4, rows - 2, cols)] = hidden_in[:, span(4, rows - 2, cols)]
    rate[:, span(1, rows - 2, cols)] = rate_in[:, span(1, rows - 2, cols)]

    side[...] = strips[...].astype(F32)
    up_tail = above[:, 3 * cols :].astype(F32)
    down_tail = below[:, 3 * cols :].astype(F32)
    for column in range(10):
        at = slice(column * GROUP, (column + 1) * GROUP)
        side[at, 0:3] = up_tail[:, column * 3 : column * 3 + 3]
        side[at, 3 + rows : 6 + rows] = down_tail[:, column * 3 : column * 3 + 3]

    insides = strip_inside(place, rows, lat_count, lon_count)
    hidden_side = strip_hidden(side, one_strip, insides, (0, 1, 2, 5, 6, 7))
    hidden_taps = [turned_rows(value.astype(F32)) for value in hidden_side]
    slope_side = []
    for first, label_column, inside in ((0, 2, insides[1]), (3, 7, insides[2])):
        pre = None
        for col in range(3):
            weight = jnp.concatenate(
                [two_main[u * feat : (u + 1) * feat, col * feat : (col + 1) * feat] for u in range(3)], axis=1
            )
            term = dot(weight, hidden_taps[first + col])
            pre = term if pre is None else pre + term
        at = label_column * GROUP + bands
        label = side[at : at + 1, :].astype(jnp.int32)
        slope_side.append(head_stage(pre, label, inside, head_pad[...], head_turn[...], classes)[2])

    band_sides = (
        side[2 * GROUP : 3 * GROUP, :].astype(BF16),
        side[7 * GROUP : 8 * GROUP, :].astype(BF16),
    )
    put_shifted(band_rows, above[:, 0 : 3 * cols], 0, 3, *band_sides, GROUP, cols)
    put_shifted(band_rows, below[:, 0 : 3 * cols], rows + 3, 3, *band_sides, GROUP, cols)

    top_inside, bottom_inside = lat > 0, lat < lat_count - 1
    hidden_sides = (hidden_side[1], hidden_side[4])
    hidden_chunk(one_main, band_rows, hidden_rows, None, 1, 2, top_inside, hidden_sides, cols)
    hidden_chunk(one_main, band_rows, hidden_rows, rate, 3, 1, None, hidden_sides, cols)
    hidden_chunk(one_main, band_rows, hidden_rows, rate, rows + 2, 1, None, hidden_sides, cols)
    hidden_chunk(one_main, band_rows, hidden_rows, None, rows + 3, 2, bottom_inside, hidden_sides, cols)

    def label_of(row, count):
        return band_rows[GROUP + bands : GROUP + bands + 1, span(row, count, cols)].astype(F32).astype(jnp.int32)

    for row, mask in ((2, top_inside), (rows + 3, bottom_inside)):
        pre = conv_rows(two_main, hidden_rows, row, 1, cols)
        slope = head_stage(pre, label_of(row, 1), mask, head_pad[...], head_turn[...], classes)[2]
        put_shifted(slope_rows, slope, row, 1, *slope_side, feat, cols)

    for row in (1, rows + 3):
        slope_own[:, span(row, 2, cols)] = jnp.zeros((feat, 2 * cols), BF16)
    grad_head = jnp.zeros((feat, GROUP), F32)
    loss_sum = jnp.zeros((1, 1), F32)
    for row in range(3, rows + 3, step):
        pre = conv_rows(two_main, hidden_rows, row, step, cols)
        skip, error, slope, loss = head_stage(
            pre, label_of(row, step), None, head_pad[...], head_turn[...], classes
        )
        skip_out[:, span(row - 3, step, cols)] = skip
        slope_own[:, span(row, step, cols)] = slope
        grad_head = grad_head + dot_nt(skip, error)
        put_shifted(slope_rows, slope, row, step, *slope_side, feat, cols)
        loss_sum = loss_sum + jnp.sum(loss, axis=1, keepdims=True)

    def grad_of(slope_ref, value_ref):
        total = None
        for row in range(2, rows + 4, 11):
            count = min(11, rows + 4 - row)
            term = dot_nt(below_above(slope_ref, row, count, cols), value_ref[:, span(row, count, cols)])
            total = term if total is None else total + term
        return total

    sums[...] = jnp.zeros_like(sums)
    sums[:, 0 : 3 * feat] = grad_of(slope_own, hidden_rows)
    for row in range(3, rows + 3, step):
        back = conv_rows(two_back, slope_rows, row, step, cols)
        slope_own[:, span(row, step, cols)] = (back * rate[:, span(row - 3, step, cols)]).astype(BF16)
    sums[:, 3 * feat : 3 * feat + 3 * GROUP] = grad_of(slope_own, band_rows)
    at = 3 * feat + 3 * GROUP
    sums[0:feat, at : at + GROUP] = grad_head
    sums[feat : feat + 1, at : at + 1] = loss_sum
    half = 3 * feat // 2
    core = lon % 2
    keep_out[...] = sums[pl.ds(pl.multiple_of(core * half, 8), half), :]
    send_out[...] = sums[pl.ds(pl.multiple_of((1 - core) * half, 8), half), :]


def finish_kernel(pixels, me_ref, own, mate, grad_one, grad_two, grad_head, loss, sums):
    half = own.shape[0]
    feat = grad_two.shape[1]
    bands = grad_one.shape[1]
    classes = grad_head.shape[0]
    core = me_ref[0] % 2
    scale = 1.0 / pixels
    sums[pl.ds(pl.multiple_of(core * half, 8), half), :] = own[...] * scale
    sums[pl.ds(pl.multiple_of((1 - core) * half, 8), half), :] = mate[...] * scale
    at = 3 * feat
    turned = jnp.transpose(sums[:, at : at + 3 * GROUP + GROUP])
    for tap in range(9):
        u, v = tap // 3, tap % 3
        grad_two[tap] = sums[u * feat : (u + 1) * feat, v * feat : (v + 1) * feat]
        grad_one[tap] = turned[v * GROUP : v * GROUP + bands, u * feat : (u + 1) * feat]
    grad_head[...] = turned[3 * GROUP : 3 * GROUP + classes, 0:feat]
    loss[...] = turned[3 * GROUP : 3 * GROUP + 1, feat : feat + 1]


def tree_sum(values):
    values = list(values)
    while len(values) > 1:
        values = [values[i] + values[i + 1] for i in range(0, len(values), 2)]
    return values[0]


def body(
    patches,
    requests,
    footprint,
    weight_index,
    composite_weights,
    labels,
    conv1_weight,
    conv2_weight,
    head_weight,
):
    lon_count = lax.axis_size("lon")
    lat_count = lax.axis_size("lat")
    chips = lon_count // 2
    rows, slots = footprint.shape
    cols = labels.shape[1]
    store, row_width = patches.shape
    bands = row_width // cols
    bucket = requests.shape[1] // lon_count
    feat = conv2_weight.shape[1]
    classes = head_weight.shape[0]
    vmem = pl.BlockSpec(memory_space=pltpu.VMEM)
    smem = pl.BlockSpec(memory_space=pltpu.SMEM)

    lon = lax.axis_index("lon")
    place = jnp.stack([lax.axis_index("lat"), lon]).astype(jnp.int32)
    me = lon.astype(jnp.int32).reshape(1)

    def by_lon(value, move):
        return lax.ppermute(value, "lon", [(i, i ^ move) for i in range(lon_count)])

    mate_patches = by_lon(patches, 1)
    plan = call(
        plan_kernel,
        struct((lon_count, 16, 128), F32),
        in_specs=[vmem, vmem, vmem, smem, vmem],
    )(requests, footprint.T, weight_index.T, composite_weights, labels)
    plans = lax.all_to_all(plan, "lon", split_axis=0, concat_axis=0, tiled=True)
    stored, edge = call(
        functools.partial(store_kernel, bands),
        [struct((2 * store, row_width), BF16), struct((6 * GROUP, 2 * store), BF16)],
        in_specs=[smem, vmem, vmem],
    )(me, patches, mate_patches)
    spread = call(
        functools.partial(spread_kernel, rows, slots, bucket, store),
        struct((lon_count + 2, 2 * rows, 2 * store), BF16),
        in_specs=[smem, vmem],
    )(me, plans)
    parts = []
    for move in range(chips - 1, -1, -1):
        part = call(
            functools.partial(part_kernel, move),
            struct((rows, row_width + 2 * rows), BF16),
            in_specs=[smem, vmem, vmem, vmem],
        )(me, spread, stored, edge)
        parts.append(by_lon(part, 2 * move) if move else part)
    main, strips, upper, lower = call(
        functools.partial(composite_kernel, bands),
        [
            struct((GROUP, rows * cols), BF16),
            struct((10 * GROUP, 128), BF16),
            struct((GROUP, 3 * cols + 128), BF16),
            struct((GROUP, 3 * cols + 128), BF16),
        ],
        [
            pltpu.VMEM((GROUP * rows, cols), F32),
            pltpu.VMEM((10 * GROUP, 128), F32),
            pltpu.VMEM((GROUP, 128), F32),
        ],
        in_specs=[smem] + [vmem] * (2 + chips),
    )(me, plans, labels, *parts)
    below = lax.ppermute(upper, "lat", [(i + 1, i) for i in range(lat_count - 1)])
    above = lax.ppermute(lower, "lat", [(i, i + 1) for i in range(lat_count - 1)])

    one_main, one_strip, two_main, two_back, head_pad, head_turn = call(
        weights_kernel,
        [
            struct((feat, 9 * GROUP), BF16),
            struct((feat, 9 * GROUP), BF16),
            struct((3 * feat, 3 * feat), BF16),
            struct((3 * feat, 3 * feat), BF16),
            struct((GROUP, feat), BF16),
            struct((feat, GROUP), BF16),
        ],
        [pltpu.VMEM((9 * GROUP, feat), F32), pltpu.VMEM((128, 128), F32)],
    )(conv1_weight.transpose(0, 2, 1), conv2_weight, head_weight)

    ext = rows + 6
    step = 16
    band_rows, hidden_rows, rate = call(
        functools.partial(inner_kernel, rows, cols, lat_count, lon_count, step),
        [
            struct((3 * GROUP, ext * cols), BF16),
            struct((3 * feat, ext * cols), BF16),
            struct((feat, rows * cols), F32),
        ],
        [pltpu.VMEM((10 * GROUP, 128), F32)],
        in_specs=[smem] + [vmem] * 4,
        cost_estimate=pl.CostEstimate(flops=10**8, bytes_accessed=10**7, transcendentals=0),
    )(place, main, strips, one_main, one_strip)
    half = 3 * feat // 2
    sum_width = 3 * feat + 4 * GROUP
    skip, keep, send = call(
        functools.partial(outer_kernel, bands, classes, rows, cols, lat_count, lon_count, step),
        [
            struct((feat, rows * cols), BF16),
            struct((half, sum_width), F32),
            struct((half, sum_width), F32),
        ],
        [
            pltpu.VMEM((3 * GROUP, ext * cols), BF16),
            pltpu.VMEM((10 * GROUP, 128), F32),
            pltpu.VMEM((3 * feat, ext * cols), BF16),
            pltpu.VMEM((feat, rows * cols), F32),
            pltpu.VMEM((3 * feat, ext * cols), BF16),
            pltpu.VMEM((feat, ext * cols), BF16),
            pltpu.VMEM((3 * feat, sum_width), F32),
        ],
        in_specs=[smem] + [vmem] * 12,
    )(
        place, strips, above, below, band_rows, hidden_rows, rate,
        one_main, one_strip, two_main, two_back, head_pad, head_turn,
    )

    total = keep + by_lon(send, 1)
    total = tree_sum([total] + [by_lon(total, 2 * move) for move in range(1, chips)])
    sent = total.astype(BF16)
    total = tree_sum(
        [sent.astype(F32)]
        + [
            lax.ppermute(sent, "lat", [(i, i ^ move) for i in range(lat_count)]).astype(F32)
            for move in range(1, lat_count)
        ]
    )
    other = by_lon(total, 1)
    pixels = rows * cols * lat_count * lon_count
    grad_one, grad_two, grad_head, loss = call(
        functools.partial(finish_kernel, pixels),
        [
            struct((9, bands, feat), F32),
            struct((9, feat, feat), F32),
            struct((classes, feat), F32),
            struct((1, 1), F32),
        ],
        [pltpu.VMEM((3 * feat, sum_width), F32)],
        in_specs=[smem, vmem, vmem],
    )(me, total, other)
    return skip.reshape(feat, rows, cols), grad_one.transpose(0, 2, 1), grad_two, grad_head, loss.reshape(())


def solution(mesh):
    placed = (
        P(("lat", "lon"), None),
        P("lat", "lon"),
        P("lat", "lon"),
        P("lat", "lon"),
        P(),
        P("lat", "lon"),
        P(),
        P(),
        P(),
    )
    return jax.shard_map(
        body,
        mesh=mesh,
        in_specs=placed,
        out_specs=(P(None, "lat", "lon"), P(), P(), P(), P()),
        check_vma=False,
    )
```

time: 94.4 us -> 74 us (0.78)
  Pallas kernels: 35.2 us -> 19.3 us
  waiting for transfers between devices: 28.3 us -> 22.8 us
  local copies, waits for them, and re-layouts: 5.88 us -> 7.31 us
    pallas_call x4 -> x10, Pallas kernels: 34.1 us -> 18.4 us  [the longest x1 8.37 us: body(): call(functools.partial(outer_kernel, bands, classes, rows, cols, lat_coun...]
    ppermute x3, waiting for transfers between devices: 7.74 us -> 4.02 us  [body(): lax.ppermute(sent, 'lat', [(i, i ^ move) for i in range(lat_count)])]
    unnamed x21, local copies, waits for them, and re-layouts: 5.23 us -> 7.31 us
    ppermute x1, waiting for transfers between devices: 2.08 us -> 0.01 us  [body(): lax.ppermute(upper, 'lat', [(i + 1, i) for i in range(lat_count - 1)])]
  transfers between devices with their start and end apart: 15 -> 15, of which waited for: 10 -> 8; matrix products, arithmetic and copies ran while one was open for 3% -> 2% of each run, Pallas kernels for 1% -> 8%
where the time goes in v1:
time: 74 us; the launch traced here: 73.4 us
  starting transfers between devices  23.1 us (31%)
  waiting for transfers between devices  22.8 us (31%)
  Pallas kernels  19.3 us (26%)
  local copies, waits for them, and re-layouts  7.31 us (10%)
  between operations  0.76 us (1%)
    ppermute x9, waiting for transfers between devices, by_lon(): return lax.ppermute(value, 'lon', [(i, i ^ move) for i in range(lon_count)])  14.6 us
    ppermute x9, starting transfers between devices, by_lon(): return lax.ppermute(value, 'lon', [(i, i ^ move) for i in range(lon_count)])  9.43 us
    pallas_call x1, Pallas kernels, body(): call(functools.partial(outer_kernel, bands, classes, rows, cols, lat_coun...  8.37 us
    unnamed x21, local copies, waits for them, and re-layouts  7.31 us
    all_to_all x1, starting transfers between devices, body(): plans = lax.all_to_all(plan, 'lon', split_axis=0, concat_axis=0, tiled=True)  5.28 us
    all_to_all x1, waiting for transfers between devices, body(): plans = lax.all_to_all(plan, 'lon', split_axis=0, concat_axis=0, tiled=True)  4.16 us
    ppermute x3, waiting for transfers between devices, body(): lax.ppermute(sent, 'lat', [(i, i ^ move) for i in range(lat_count)])  4.02 us
    ppermute x3, starting transfers between devices, body(): lax.ppermute(sent, 'lat', [(i, i ^ move) for i in range(lat_count)])  3.72 us
  transfers between devices with their start and end apart: 15, of which 8 were waited for; matrix products, arithmetic and copies ran while one was open for 2% of the time, Pallas kernels for 8%

profile of v1, /device:TPU:1, one launch (start us, length us, event | category | flops | bytes accessed | tf_op | source)
XLA Modules:
  0.0 73.4 jit_solution(14590781103268073966)
XLA Ops:
  0.6 0.1 collective-permute-start
  0.8 0.8 %copy-done.2 = s32[64,128]{1,0:T(8,128)S(1)} copy-done((s32[64,128]{1,0:T(8,128)S(1)}, s32[64,128]{1,0:T(8,128)}, u32[]{:S(2)}) %copy-start.2) | copy-done | bytes 32792
  1.5 0.7 copy-done.6
  2.2 0.7 copy-done.7
  2.9 0.7 copy-done.8
  3.6 0.7 copy-done.9
  4.2 1.4 %shard_map.128 = f32[8,16,128]{2,1,0:T(8,128)} custom-call(s32[1,512]{1,0:T(1,128)S(1)} %copy-done.8, s32[8,64]{1,0:T(8,128)S(1)} %bitcast.11, s32[8,64]{1,0:T(8,128)S(1)} %bitcast.12, f32[16]{0:T(128)S(1)} %copy-done.9, s32[64,128]{1,0:T(8,128)S(1)} %copy-done.2), custom_call_target="tpu_custom_call" | custom-call | tf_op jit(solution)/shard_map/pallas_call | solution.py:488
  5.6 5.3 %all-to-all-start = ((f32[8,16,128]{2,1,0:T(8,128)}), f32[8,16,128]{2,1,0:T(8,128)S(1)}, u32[]{:S(2)}, u32[]{:S(2)}) async-start(f32[8,16,128]{2,1,0:T(8,128)} %shard_map.128), calls=%async_computation | async-start | bytes 131072 | tf_op jit(solution)/shard_map/all_to_all | solution.py:493
  10.9 4.2 %all-to-all-done.plans = f32[8,16,128]{2,1,0:T(8,128)S(1)} async-done(((f32[8,16,128]{2,1,0:T(8,128)}), f32[8,16,128]{2,1,0:T(8,128)S(1)}, u32[]{:S(2)}, u32[]{:S(2)}) %all-to-all-start) | async-done | bytes 65568 | tf_op jit(solution)/shard_map/all_to_all | solution.py:493
  15.0 2.1 %shard_map.129.spread = bf16[10,128,384]{2,1,0:T(8,128)(2,1)S(1)} custom-call(s32[1]{0:T(128)} %bitcast.1.me_ref, f32[8,16,128]{2,1,0:T(8,128)S(1)} %all-to-all-done.plans), custom_call_target="tpu_custom_call" | custom-call | tf_op jit(solution)/shard_map/pallas_call | solution.py:499
  17.2 0.0 copy-start
  17.2 1.1 %copy-done = bf16[192,1536]{1,0:T(8,128)(2,1)S(1)} copy-done((bf16[192,1536]{1,0:T(8,128)(2,1)S(1)}, bf16[192,1536]{1,0:T(8,128)(2,1)}, u32[]{:S(2)}) %copy-start) | copy-done | bytes 589848
  18.2 0.7 shard_map.130
  18.9 0.6 shard_map.133
  19.5 0.6 shard_map.132
  20.0 1.2 %shard_map.131 = bf16[64,1664]{1,0:T(8,128)(2,1)} custom-call(s32[1]{0:T(128)} %bitcast.1.me_ref, bf16[10,128,384]{2,1,0:T(8,128)(2,1)S(1)} %shard_map.129.spread, bf16[384,1536]{1,0:T(8,128)(2,1)S(1)} %get-tuple-element.27.stored, bf16[96,384]{1,0:T(8,128)(2,1)S(1)} %get-tuple-element.28.edge), custom_call_target="tpu_custom_call" | custom-call | tf_op jit(solution)/shard_map/pallas_call | solution.py:506
  21.3 0.6 collective-permute-start.1
  21.9 1.2 %collective-permute-start.2 = (bf16[64,1664]{1,0:T(8,128)(2,1)S(1)}, bf16[64,1664]{1,0:T(8,128)(2,1)S(1)}, u32[]{:S(2)}, u32[]{:S(2)}) collective-permute-start(bf16[64,1664]{1,0:T(8,128)(2,1)S(1)} %shard_map.132), channel_id=1, source_target_pairs={{0,4},{1,5},{2,6},{3,7},{4,0},{5,1},{6,2},{7,3},{8,12},{9,13},{10,... | collective-permute-start | bytes 638984 | tf_op jit(solution)/shard_map/ppermute | solution.py:485
  23.0 0.9 %collective-permute-start.3 = (bf16[64,1664]{1,0:T(8,128)(2,1)S(1)}, bf16[64,1664]{1,0:T(8,128)(2,1)S(1)}, u32[]{:S(2)}, u32[]{:S(2)}) collective-permute-start(bf16[64,1664]{1,0:T(8,128)(2,1)S(1)} %shard_map.133), channel_id=1, source_target_pairs={{0,2},{1,3},{2,0},{3,1},{4,6},{5,7},{6,4},{7,5},{8,10},{9,11},{10,... | collective-permute-start | bytes 638984 | tf_op jit(solution)/shard_map/ppermute | solution.py:485
  23.9 0.6 shard_map.134.refs_3_
  24.5 3.9 %collective-permute-done.1.refs_0_ = bf16[64,1664]{1,0:T(8,128)(2,1)S(1)} collective-permute-done((bf16[64,1664]{1,0:T(8,128)(2,1)}, bf16[64,1664]{1,0:T(8,128)(2,1)S(1)}, u32[]{:S(2)}, u32[]{:S(2)}) %collective-permute-start.1) | collective-permute-done | bytes 213024 | tf_op jit(solution)/shard_map/ppermute | solution.py:485
  28.4 4.6 %collective-permute-done.2.refs_1_ = bf16[64,1664]{1,0:T(8,128)(2,1)S(1)} collective-permute-done((bf16[64,1664]{1,0:T(8,128)(2,1)S(1)}, bf16[64,1664]{1,0:T(8,128)(2,1)S(1)}, u32[]{:S(2)}, u32[]{:S(2)}) %collective-permute-start.2) | collective-permute-done | bytes 213024 | tf_op jit(solution)/shard_map/ppermute | solution.py:485
  33.0 0.8 %copy-done.3 = s32[64,128]{1,0:T(8,128)S(1)} copy-done((s32[64,128]{1,0:T(8,128)S(1)}, s32[64,128]{1,0:T(8,128)}, u32[]{:S(2)}) %copy-start.3) | copy-done | bytes 32792
  33.8 0.8 %shard_map.135 = (bf16[16,8192]{1,0:T(8,128)(2,1)S(1)}, bf16[160,128]{1,0:T(8,128)(2,1)S(1)}, bf16[16,512]{1,0:T(8,128)(2,1)S(1)}, bf16[16,512]{1,0:T(8,128)(2,1)S(1)}) custom-call(s32[1]{0:T(128)} %bitcast.1.me_ref, f32[8,16,128]{2,1,0:T(8,128)S(1)} %all-to-all-done.plans, s32[64,128]{1,0:T(8,128)S(1)} %copy-done.3, ...), custom_call_target="tpu_custom_call" | custom-call | tf_op jit(solution)/shard_map/pallas_call | solution.py:512
  34.6 3.2 %collective-permute-start.4 = (bf16[16,512]{1,0:T(8,128)(2,1)S(1)}, bf16[16,512]{1,0:T(8,128)(2,1)S(1)}, u32[]{:S(2)}, u32[]{:S(2)}) collective-permute-start(bf16[16,512]{1,0:T(8,128)(2,1)S(1)} %get-tuple-element.30), channel_id=1, source_target_pairs={{0,8},{8,16},{16,24},{1,9},{9,17},{17,25},{2,10},{10,18},{18,26},{... | collective-permute-start | bytes 49160 | tf_op jit(solution)/shard_map/ppermute | solution.py:528
  37.8 1.5 %collective-permute-start.5 = (bf16[16,512]{1,0:T(8,128)(2,1)S(1)}, bf16[16,512]{1,0:T(8,128)(2,1)S(1)}, u32[]{:S(2)}, u32[]{:S(2)}) collective-permute-start(bf16[16,512]{1,0:T(8,128)(2,1)S(1)} %get-tuple-element.31), channel_id=1, source_target_pairs={{8,0},{16,8},{24,16},{9,1},{17,9},{25,17},{10,2},{18,10},{26,18},{... | collective-permute-start | bytes 49160 | tf_op jit(solution)/shard_map/ppermute | solution.py:527
  39.3 0.1 pad_add_fusion.place
  39.3 0.8 %copy-done.4 = bf16[9,64,12]{1,2,0:T(8,128)(2,1)S(1)} copy-done((bf16[9,64,12]{1,2,0:T(8,128)(2,1)S(1)}, bf16[9,64,12]{1,2,0:T(8,128)(2,1)}, u32[]{:S(2)}) %copy-start.4) | copy-done | bytes 13848
  40.1 0.2 shard_map.136
  40.3 2.0 %shard_map.137 = (bf16[48,8960]{1,0:T(8,128)(2,1)S(1)}, bf16[192,8960]{1,0:T(8,128)(2,1)S(1)}, f32[64,8192]{1,0:T(8,128)S(1)}) custom-call(s32[2]{0:T(128)S(1)} %pad_add_fusion.place, bf16[16,8192]{1,0:T(8,128)(2,1)S(1)} %get-tuple-element.32.main, bf16[160,128]{1,0:T(8,128)(2,1)S(1)} %get-tuple-element.29.strips, ...), custom_call_target="tpu_custom_call" | custom-call | flops 100000000 | bytes 10000000 | tf_op jit(solution)/shard_map/pallas_call | solution.py:545
  42.3 8.4 %shard_map.138 = (bf16[64,8192]{1,0:T(8,128)(2,1)S(1)}, f32[96,256]{1,0:T(8,128)S(1)}, f32[96,256]{1,0:T(8,128)S(1)}) custom-call(s32[2]{0:T(128)S(1)} %pad_add_fusion.place, bf16[160,128]{1,0:T(8,128)(2,1)S(1)} %get-tuple-element.29.strips, bf16[16,512]{1,0:T(8,128)(2,1)S(1)} %collective-permute-done.4.above, ...), custom_call_target="tpu_custom_call" | custom-call | tf_op jit(solution)/shard_map/pallas_call | solution.py:558
  50.7 2.5 %collective-permute-start.6 = (f32[96,256]{1,0:T(8,128)S(1)}, f32[96,256]{1,0:T(8,128)S(1)}, u32[]{:S(2)}, u32[]{:S(2)}) collective-permute-start(f32[96,256]{1,0:T(8,128)S(1)} %get-tuple-element.44), channel_id=1, source_target_pairs={{0,1},{1,0},{2,3},{3,2},{4,5},{5,4},{6,7},{7,6},{8,9},{9,8},{10,11... | collective-permute-start | bytes 294920 | tf_op jit(solution)/shard_map/ppermute | solution.py:485
  53.2 0.9 %collective-permute-done.6 = f32[96,256]{1,0:T(8,128)S(1)} collective-permute-done((f32[96,256]{1,0:T(8,128)S(1)}, f32[96,256]{1,0:T(8,128)S(1)}, u32[]{:S(2)}, u32[]{:S(2)}) %collective-permute-start.6) | collective-permute-done | bytes 98336 | tf_op jit(solution)/shard_map/ppermute | solution.py:485
  54.2 1.2 %collective-permute-start.9 = (f32[96,256]{1,0:T(8,128)S(1)}, f32[96,256]{1,0:T(8,128)S(1)}, u32[]{:S(2)}, u32[]{:S(2)}) collective-permute-start(f32[96,256]{1,0:T(8,128)S(1)} %add.21), channel_id=1, source_target_pairs={{0,6},{1,7},{2,4},{3,5},{4,2},{5,3},{6,0},{7,1},{8,14},{9,15},{10,... | collective-permute-start | bytes 294920 | tf_op jit(solution)/shard_map/ppermute | solution.py:485
  55.4 1.1 %collective-permute-start.8 = (f32[96,256]{1,0:T(8,128)S(1)}, f32[96,256]{1,0:T(8,128)S(1)}, u32[]{:S(2)}, u32[]{:S(2)}) collective-permute-start(f32[96,256]{1,0:T(8,128)S(1)} %add.21), channel_id=1, source_target_pairs={{0,4},{1,5},{2,6},{3,7},{4,0},{5,1},{6,2},{7,3},{8,12},{9,13},{10,... | collective-permute-start | bytes 294920 | tf_op jit(solution)/shard_map/ppermute | solution.py:485
  56.5 0.4 collective-permute-start.7
  56.9 2.3 %collective-permute-done.9 = f32[96,256]{1,0:T(8,128)S(1)} collective-permute-done((f32[96,256]{1,0:T(8,128)S(1)}, f32[96,256]{1,0:T(8,128)S(1)}, u32[]{:S(2)}, u32[]{:S(2)}) %collective-permute-start.9) | collective-permute-done | bytes 98336 | tf_op jit(solution)/shard_map/ppermute | solution.py:485
  59.1 2.8 %collective-permute-done.8 = f32[96,256]{1,0:T(8,128)S(1)} collective-permute-done((f32[96,256]{1,0:T(8,128)S(1)}, f32[96,256]{1,0:T(8,128)S(1)}, u32[]{:S(2)}, u32[]{:S(2)}) %collective-permute-start.8) | collective-permute-done | bytes 98336 | tf_op jit(solution)/shard_map/ppermute | solution.py:485
  61.9 0.0 collective-permute-done.7
  62.0 3.4 %collective-permute-start.12 = (bf16[96,256]{1,0:T(8,128)(2,1)S(1)}, bf16[96,256]{1,0:T(8,128)(2,1)S(1)}, u32[]{:S(2)}, u32[]{:S(2)}) collective-permute-start(bf16[96,256]{1,0:T(8,128)(2,1)S(1)} %add_convert_fusion), channel_id=1, source_target_pairs={{0,24},{8,16},{16,8},{24,0},{1,25},{9,17},{17,9},{25,1},{2,26},{10... | collective-permute-start | bytes 147464 | tf_op jit(solution)/shard_map/ppermute | solution.py:586
  65.3 0.4 collective-permute-start.10
  65.7 1.2 %collective-permute-done.12 = bf16[96,256]{1,0:T(8,128)(2,1)S(1)} collective-permute-done((bf16[96,256]{1,0:T(8,128)(2,1)S(1)}, bf16[96,256]{1,0:T(8,128)(2,1)S(1)}, u32[]{:S(2)}, u32[]{:S(2)}) %collective-permute-start.12) | collective-permute-done | bytes 49184 | tf_op jit(solution)/shard_map/ppermute | solution.py:586
  66.9 2.9 %collective-permute-done.11 = bf16[96,256]{1,0:T(8,128)(2,1)S(1)} collective-permute-done((bf16[96,256]{1,0:T(8,128)(2,1)S(1)}, bf16[96,256]{1,0:T(8,128)(2,1)S(1)}, u32[]{:S(2)}, u32[]{:S(2)}) %collective-permute-start.11) | collective-permute-done | bytes 49184 | tf_op jit(solution)/shard_map/ppermute | solution.py:586
  69.7 0.0 collective-permute-done.10
  69.7 1.5 %collective-permute-start.13 = (f32[96,256]{1,0:T(8,128)S(1)}, f32[96,256]{1,0:T(8,128)S(1)}, u32[]{:S(2)}, u32[]{:S(2)}) collective-permute-start(f32[96,256]{1,0:T(8,128)S(1)} %add_add_fusion.own), channel_id=1, source_target_pairs={{0,1},{1,0},{2,3},{3,2},{4,5},{5,4},{6,7},{7,6},{8,9},{9,8},{10,11... | collective-permute-start | bytes 294920 | tf_op jit(solution)/shard_map/ppermute | solution.py:485
  71.2 1.3 %copy.14 = bf16[8,8,64,128]{3,2,1,0:T(8,128)(2,1)} copy(bf16[8,8,64,128]{3,1,2,0:T(8,128)(2,1)S(1)} %bitcast.9) | data formatting | bytes 2097152
  72.4 0.0 collective-permute-done.13.mate
  72.5 1.0 %shard_map.139 = (f32[9,12,64]{2,1,0:T(8,128)}, f32[9,64,64]{2,1,0:T(8,128)}, f32[11,64]{1,0:T(8,128)}, f32[1,1]{1,0:T(1,128)}) custom-call(s32[1]{0:T(128)} %bitcast.1.me_ref, f32[96,256]{1,0:T(8,128)S(1)} %add_add_fusion.own, f32[96,256]{1,0:T(8,128)S(1)} %collective-permute-done.13.mate), custom_call_target="tpu_custom_call" | custom-call | tf_op jit(solution)/shard_map/pallas_call | solution.py:592
  (19 shorter events, 0.1 us)
Async XLA Ops:
  0.6 16.5 %collective-permute-start = (bf16[192,1536]{1,0:T(8,128)(2,1)}, bf16[192,1536]{1,0:T(8,128)(2,1)S(1)}, u32[]{:S(2)}, u32[]{:S(2)}) collective-permute-start(bf16[192,1536]{1,0:T(8,128)(2,1)} %own.1), channel_id=1, source_target_pairs={{0,1},{1,0},{2,3},{3,2},{4,5},{5,4},{6,7},{7,6},{8,9},{9,8},{10,11... | collective-permute-start | bytes 1769480 | tf_op jit(solution)/shard_map/ppermute | solution.py:485
  0.8 0.8 %copy-start.2 = (s32[64,128]{1,0:T(8,128)S(1)}, s32[64,128]{1,0:T(8,128)}, u32[]{:S(2)}) copy-start(s32[64,128]{1,0:T(8,128)} %labels.3) | copy-start | bytes 98308
  1.5 0.7 copy-start.6
  2.2 0.7 copy-start.7
  2.9 0.7 copy-start.8
  3.6 0.7 copy-start.9
  5.6 9.4 %all-to-all-start = ((f32[8,16,128]{2,1,0:T(8,128)}), f32[8,16,128]{2,1,0:T(8,128)S(1)}, u32[]{:S(2)}, u32[]{:S(2)}) async-start(f32[8,16,128]{2,1,0:T(8,128)} %shard_map.128), calls=%async_computation | async-start | bytes 131072 | tf_op jit(solution)/shard_map/all_to_all | solution.py:493
  17.2 1.1 %copy-start = (bf16[192,1536]{1,0:T(8,128)(2,1)S(1)}, bf16[192,1536]{1,0:T(8,128)(2,1)}, u32[]{:S(2)}) copy-start(bf16[192,1536]{1,0:T(8,128)(2,1)} %own.1) | copy-start | bytes 1769476
  21.3 18.1 %copy-start.1 = (bf16[9,64,64]{2,1,0:T(8,128)(2,1)S(1)}, bf16[9,64,64]{2,1,0:T(8,128)(2,1)}, u32[]{:S(2)}) copy-start(bf16[9,64,64]{2,1,0:T(8,128)(2,1)} %conv2.1) | copy-start | bytes 221188
  21.3 18.1 %copy-start.5 = (bf16[11,64]{1,0:T(8,128)(2,1)S(1)}, bf16[11,64]{1,0:T(8,128)(2,1)}, u32[]{:S(2)}) copy-start(bf16[11,64]{1,0:T(8,128)(2,1)} %head.1) | copy-start | bytes 4228
  21.3 7.1 %collective-permute-start.1 = (bf16[64,1664]{1,0:T(8,128)(2,1)}, bf16[64,1664]{1,0:T(8,128)(2,1)S(1)}, u32[]{:S(2)}, u32[]{:S(2)}) collective-permute-start(bf16[64,1664]{1,0:T(8,128)(2,1)} %shard_map.131), channel_id=1, source_target_pairs={{0,6},{1,7},{2,4},{3,5},{4,2},{5,3},{6,0},{7,1},{8,14},{9,15},{10,... | collective-permute-start | bytes 638984 | tf_op jit(solution)/shard_map/ppermute | solution.py:485
  21.9 11.2 %collective-permute-start.2 = (bf16[64,1664]{1,0:T(8,128)(2,1)S(1)}, bf16[64,1664]{1,0:T(8,128)(2,1)S(1)}, u32[]{:S(2)}, u32[]{:S(2)}) collective-permute-start(bf16[64,1664]{1,0:T(8,128)(2,1)S(1)} %shard_map.132), channel_id=1, source_target_pairs={{0,4},{1,5},{2,6},{3,7},{4,0},{5,1},{6,2},{7,3},{8,12},{9,13},{10,... | collective-permute-start | bytes 638984 | tf_op jit(solution)/shard_map/ppermute | solution.py:485
  23.0 10.0 %collective-permute-start.3 = (bf16[64,1664]{1,0:T(8,128)(2,1)S(1)}, bf16[64,1664]{1,0:T(8,128)(2,1)S(1)}, u32[]{:S(2)}, u32[]{:S(2)}) collective-permute-start(bf16[64,1664]{1,0:T(8,128)(2,1)S(1)} %shard_map.133), channel_id=1, source_target_pairs={{0,2},{1,3},{2,0},{3,1},{4,6},{5,7},{6,4},{7,5},{8,10},{9,11},{10,... | collective-permute-start | bytes 638984 | tf_op jit(solution)/shard_map/ppermute | solution.py:485
  33.0 0.8 %copy-start.3 = (s32[64,128]{1,0:T(8,128)S(1)}, s32[64,128]{1,0:T(8,128)}, u32[]{:S(2)}) copy-start(s32[64,128]{1,0:T(8,128)} %labels.3) | copy-start | bytes 98308
  34.6 7.7 %collective-permute-start.4 = (bf16[16,512]{1,0:T(8,128)(2,1)S(1)}, bf16[16,512]{1,0:T(8,128)(2,1)S(1)}, u32[]{:S(2)}, u32[]{:S(2)}) collective-permute-start(bf16[16,512]{1,0:T(8,128)(2,1)S(1)} %get-tuple-element.30), channel_id=1, source_target_pairs={{0,8},{8,16},{16,24},{1,9},{9,17},{17,25},{2,10},{10,18},{18,26},{... | collective-permute-start | bytes 49160 | tf_op jit(solution)/shard_map/ppermute | solution.py:528
  37.8 4.5 %collective-permute-start.5 = (bf16[16,512]{1,0:T(8,128)(2,1)S(1)}, bf16[16,512]{1,0:T(8,128)(2,1)S(1)}, u32[]{:S(2)}, u32[]{:S(2)}) collective-permute-start(bf16[16,512]{1,0:T(8,128)(2,1)S(1)} %get-tuple-element.31), channel_id=1, source_target_pairs={{8,0},{16,8},{24,16},{9,1},{17,9},{25,17},{10,2},{18,10},{26,18},{... | collective-permute-start | bytes 49160 | tf_op jit(solution)/shard_map/ppermute | solution.py:527
  39.3 0.8 %copy-start.4 = (bf16[9,64,12]{1,2,0:T(8,128)(2,1)S(1)}, bf16[9,64,12]{1,2,0:T(8,128)(2,1)}, u32[]{:S(2)}) copy-start(bf16[9,64,12]{1,2,0:T(8,128)(2,1)} %param.15) | copy-start | bytes 41476
  50.7 3.4 %collective-permute-start.6 = (f32[96,256]{1,0:T(8,128)S(1)}, f32[96,256]{1,0:T(8,128)S(1)}, u32[]{:S(2)}, u32[]{:S(2)}) collective-permute-start(f32[96,256]{1,0:T(8,128)S(1)} %get-tuple-element.44), channel_id=1, source_target_pairs={{0,1},{1,0},{2,3},{3,2},{4,5},{5,4},{6,7},{7,6},{8,9},{9,8},{10,11... | collective-permute-start | bytes 294920 | tf_op jit(solution)/shard_map/ppermute | solution.py:485
  54.2 5.0 %collective-permute-start.9 = (f32[96,256]{1,0:T(8,128)S(1)}, f32[96,256]{1,0:T(8,128)S(1)}, u32[]{:S(2)}, u32[]{:S(2)}) collective-permute-start(f32[96,256]{1,0:T(8,128)S(1)} %add.21), channel_id=1, source_target_pairs={{0,6},{1,7},{2,4},{3,5},{4,2},{5,3},{6,0},{7,1},{8,14},{9,15},{10,... | collective-permute-start | bytes 294920 | tf_op jit(solution)/shard_map/ppermute | solution.py:485
  55.4 6.6 %collective-permute-start.8 = (f32[96,256]{1,0:T(8,128)S(1)}, f32[96,256]{1,0:T(8,128)S(1)}, u32[]{:S(2)}, u32[]{:S(2)}) collective-permute-start(f32[96,256]{1,0:T(8,128)S(1)} %add.21), channel_id=1, source_target_pairs={{0,4},{1,5},{2,6},{3,7},{4,0},{5,1},{6,2},{7,3},{8,12},{9,13},{10,... | collective-permute-start | bytes 294920 | tf_op jit(solution)/shard_map/ppermute | solution.py:485
  56.5 5.5 %collective-permute-start.7 = (f32[96,256]{1,0:T(8,128)S(1)}, f32[96,256]{1,0:T(8,128)S(1)}, u32[]{:S(2)}, u32[]{:S(2)}) collective-permute-start(f32[96,256]{1,0:T(8,128)S(1)} %add.21), channel_id=1, source_target_pairs={{0,2},{1,3},{2,0},{3,1},{4,6},{5,7},{6,4},{7,5},{8,10},{9,11},{10,... | collective-permute-start | bytes 294920 | tf_op jit(solution)/shard_map/ppermute | solution.py:485
  62.0 4.9 %collective-permute-start.12 = (bf16[96,256]{1,0:T(8,128)(2,1)S(1)}, bf16[96,256]{1,0:T(8,128)(2,1)S(1)}, u32[]{:S(2)}, u32[]{:S(2)}) collective-permute-start(bf16[96,256]{1,0:T(8,128)(2,1)S(1)} %add_convert_fusion), channel_id=1, source_target_pairs={{0,24},{8,16},{16,8},{24,0},{1,25},{9,17},{17,9},{25,1},{2,26},{10... | collective-permute-start | bytes 147464 | tf_op jit(solution)/shard_map/ppermute | solution.py:586
  65.3 4.4 %collective-permute-start.11 = (bf16[96,256]{1,0:T(8,128)(2,1)S(1)}, bf16[96,256]{1,0:T(8,128)(2,1)S(1)}, u32[]{:S(2)}, u32[]{:S(2)}) collective-permute-start(bf16[96,256]{1,0:T(8,128)(2,1)S(1)} %add_convert_fusion), channel_id=1, source_target_pairs={{0,16},{8,24},{16,0},{24,8},{1,17},{9,25},{17,1},{25,9},{2,18},{10... | collective-permute-start | bytes 147464 | tf_op jit(solution)/shard_map/ppermute | solution.py:586
  65.3 4.4 %collective-permute-start.10 = (bf16[96,256]{1,0:T(8,128)(2,1)S(1)}, bf16[96,256]{1,0:T(8,128)(2,1)S(1)}, u32[]{:S(2)}, u32[]{:S(2)}) collective-permute-start(bf16[96,256]{1,0:T(8,128)(2,1)S(1)} %add_convert_fusion), channel_id=1, source_target_pairs={{0,8},{8,0},{16,24},{24,16},{1,9},{9,1},{17,25},{25,17},{2,10},{10... | collective-permute-start | bytes 147464 | tf_op jit(solution)/shard_map/ppermute | solution.py:586
  69.7 2.7 %collective-permute-start.13 = (f32[96,256]{1,0:T(8,128)S(1)}, f32[96,256]{1,0:T(8,128)S(1)}, u32[]{:S(2)}, u32[]{:S(2)}) collective-permute-start(f32[96,256]{1,0:T(8,128)S(1)} %add_add_fusion.own), channel_id=1, source_target_pairs={{0,1},{1,0},{2,3},{3,2},{4,5},{5,4},{6,7},{7,6},{8,9},{9,8},{10,11... | collective-permute-start | bytes 294920 | tf_op jit(solution)/shard_map/ppermute | solution.py:485

commit v2 on v1

--- a/solution.py
+++ b/solution.py
@@ -10,7 +10,7 @@
 BF16 = jnp.bfloat16
 F32 = jnp.float32
 GROUP = 16
-VMEM_LIMIT = 40 * 1024 * 1024
+VMEM_LIMIT = 28 * 1024 * 1024
 
 
 def dot(left, right):
@@ -25,12 +25,12 @@
     return lax.broadcasted_iota(jnp.int32, shape, dim)
 
 
-def call(kernel, out_shape, scratch=(), **kwargs):
+def call(kernel, out_shape, scratch=(), vmem_limit=VMEM_LIMIT, **kwargs):
     return pl.pallas_call(
         kernel,
         out_shape=out_shape,
         scratch_shapes=list(scratch),
-        compiler_params=pltpu.CompilerParams(vmem_limit_bytes=VMEM_LIMIT),
+        compiler_params=pltpu.CompilerParams(vmem_limit_bytes=vmem_limit),
         **kwargs,
     )
 
@@ -39,9 +39,30 @@
     return jax.ShapeDtypeStruct(shape, dtype)
 
 
-def plan_kernel(requests, footprint, weight_index, levels, labels, out):
+def plan_kernel(
+    store, requests_hbm, footprint_hbm, weight_index_hbm, levels_hbm, labels_hbm, out, labels_out,
+    requests, footprint, weight_index, levels, labels, sems,
+):
+    copies = [
+        pltpu.make_async_copy(source, target, sems.at[i])
+        for i, (source, target) in enumerate(
+            (
+                (footprint_hbm, footprint),
+                (requests_hbm, requests),
+                (weight_index_hbm, weight_index),
+                (levels_hbm, levels),
+                (labels_hbm, labels),
+            )
+        )
+    ]
+    for copy in copies:
+        copy.start()
+    for copy in copies:
+        copy.wait()
     slots, rows = footprint.shape
     patch_cols = labels.shape[1]
+    count = out.shape[0]
+    bucket = requests.shape[1] // count
     foot = footprint[...]
     level_of = weight_index[...]
     weight = jnp.zeros((slots, rows), F32)
@@ -49,19 +70,28 @@
         weight = jnp.where(level_of == level, levels[level], weight)
     weight = jnp.where(foot >= 0, weight, 0.0)
     weight = weight / jnp.sum(weight, axis=0, keepdims=True)
-    turned = jnp.transpose(jnp.concatenate([foot.astype(F32), weight], axis=0))
-    groups = [turned[group * 8 : group * 8 + 8] for group in range(rows // 8)]
+    flat = jnp.concatenate([foot[slot : slot + 1] for slot in range(slots)], axis=1)
+    owner = jnp.right_shift(flat, bucket.bit_length() - 1)
+    place = jnp.bitwise_and(flat, bucket - 1)
+    at_place = jnp.where(iota((bucket, slots * rows), 0) == place, 1.0, 0.0).astype(BF16)
     asked = requests[...].astype(F32)
-    asked = [asked[:, part * 128 : (part + 1) * 128] for part in range(requests.shape[1] // 128)]
+    asked = jnp.concatenate([asked[:, i * bucket : (i + 1) * bucket] for i in range(count)], axis=0)
+    offset = dot(asked.astype(BF16), at_place)
+    offset = jnp.sum(jnp.where(iota(offset.shape, 0) == owner, offset, 0.0), axis=0, keepdims=True)
+    entry = offset + (owner * store).astype(F32)
+    entry = jnp.concatenate([entry[:, slot * rows : (slot + 1) * rows] for slot in range(slots)], axis=0)
+    turned = jnp.transpose(jnp.concatenate([entry, weight], axis=0))
+    groups = jnp.concatenate([turned[group * 8 : group * 8 + 8] for group in range(rows // 8)], axis=1)
     lane = iota((8, patch_cols), 1)
     side = iota((8, patch_cols), 0)
     pick = ((side == 0) & (lane == 0)) | ((side == 1) & (lane == patch_cols - 1))
-    edges = dot_nt(jnp.where(pick, 1.0, 0.0).astype(BF16), labels[...].astype(F32).astype(BF16))
-    edges = jnp.concatenate([edges[0:1], edges[1:2]], axis=1)
-    lower = jnp.concatenate(asked + [edges, jnp.zeros((7 - len(asked), 128), F32)], axis=0)
-    whole = jnp.concatenate([jnp.concatenate(groups, axis=1), lower], axis=0)
-    for target in range(out.shape[0]):
-        out[target] = whole
+    label = labels[...].astype(F32)
+    labels_out[...] = label
+    edges = dot_nt(jnp.where(pick, 1.0, 0.0).astype(BF16), label.astype(BF16))
+    edges = jnp.concatenate([edges, jnp.concatenate([edges[1:2], edges[0:7]], axis=0)], axis=1)
+    for target in range(count):
+        out[target, 0:8, :] = groups
+        out[target, 8:16, :] = edges
 
 
 def store_kernel(bands, me_ref, own, mate, stored, edge):
@@ -82,62 +112,52 @@
     edge[...] = total.astype(BF16)
 
 
-def spread_kernel(tile_rows, slots, bucket, store, me_ref, plans, spread):
+def part_kernel(moves, slots, me_ref, plans, stored, edge, *refs):
+    outs, weights = refs[:-1], refs[-1]
     count = plans.shape[0]
-    chip = me_ref[0] // 2
-    zero_tile = jnp.zeros(spread.shape[1:], spread.dtype)
-    spread[0] = zero_tile
-    spread[count + 1] = zero_tile
-    pair = 2 * bucket
-    target = (iota((8, pair), 1) + chip * pair).astype(F32)
-    store_row = iota((2 * store, pair), 0)
-    store_base = jnp.where(iota((2 * store, pair), 1) >= bucket, store, 0)
-    relative = (store_row - store_base).astype(F32)
-    for tile in range(count):
-        groups = []
+    tile_rows = outs[0].shape[0]
+    held, row_width = stored.shape
+    me = me_ref[0]
+    column = iota((8, held), 1).astype(F32) + (me // 2 * held).astype(F32)
+
+    def put_weights(index, at):
+        there = (index >= 0) & (index < count)
+        entries = plans[jnp.clip(index, 0, count - 1), 0:8, :]
         for group in range(tile_rows // 8):
             base = group * 2 * slots
-            total = jnp.zeros((8, pair), F32)
+            total = jnp.zeros((8, held), F32)
             for slot in range(slots):
-                entry = plans[tile, 0:8, base + slot : base + slot + 1]
-                weight = plans[tile, 0:8, base + slots + slot : base + slots + slot + 1]
-                total = total + jnp.where(entry == target, weight, 0.0)
-            groups.append(total)
-        at_place = jnp.concatenate(groups, axis=0)
-        if pair == 128:
-            asked = plans[tile, pl.ds(8 + chip, 1), :]
+                entry = entries[:, base + slot : base + slot + 1]
+                weight = entries[:, base + slots + slot : base + slots + slot + 1]
+                total = total + jnp.where(entry == column, weight, 0.0)
+            total = jnp.where(there, total, 0.0)
+            high = total.astype(BF16).astype(F32)
+            weights[at, group * 8 : group * 8 + 8, :] = high
+            weights[at, tile_rows + group * 8 : tile_rows + group * 8 + 8, :] = total - high
+
+    if len(moves) > 1:
+        for index in range(-1, count + 1):
+            put_weights(index, index + 1)
+    for move, out in zip(moves, outs, strict=True):
+        tile = 2 * jnp.bitwise_xor(me // 2, move) + me % 2
+        if len(moves) > 1:
+            at = tile + 1
         else:
-            start = chip * pair
-            asked = plans[tile, pl.ds(8 + start // 128, 1), :]
-            asked = pltpu.roll(jnp.broadcast_to(asked, (8, 128)), (128 - start % 128) % 128, 1)[0:1, 0:pair]
-        hit = jnp.where(relative == asked, 1.0, 0.0).astype(BF16)
-        high = at_place.astype(BF16)
-        low = (at_place - high.astype(F32)).astype(BF16)
-        both = dot_nt(jnp.concatenate([high, low], axis=0), hit)
-        over_rows = both[:tile_rows] + both[tile_rows:]
-        high = over_rows.astype(BF16)
-        low = (over_rows - high.astype(F32)).astype(BF16)
-        spread[tile + 1, 0:tile_rows] = high
-        spread[tile + 1, tile_rows : 2 * tile_rows] = low
-
-
-def part_kernel(move, me_ref, spread, stored, edge, out):
-    tile_rows = out.shape[0]
-    row_width = stored.shape[1]
-    me = me_ref[0]
-    tile = 2 * jnp.bitwise_xor(me // 2, move) + me % 2
-    weights = spread[tile + 1]
-    for start in range(0, row_width, 512):
-        stop = min(start + 512, row_width)
-        both = dot(weights, stored[:, start:stop])
-        out[:, start:stop] = (both[:tile_rows] + both[tile_rows:]).astype(BF16)
-    left = dot_nt(edge[0 : 3 * GROUP], spread[tile])
-    right = dot_nt(edge[3 * GROUP : 6 * GROUP], spread[tile + 2])
-    sides = jnp.concatenate(
-        [left[:, :tile_rows] + left[:, tile_rows:], right[:, :tile_rows] + right[:, tile_rows:]], axis=1
-    )
-    out[0 : 3 * GROUP, row_width:] = sides.astype(BF16)
-    out[3 * GROUP :, row_width:] = jnp.zeros((tile_rows - 3 * GROUP, 2 * tile_rows), BF16)
+            at = 1
+            for i in range(3):
+                put_weights(tile - 1 + i, i)
+        row_weights = weights[at].astype(BF16)
+        for start in range(0, row_width, 512):
+            stop = min(start + 512, row_width)
+            both = dot(row_weights, stored[:, start:stop])
+            out[:, start:stop] = (both[:tile_rows] + both[tile_rows:]).astype(out.dtype)
+        left = dot_nt(edge[0 : 3 * GROUP], weights[at - 1].astype(BF16))
+        right = dot_nt(edge[3 * GROUP : 6 * GROUP], weights[at + 1].astype(BF16))
+        sides = jnp.concatenate(
+            [left[:, :tile_rows] + left[:, tile_rows:], right[:, :tile_rows] + right[:, tile_rows:]], axis=1
+        )
+        out[0 : 3 * GROUP, row_width:] = sides.astype(out.dtype)
+        out[3 * GROUP :, row_width:] = jnp.zeros((tile_rows - 3 * GROUP, 2 * tile_rows), out.dtype)
 
 
 def composite_kernel(bands, me_ref, plans, labels, *refs):
@@ -154,7 +174,7 @@
         for part in parts[1:]:
             total = total + part[:, columns].astype(F32)
         bank[band * tile_rows : (band + 1) * tile_rows, :] = total
-    bank[bands * tile_rows : (bands + 1) * tile_rows, :] = labels[...].astype(F32)
+    bank[bands * tile_rows : (bands + 1) * tile_rows, :] = labels[...]
     bank[(bands + 1) * tile_rows : GROUP * tile_rows, :] = jnp.zeros(
         ((GROUP - bands - 1) * tile_rows, patch_cols), F32
     )
@@ -169,8 +189,8 @@
     side[...] = jnp.zeros_like(side)
     side[0 : 3 * GROUP, 3 : 3 + tile_rows] = far[:, :tile_rows]
     side[7 * GROUP : 10 * GROUP, 3 : 3 + tile_rows] = far[:, tile_rows:]
-    before = plans[jnp.maximum(me - 1, 0), 12:13, tile_rows : 2 * tile_rows]
-    after = plans[jnp.minimum(me + 1, count - 1), 12:13, 0:tile_rows]
+    before = plans[jnp.maximum(me - 1, 0), 8:9, tile_rows : 2 * tile_rows]
+    after = plans[jnp.minimum(me + 1, count - 1), 8:9, 0:tile_rows]
     side[2 * GROUP + bands : 2 * GROUP + bands + 1, 3 : 3 + tile_rows] = before
     side[7 * GROUP + bands : 7 * GROUP + bands + 1, 3 : 3 + tile_rows] = after
     row_id = iota((4 * GROUP, patch_cols), 0)
@@ -484,31 +504,42 @@
     def by_lon(value, move):
         return lax.ppermute(value, "lon", [(i, i ^ move) for i in range(lon_count)])
 
+    hbm = pl.BlockSpec(memory_space=pltpu.HBM)
+    plan, tile_labels = call(
+        functools.partial(plan_kernel, store),
+        [struct((lon_count, 16, 128), F32), struct((rows, cols), F32)],
+        [
+            pltpu.VMEM(requests.shape, jnp.int32),
+            pltpu.VMEM((slots, rows), jnp.int32),
+            pltpu.VMEM((slots, rows), jnp.int32),
+            pltpu.SMEM(composite_weights.shape, F32),
+            pltpu.VMEM(labels.shape, jnp.int32),
+            pltpu.SemaphoreType.DMA((5,)),
+        ],
+        vmem_limit=63 * 1024 * 1024,
+        in_specs=[hbm] * 5,
+    )(requests, footprint.T, weight_index.T, composite_weights, labels)
+    plan, patches = lax.optimization_barrier((plan, patches))
     mate_patches = by_lon(patches, 1)
-    plan = call(
-        plan_kernel,
-        struct((lon_count, 16, 128), F32),
-        in_specs=[vmem, vmem, vmem, smem, vmem],
-    )(requests, footprint.T, weight_index.T, composite_weights, labels)
     plans = lax.all_to_all(plan, "lon", split_axis=0, concat_axis=0, tiled=True)
     stored, edge = call(
         functools.partial(store_kernel, bands),
         [struct((2 * store, row_width), BF16), struct((6 * GROUP, 2 * store), BF16)],
         in_specs=[smem, vmem, vmem],
+        cost_estimate=pl.CostEstimate(flops=10**9, bytes_accessed=10**7, transcendentals=0),
     )(me, patches, mate_patches)
-    spread = call(
-        functools.partial(spread_kernel, rows, slots, bucket, store),
-        struct((lon_count + 2, 2 * rows, 2 * store), BF16),
-        in_specs=[smem, vmem],
-    )(me, plans)
+    plans, stored, edge = lax.optimization_barrier((plans, stored, edge))
+    moves = list(range(chips - 1, 0, -1))
     parts = []
-    for move in range(chips - 1, -1, -1):
-        part = call(
-            functools.partial(part_kernel, move),
-            struct((rows, row_width + 2 * rows), BF16),
+    for some in (moves, [0]):
+        parts += call(
+            functools.partial(part_kernel, some, slots),
+            [struct((rows, row_width + 2 * rows), BF16 if move else F32) for move in some],
+            [pltpu.VMEM((lon_count + 2 if len(some) > 1 else 3, 2 * rows, 2 * store), F32)],
             in_specs=[smem, vmem, vmem, vmem],
-        )(me, spread, stored, edge)
-        parts.append(by_lon(part, 2 * move) if move else part)
+            cost_estimate=pl.CostEstimate(flops=10**9, bytes_accessed=10**7, transcendentals=0),
+        )(me, plans, stored, edge)
+    parts = [by_lon(part, 2 * move) for move, part in zip(moves, parts)] + parts[-1:]
     main, strips, upper, lower = call(
         functools.partial(composite_kernel, bands),
         [
@@ -523,7 +554,7 @@
             pltpu.VMEM((GROUP, 128), F32),
         ],
         in_specs=[smem] + [vmem] * (2 + chips),
-    )(me, plans, labels, *parts)
+    )(me, plans, tile_labels, *parts)
     below = lax.ppermute(upper, "lat", [(i + 1, i) for i in range(lat_count - 1)])
     above = lax.ppermute(lower, "lat", [(i, i + 1) for i in range(lat_count - 1)])
 

time: 74 us -> 66.5 us (0.90)
  local copies, waits for them, and re-layouts: 7.31 us -> 2.33 us
  waiting for transfers between devices: 22.8 us -> 20.7 us
    unnamed x21 -> x11, local copies, waits for them, and re-layouts: 7.31 us -> 2.33 us
    all_to_all x1, waiting for transfers between devices: 4.16 us -> 2.39 us  [body(): plans = lax.all_to_all(plan, 'lon', split_axis=0, concat_axis=0, tiled=True)]
    pallas_call x6 -> x3, Pallas kernels: 6.39 us -> 6.15 us  [the longest x2 4.24 us: body(): call(functools.partial(part_kernel, some, slots), [struct((rows, row_widt...]
  transfers between devices with their start and end apart: 15 -> 15, of which waited for: 8 -> 9; matrix products, arithmetic and copies ran while one was open for 2% -> 2% of each run, Pallas kernels for 8% -> 6%
where the time goes in v2:
time: 66.5 us; the launch traced here: 66.2 us
  starting transfers between devices  23.3 us (35%)
  waiting for transfers between devices  20.7 us (31%)
  Pallas kernels  19 us (29%)
  local copies, waits for them, and re-layouts  2.33 us (4%)
  between operations  0.74 us (1%)
    ppermute x9, waiting for transfers between devices, by_lon(): return lax.ppermute(value, 'lon', [(i, i ^ move) for i in range(lon_count)])  14.2 us
    ppermute x9, starting transfers between devices, by_lon(): return lax.ppermute(value, 'lon', [(i, i ^ move) for i in range(lon_count)])  9.7 us
    pallas_call x1, Pallas kernels, body(): call(functools.partial(outer_kernel, bands, classes, rows, cols, lat_coun...  8.28 us
    all_to_all x1, starting transfers between devices, body(): plans = lax.all_to_all(plan, 'lon', split_axis=0, concat_axis=0, tiled=True)  5.28 us
    pallas_call x2, Pallas kernels, body(): call(functools.partial(part_kernel, some, slots), [struct((rows, row_widt...  4.24 us
    ppermute x3, starting transfers between devices, body(): lax.ppermute(sent, 'lat', [(i, i ^ move) for i in range(lat_count)])  3.61 us
    ppermute x3, waiting for transfers between devices, body(): lax.ppermute(sent, 'lat', [(i, i ^ move) for i in range(lat_count)])  3.34 us
    ppermute x1, starting transfers between devices, body(): lax.ppermute(lower, 'lat', [(i, i + 1) for i in range(lat_count - 1)])  3.2 us
  transfers between devices with their start and end apart: 15, of which 9 were waited for; matrix products, arithmetic and copies ran while one was open for 2% of the time, Pallas kernels for 6%

profile of v2, /device:TPU:1, one launch (start us, length us, event | category | flops | bytes accessed | tf_op | source)
XLA Modules:
  0.0 66.2 jit_solution(13304687383452936563)
XLA Ops:
  0.6 1.9 %shard_map.128 = (f32[8,16,128]{2,1,0:T(8,128)}, f32[64,128]{1,0:T(8,128)}) custom-call(s32[1,512]{1,0:T(1,128)} %requests_hbm.1, s32[8,64]{1,0:T(8,128)} %bitcast.12, s32[8,64]{1,0:T(8,128)} %bitcast.13, f32[16]{0:T(128)} %levels_hbm.1, s32[64,128]{1,0:T(8,128)} %labels_hbm.1), custom_call_target="tpu_custom_call" | custom-call | tf_op jit(solution)/shard_map/pallas_call | solution.py:508
  2.6 0.1 collective-permute-start
  2.7 5.3 %all-to-all-start = ((f32[8,16,128]{2,1,0:T(8,128)}), f32[8,16,128]{2,1,0:T(8,128)S(1)}, u32[]{:S(2)}, u32[]{:S(2)}) async-start(f32[8,16,128]{2,1,0:T(8,128)} %get-tuple-element.38), calls=%async_computation | async-start | bytes 131072 | tf_op jit(solution)/shard_map/all_to_all | solution.py:524
  8.0 0.0 collective-permute-done.mate
  8.0 0.0 copy-start.4
  8.0 1.1 %copy-done.4 = bf16[192,1536]{1,0:T(8,128)(2,1)S(1)} copy-done((bf16[192,1536]{1,0:T(8,128)(2,1)S(1)}, bf16[192,1536]{1,0:T(8,128)(2,1)}, u32[]{:S(2)}) %copy-start.4) | copy-done | bytes 589848
  9.0 0.7 %shard_map.129 = (bf16[384,1536]{1,0:T(8,128)(2,1)S(1)}, bf16[96,384]{1,0:T(8,128)(2,1)S(1)}) custom-call(s32[1]{0:T(128)} %bitcast.1.me_ref, bf16[192,1536]{1,0:T(8,128)(2,1)S(1)} %copy-done.4, bf16[192,1536]{1,0:T(8,128)(2,1)S(1)} %collective-permute-done.mate), custom_call_target="tpu_custom_call" | custom-call | flops 1000000000 | bytes 10000000 | tf_op jit(solution)/shard_map/pallas_call | solution.py:525
  9.7 2.4 %all-to-all-done.plans = f32[8,16,128]{2,1,0:T(8,128)S(1)} async-done(((f32[8,16,128]{2,1,0:T(8,128)}), f32[8,16,128]{2,1,0:T(8,128)S(1)}, u32[]{:S(2)}, u32[]{:S(2)}) %all-to-all-start) | async-done | bytes 65568 | tf_op jit(solution)/shard_map/all_to_all | solution.py:524
  12.1 3.1 %shard_map.130 = (bf16[64,1664]{1,0:T(8,128)(2,1)S(1)}, bf16[64,1664]{1,0:T(8,128)(2,1)S(1)}, bf16[64,1664]{1,0:T(8,128)(2,1)S(1)}) custom-call(s32[1]{0:T(128)} %bitcast.1.me_ref, f32[8,16,128]{2,1,0:T(8,128)S(1)} %all-to-all-done.plans, bf16[384,1536]{1,0:T(8,128)(2,1)S(1)} %get-tuple-element.44.stored, bf16[96,384]{1,0:T(8,128)(2,1)S(1)} %get-tuple-element.45.edge), custom_call_target="tpu_custom_call" | custom-call | flops 1000000000 | bytes 10000000 | tf_op jit(solution)/shard_map/pallas_call | solution.py:535
  15.3 0.0 copy-start.2
  15.3 0.6 collective-permute-start.1
  15.9 1.2 %collective-permute-start.2 = (bf16[64,1664]{1,0:T(8,128)(2,1)S(1)}, bf16[64,1664]{1,0:T(8,128)(2,1)S(1)}, u32[]{:S(2)}, u32[]{:S(2)}) collective-permute-start(bf16[64,1664]{1,0:T(8,128)(2,1)S(1)} %get-tuple-element.47), channel_id=1, source_target_pairs={{0,4},{1,5},{2,6},{3,7},{4,0},{5,1},{6,2},{7,3},{8,12},{9,13},{10,... | collective-permute-start | bytes 638984 | tf_op jit(solution)/shard_map/ppermute | solution.py:505
  17.1 0.9 %collective-permute-start.3 = (bf16[64,1664]{1,0:T(8,128)(2,1)S(1)}, bf16[64,1664]{1,0:T(8,128)(2,1)S(1)}, u32[]{:S(2)}, u32[]{:S(2)}) collective-permute-start(bf16[64,1664]{1,0:T(8,128)(2,1)S(1)} %get-tuple-element.48), channel_id=1, source_target_pairs={{0,2},{1,3},{2,0},{3,1},{4,6},{5,7},{6,4},{7,5},{8,10},{9,11},{10,... | collective-permute-start | bytes 638984 | tf_op jit(solution)/shard_map/ppermute | solution.py:505
  18.0 1.1 %shard_map.131.refs_3_ = f32[64,1664]{1,0:T(8,128)S(1)} custom-call(s32[1]{0:T(128)} %bitcast.1.me_ref, f32[8,16,128]{2,1,0:T(8,128)S(1)} %all-to-all-done.plans, bf16[384,1536]{1,0:T(8,128)(2,1)S(1)} %get-tuple-element.44.stored, bf16[96,384]{1,0:T(8,128)(2,1)S(1)} %get-tuple-element.45.edge), custom_call_target="tpu_custom_call" | custom-call | flops 1000000000 | bytes 10000000 | tf_op jit(solution)/shard_map/pallas_call | solution.py:535
  19.1 3.1 %collective-permute-done.1.refs_0_ = bf16[64,1664]{1,0:T(8,128)(2,1)S(1)} collective-permute-done((bf16[64,1664]{1,0:T(8,128)(2,1)S(1)}, bf16[64,1664]{1,0:T(8,128)(2,1)S(1)}, u32[]{:S(2)}, u32[]{:S(2)}) %collective-permute-start.1) | collective-permute-done | bytes 213024 | tf_op jit(solution)/shard_map/ppermute | solution.py:505
  22.2 5.1 %collective-permute-done.2.refs_1_ = bf16[64,1664]{1,0:T(8,128)(2,1)S(1)} collective-permute-done((bf16[64,1664]{1,0:T(8,128)(2,1)S(1)}, bf16[64,1664]{1,0:T(8,128)(2,1)S(1)}, u32[]{:S(2)}, u32[]{:S(2)}) %collective-permute-start.2) | collective-permute-done | bytes 213024 | tf_op jit(solution)/shard_map/ppermute | solution.py:505
  27.3 0.0 collective-permute-done.3.refs_2_
  27.3 0.0 copy-done.2
  27.3 0.8 %shard_map.132 = (bf16[16,8192]{1,0:T(8,128)(2,1)S(1)}, bf16[160,128]{1,0:T(8,128)(2,1)S(1)}, bf16[16,512]{1,0:T(8,128)(2,1)S(1)}, bf16[16,512]{1,0:T(8,128)(2,1)S(1)}) custom-call(s32[1]{0:T(128)} %bitcast.1.me_ref, f32[8,16,128]{2,1,0:T(8,128)S(1)} %all-to-all-done.plans, f32[64,128]{1,0:T(8,128)S(1)} %copy-done.2, ...), custom_call_target="tpu_custom_call" | custom-call | tf_op jit(solution)/shard_map/pallas_call | solution.py:543
  28.1 3.2 %collective-permute-start.4 = (bf16[16,512]{1,0:T(8,128)(2,1)S(1)}, bf16[16,512]{1,0:T(8,128)(2,1)S(1)}, u32[]{:S(2)}, u32[]{:S(2)}) collective-permute-start(bf16[16,512]{1,0:T(8,128)(2,1)S(1)} %get-tuple-element.50), channel_id=1, source_target_pairs={{0,8},{8,16},{16,24},{1,9},{9,17},{17,25},{2,10},{10,18},{18,26},{... | collective-permute-start | bytes 49160 | tf_op jit(solution)/shard_map/ppermute | solution.py:559
  31.3 1.5 %collective-permute-start.5 = (bf16[16,512]{1,0:T(8,128)(2,1)S(1)}, bf16[16,512]{1,0:T(8,128)(2,1)S(1)}, u32[]{:S(2)}, u32[]{:S(2)}) collective-permute-start(bf16[16,512]{1,0:T(8,128)(2,1)S(1)} %get-tuple-element.51), channel_id=1, source_target_pairs={{8,0},{16,8},{24,16},{9,1},{17,9},{25,17},{10,2},{18,10},{26,18},{... | collective-permute-start | bytes 49160 | tf_op jit(solution)/shard_map/ppermute | solution.py:558
  32.8 0.1 pad_add_fusion.place
  32.8 0.0 copy-done
  32.8 0.0 copy-done.1
  32.8 0.0 copy-done.3
  32.9 0.2 shard_map.133
  33.0 2.0 %shard_map.134 = (bf16[48,8960]{1,0:T(8,128)(2,1)S(1)}, bf16[192,8960]{1,0:T(8,128)(2,1)S(1)}, f32[64,8192]{1,0:T(8,128)S(1)}) custom-call(s32[2]{0:T(128)S(1)} %pad_add_fusion.place, bf16[16,8192]{1,0:T(8,128)(2,1)S(1)} %get-tuple-element.52.main, bf16[160,128]{1,0:T(8,128)(2,1)S(1)} %get-tuple-element.49.strips, ...), custom_call_target="tpu_custom_call" | custom-call | flops 100000000 | bytes 10000000 | tf_op jit(solution)/shard_map/pallas_call | solution.py:576
  35.0 0.0 collective-permute-done.4.above
  35.0 0.7 %collective-permute-done.5.below = bf16[16,512]{1,0:T(8,128)(2,1)S(1)} collective-permute-done((bf16[16,512]{1,0:T(8,128)(2,1)S(1)}, bf16[16,512]{1,0:T(8,128)(2,1)S(1)}, u32[]{:S(2)}, u32[]{:S(2)}) %collective-permute-start.5) | collective-permute-done | bytes 16416 | tf_op jit(solution)/shard_map/ppermute | solution.py:558
  35.8 8.3 %shard_map.135 = (bf16[64,8192]{1,0:T(8,128)(2,1)S(1)}, f32[96,256]{1,0:T(8,128)S(1)}, f32[96,256]{1,0:T(8,128)S(1)}) custom-call(s32[2]{0:T(128)S(1)} %pad_add_fusion.place, bf16[160,128]{1,0:T(8,128)(2,1)S(1)} %get-tuple-element.49.strips, bf16[16,512]{1,0:T(8,128)(2,1)S(1)} %collective-permute-done.4.above, ...), custom_call_target="tpu_custom_call" | custom-call | tf_op jit(solution)/shard_map/pallas_call | solution.py:589
  44.1 2.3 %collective-permute-start.6 = (f32[96,256]{1,0:T(8,128)S(1)}, f32[96,256]{1,0:T(8,128)S(1)}, u32[]{:S(2)}, u32[]{:S(2)}) collective-permute-start(f32[96,256]{1,0:T(8,128)S(1)} %get-tuple-element.64), channel_id=1, source_target_pairs={{0,1},{1,0},{2,3},{3,2},{4,5},{5,4},{6,7},{7,6},{8,9},{9,8},{10,11... | collective-permute-start | bytes 294920 | tf_op jit(solution)/shard_map/ppermute | solution.py:505
  46.4 0.9 %collective-permute-done.6 = f32[96,256]{1,0:T(8,128)S(1)} collective-permute-done((f32[96,256]{1,0:T(8,128)S(1)}, f32[96,256]{1,0:T(8,128)S(1)}, u32[]{:S(2)}, u32[]{:S(2)}) %collective-permute-start.6) | collective-permute-done | bytes 98336 | tf_op jit(solution)/shard_map/ppermute | solution.py:505
  47.4 1.0 %collective-permute-start.9 = (f32[96,256]{1,0:T(8,128)S(1)}, f32[96,256]{1,0:T(8,128)S(1)}, u32[]{:S(2)}, u32[]{:S(2)}) collective-permute-start(f32[96,256]{1,0:T(8,128)S(1)} %add.21), channel_id=1, source_target_pairs={{0,6},{1,7},{2,4},{3,5},{4,2},{5,3},{6,0},{7,1},{8,14},{9,15},{10,... | collective-permute-start | bytes 294920 | tf_op jit(solution)/shard_map/ppermute | solution.py:505
  48.4 1.1 %collective-permute-start.8 = (f32[96,256]{1,0:T(8,128)S(1)}, f32[96,256]{1,0:T(8,128)S(1)}, u32[]{:S(2)}, u32[]{:S(2)}) collective-permute-start(f32[96,256]{1,0:T(8,128)S(1)} %add.21), channel_id=1, source_target_pairs={{0,4},{1,5},{2,6},{3,7},{4,0},{5,1},{6,2},{7,3},{8,12},{9,13},{10,... | collective-permute-start | bytes 294920 | tf_op jit(solution)/shard_map/ppermute | solution.py:505
  49.5 0.6 collective-permute-start.7
  50.1 2.3 %collective-permute-done.9 = f32[96,256]{1,0:T(8,128)S(1)} collective-permute-done((f32[96,256]{1,0:T(8,128)S(1)}, f32[96,256]{1,0:T(8,128)S(1)}, u32[]{:S(2)}, u32[]{:S(2)}) %collective-permute-start.9) | collective-permute-done | bytes 98336 | tf_op jit(solution)/shard_map/ppermute | solution.py:505
  52.4 2.8 %collective-permute-done.8 = f32[96,256]{1,0:T(8,128)S(1)} collective-permute-done((f32[96,256]{1,0:T(8,128)S(1)}, f32[96,256]{1,0:T(8,128)S(1)}, u32[]{:S(2)}, u32[]{:S(2)}) %collective-permute-start.8) | collective-permute-done | bytes 98336 | tf_op jit(solution)/shard_map/ppermute | solution.py:505
  55.1 0.0 collective-permute-done.7
  55.2 2.6 %collective-permute-start.12 = (bf16[96,256]{1,0:T(8,128)(2,1)S(1)}, bf16[96,256]{1,0:T(8,128)(2,1)S(1)}, u32[]{:S(2)}, u32[]{:S(2)}) collective-permute-start(bf16[96,256]{1,0:T(8,128)(2,1)S(1)} %add_convert_fusion), channel_id=1, source_target_pairs={{0,24},{8,16},{16,8},{24,0},{1,25},{9,17},{17,9},{25,1},{2,26},{10... | collective-permute-start | bytes 147464 | tf_op jit(solution)/shard_map/ppermute | solution.py:617
  57.8 0.0 collective-permute-start.11
  57.8 1.0 %collective-permute-start.10 = (bf16[96,256]{1,0:T(8,128)(2,1)S(1)}, bf16[96,256]{1,0:T(8,128)(2,1)S(1)}, u32[]{:S(2)}, u32[]{:S(2)}) collective-permute-start(bf16[96,256]{1,0:T(8,128)(2,1)S(1)} %add_convert_fusion), channel_id=1, source_target_pairs={{0,8},{8,0},{16,24},{24,16},{1,9},{9,1},{17,25},{25,17},{2,10},{10... | collective-permute-start | bytes 147464 | tf_op jit(solution)/shard_map/ppermute | solution.py:617
  58.8 1.2 %collective-permute-done.12 = bf16[96,256]{1,0:T(8,128)(2,1)S(1)} collective-permute-done((bf16[96,256]{1,0:T(8,128)(2,1)S(1)}, bf16[96,256]{1,0:T(8,128)(2,1)S(1)}, u32[]{:S(2)}, u32[]{:S(2)}) %collective-permute-start.12) | collective-permute-done | bytes 49184 | tf_op jit(solution)/shard_map/ppermute | solution.py:617
  60.0 2.1 %collective-permute-done.11 = bf16[96,256]{1,0:T(8,128)(2,1)S(1)} collective-permute-done((bf16[96,256]{1,0:T(8,128)(2,1)S(1)}, bf16[96,256]{1,0:T(8,128)(2,1)S(1)}, u32[]{:S(2)}, u32[]{:S(2)}) %collective-permute-start.11) | collective-permute-done | bytes 49184 | tf_op jit(solution)/shard_map/ppermute | solution.py:617
  62.1 0.0 collective-permute-done.10
  62.2 1.8 %collective-permute-start.13 = (f32[96,256]{1,0:T(8,128)S(1)}, f32[96,256]{1,0:T(8,128)S(1)}, u32[]{:S(2)}, u32[]{:S(2)}) collective-permute-start(f32[96,256]{1,0:T(8,128)S(1)} %add_add_fusion.own), channel_id=1, source_target_pairs={{0,1},{1,0},{2,3},{3,2},{4,5},{5,4},{6,7},{7,6},{8,9},{9,8},{10,11... | collective-permute-start | bytes 294920 | tf_op jit(solution)/shard_map/ppermute | solution.py:505
  64.0 1.3 %copy.14 = bf16[8,8,64,128]{3,2,1,0:T(8,128)(2,1)} copy(bf16[8,8,64,128]{3,1,2,0:T(8,128)(2,1)S(1)} %bitcast.9) | data formatting | bytes 2097152
  65.2 0.0 collective-permute-done.13.mate
  65.2 1.0 %shard_map.136 = (f32[9,12,64]{2,1,0:T(8,128)}, f32[9,64,64]{2,1,0:T(8,128)}, f32[11,64]{1,0:T(8,128)}, f32[1,1]{1,0:T(1,128)}) custom-call(s32[1]{0:T(128)} %bitcast.1.me_ref, f32[96,256]{1,0:T(8,128)S(1)} %add_add_fusion.own, f32[96,256]{1,0:T(8,128)S(1)} %collective-permute-done.13.mate), custom_call_target="tpu_custom_call" | custom-call | tf_op jit(solution)/shard_map/pallas_call | solution.py:623
  (6 shorter events, 0.1 us)
Async XLA Ops:
  2.6 5.4 %collective-permute-start = (bf16[192,1536]{1,0:T(8,128)(2,1)}, bf16[192,1536]{1,0:T(8,128)(2,1)S(1)}, u32[]{:S(2)}, u32[]{:S(2)}) collective-permute-start(bf16[192,1536]{1,0:T(8,128)(2,1)} %own), channel_id=1, source_target_pairs={{0,1},{1,0},{2,3},{3,2},{4,5},{5,4},{6,7},{7,6},{8,9},{9,8},{10,11... | collective-permute-start | bytes 1769480 | tf_op jit(solution)/shard_map/ppermute | solution.py:505
  2.7 9.4 %all-to-all-start = ((f32[8,16,128]{2,1,0:T(8,128)}), f32[8,16,128]{2,1,0:T(8,128)S(1)}, u32[]{:S(2)}, u32[]{:S(2)}) async-start(f32[8,16,128]{2,1,0:T(8,128)} %get-tuple-element.38), calls=%async_computation | async-start | bytes 131072 | tf_op jit(solution)/shard_map/all_to_all | solution.py:524
  8.0 1.1 %copy-start.4 = (bf16[192,1536]{1,0:T(8,128)(2,1)S(1)}, bf16[192,1536]{1,0:T(8,128)(2,1)}, u32[]{:S(2)}) copy-start(bf16[192,1536]{1,0:T(8,128)(2,1)} %own) | copy-start | bytes 1769476
  15.3 12.0 %copy-start.2 = (f32[64,128]{1,0:T(8,128)S(1)}, f32[64,128]{1,0:T(8,128)}, u32[]{:S(2)}) copy-start(f32[64,128]{1,0:T(8,128)} %get-tuple-element.43.labels) | copy-start | bytes 98308
  15.3 7.0 %collective-permute-start.1 = (bf16[64,1664]{1,0:T(8,128)(2,1)S(1)}, bf16[64,1664]{1,0:T(8,128)(2,1)S(1)}, u32[]{:S(2)}, u32[]{:S(2)}) collective-permute-start(bf16[64,1664]{1,0:T(8,128)(2,1)S(1)} %get-tuple-element.46), channel_id=1, source_target_pairs={{0,6},{1,7},{2,4},{3,5},{4,2},{5,3},{6,0},{7,1},{8,14},{9,15},{10,... | collective-permute-start | bytes 638984 | tf_op jit(solution)/shard_map/ppermute | solution.py:505
  15.9 11.4 %collective-permute-start.2 = (bf16[64,1664]{1,0:T(8,128)(2,1)S(1)}, bf16[64,1664]{1,0:T(8,128)(2,1)S(1)}, u32[]{:S(2)}, u32[]{:S(2)}) collective-permute-start(bf16[64,1664]{1,0:T(8,128)(2,1)S(1)} %get-tuple-element.47), channel_id=1, source_target_pairs={{0,4},{1,5},{2,6},{3,7},{4,0},{5,1},{6,2},{7,3},{8,12},{9,13},{10,... | collective-permute-start | bytes 638984 | tf_op jit(solution)/shard_map/ppermute | solution.py:505
  17.1 10.2 %collective-permute-start.3 = (bf16[64,1664]{1,0:T(8,128)(2,1)S(1)}, bf16[64,1664]{1,0:T(8,128)(2,1)S(1)}, u32[]{:S(2)}, u32[]{:S(2)}) collective-permute-start(bf16[64,1664]{1,0:T(8,128)(2,1)S(1)} %get-tuple-element.48), channel_id=1, source_target_pairs={{0,2},{1,3},{2,0},{3,1},{4,6},{5,7},{6,4},{7,5},{8,10},{9,11},{10,... | collective-permute-start | bytes 638984 | tf_op jit(solution)/shard_map/ppermute | solution.py:505
  18.0 14.9 %copy-start = (bf16[9,64,64]{2,1,0:T(8,128)(2,1)S(1)}, bf16[9,64,64]{2,1,0:T(8,128)(2,1)}, u32[]{:S(2)}) copy-start(bf16[9,64,64]{2,1,0:T(8,128)(2,1)} %conv2.1) | copy-start | bytes 221188
  18.0 14.9 %copy-start.1 = (bf16[9,64,12]{1,2,0:T(8,128)(2,1)S(1)}, bf16[9,64,12]{1,2,0:T(8,128)(2,1)}, u32[]{:S(2)}) copy-start(bf16[9,64,12]{1,2,0:T(8,128)(2,1)} %param.15) | copy-start | bytes 41476
  18.0 14.9 %copy-start.3 = (bf16[11,64]{1,0:T(8,128)(2,1)S(1)}, bf16[11,64]{1,0:T(8,128)(2,1)}, u32[]{:S(2)}) copy-start(bf16[11,64]{1,0:T(8,128)(2,1)} %head.1) | copy-start | bytes 4228
  28.1 7.0 %collective-permute-start.4 = (bf16[16,512]{1,0:T(8,128)(2,1)S(1)}, bf16[16,512]{1,0:T(8,128)(2,1)S(1)}, u32[]{:S(2)}, u32[]{:S(2)}) collective-permute-start(bf16[16,512]{1,0:T(8,128)(2,1)S(1)} %get-tuple-element.50), channel_id=1, source_target_pairs={{0,8},{8,16},{16,24},{1,9},{9,17},{17,25},{2,10},{10,18},{18,26},{... | collective-permute-start | bytes 49160 | tf_op jit(solution)/shard_map/ppermute | solution.py:559
  31.3 4.5 %collective-permute-start.5 = (bf16[16,512]{1,0:T(8,128)(2,1)S(1)}, bf16[16,512]{1,0:T(8,128)(2,1)S(1)}, u32[]{:S(2)}, u32[]{:S(2)}) collective-permute-start(bf16[16,512]{1,0:T(8,128)(2,1)S(1)} %get-tuple-element.51), channel_id=1, source_target_pairs={{8,0},{16,8},{24,16},{9,1},{17,9},{25,17},{10,2},{18,10},{26,18},{... | collective-permute-start | bytes 49160 | tf_op jit(solution)/shard_map/ppermute | solution.py:558
  44.1 3.3 %collective-permute-start.6 = (f32[96,256]{1,0:T(8,128)S(1)}, f32[96,256]{1,0:T(8,128)S(1)}, u32[]{:S(2)}, u32[]{:S(2)}) collective-permute-start(f32[96,256]{1,0:T(8,128)S(1)} %get-tuple-element.64), channel_id=1, source_target_pairs={{0,1},{1,0},{2,3},{3,2},{4,5},{5,4},{6,7},{7,6},{8,9},{9,8},{10,11... | collective-permute-start | bytes 294920 | tf_op jit(solution)/shard_map/ppermute | solution.py:505
  47.4 5.0 %collective-permute-start.9 = (f32[96,256]{1,0:T(8,128)S(1)}, f32[96,256]{1,0:T(8,128)S(1)}, u32[]{:S(2)}, u32[]{:S(2)}) collective-permute-start(f32[96,256]{1,0:T(8,128)S(1)} %add.21), channel_id=1, source_target_pairs={{0,6},{1,7},{2,4},{3,5},{4,2},{5,3},{6,0},{7,1},{8,14},{9,15},{10,... | collective-permute-start | bytes 294920 | tf_op jit(solution)/shard_map/ppermute | solution.py:505
  48.4 6.8 %collective-permute-start.8 = (f32[96,256]{1,0:T(8,128)S(1)}, f32[96,256]{1,0:T(8,128)S(1)}, u32[]{:S(2)}, u32[]{:S(2)}) collective-permute-start(f32[96,256]{1,0:T(8,128)S(1)} %add.21), channel_id=1, source_target_pairs={{0,4},{1,5},{2,6},{3,7},{4,0},{5,1},{6,2},{7,3},{8,12},{9,13},{10,... | collective-permute-start | bytes 294920 | tf_op jit(solution)/shard_map/ppermute | solution.py:505
  49.5 5.6 %collective-permute-start.7 = (f32[96,256]{1,0:T(8,128)S(1)}, f32[96,256]{1,0:T(8,128)S(1)}, u32[]{:S(2)}, u32[]{:S(2)}) collective-permute-start(f32[96,256]{1,0:T(8,128)S(1)} %add.21), channel_id=1, source_target_pairs={{0,2},{1,3},{2,0},{3,1},{4,6},{5,7},{6,4},{7,5},{8,10},{9,11},{10,... | collective-permute-start | bytes 294920 | tf_op jit(solution)/shard_map/ppermute | solution.py:505
  55.2 4.8 %collective-permute-start.12 = (bf16[96,256]{1,0:T(8,128)(2,1)S(1)}, bf16[96,256]{1,0:T(8,128)(2,1)S(1)}, u32[]{:S(2)}, u32[]{:S(2)}) collective-permute-start(bf16[96,256]{1,0:T(8,128)(2,1)S(1)} %add_convert_fusion), channel_id=1, source_target_pairs={{0,24},{8,16},{16,8},{24,0},{1,25},{9,17},{17,9},{25,1},{2,26},{10... | collective-permute-start | bytes 147464 | tf_op jit(solution)/shard_map/ppermute | solution.py:617
  57.8 4.4 %collective-permute-start.11 = (bf16[96,256]{1,0:T(8,128)(2,1)S(1)}, bf16[96,256]{1,0:T(8,128)(2,1)S(1)}, u32[]{:S(2)}, u32[]{:S(2)}) collective-permute-start(bf16[96,256]{1,0:T(8,128)(2,1)S(1)} %add_convert_fusion), channel_id=1, source_target_pairs={{0,16},{8,24},{16,0},{24,8},{1,17},{9,25},{17,1},{25,9},{2,18},{10... | collective-permute-start | bytes 147464 | tf_op jit(solution)/shard_map/ppermute | solution.py:617
  57.8 4.4 %collective-permute-start.10 = (bf16[96,256]{1,0:T(8,128)(2,1)S(1)}, bf16[96,256]{1,0:T(8,128)(2,1)S(1)}, u32[]{:S(2)}, u32[]{:S(2)}) collective-permute-start(bf16[96,256]{1,0:T(8,128)(2,1)S(1)} %add_convert_fusion), channel_id=1, source_target_pairs={{0,8},{8,0},{16,24},{24,16},{1,9},{9,1},{17,25},{25,17},{2,10},{10... | collective-permute-start | bytes 147464 | tf_op jit(solution)/shard_map/ppermute | solution.py:617
  62.2 3.1 %collective-permute-start.13 = (f32[96,256]{1,0:T(8,128)S(1)}, f32[96,256]{1,0:T(8,128)S(1)}, u32[]{:S(2)}, u32[]{:S(2)}) collective-permute-start(f32[96,256]{1,0:T(8,128)S(1)} %add_add_fusion.own), channel_id=1, source_target_pairs={{0,1},{1,0},{2,3},{3,2},{4,5},{5,4},{6,7},{7,6},{8,9},{9,8},{10,11... | collective-permute-start | bytes 294920 | tf_op jit(solution)/shard_map/ppermute | solution.py:505

commit v3 on v2

--- a/solution.py
+++ b/solution.py
@@ -80,18 +80,17 @@
     offset = jnp.sum(jnp.where(iota(offset.shape, 0) == owner, offset, 0.0), axis=0, keepdims=True)
     entry = offset + (owner * store).astype(F32)
     entry = jnp.concatenate([entry[:, slot * rows : (slot + 1) * rows] for slot in range(slots)], axis=0)
-    turned = jnp.transpose(jnp.concatenate([entry, weight], axis=0))
-    groups = jnp.concatenate([turned[group * 8 : group * 8 + 8] for group in range(rows // 8)], axis=1)
     lane = iota((8, patch_cols), 1)
     side = iota((8, patch_cols), 0)
     pick = ((side == 0) & (lane == 0)) | ((side == 1) & (lane == patch_cols - 1))
     label = labels[...].astype(F32)
     labels_out[...] = label
     edges = dot_nt(jnp.where(pick, 1.0, 0.0).astype(BF16), label.astype(BF16))
-    edges = jnp.concatenate([edges, jnp.concatenate([edges[1:2], edges[0:7]], axis=0)], axis=1)
+    entries = jnp.concatenate([entry, edges], axis=1)
+    weights = jnp.concatenate([weight, jnp.zeros_like(weight)], axis=1)
     for target in range(count):
-        out[target, 0:8, :] = groups
-        out[target, 8:16, :] = edges
+        out[target, 0:slots, :] = entries
+        out[target, slots : 2 * slots, :] = weights
 
 
 def store_kernel(bands, me_ref, own, mate, stored, edge):
@@ -112,52 +111,53 @@
     edge[...] = total.astype(BF16)
 
 
-def part_kernel(moves, slots, me_ref, plans, stored, edge, *refs):
-    outs, weights = refs[:-1], refs[-1]
-    count = plans.shape[0]
-    tile_rows = outs[0].shape[0]
+def put_weights(plans, chip, first, target):
+    held, lanes = target.shape
+    rows = lanes // 2
+    slots = plans.shape[1] // 2
+    both = jnp.concatenate([plans[2 * chip, :, 0:rows], plans[2 * chip + 1, :, 0:rows]], axis=1)
+    entries, weights = both[0:slots] - first, both[slots:]
+    for start in range(0, held, 64):
+        stored_row = (iota((64, lanes), 0) + start).astype(F32)
+        total = jnp.zeros((64, lanes), F32)
+        for slot in range(slots):
+            total = total + jnp.where(entries[slot : slot + 1] == stored_row, weights[slot : slot + 1], 0.0)
+        target[start : start + 64, :] = total
+
+
+def high_low(value):
+    high = value.astype(BF16)
+    return high, (value - high.astype(F32)).astype(BF16)
+
+
+def part_kernel(moves, me_ref, plans, stored, edge, *refs):
+    outs, (over, turned, sides) = refs[:-3], refs[-3:]
+    chips = plans.shape[0] // 2
+    rows = outs[0].shape[0]
     held, row_width = stored.shape
     me = me_ref[0]
-    column = iota((8, held), 1).astype(F32) + (me // 2 * held).astype(F32)
-
-    def put_weights(index, at):
-        there = (index >= 0) & (index < count)
-        entries = plans[jnp.clip(index, 0, count - 1), 0:8, :]
-        for group in range(tile_rows // 8):
-            base = group * 2 * slots
-            total = jnp.zeros((8, held), F32)
-            for slot in range(slots):
-                entry = entries[:, base + slot : base + slot + 1]
-                weight = entries[:, base + slots + slot : base + slots + slot + 1]
-                total = total + jnp.where(entry == column, weight, 0.0)
-            total = jnp.where(there, total, 0.0)
-            high = total.astype(BF16).astype(F32)
-            weights[at, group * 8 : group * 8 + 8, :] = high
-            weights[at, tile_rows + group * 8 : tile_rows + group * 8 + 8, :] = total - high
-
-    if len(moves) > 1:
-        for index in range(-1, count + 1):
-            put_weights(index, index + 1)
+    here, core = me // 2, me % 2
+    first = (here * held).astype(F32)
+    sides[0] = jnp.zeros(sides.shape[1:], F32)
+    sides[chips + 1] = jnp.zeros(sides.shape[1:], F32)
+    for chip in range(chips):
+        put_weights(plans, chip, first, over.at[chip])
+        high, low = high_low(over[chip])
+        sides[chip + 1] = dot(edge[...], high) + dot(edge[...], low)
     for move, out in zip(moves, outs, strict=True):
-        tile = 2 * jnp.bitwise_xor(me // 2, move) + me % 2
-        if len(moves) > 1:
-            at = tile + 1
-        else:
-            at = 1
-            for i in range(3):
-                put_weights(tile - 1 + i, i)
-        row_weights = weights[at].astype(BF16)
+        chip = jnp.bitwise_xor(here, move)
+        turned[...] = jnp.transpose(over[chip])
+        high, low = high_low(turned[pl.ds(pl.multiple_of(core * rows, 8), rows), :])
+        both = jnp.concatenate([high, low], axis=0)
         for start in range(0, row_width, 512):
             stop = min(start + 512, row_width)
-            both = dot(row_weights, stored[:, start:stop])
-            out[:, start:stop] = (both[:tile_rows] + both[tile_rows:]).astype(out.dtype)
-        left = dot_nt(edge[0 : 3 * GROUP], weights[at - 1].astype(BF16))
-        right = dot_nt(edge[3 * GROUP : 6 * GROUP], weights[at + 1].astype(BF16))
-        sides = jnp.concatenate(
-            [left[:, :tile_rows] + left[:, tile_rows:], right[:, :tile_rows] + right[:, tile_rows:]], axis=1
-        )
-        out[0 : 3 * GROUP, row_width:] = sides.astype(out.dtype)
-        out[3 * GROUP :, row_width:] = jnp.zeros((tile_rows - 3 * GROUP, 2 * tile_rows), out.dtype)
+            product = dot(both, stored[:, start:stop])
+            out[:, start:stop] = (product[:rows] + product[rows:]).astype(out.dtype)
+        near, before, after = sides[chip + 1], sides[chip], sides[chip + 2]
+        left = jnp.where(core == 1, near[0 : 3 * GROUP, 0:rows], before[0 : 3 * GROUP, rows:])
+        right = jnp.where(core == 0, near[3 * GROUP :, rows:], after[3 * GROUP :, 0:rows])
+        out[0 : 3 * GROUP, row_width:] = jnp.concatenate([left, right], axis=1).astype(out.dtype)
+        out[3 * GROUP :, row_width:] = jnp.zeros((rows - 3 * GROUP, 2 * rows), out.dtype)
 
 
 def composite_kernel(bands, me_ref, plans, labels, *refs):
@@ -189,8 +189,8 @@
     side[...] = jnp.zeros_like(side)
     side[0 : 3 * GROUP, 3 : 3 + tile_rows] = far[:, :tile_rows]
     side[7 * GROUP : 10 * GROUP, 3 : 3 + tile_rows] = far[:, tile_rows:]
-    before = plans[jnp.maximum(me - 1, 0), 8:9, tile_rows : 2 * tile_rows]
-    after = plans[jnp.minimum(me + 1, count - 1), 8:9, 0:tile_rows]
+    before = plans[jnp.maximum(me - 1, 0), 1:2, tile_rows : 2 * tile_rows]
+    after = plans[jnp.minimum(me + 1, count - 1), 0:1, tile_rows : 2 * tile_rows]
     side[2 * GROUP + bands : 2 * GROUP + bands + 1, 3 : 3 + tile_rows] = before
     side[7 * GROUP + bands : 7 * GROUP + bands + 1, 3 : 3 + tile_rows] = after
     row_id = iota((4 * GROUP, patch_cols), 0)
@@ -315,14 +315,19 @@
 def strip_hidden(side, one_strip, insides, firsts):
     inside, left_inside, right_inside = insides
     taps = {}
-    hidden = []
     for first in firsts:
         for column in range(first, first + 3):
             if column not in taps:
                 taps[column] = turned_rows(side[column * GROUP : (column + 1) * GROUP, :])
-        pre = dot(one_strip[...], jnp.concatenate([taps[first + i] for i in range(3)], axis=0))
+    near = jnp.concatenate(
+        [jnp.concatenate([taps[first + i] for first in firsts], axis=1) for i in range(3)], axis=0
+    )
+    pre = dot(one_strip[...], near)
+    soft = pre * sigmoid(pre)
+    hidden = []
+    for i, first in enumerate(firsts):
         mask = left_inside if first in (0, 1) else right_inside if first in (6, 7) else inside
-        hidden.append(jnp.where(mask, pre * sigmoid(pre), 0.0).astype(BF16))
+        hidden.append(jnp.where(mask, soft[:, i * 128 : (i + 1) * 128], 0.0))
     return hidden
 
 
@@ -339,15 +344,16 @@
 
 def inner_kernel(rows, cols, lat_count, lon_count, step, place, main, strips, one_main, one_strip, band_rows, hidden_rows, rate, side):
     side[...] = strips[...].astype(F32)
-    hidden_left, hidden_right = strip_hidden(
-        side, one_strip, strip_inside(place, rows, lat_count, lon_count), (1, 6)
-    )
+    hidden_sides = [
+        hidden.astype(BF16)
+        for hidden in strip_hidden(side, one_strip, strip_inside(place, rows, lat_count, lon_count), (1, 6))
+    ]
     band_sides = (strips[2 * GROUP : 3 * GROUP, :], strips[7 * GROUP : 8 * GROUP, :])
     for row in range(0, rows, step):
         put_shifted(band_rows, main[:, span(row, step, cols)], row + 3, step, *band_sides, GROUP, cols)
     for row in range(4, rows + 2, step):
         count = min(step, rows + 2 - row)
-        hidden_chunk(one_main, band_rows, hidden_rows, rate, row, count, None, (hidden_left, hidden_right), cols)
+        hidden_chunk(one_main, band_rows, hidden_rows, rate, row, count, None, hidden_sides, cols)
 
 
 def outer_kernel(
@@ -373,19 +379,14 @@
 
     insides = strip_inside(place, rows, lat_count, lon_count)
     hidden_side = strip_hidden(side, one_strip, insides, (0, 1, 2, 5, 6, 7))
-    hidden_taps = [turned_rows(value.astype(F32)) for value in hidden_side]
-    slope_side = []
-    for first, label_column, inside in ((0, 2, insides[1]), (3, 7, insides[2])):
-        pre = None
-        for col in range(3):
-            weight = jnp.concatenate(
-                [two_main[u * feat : (u + 1) * feat, col * feat : (col + 1) * feat] for u in range(3)], axis=1
-            )
-            term = dot(weight, hidden_taps[first + col])
-            pre = term if pre is None else pre + term
-        at = label_column * GROUP + bands
-        label = side[at : at + 1, :].astype(jnp.int32)
-        slope_side.append(head_stage(pre, label, inside, head_pad[...], head_turn[...], classes)[2])
+    hidden_taps = [turned_rows(value) for value in hidden_side]
+    strip_pre = None
+    for col in range(3):
+        weight = jnp.concatenate(
+            [two_main[u * feat : (u + 1) * feat, col * feat : (col + 1) * feat] for u in range(3)], axis=1
+        )
+        term = dot(weight, jnp.concatenate([hidden_taps[col], hidden_taps[3 + col]], axis=1))
+        strip_pre = term if strip_pre is None else strip_pre + term
 
     band_sides = (
         side[2 * GROUP : 3 * GROUP, :].astype(BF16),
@@ -395,19 +396,42 @@
     put_shifted(band_rows, below[:, 0 : 3 * cols], rows + 3, 3, *band_sides, GROUP, cols)
 
     top_inside, bottom_inside = lat > 0, lat < lat_count - 1
-    hidden_sides = (hidden_side[1], hidden_side[4])
-    hidden_chunk(one_main, band_rows, hidden_rows, None, 1, 2, top_inside, hidden_sides, cols)
-    hidden_chunk(one_main, band_rows, hidden_rows, rate, 3, 1, None, hidden_sides, cols)
-    hidden_chunk(one_main, band_rows, hidden_rows, rate, rows + 2, 1, None, hidden_sides, cols)
-    hidden_chunk(one_main, band_rows, hidden_rows, None, rows + 3, 2, bottom_inside, hidden_sides, cols)
+    hidden_sides = (hidden_side[1].astype(BF16), hidden_side[4].astype(BF16))
+    near = jnp.concatenate(
+        [above_below(band_rows, 1, 3, cols), above_below(band_rows, rows + 2, 3, cols)], axis=1
+    )
+    pre = dot(one_main[...], near)
+    gate = sigmoid(pre)
+    soft = pre * gate
+    ends = gate + soft * (1.0 - gate)
+    rate[:, span(0, 1, cols)] = ends[:, span(2, 1, cols)]
+    rate[:, span(rows - 1, 1, cols)] = ends[:, span(3, 1, cols)]
+    lane = iota((1, 6 * cols), 1)
+    soft = jnp.where(((lane >= 2 * cols) | top_inside) & ((lane < 4 * cols) | bottom_inside), soft, 0.0)
+    soft = soft.astype(BF16)
+    put_shifted(hidden_rows, soft[:, span(0, 3, cols)], 1, 3, *hidden_sides, feat, cols)
+    put_shifted(hidden_rows, soft[:, span(3, 3, cols)], rows + 2, 3, *hidden_sides, feat, cols)
 
     def label_of(row, count):
         return band_rows[GROUP + bands : GROUP + bands + 1, span(row, count, cols)].astype(F32).astype(jnp.int32)
 
-    for row, mask in ((2, top_inside), (rows + 3, bottom_inside)):
-        pre = conv_rows(two_main, hidden_rows, row, 1, cols)
-        slope = head_stage(pre, label_of(row, 1), mask, head_pad[...], head_turn[...], classes)[2]
-        put_shifted(slope_rows, slope, row, 1, *slope_side, feat, cols)
+    pre = [conv_rows(two_main, hidden_rows, row, 1, cols) for row in (2, rows + 3)]
+    label = [side[c * GROUP + bands : c * GROUP + bands + 1, :].astype(jnp.int32) for c in (2, 7)]
+    label += [label_of(row, 1) for row in (2, rows + 3)]
+    ones = jnp.ones((1, cols), jnp.int32)
+    mask = [jnp.where(inside, 1, 0) for inside in insides[1:]]
+    mask += [jnp.where(inside, ones, 0) for inside in (top_inside, bottom_inside)]
+    slope = head_stage(
+        jnp.concatenate([strip_pre] + pre, axis=1),
+        jnp.concatenate(label, axis=1),
+        jnp.concatenate(mask, axis=1) > 0,
+        head_pad[...],
+        head_turn[...],
+        classes,
+    )[2]
+    slope_side = (slope[:, 0:128], slope[:, 128:256])
+    put_shifted(slope_rows, slope[:, 256 : 256 + cols], 2, 1, *slope_side, feat, cols)
+    put_shifted(slope_rows, slope[:, 256 + cols :], rows + 3, 1, *slope_side, feat, cols)
 
     for row in (1, rows + 3):
         slope_own[:, span(row, 2, cols)] = jnp.zeros((feat, 2 * cols), BF16)
@@ -424,20 +448,20 @@
         put_shifted(slope_rows, slope, row, step, *slope_side, feat, cols)
         loss_sum = loss_sum + jnp.sum(loss, axis=1, keepdims=True)
 
-    def grad_of(slope_ref, value_ref):
+    def grad_of(product):
         total = None
         for row in range(2, rows + 4, 11):
             count = min(11, rows + 4 - row)
-            term = dot_nt(below_above(slope_ref, row, count, cols), value_ref[:, span(row, count, cols)])
+            term = product(below_above(slope_own, row, count, cols), span(row, count, cols))
             total = term if total is None else total + term
         return total
 
     sums[...] = jnp.zeros_like(sums)
-    sums[:, 0 : 3 * feat] = grad_of(slope_own, hidden_rows)
+    sums[:, 0 : 3 * feat] = grad_of(lambda slopes, at: dot_nt(slopes, hidden_rows[:, at]))
     for row in range(3, rows + 3, step):
         back = conv_rows(two_back, slope_rows, row, step, cols)
         slope_own[:, span(row, step, cols)] = (back * rate[:, span(row - 3, step, cols)]).astype(BF16)
-    sums[:, 3 * feat : 3 * feat + 3 * GROUP] = grad_of(slope_own, band_rows)
+    sums[:, 3 * feat : 3 * feat + 3 * GROUP] = grad_of(lambda slopes, at: dot_nt(slopes, band_rows[:, at]))
     at = 3 * feat + 3 * GROUP
     sums[0:feat, at : at + GROUP] = grad_head
     sums[feat : feat + 1, at : at + 1] = loss_sum
@@ -463,13 +487,14 @@
         grad_two[tap] = sums[u * feat : (u + 1) * feat, v * feat : (v + 1) * feat]
         grad_one[tap] = turned[v * GROUP : v * GROUP + bands, u * feat : (u + 1) * feat]
     grad_head[...] = turned[3 * GROUP : 3 * GROUP + classes, 0:feat]
-    loss[...] = turned[3 * GROUP : 3 * GROUP + 1, feat : feat + 1]
+    loss_row = turned[3 * GROUP : 3 * GROUP + 1]
+    loss[...] = loss_row[:, feat : feat + 1] + loss_row[:, feat + GROUP : feat + GROUP + 1]
 
 
 def tree_sum(values):
     values = list(values)
     while len(values) > 1:
-        values = [values[i] + values[i + 1] for i in range(0, len(values), 2)]
+        values = [values[i + 1] + values[i] for i in range(0, len(values), 2)]
     return values[0]
 
 
@@ -533,9 +558,13 @@
     parts = []
     for some in (moves, [0]):
         parts += call(
-            functools.partial(part_kernel, some, slots),
+            functools.partial(part_kernel, some),
             [struct((rows, row_width + 2 * rows), BF16 if move else F32) for move in some],
-            [pltpu.VMEM((lon_count + 2 if len(some) > 1 else 3, 2 * rows, 2 * store), F32)],
+            [
+                pltpu.VMEM((chips, 2 * store, 2 * rows), F32),
+                pltpu.VMEM((2 * rows, 2 * store), F32),
+                pltpu.VMEM((chips + 2, 6 * GROUP, 2 * rows), F32),
+            ],
             in_specs=[smem, vmem, vmem, vmem],
             cost_estimate=pl.CostEstimate(flops=10**9, bytes_accessed=10**7, transcendentals=0),
         )(me, plans, stored, edge)
@@ -572,7 +601,7 @@
     )(conv1_weight.transpose(0, 2, 1), conv2_weight, head_weight)
 
     ext = rows + 6
-    step = 16
+    step, outer_step = 16, 32
     band_rows, hidden_rows, rate = call(
         functools.partial(inner_kernel, rows, cols, lat_count, lon_count, step),
         [
@@ -587,7 +616,7 @@
     half = 3 * feat // 2
     sum_width = 3 * feat + 4 * GROUP
     skip, keep, send = call(
-        functools.partial(outer_kernel, bands, classes, rows, cols, lat_count, lon_count, step),
+        functools.partial(outer_kernel, bands, classes, rows, cols, lat_count, lon_count, outer_step),
         [
             struct((feat, rows * cols), BF16),
             struct((half, sum_width), F32),
@@ -608,16 +637,25 @@
         one_main, one_strip, two_main, two_back, head_pad, head_turn,
     )
 
+    row_id, lane_id = iota((half, sum_width), 0), iota((half, sum_width), 1)
+    at_loss = lane_id == 3 * feat + 3 * GROUP
+    at_loss, at_rest = at_loss & (row_id == feat), at_loss & (row_id == feat + GROUP)
+
+    def sum_over(value, axis, moves):
+        value = jnp.where(at_loss, value + jnp.roll(value, -GROUP, axis=0), value)
+        rounded = lax.reduce_precision(value, 8, 7)
+        rest = lax.reduce_precision(jnp.roll(value - rounded, GROUP, axis=0), 8, 7)
+        rounded = jnp.where(at_rest, rest, rounded)
+        sent = rounded.astype(BF16)
+        size = lax.axis_size(axis)
+        terms = [rounded]
+        for move in moves:
+            terms.append(lax.ppermute(sent, axis, [(i, i ^ move) for i in range(size)]).astype(F32))
+        return tree_sum(terms)
+
     total = keep + by_lon(send, 1)
-    total = tree_sum([total] + [by_lon(total, 2 * move) for move in range(1, chips)])
-    sent = total.astype(BF16)
-    total = tree_sum(
-        [sent.astype(F32)]
-        + [
-            lax.ppermute(sent, "lat", [(i, i ^ move) for i in range(lat_count)]).astype(F32)
-            for move in range(1, lat_count)
-        ]
-    )
+    total = sum_over(total, "lon", range(2, lon_count, 2))
+    total = sum_over(total, "lat", range(1, lat_count))
     other = by_lon(total, 1)
     pixels = rows * cols * lat_count * lon_count
     grad_one, grad_two, grad_head, loss = call(

time: 66.5 us -> 62.8 us (0.944)
  Pallas kernels: 19 us -> 16.1 us
  waiting for transfers between devices: 20.7 us -> 19 us
    ppermute x9 -> x6, waiting for transfers between devices: 14.2 us -> 8.96 us  [by_lon(): return lax.ppermute(value, 'lon', [(i, i ^ move) for i in range(lon_count)])]
    ppermute x3 -> x6, waiting for transfers between devices: 3.34 us -> 6.91 us  [sum_over(): lax.ppermute(sent, axis, [(i, i ^ move) for i in range(size)]).astype(F32)]
    ppermute x3 -> x6, starting transfers between devices: 3.61 us -> 6.33 us  [sum_over(): lax.ppermute(sent, axis, [(i, i ^ move) for i in range(size)]).astype(F32)]
    ppermute x9 -> x6, starting transfers between devices: 9.7 us -> 7.35 us  [by_lon(): return lax.ppermute(value, 'lon', [(i, i ^ move) for i in range(lon_count)])]
    pallas_call x1, Pallas kernels: 8.28 us -> 6.74 us  [body(): call(functools.partial(outer_kernel, bands, classes, rows, cols, lat_coun...]
    pallas_call x2, Pallas kernels: 4.24 us -> 2.92 us  [body(): call(functools.partial(part_kernel, some), [struct((rows, row_width + 2 *...]
  transfers between devices with their start and end apart: 15 -> 15, of which waited for: 9 -> 9; matrix products, arithmetic and copies ran while one was open for 2% -> 2% of each run, Pallas kernels for 6% -> 7%
where the time goes in v3:
time: 62.8 us; the launch traced here: 62.5 us
  starting transfers between devices  23.6 us (38%)
  waiting for transfers between devices  19 us (30%)
  Pallas kernels  16.1 us (26%)
  local copies, waits for them, and re-layouts  2.38 us (4%)
  between operations  0.85 us (1%)
    ppermute x6, waiting for transfers between devices, by_lon(): return lax.ppermute(value, 'lon', [(i, i ^ move) for i in range(lon_count)])  8.96 us
    ppermute x6, starting transfers between devices, by_lon(): return lax.ppermute(value, 'lon', [(i, i ^ move) for i in range(lon_count)])  7.35 us
    ppermute x6, waiting for transfers between devices, sum_over(): lax.ppermute(sent, axis, [(i, i ^ move) for i in range(size)]).astype(F32)  6.91 us
    pallas_call x1, Pallas kernels, body(): call(functools.partial(outer_kernel, bands, classes, rows, cols, lat_coun...  6.74 us
    ppermute x6, starting transfers between devices, sum_over(): lax.ppermute(sent, axis, [(i, i ^ move) for i in range(size)]).astype(F32)  6.33 us
    all_to_all x1, starting transfers between devices, body(): plans = lax.all_to_all(plan, 'lon', split_axis=0, concat_axis=0, tiled=True)  5.28 us
    ppermute x1, starting transfers between devices, body(): lax.ppermute(lower, 'lat', [(i, i + 1) for i in range(lat_count - 1)])  3.2 us
    pallas_call x2, Pallas kernels, body(): call(functools.partial(part_kernel, some), [struct((rows, row_width + 2 *...  2.92 us
  transfers between devices with their start and end apart: 15, of which 9 were waited for; matrix products, arithmetic and copies ran while one was open for 2% of the time, Pallas kernels for 7%

profile of v3, /device:TPU:1, one launch (start us, length us, event | category | flops | bytes accessed | tf_op | source)
XLA Modules:
  0.0 62.5 jit_solution(18315595363339069904)
XLA Ops:
  0.6 1.8 %shard_map.128 = (f32[8,16,128]{2,1,0:T(8,128)}, f32[64,128]{1,0:T(8,128)}) custom-call(s32[1,512]{1,0:T(1,128)} %requests_hbm.1, s32[8,64]{1,0:T(8,128)} %bitcast.12, s32[8,64]{1,0:T(8,128)} %bitcast.13, f32[16]{0:T(128)} %levels_hbm.1, s32[64,128]{1,0:T(8,128)} %labels_hbm.1), custom_call_target="tpu_custom_call" | custom-call | tf_op jit(solution)/shard_map/pallas_call | solution.py:533
  2.4 0.1 collective-permute-start
  2.5 5.3 %all-to-all-start = ((f32[8,16,128]{2,1,0:T(8,128)}), f32[8,16,128]{2,1,0:T(8,128)S(1)}, u32[]{:S(2)}, u32[]{:S(2)}) async-start(f32[8,16,128]{2,1,0:T(8,128)} %get-tuple-element.38), calls=%async_computation | async-start | bytes 131072 | tf_op jit(solution)/shard_map/all_to_all | solution.py:549
  7.8 0.0 collective-permute-done.mate
  7.8 1.1 %copy-done.4 = bf16[192,1536]{1,0:T(8,128)(2,1)S(1)} copy-done((bf16[192,1536]{1,0:T(8,128)(2,1)S(1)}, bf16[192,1536]{1,0:T(8,128)(2,1)}, u32[]{:S(2)}) %copy-start.4) | copy-done | bytes 589848
  8.9 0.7 %shard_map.129 = (bf16[384,1536]{1,0:T(8,128)(2,1)S(1)}, bf16[96,384]{1,0:T(8,128)(2,1)S(1)}) custom-call(s32[1]{0:T(128)} %bitcast.1.me_ref, bf16[192,1536]{1,0:T(8,128)(2,1)S(1)} %copy-done.4, bf16[192,1536]{1,0:T(8,128)(2,1)S(1)} %collective-permute-done.mate), custom_call_target="tpu_custom_call" | custom-call | flops 1000000000 | bytes 10000000 | tf_op jit(solution)/shard_map/pallas_call | solution.py:550
  9.6 2.4 %all-to-all-done.plans = f32[8,16,128]{2,1,0:T(8,128)S(1)} async-done(((f32[8,16,128]{2,1,0:T(8,128)}), f32[8,16,128]{2,1,0:T(8,128)S(1)}, u32[]{:S(2)}, u32[]{:S(2)}) %all-to-all-start) | async-done | bytes 65568 | tf_op jit(solution)/shard_map/all_to_all | solution.py:549
  12.0 1.7 %shard_map.130 = (bf16[64,1664]{1,0:T(8,128)(2,1)S(1)}, bf16[64,1664]{1,0:T(8,128)(2,1)S(1)}, bf16[64,1664]{1,0:T(8,128)(2,1)S(1)}) custom-call(s32[1]{0:T(128)} %bitcast.1.me_ref, f32[8,16,128]{2,1,0:T(8,128)S(1)} %all-to-all-done.plans, bf16[384,1536]{1,0:T(8,128)(2,1)S(1)} %get-tuple-element.44.stored, bf16[96,384]{1,0:T(8,128)(2,1)S(1)} %get-tuple-element.45.edge), custom_call_target="tpu_custom_call" | custom-call | flops 1000000000 | bytes 10000000 | tf_op jit(solution)/shard_map/pallas_call | solution.py:560
  13.7 0.0 copy-start.2
  13.7 0.6 %collective-permute-start.1 = (bf16[64,1664]{1,0:T(8,128)(2,1)S(1)}, bf16[64,1664]{1,0:T(8,128)(2,1)S(1)}, u32[]{:S(2)}, u32[]{:S(2)}) collective-permute-start(bf16[64,1664]{1,0:T(8,128)(2,1)S(1)} %get-tuple-element.46), channel_id=1, source_target_pairs={{0,6},{1,7},{2,4},{3,5},{4,2},{5,3},{6,0},{7,1},{8,14},{9,15},{10,... | collective-permute-start | bytes 638984 | tf_op jit(solution)/shard_map/ppermute | solution.py:530
  14.3 1.2 %collective-permute-start.2 = (bf16[64,1664]{1,0:T(8,128)(2,1)S(1)}, bf16[64,1664]{1,0:T(8,128)(2,1)S(1)}, u32[]{:S(2)}, u32[]{:S(2)}) collective-permute-start(bf16[64,1664]{1,0:T(8,128)(2,1)S(1)} %get-tuple-element.47), channel_id=1, source_target_pairs={{0,4},{1,5},{2,6},{3,7},{4,0},{5,1},{6,2},{7,3},{8,12},{9,13},{10,... | collective-permute-start | bytes 638984 | tf_op jit(solution)/shard_map/ppermute | solution.py:530
  15.5 0.9 %collective-permute-start.3 = (bf16[64,1664]{1,0:T(8,128)(2,1)S(1)}, bf16[64,1664]{1,0:T(8,128)(2,1)S(1)}, u32[]{:S(2)}, u32[]{:S(2)}) collective-permute-start(bf16[64,1664]{1,0:T(8,128)(2,1)S(1)} %get-tuple-element.48), channel_id=1, source_target_pairs={{0,2},{1,3},{2,0},{3,1},{4,6},{5,7},{6,4},{7,5},{8,10},{9,11},{10,... | collective-permute-start | bytes 638984 | tf_op jit(solution)/shard_map/ppermute | solution.py:530
  16.4 0.0 copy-start.3
  16.4 1.2 %shard_map.131.refs_3_ = f32[64,1664]{1,0:T(8,128)S(1)} custom-call(s32[1]{0:T(128)} %bitcast.1.me_ref, f32[8,16,128]{2,1,0:T(8,128)S(1)} %all-to-all-done.plans, bf16[384,1536]{1,0:T(8,128)(2,1)S(1)} %get-tuple-element.44.stored, bf16[96,384]{1,0:T(8,128)(2,1)S(1)} %get-tuple-element.45.edge), custom_call_target="tpu_custom_call" | custom-call | flops 1000000000 | bytes 10000000 | tf_op jit(solution)/shard_map/pallas_call | solution.py:560
  17.7 3.0 %collective-permute-done.1.refs_0_ = bf16[64,1664]{1,0:T(8,128)(2,1)S(1)} collective-permute-done((bf16[64,1664]{1,0:T(8,128)(2,1)S(1)}, bf16[64,1664]{1,0:T(8,128)(2,1)S(1)}, u32[]{:S(2)}, u32[]{:S(2)}) %collective-permute-start.1) | collective-permute-done | bytes 213024 | tf_op jit(solution)/shard_map/ppermute | solution.py:530
  20.6 5.0 %collective-permute-done.2.refs_1_ = bf16[64,1664]{1,0:T(8,128)(2,1)S(1)} collective-permute-done((bf16[64,1664]{1,0:T(8,128)(2,1)S(1)}, bf16[64,1664]{1,0:T(8,128)(2,1)S(1)}, u32[]{:S(2)}, u32[]{:S(2)}) %collective-permute-start.2) | collective-permute-done | bytes 213024 | tf_op jit(solution)/shard_map/ppermute | solution.py:530
  25.7 0.0 collective-permute-done.3.refs_2_
  25.7 0.8 %shard_map.132 = (bf16[16,8192]{1,0:T(8,128)(2,1)S(1)}, bf16[160,128]{1,0:T(8,128)(2,1)S(1)}, bf16[16,512]{1,0:T(8,128)(2,1)S(1)}, bf16[16,512]{1,0:T(8,128)(2,1)S(1)}) custom-call(s32[1]{0:T(128)} %bitcast.1.me_ref, f32[8,16,128]{2,1,0:T(8,128)S(1)} %all-to-all-done.plans, f32[64,128]{1,0:T(8,128)S(1)} %copy-done.2, ...), custom_call_target="tpu_custom_call" | custom-call | tf_op jit(solution)/shard_map/pallas_call | solution.py:572
  26.5 3.2 %collective-permute-start.4 = (bf16[16,512]{1,0:T(8,128)(2,1)S(1)}, bf16[16,512]{1,0:T(8,128)(2,1)S(1)}, u32[]{:S(2)}, u32[]{:S(2)}) collective-permute-start(bf16[16,512]{1,0:T(8,128)(2,1)S(1)} %get-tuple-element.50), channel_id=1, source_target_pairs={{0,8},{8,16},{16,24},{1,9},{9,17},{17,25},{2,10},{10,18},{18,26},{... | collective-permute-start | bytes 49160 | tf_op jit(solution)/shard_map/ppermute | solution.py:588
  29.7 1.5 %collective-permute-start.5 = (bf16[16,512]{1,0:T(8,128)(2,1)S(1)}, bf16[16,512]{1,0:T(8,128)(2,1)S(1)}, u32[]{:S(2)}, u32[]{:S(2)}) collective-permute-start(bf16[16,512]{1,0:T(8,128)(2,1)S(1)} %get-tuple-element.51), channel_id=1, source_target_pairs={{8,0},{16,8},{24,16},{9,1},{17,9},{25,17},{10,2},{18,10},{26,18},{... | collective-permute-start | bytes 49160 | tf_op jit(solution)/shard_map/ppermute | solution.py:587
  31.2 0.1 pad_add_fusion.place
  31.2 0.2 shard_map.133
  31.4 2.0 %shard_map.134 = (bf16[48,8960]{1,0:T(8,128)(2,1)S(1)}, bf16[192,8960]{1,0:T(8,128)(2,1)S(1)}, f32[64,8192]{1,0:T(8,128)S(1)}) custom-call(s32[2]{0:T(128)S(1)} %pad_add_fusion.place, bf16[16,8192]{1,0:T(8,128)(2,1)S(1)} %get-tuple-element.52.main, bf16[160,128]{1,0:T(8,128)(2,1)S(1)} %get-tuple-element.49.strips, ...), custom_call_target="tpu_custom_call" | custom-call | flops 100000000 | bytes 10000000 | tf_op jit(solution)/shard_map/pallas_call | solution.py:605
  33.4 0.0 collective-permute-done.4.above
  33.4 0.7 %collective-permute-done.5.below = bf16[16,512]{1,0:T(8,128)(2,1)S(1)} collective-permute-done((bf16[16,512]{1,0:T(8,128)(2,1)S(1)}, bf16[16,512]{1,0:T(8,128)(2,1)S(1)}, u32[]{:S(2)}, u32[]{:S(2)}) %collective-permute-start.5) | collective-permute-done | bytes 16416 | tf_op jit(solution)/shard_map/ppermute | solution.py:587
  34.2 6.7 %shard_map.135 = (bf16[64,8192]{1,0:T(8,128)(2,1)S(1)}, f32[96,256]{1,0:T(8,128)S(1)}, f32[96,256]{1,0:T(8,128)S(1)}) custom-call(s32[2]{0:T(128)S(1)} %pad_add_fusion.place, bf16[160,128]{1,0:T(8,128)(2,1)S(1)} %get-tuple-element.49.strips, bf16[16,512]{1,0:T(8,128)(2,1)S(1)} %collective-permute-done.4.above, ...), custom_call_target="tpu_custom_call" | custom-call | tf_op jit(solution)/shard_map/pallas_call | solution.py:618
  40.9 2.4 %collective-permute-start.6 = (f32[96,256]{1,0:T(8,128)S(1)}, f32[96,256]{1,0:T(8,128)S(1)}, u32[]{:S(2)}, u32[]{:S(2)}) collective-permute-start(f32[96,256]{1,0:T(8,128)S(1)} %get-tuple-element.64), channel_id=1, source_target_pairs={{0,1},{1,0},{2,3},{3,2},{4,5},{5,4},{6,7},{7,6},{8,9},{9,8},{10,11... | collective-permute-start | bytes 294920 | tf_op jit(solution)/shard_map/ppermute | solution.py:530
  43.3 0.9 %collective-permute-done.6 = f32[96,256]{1,0:T(8,128)S(1)} collective-permute-done((f32[96,256]{1,0:T(8,128)S(1)}, f32[96,256]{1,0:T(8,128)S(1)}, u32[]{:S(2)}, u32[]{:S(2)}) %collective-permute-start.6) | collective-permute-done | bytes 98336 | tf_op jit(solution)/shard_map/ppermute | solution.py:530
  44.2 0.1 reduce-precision_subtract_fusion.1
  44.4 0.1 fusion.1
  44.5 1.0 %collective-permute-start.7 = (bf16[96,256]{1,0:T(8,128)(2,1)S(1)}, bf16[96,256]{1,0:T(8,128)(2,1)S(1)}, u32[]{:S(2)}, u32[]{:S(2)}) collective-permute-start(bf16[96,256]{1,0:T(8,128)(2,1)S(1)} %get-tuple-element.71), channel_id=1, source_target_pairs={{0,6},{1,7},{2,4},{3,5},{4,2},{5,3},{6,0},{7,1},{8,14},{9,15},{10,... | collective-permute-start | bytes 147464 | tf_op jit(solution)/shard_map/ppermute | solution.py:653
  45.5 1.1 %collective-permute-start.8 = (bf16[96,256]{1,0:T(8,128)(2,1)S(1)}, bf16[96,256]{1,0:T(8,128)(2,1)S(1)}, u32[]{:S(2)}, u32[]{:S(2)}) collective-permute-start(bf16[96,256]{1,0:T(8,128)(2,1)S(1)} %get-tuple-element.71), channel_id=1, source_target_pairs={{0,4},{1,5},{2,6},{3,7},{4,0},{5,1},{6,2},{7,3},{8,12},{9,13},{10,... | collective-permute-start | bytes 147464 | tf_op jit(solution)/shard_map/ppermute | solution.py:653
  46.6 0.6 collective-permute-start.9
  47.2 1.2 %collective-permute-done.7 = bf16[96,256]{1,0:T(8,128)(2,1)S(1)} collective-permute-done((bf16[96,256]{1,0:T(8,128)(2,1)S(1)}, bf16[96,256]{1,0:T(8,128)(2,1)S(1)}, u32[]{:S(2)}, u32[]{:S(2)}) %collective-permute-start.7) | collective-permute-done | bytes 49184 | tf_op jit(solution)/shard_map/ppermute | solution.py:653
  48.4 1.5 %collective-permute-done.8 = bf16[96,256]{1,0:T(8,128)(2,1)S(1)} collective-permute-done((bf16[96,256]{1,0:T(8,128)(2,1)S(1)}, bf16[96,256]{1,0:T(8,128)(2,1)S(1)}, u32[]{:S(2)}, u32[]{:S(2)}) %collective-permute-start.8) | collective-permute-done | bytes 49184 | tf_op jit(solution)/shard_map/ppermute | solution.py:653
  49.9 0.0 collective-permute-done.9
  50.0 0.1 reduce-precision_subtract_fusion
  50.1 0.1 fusion
  50.2 2.6 %collective-permute-start.10 = (bf16[96,256]{1,0:T(8,128)(2,1)S(1)}, bf16[96,256]{1,0:T(8,128)(2,1)S(1)}, u32[]{:S(2)}, u32[]{:S(2)}) collective-permute-start(bf16[96,256]{1,0:T(8,128)(2,1)S(1)} %get-tuple-element.69), channel_id=1, source_target_pairs={{0,24},{8,16},{16,8},{24,0},{1,25},{9,17},{17,9},{25,1},{2,26},{10... | collective-permute-start | bytes 147464 | tf_op jit(solution)/shard_map/ppermute | solution.py:653
  52.8 0.0 collective-permute-start.11
  52.8 1.0 %collective-permute-start.12 = (bf16[96,256]{1,0:T(8,128)(2,1)S(1)}, bf16[96,256]{1,0:T(8,128)(2,1)S(1)}, u32[]{:S(2)}, u32[]{:S(2)}) collective-permute-start(bf16[96,256]{1,0:T(8,128)(2,1)S(1)} %get-tuple-element.69), channel_id=1, source_target_pairs={{0,8},{8,0},{16,24},{24,16},{1,9},{9,1},{17,25},{25,17},{2,10},{10... | collective-permute-start | bytes 147464 | tf_op jit(solution)/shard_map/ppermute | solution.py:653
  53.8 1.2 %collective-permute-done.10 = bf16[96,256]{1,0:T(8,128)(2,1)S(1)} collective-permute-done((bf16[96,256]{1,0:T(8,128)(2,1)S(1)}, bf16[96,256]{1,0:T(8,128)(2,1)S(1)}, u32[]{:S(2)}, u32[]{:S(2)}) %collective-permute-start.10) | collective-permute-done | bytes 49184 | tf_op jit(solution)/shard_map/ppermute | solution.py:653
  55.0 3.0 %collective-permute-done.11 = bf16[96,256]{1,0:T(8,128)(2,1)S(1)} collective-permute-done((bf16[96,256]{1,0:T(8,128)(2,1)S(1)}, bf16[96,256]{1,0:T(8,128)(2,1)S(1)}, u32[]{:S(2)}, u32[]{:S(2)}) %collective-permute-start.11) | collective-permute-done | bytes 49184 | tf_op jit(solution)/shard_map/ppermute | solution.py:653
  58.0 0.0 collective-permute-done.12
  58.0 2.2 %collective-permute-start.13 = (f32[96,256]{1,0:T(8,128)S(1)}, f32[96,256]{1,0:T(8,128)S(1)}, u32[]{:S(2)}, u32[]{:S(2)}) collective-permute-start(f32[96,256]{1,0:T(8,128)S(1)} %add_add_fusion.own), channel_id=1, source_target_pairs={{0,1},{1,0},{2,3},{3,2},{4,5},{5,4},{6,7},{7,6},{8,9},{9,8},{10,11... | collective-permute-start | bytes 294920 | tf_op jit(solution)/shard_map/ppermute | solution.py:530
  60.2 1.3 %copy.14 = bf16[8,8,64,128]{3,2,1,0:T(8,128)(2,1)} copy(bf16[8,8,64,128]{3,1,2,0:T(8,128)(2,1)S(1)} %bitcast.9) | data formatting | bytes 2097152
  61.4 0.0 collective-permute-done.13.mate
  61.4 1.0 %shard_map.136 = (f32[9,12,64]{2,1,0:T(8,128)}, f32[9,64,64]{2,1,0:T(8,128)}, f32[11,64]{1,0:T(8,128)}, f32[1,1]{1,0:T(1,128)}) custom-call(s32[1]{0:T(128)} %bitcast.1.me_ref, f32[96,256]{1,0:T(8,128)S(1)} %add_add_fusion.own, f32[96,256]{1,0:T(8,128)S(1)} %collective-permute-done.13.mate), custom_call_target="tpu_custom_call" | custom-call | tf_op jit(solution)/shard_map/pallas_call | solution.py:661
  (20 shorter events, 0.1 us)
Async XLA Ops:
  2.4 5.4 %collective-permute-start = (bf16[192,1536]{1,0:T(8,128)(2,1)}, bf16[192,1536]{1,0:T(8,128)(2,1)S(1)}, u32[]{:S(2)}, u32[]{:S(2)}) collective-permute-start(bf16[192,1536]{1,0:T(8,128)(2,1)} %own), channel_id=1, source_target_pairs={{0,1},{1,0},{2,3},{3,2},{4,5},{5,4},{6,7},{7,6},{8,9},{9,8},{10,11... | collective-permute-start | bytes 1769480 | tf_op jit(solution)/shard_map/ppermute | solution.py:530
  2.5 9.4 %all-to-all-start = ((f32[8,16,128]{2,1,0:T(8,128)}), f32[8,16,128]{2,1,0:T(8,128)S(1)}, u32[]{:S(2)}, u32[]{:S(2)}) async-start(f32[8,16,128]{2,1,0:T(8,128)} %get-tuple-element.38), calls=%async_computation | async-start | bytes 131072 | tf_op jit(solution)/shard_map/all_to_all | solution.py:549
  7.8 1.1 %copy-start.4 = (bf16[192,1536]{1,0:T(8,128)(2,1)S(1)}, bf16[192,1536]{1,0:T(8,128)(2,1)}, u32[]{:S(2)}) copy-start(bf16[192,1536]{1,0:T(8,128)(2,1)} %own) | copy-start | bytes 1769476
  13.7 12.0 %copy-start.2 = (f32[64,128]{1,0:T(8,128)S(1)}, f32[64,128]{1,0:T(8,128)}, u32[]{:S(2)}) copy-start(f32[64,128]{1,0:T(8,128)} %get-tuple-element.43.labels) | copy-start | bytes 98308
  13.7 7.0 %collective-permute-start.1 = (bf16[64,1664]{1,0:T(8,128)(2,1)S(1)}, bf16[64,1664]{1,0:T(8,128)(2,1)S(1)}, u32[]{:S(2)}, u32[]{:S(2)}) collective-permute-start(bf16[64,1664]{1,0:T(8,128)(2,1)S(1)} %get-tuple-element.46), channel_id=1, source_target_pairs={{0,6},{1,7},{2,4},{3,5},{4,2},{5,3},{6,0},{7,1},{8,14},{9,15},{10,... | collective-permute-start | bytes 638984 | tf_op jit(solution)/shard_map/ppermute | solution.py:530
  14.3 11.4 %collective-permute-start.2 = (bf16[64,1664]{1,0:T(8,128)(2,1)S(1)}, bf16[64,1664]{1,0:T(8,128)(2,1)S(1)}, u32[]{:S(2)}, u32[]{:S(2)}) collective-permute-start(bf16[64,1664]{1,0:T(8,128)(2,1)S(1)} %get-tuple-element.47), channel_id=1, source_target_pairs={{0,4},{1,5},{2,6},{3,7},{4,0},{5,1},{6,2},{7,3},{8,12},{9,13},{10,... | collective-permute-start | bytes 638984 | tf_op jit(solution)/shard_map/ppermute | solution.py:530
  15.5 10.2 %collective-permute-start.3 = (bf16[64,1664]{1,0:T(8,128)(2,1)S(1)}, bf16[64,1664]{1,0:T(8,128)(2,1)S(1)}, u32[]{:S(2)}, u32[]{:S(2)}) collective-permute-start(bf16[64,1664]{1,0:T(8,128)(2,1)S(1)} %get-tuple-element.48), channel_id=1, source_target_pairs={{0,2},{1,3},{2,0},{3,1},{4,6},{5,7},{6,4},{7,5},{8,10},{9,11},{10,... | collective-permute-start | bytes 638984 | tf_op jit(solution)/shard_map/ppermute | solution.py:530
  16.4 14.8 %copy-start = (bf16[9,64,64]{2,1,0:T(8,128)(2,1)S(1)}, bf16[9,64,64]{2,1,0:T(8,128)(2,1)}, u32[]{:S(2)}) copy-start(bf16[9,64,64]{2,1,0:T(8,128)(2,1)} %conv2.1) | copy-start | bytes 221188
  16.4 14.8 %copy-start.1 = (bf16[9,64,12]{1,2,0:T(8,128)(2,1)S(1)}, bf16[9,64,12]{1,2,0:T(8,128)(2,1)}, u32[]{:S(2)}) copy-start(bf16[9,64,12]{1,2,0:T(8,128)(2,1)} %param.15) | copy-start | bytes 41476
  16.4 14.8 %copy-start.3 = (bf16[11,64]{1,0:T(8,128)(2,1)S(1)}, bf16[11,64]{1,0:T(8,128)(2,1)}, u32[]{:S(2)}) copy-start(bf16[11,64]{1,0:T(8,128)(2,1)} %head.1) | copy-start | bytes 4228
  26.5 6.9 %collective-permute-start.4 = (bf16[16,512]{1,0:T(8,128)(2,1)S(1)}, bf16[16,512]{1,0:T(8,128)(2,1)S(1)}, u32[]{:S(2)}, u32[]{:S(2)}) collective-permute-start(bf16[16,512]{1,0:T(8,128)(2,1)S(1)} %get-tuple-element.50), channel_id=1, source_target_pairs={{0,8},{8,16},{16,24},{1,9},{9,17},{17,25},{2,10},{10,18},{18,26},{... | collective-permute-start | bytes 49160 | tf_op jit(solution)/shard_map/ppermute | solution.py:588
  29.7 4.5 %collective-permute-start.5 = (bf16[16,512]{1,0:T(8,128)(2,1)S(1)}, bf16[16,512]{1,0:T(8,128)(2,1)S(1)}, u32[]{:S(2)}, u32[]{:S(2)}) collective-permute-start(bf16[16,512]{1,0:T(8,128)(2,1)S(1)} %get-tuple-element.51), channel_id=1, source_target_pairs={{8,0},{16,8},{24,16},{9,1},{17,9},{25,17},{10,2},{18,10},{26,18},{... | collective-permute-start | bytes 49160 | tf_op jit(solution)/shard_map/ppermute | solution.py:587
  40.9 3.3 %collective-permute-start.6 = (f32[96,256]{1,0:T(8,128)S(1)}, f32[96,256]{1,0:T(8,128)S(1)}, u32[]{:S(2)}, u32[]{:S(2)}) collective-permute-start(f32[96,256]{1,0:T(8,128)S(1)} %get-tuple-element.64), channel_id=1, source_target_pairs={{0,1},{1,0},{2,3},{3,2},{4,5},{5,4},{6,7},{7,6},{8,9},{9,8},{10,11... | collective-permute-start | bytes 294920 | tf_op jit(solution)/shard_map/ppermute | solution.py:530
  44.5 4.0 %collective-permute-start.7 = (bf16[96,256]{1,0:T(8,128)(2,1)S(1)}, bf16[96,256]{1,0:T(8,128)(2,1)S(1)}, u32[]{:S(2)}, u32[]{:S(2)}) collective-permute-start(bf16[96,256]{1,0:T(8,128)(2,1)S(1)} %get-tuple-element.71), channel_id=1, source_target_pairs={{0,6},{1,7},{2,4},{3,5},{4,2},{5,3},{6,0},{7,1},{8,14},{9,15},{10,... | collective-permute-start | bytes 147464 | tf_op jit(solution)/shard_map/ppermute | solution.py:653
  45.5 4.4 %collective-permute-start.8 = (bf16[96,256]{1,0:T(8,128)(2,1)S(1)}, bf16[96,256]{1,0:T(8,128)(2,1)S(1)}, u32[]{:S(2)}, u32[]{:S(2)}) collective-permute-start(bf16[96,256]{1,0:T(8,128)(2,1)S(1)} %get-tuple-element.71), channel_id=1, source_target_pairs={{0,4},{1,5},{2,6},{3,7},{4,0},{5,1},{6,2},{7,3},{8,12},{9,13},{10,... | collective-permute-start | bytes 147464 | tf_op jit(solution)/shard_map/ppermute | solution.py:653
  46.6 3.3 %collective-permute-start.9 = (bf16[96,256]{1,0:T(8,128)(2,1)S(1)}, bf16[96,256]{1,0:T(8,128)(2,1)S(1)}, u32[]{:S(2)}, u32[]{:S(2)}) collective-permute-start(bf16[96,256]{1,0:T(8,128)(2,1)S(1)} %get-tuple-element.71), channel_id=1, source_target_pairs={{0,2},{1,3},{2,0},{3,1},{4,6},{5,7},{6,4},{7,5},{8,10},{9,11},{10,... | collective-permute-start | bytes 147464 | tf_op jit(solution)/shard_map/ppermute | solution.py:653
  50.2 4.8 %collective-permute-start.10 = (bf16[96,256]{1,0:T(8,128)(2,1)S(1)}, bf16[96,256]{1,0:T(8,128)(2,1)S(1)}, u32[]{:S(2)}, u32[]{:S(2)}) collective-permute-start(bf16[96,256]{1,0:T(8,128)(2,1)S(1)} %get-tuple-element.69), channel_id=1, source_target_pairs={{0,24},{8,16},{16,8},{24,0},{1,25},{9,17},{17,9},{25,1},{2,26},{10... | collective-permute-start | bytes 147464 | tf_op jit(solution)/shard_map/ppermute | solution.py:653
  52.8 5.2 %collective-permute-start.11 = (bf16[96,256]{1,0:T(8,128)(2,1)S(1)}, bf16[96,256]{1,0:T(8,128)(2,1)S(1)}, u32[]{:S(2)}, u32[]{:S(2)}) collective-permute-start(bf16[96,256]{1,0:T(8,128)(2,1)S(1)} %get-tuple-element.69), channel_id=1, source_target_pairs={{0,16},{8,24},{16,0},{24,8},{1,17},{9,25},{17,1},{25,9},{2,18},{10... | collective-permute-start | bytes 147464 | tf_op jit(solution)/shard_map/ppermute | solution.py:653
  52.8 5.2 %collective-permute-start.12 = (bf16[96,256]{1,0:T(8,128)(2,1)S(1)}, bf16[96,256]{1,0:T(8,128)(2,1)S(1)}, u32[]{:S(2)}, u32[]{:S(2)}) collective-permute-start(bf16[96,256]{1,0:T(8,128)(2,1)S(1)} %get-tuple-element.69), channel_id=1, source_target_pairs={{0,8},{8,0},{16,24},{24,16},{1,9},{9,1},{17,25},{25,17},{2,10},{10... | collective-permute-start | bytes 147464 | tf_op jit(solution)/shard_map/ppermute | solution.py:653
  58.0 3.4 %collective-permute-start.13 = (f32[96,256]{1,0:T(8,128)S(1)}, f32[96,256]{1,0:T(8,128)S(1)}, u32[]{:S(2)}, u32[]{:S(2)}) collective-permute-start(f32[96,256]{1,0:T(8,128)S(1)} %add_add_fusion.own), channel_id=1, source_target_pairs={{0,1},{1,0},{2,3},{3,2},{4,5},{5,4},{6,7},{7,6},{8,9},{9,8},{10,11... | collective-permute-start | bytes 294920 | tf_op jit(solution)/shard_map/ppermute | solution.py:530

commit v4 on v3

--- a/solution.py
+++ b/solution.py
@@ -130,11 +130,14 @@
     return high, (value - high.astype(F32)).astype(BF16)
 
 
-def part_kernel(moves, me_ref, plans, stored, edge, *refs):
-    outs, (over, turned, sides) = refs[:-3], refs[-3:]
+END_LINES = 80
+
+
+def ends_part_kernel(moves, bands, me_ref, plans, stored, edge, row_weights, *refs):
+    smalls, (over, sides, product, lines) = refs[:-4], refs[-4:]
     chips = plans.shape[0] // 2
-    rows = outs[0].shape[0]
-    held, row_width = stored.shape
+    _, rows, held = row_weights.shape
+    cols = stored.shape[1] // bands
     me = me_ref[0]
     here, core = me // 2, me % 2
     first = (here * held).astype(F32)
@@ -144,29 +147,80 @@
         put_weights(plans, chip, first, over.at[chip])
         high, low = high_low(over[chip])
         sides[chip + 1] = dot(edge[...], high) + dot(edge[...], low)
-    for move, out in zip(moves, outs, strict=True):
+    ends = []
+    for i, move in enumerate(moves):
+        both = jnp.transpose(over[jnp.bitwise_xor(here, move)])
+        weights = jnp.where(core == 0, both[0:rows], both[rows:])
+        row_weights[i] = weights
+        ends += [weights[0:3], weights[rows - 3 : rows]]
+    high, low = high_low(jnp.concatenate(ends, axis=0))
+    count = high.shape[0]
+    both = dot(jnp.concatenate([high, low], axis=0), stored[...])
+    product[...] = both[0:count] + both[count:]
+    for i, (move, small) in enumerate(zip(moves, smalls, strict=True)):
+        lines[...] = jnp.zeros_like(lines)
+        for band in range(bands):
+            lines[6 * band : 6 * band + 6, :] = product[6 * i : 6 * i + 6, band * cols : (band + 1) * cols]
+        small[0:END_LINES, :] = lines[...].astype(small.dtype)
         chip = jnp.bitwise_xor(here, move)
-        turned[...] = jnp.transpose(over[chip])
-        high, low = high_low(turned[pl.ds(pl.multiple_of(core * rows, 8), rows), :])
+        near, before, after = sides[chip + 1], sides[chip], sides[chip + 2]
+        left = jnp.where(core == 1, near[0 : 3 * GROUP, 0:rows], before[0 : 3 * GROUP, rows:])
+        right = jnp.where(core == 0, near[3 * GROUP :, rows:], after[3 * GROUP :, 0:rows])
+        small[END_LINES:, :] = jnp.concatenate([left, right], axis=1).astype(small.dtype)
+
+
+def part_kernel(indices, stored, row_weights, *outs):
+    rows = outs[0].shape[0]
+    row_width = stored.shape[1]
+    for index, out in zip(indices, outs, strict=True):
+        high, low = high_low(row_weights[index])
         both = jnp.concatenate([high, low], axis=0)
         for start in range(0, row_width, 512):
             stop = min(start + 512, row_width)
             product = dot(both, stored[:, start:stop])
             out[:, start:stop] = (product[:rows] + product[rows:]).astype(out.dtype)
-        near, before, after = sides[chip + 1], sides[chip], sides[chip + 2]
-        left = jnp.where(core == 1, near[0 : 3 * GROUP, 0:rows], before[0 : 3 * GROUP, rows:])
-        right = jnp.where(core == 0, near[3 * GROUP :, rows:], after[3 * GROUP :, 0:rows])
-        out[0 : 3 * GROUP, row_width:] = jnp.concatenate([left, right], axis=1).astype(out.dtype)
-        out[3 * GROUP :, row_width:] = jnp.zeros((rows - 3 * GROUP, 2 * rows), out.dtype)
+
+
+def ends_kernel(bands, me_ref, plans, labels, *refs):
+    count = plans.shape[0]
+    rows, cols = labels.shape
+    smalls, (upper, lower, total, bundle) = refs[:-4], refs[-4:]
+    me = me_ref[0]
+    value = smalls[0][...].astype(F32)
+    for small in smalls[1:]:
+        value = value + small[...].astype(F32)
+    total[...] = value
+    before = plans[jnp.maximum(me - 1, 0), 1:2, rows : 2 * rows]
+    after = plans[jnp.minimum(me + 1, count - 1), 0:1, rows : 2 * rows]
+    for target, start, end in ((upper, 0, 0), (lower, rows - 3, 3)):
+        bundle[...] = jnp.zeros_like(bundle)
+        for i in range(3):
+            line = jnp.concatenate(
+                [
+                    total[pl.ds(end + i, bands, stride=6), :],
+                    labels[start + i : start + i + 1, :],
+                    jnp.zeros((GROUP - bands - 1, cols), F32),
+                ],
+                axis=0,
+            )
+            target[:, i * cols : (i + 1) * cols] = line.astype(BF16)
+            for column, at in ((3, 0), (4, 1), (5, cols - 2), (6, cols - 1)):
+                bundle[:, column * 3 + i : column * 3 + i + 1] = line[:, at : at + 1]
+        for column in range(3):
+            group = total[END_LINES + column * GROUP : END_LINES + (column + 1) * GROUP, :]
+            bundle[:, column * 3 : column * 3 + 3] = group[:, start : start + 3]
+            at = (column + 7) * 3
+            bundle[:, at : at + 3] = group[:, rows + start : rows + start + 3]
+        bundle[bands : bands + 1, 6:9] = before[:, start : start + 3]
+        bundle[bands : bands + 1, 21:24] = after[:, start : start + 3]
+        target[:, 3 * cols :] = bundle[...].astype(BF16)
 
 
 def composite_kernel(bands, me_ref, plans, labels, *refs):
     count = plans.shape[0]
     tile_rows, patch_cols = labels.shape
-    chips = count // 2
-    parts = refs[:chips]
-    main, strips, upper, lower, bank, side, bundle = refs[chips:]
-    row_width = bands * patch_cols
+    inputs, (main, strips, bank, side) = refs[:-4], refs[-4:]
+    parts, smalls = inputs[: len(inputs) // 2], inputs[len(inputs) // 2 :]
     me = me_ref[0]
     for band in range(bands):
         columns = slice(band * patch_cols, (band + 1) * patch_cols)
@@ -183,9 +237,9 @@
             pl.ds(row, GROUP, stride=tile_rows), :
         ].astype(BF16)
 
-    far = parts[0][0 : 3 * GROUP, row_width : row_width + 2 * tile_rows].astype(F32)
-    for part in parts[1:]:
-        far = far + part[0 : 3 * GROUP, row_width : row_width + 2 * tile_rows].astype(F32)
+    far = smalls[0][END_LINES:, :].astype(F32)
+    for small in smalls[1:]:
+        far = far + small[END_LINES:, :].astype(F32)
     side[...] = jnp.zeros_like(side)
     side[0 : 3 * GROUP, 3 : 3 + tile_rows] = far[:, :tile_rows]
     side[7 * GROUP : 10 * GROUP, 3 : 3 + tile_rows] = far[:, tile_rows:]
@@ -204,15 +258,6 @@
         near = near + dot_nt(jnp.where(pick, 1.0, 0.0).astype(BF16), tile)
     side[3 * GROUP : 7 * GROUP, 3 : 3 + tile_rows] = near
     strips[...] = side[...].astype(BF16)
-
-    for target, start in ((upper, 0), (lower, tile_rows - 3)):
-        target[:, 0 : 3 * patch_cols] = main[:, start * patch_cols : (start + 3) * patch_cols]
-        bundle[...] = jnp.zeros_like(bundle)
-        for column in range(10):
-            bundle[:, column * 3 : column * 3 + 3] = side[
-                column * GROUP : (column + 1) * GROUP, 3 + start : 6 + start
-            ]
-        target[:, 3 * patch_cols :] = bundle[...].astype(BF16)
 
 
 def weights_kernel(conv1, conv2, head, one_main, one_strip, two_main, two_back, head_pad, head_turn, wide, tall):
@@ -342,32 +387,19 @@
     put_shifted(hidden_rows, soft.astype(BF16), row, count, *sides, pre.shape[0], cols)
 
 
-def inner_kernel(rows, cols, lat_count, lon_count, step, place, main, strips, one_main, one_strip, band_rows, hidden_rows, rate, side):
-    side[...] = strips[...].astype(F32)
-    hidden_sides = [
-        hidden.astype(BF16)
-        for hidden in strip_hidden(side, one_strip, strip_inside(place, rows, lat_count, lon_count), (1, 6))
-    ]
-    band_sides = (strips[2 * GROUP : 3 * GROUP, :], strips[7 * GROUP : 8 * GROUP, :])
-    for row in range(0, rows, step):
-        put_shifted(band_rows, main[:, span(row, step, cols)], row + 3, step, *band_sides, GROUP, cols)
-    for row in range(4, rows + 2, step):
-        count = min(step, rows + 2 - row)
-        hidden_chunk(one_main, band_rows, hidden_rows, rate, row, count, None, hidden_sides, cols)
-
-
-def outer_kernel(
+def label_rows(band_rows, bands, row, count, cols):
+    return band_rows[GROUP + bands : GROUP + bands + 1, span(row, count, cols)].astype(F32).astype(jnp.int32)
+
+
+def network_kernel(
     bands, classes, rows, cols, lat_count, lon_count, step,
-    place, strips, above, below, band_in, hidden_in, rate_in,
+    place, main, strips, above, below,
     one_main, one_strip, two_main, two_back, head_pad, head_turn,
     skip_out, keep_out, send_out,
     band_rows, side, hidden_rows, rate, slope_rows, slope_own, sums,
 ):
     feat = head_turn.shape[0]
     lat, lon = place[0], place[1]
-    band_rows[:, span(3, rows, cols)] = band_in[:, span(3, rows, cols)]
-    hidden_rows[:, span(4, rows - 2, cols)] = hidden_in[:, span(4, rows - 2, cols)]
-    rate[:, span(1, rows - 2, cols)] = rate_in[:, span(1, rows - 2, cols)]
 
     side[...] = strips[...].astype(F32)
     up_tail = above[:, 3 * cols :].astype(F32)
@@ -394,30 +426,26 @@
     )
     put_shifted(band_rows, above[:, 0 : 3 * cols], 0, 3, *band_sides, GROUP, cols)
     put_shifted(band_rows, below[:, 0 : 3 * cols], rows + 3, 3, *band_sides, GROUP, cols)
+    put_shifted(band_rows, main[...], 3, rows, *band_sides, GROUP, cols)
 
     top_inside, bottom_inside = lat > 0, lat < lat_count - 1
     hidden_sides = (hidden_side[1].astype(BF16), hidden_side[4].astype(BF16))
     near = jnp.concatenate(
-        [above_below(band_rows, 1, 3, cols), above_below(band_rows, rows + 2, 3, cols)], axis=1
+        [above_below(band_rows, 1, 2, cols), above_below(band_rows, rows + 3, 2, cols)], axis=1
     )
     pre = dot(one_main[...], near)
-    gate = sigmoid(pre)
-    soft = pre * gate
-    ends = gate + soft * (1.0 - gate)
-    rate[:, span(0, 1, cols)] = ends[:, span(2, 1, cols)]
-    rate[:, span(rows - 1, 1, cols)] = ends[:, span(3, 1, cols)]
-    lane = iota((1, 6 * cols), 1)
-    soft = jnp.where(((lane >= 2 * cols) | top_inside) & ((lane < 4 * cols) | bottom_inside), soft, 0.0)
-    soft = soft.astype(BF16)
-    put_shifted(hidden_rows, soft[:, span(0, 3, cols)], 1, 3, *hidden_sides, feat, cols)
-    put_shifted(hidden_rows, soft[:, span(3, 3, cols)], rows + 2, 3, *hidden_sides, feat, cols)
-
-    def label_of(row, count):
-        return band_rows[GROUP + bands : GROUP + bands + 1, span(row, count, cols)].astype(F32).astype(jnp.int32)
+    soft = pre * sigmoid(pre)
+    lane = iota((1, 4 * cols), 1)
+    inside = ((lane >= 2 * cols) | top_inside) & ((lane < 2 * cols) | bottom_inside)
+    soft = jnp.where(inside, soft, 0.0).astype(BF16)
+    put_shifted(hidden_rows, soft[:, span(0, 2, cols)], 1, 2, *hidden_sides, feat, cols)
+    put_shifted(hidden_rows, soft[:, span(2, 2, cols)], rows + 3, 2, *hidden_sides, feat, cols)
+    for row in range(3, rows + 3, step):
+        hidden_chunk(one_main, band_rows, hidden_rows, rate, row, step, None, hidden_sides, cols)
 
     pre = [conv_rows(two_main, hidden_rows, row, 1, cols) for row in (2, rows + 3)]
     label = [side[c * GROUP + bands : c * GROUP + bands + 1, :].astype(jnp.int32) for c in (2, 7)]
-    label += [label_of(row, 1) for row in (2, rows + 3)]
+    label += [label_rows(band_rows, bands, row, 1, cols) for row in (2, rows + 3)]
     ones = jnp.ones((1, cols), jnp.int32)
     mask = [jnp.where(inside, 1, 0) for inside in insides[1:]]
     mask += [jnp.where(inside, ones, 0) for inside in (top_inside, bottom_inside)]
@@ -439,9 +467,8 @@
     loss_sum = jnp.zeros((1, 1), F32)
     for row in range(3, rows + 3, step):
         pre = conv_rows(two_main, hidden_rows, row, step, cols)
-        skip, error, slope, loss = head_stage(
-            pre, label_of(row, step), None, head_pad[...], head_turn[...], classes
-        )
+        label = label_rows(band_rows, bands, row, step, cols)
+        skip, error, slope, loss = head_stage(pre, label, None, head_pad[...], head_turn[...], classes)
         skip_out[:, span(row - 3, step, cols)] = skip
         slope_own[:, span(row, step, cols)] = slope
         grad_head = grad_head + dot_nt(skip, error)
@@ -494,7 +521,7 @@
 def tree_sum(values):
     values = list(values)
     while len(values) > 1:
-        values = [values[i + 1] + values[i] for i in range(0, len(values), 2)]
+        values = [values[i] + values[i + 1] for i in range(0, len(values), 2)]
     return values[0]
 
 
@@ -554,36 +581,45 @@
         cost_estimate=pl.CostEstimate(flops=10**9, bytes_accessed=10**7, transcendentals=0),
     )(me, patches, mate_patches)
     plans, stored, edge = lax.optimization_barrier((plans, stored, edge))
-    moves = list(range(chips - 1, 0, -1))
+    moves = list(range(chips - 1, -1, -1))
+    cost = pl.CostEstimate(flops=10**9, bytes_accessed=10**7, transcendentals=0)
+    row_weights, *smalls = call(
+        functools.partial(ends_part_kernel, moves, bands),
+        [struct((chips, rows, 2 * store), F32)]
+        + [struct((END_LINES + 3 * GROUP, cols), BF16 if move else F32) for move in moves],
+        [
+            pltpu.VMEM((chips, 2 * store, 2 * rows), F32),
+            pltpu.VMEM((chips + 2, 6 * GROUP, 2 * rows), F32),
+            pltpu.VMEM((6 * chips, row_width), F32),
+            pltpu.VMEM((END_LINES, cols), F32),
+        ],
+        in_specs=[smem, vmem, vmem, vmem],
+        cost_estimate=cost,
+    )(me, plans, stored, edge)
+    smalls = [by_lon(small, 2 * move) if move else small for move, small in zip(moves, smalls)]
     parts = []
-    for some in (moves, [0]):
+    for some in (moves[:-1], moves[-1:]):
         parts += call(
-            functools.partial(part_kernel, some),
-            [struct((rows, row_width + 2 * rows), BF16 if move else F32) for move in some],
-            [
-                pltpu.VMEM((chips, 2 * store, 2 * rows), F32),
-                pltpu.VMEM((2 * rows, 2 * store), F32),
-                pltpu.VMEM((chips + 2, 6 * GROUP, 2 * rows), F32),
-            ],
-            in_specs=[smem, vmem, vmem, vmem],
-            cost_estimate=pl.CostEstimate(flops=10**9, bytes_accessed=10**7, transcendentals=0),
-        )(me, plans, stored, edge)
-    parts = [by_lon(part, 2 * move) for move, part in zip(moves, parts)] + parts[-1:]
-    main, strips, upper, lower = call(
+            functools.partial(part_kernel, [moves.index(move) for move in some]),
+            [struct((rows, row_width), BF16 if move else F32) for move in some],
+            in_specs=[vmem, vmem],
+            cost_estimate=cost,
+        )(stored, row_weights)
+    parts = [by_lon(part, 2 * move) if move else part for move, part in zip(moves, parts)]
+    upper, lower = call(
+        functools.partial(ends_kernel, bands),
+        [struct((GROUP, 3 * cols + 128), BF16)] * 2,
+        [pltpu.VMEM((END_LINES + 3 * GROUP, cols), F32), pltpu.VMEM((GROUP, 128), F32)],
+        in_specs=[smem] + [vmem] * (2 + chips),
+        cost_estimate=pl.CostEstimate(flops=3 * 10**10, bytes_accessed=10**7, transcendentals=0),
+    )(me, plans, tile_labels, *smalls)
+    main, strips = call(
         functools.partial(composite_kernel, bands),
-        [
-            struct((GROUP, rows * cols), BF16),
-            struct((10 * GROUP, 128), BF16),
-            struct((GROUP, 3 * cols + 128), BF16),
-            struct((GROUP, 3 * cols + 128), BF16),
-        ],
-        [
-            pltpu.VMEM((GROUP * rows, cols), F32),
-            pltpu.VMEM((10 * GROUP, 128), F32),
-            pltpu.VMEM((GROUP, 128), F32),
-        ],
-        in_specs=[smem] + [vmem] * (2 + chips),
-    )(me, plans, tile_labels, *parts)
+        [struct((GROUP, rows * cols), BF16), struct((10 * GROUP, 128), BF16)],
+        [pltpu.VMEM((GROUP * rows, cols), F32), pltpu.VMEM((10 * GROUP, 128), F32)],
+        in_specs=[smem] + [vmem] * (2 + 2 * chips),
+        cost_estimate=cost,
+    )(me, plans, tile_labels, *parts, *smalls)
     below = lax.ppermute(upper, "lat", [(i + 1, i) for i in range(lat_count - 1)])
     above = lax.ppermute(lower, "lat", [(i, i + 1) for i in range(lat_count - 1)])
 
@@ -601,22 +637,10 @@
     )(conv1_weight.transpose(0, 2, 1), conv2_weight, head_weight)
 
     ext = rows + 6
-    step, outer_step = 16, 32
-    band_rows, hidden_rows, rate = call(
-        functools.partial(inner_kernel, rows, cols, lat_count, lon_count, step),
-        [
-            struct((3 * GROUP, ext * cols), BF16),
-            struct((3 * feat, ext * cols), BF16),
-            struct((feat, rows * cols), F32),
-        ],
-        [pltpu.VMEM((10 * GROUP, 128), F32)],
-        in_specs=[smem] + [vmem] * 4,
-        cost_estimate=pl.CostEstimate(flops=10**8, bytes_accessed=10**7, transcendentals=0),
-    )(place, main, strips, one_main, one_strip)
     half = 3 * feat // 2
     sum_width = 3 * feat + 4 * GROUP
     skip, keep, send = call(
-        functools.partial(outer_kernel, bands, classes, rows, cols, lat_count, lon_count, outer_step),
+        functools.partial(network_kernel, bands, classes, rows, cols, lat_count, lon_count, 32),
         [
             struct((feat, rows * cols), BF16),
             struct((half, sum_width), F32),
@@ -631,9 +655,9 @@
             pltpu.VMEM((feat, ext * cols), BF16),
             pltpu.VMEM((3 * feat, sum_width), F32),
         ],
-        in_specs=[smem] + [vmem] * 12,
+        in_specs=[smem] + [vmem] * 10,
     )(
-        place, strips, above, below, band_rows, hidden_rows, rate,
+        place, main, strips, above, below,
         one_main, one_strip, two_main, two_back, head_pad, head_turn,
     )
 

time: 62.8 us -> 58.9 us (0.938)
  waiting for transfers between devices: 19 us -> 12.4 us
  local copies, waits for them, and re-layouts: 2.38 us -> 4.72 us
  starting transfers between devices: 23.6 us -> 25.8 us
  Pallas kernels: 16.1 us -> 14.1 us
    ppermute x6 -> x9, waiting for transfers between devices: 8.96 us -> 5.61 us  [by_lon(): return lax.ppermute(value, 'lon', [(i, i ^ move) for i in range(lon_count)])]
    all_to_all x1, waiting for transfers between devices: 2.4 us -> 0.01 us  [body(): plans = lax.all_to_all(plan, 'lon', split_axis=0, concat_axis=0, tiled=True)]
    unnamed x11, local copies, waits for them, and re-layouts: 2.33 us -> 4.68 us
    ppermute x6 -> x9, starting transfers between devices: 7.35 us -> 9.66 us  [by_lon(): return lax.ppermute(value, 'lon', [(i, i ^ move) for i in range(lon_count)])]
    pallas_call x4 -> x5, Pallas kernels: 11.6 us -> 9.79 us  [the longest x1 7.18 us: body(): call(functools.partial(network_kernel, bands, classes, rows, cols, lat_co...]
    ppermute x1, waiting for transfers between devices: 0.74 us -> 0.01 us  [body(): lax.ppermute(upper, 'lat', [(i + 1, i) for i in range(lat_count - 1)])]
  transfers between devices with their start and end apart: 15 -> 18, of which waited for: 9 -> 7; matrix products, arithmetic and copies ran while one was open for 2% -> 2% of each run, Pallas kernels for 7% -> 4%
where the time goes in v4:
time: 58.9 us; the launch traced here: 58.4 us
  starting transfers between devices  25.8 us (44%)
  Pallas kernels  14.1 us (24%)
  waiting for transfers between devices  12.4 us (21%)
  local copies, waits for them, and re-layouts  4.72 us (8%)
  between operations  0.86 us (1%)
    ppermute x9, starting transfers between devices, by_lon(): return lax.ppermute(value, 'lon', [(i, i ^ move) for i in range(lon_count)])  9.66 us
    pallas_call x1, Pallas kernels, body(): call(functools.partial(network_kernel, bands, classes, rows, cols, lat_co...  7.18 us
    ppermute x6, waiting for transfers between devices, sum_over(): lax.ppermute(sent, axis, [(i, i ^ move) for i in range(size)]).astype(F32)  6.78 us
    ppermute x6, starting transfers between devices, sum_over(): lax.ppermute(sent, axis, [(i, i ^ move) for i in range(size)]).astype(F32)  6.33 us
    ppermute x9, waiting for transfers between devices, by_lon(): return lax.ppermute(value, 'lon', [(i, i ^ move) for i in range(lon_count)])  5.61 us
    all_to_all x1, starting transfers between devices, body(): plans = lax.all_to_all(plan, 'lon', split_axis=0, concat_axis=0, tiled=True)  5.28 us
    unnamed x11, local copies, waits for them, and re-layouts  4.68 us
    ppermute x1, starting transfers between devices, body(): lax.ppermute(lower, 'lat', [(i, i + 1) for i in range(lat_count - 1)])  3.2 us
  transfers between devices with their start and end apart: 18, of which 7 were waited for; matrix products, arithmetic and copies ran while one was open for 2% of the time, Pallas kernels for 4%

profile of v4, /device:TPU:1, one launch (start us, length us, event | category | flops | bytes accessed | tf_op | source)
XLA Modules:
  0.0 58.4 jit_solution(9785743483829394737)
XLA Ops:
  0.6 1.8 %shard_map.128 = (f32[8,16,128]{2,1,0:T(8,128)}, f32[64,128]{1,0:T(8,128)}) custom-call(s32[1,512]{1,0:T(1,128)} %requests_hbm.1, s32[8,64]{1,0:T(8,128)} %bitcast.12, s32[8,64]{1,0:T(8,128)} %bitcast.13, f32[16]{0:T(128)} %levels_hbm.1, s32[64,128]{1,0:T(8,128)} %labels_hbm.1), custom_call_target="tpu_custom_call" | custom-call | tf_op jit(solution)/shard_map/pallas_call | solution.py:560
  2.4 0.1 collective-permute-start
  2.5 5.3 %all-to-all-start = ((f32[8,16,128]{2,1,0:T(8,128)}), f32[8,16,128]{2,1,0:T(8,128)S(1)}, u32[]{:S(2)}, u32[]{:S(2)}) async-start(f32[8,16,128]{2,1,0:T(8,128)} %get-tuple-element.40), calls=%async_computation | async-start | bytes 131072 | tf_op jit(solution)/shard_map/all_to_all | solution.py:576
  7.8 0.9 %copy-done = bf16[9,64,64]{2,1,0:T(8,128)(2,1)S(1)} copy-done((bf16[9,64,64]{2,1,0:T(8,128)(2,1)S(1)}, bf16[9,64,64]{2,1,0:T(8,128)(2,1)}, u32[]{:S(2)}) %copy-start) | copy-done | bytes 73752
  8.7 0.8 %copy-done.1 = bf16[9,64,12]{1,2,0:T(8,128)(2,1)S(1)} copy-done((bf16[9,64,12]{1,2,0:T(8,128)(2,1)S(1)}, bf16[9,64,12]{1,2,0:T(8,128)(2,1)}, u32[]{:S(2)}) %copy-start.1) | copy-done | bytes 13848
  9.5 0.7 %copy-done.2 = bf16[11,64]{1,0:T(8,128)(2,1)S(1)} copy-done((bf16[11,64]{1,0:T(8,128)(2,1)S(1)}, bf16[11,64]{1,0:T(8,128)(2,1)}, u32[]{:S(2)}) %copy-start.2) | copy-done | bytes 1432
  10.2 0.2 shard_map.135
  10.4 0.1 pad_add_fusion.place
  10.4 0.0 collective-permute-done.mate
  10.5 1.1 %copy-done.3 = bf16[192,1536]{1,0:T(8,128)(2,1)S(1)} copy-done((bf16[192,1536]{1,0:T(8,128)(2,1)S(1)}, bf16[192,1536]{1,0:T(8,128)(2,1)}, u32[]{:S(2)}) %copy-start.3) | copy-done | bytes 589848
  11.5 0.7 %shard_map.129 = (bf16[384,1536]{1,0:T(8,128)(2,1)S(1)}, bf16[96,384]{1,0:T(8,128)(2,1)S(1)}) custom-call(s32[1]{0:T(128)} %bitcast.1.me_ref, bf16[192,1536]{1,0:T(8,128)(2,1)S(1)} %copy-done.3, bf16[192,1536]{1,0:T(8,128)(2,1)S(1)} %collective-permute-done.mate), custom_call_target="tpu_custom_call" | custom-call | flops 1000000000 | bytes 10000000 | tf_op jit(solution)/shard_map/pallas_call | solution.py:577
  12.2 0.0 all-to-all-done.plans
  12.2 1.3 %shard_map.130 = (f32[4,64,384]{2,1,0:T(8,128)S(1)}, bf16[128,128]{1,0:T(8,128)(2,1)S(1)}, bf16[128,128]{1,0:T(8,128)(2,1)S(1)}, bf16[128,128]{1,0:T(8,128)(2,1)S(1)}, f32[128,128]{1,0:T(8,128)S(1)}) custom-call(s32[1]{0:T(128)} %bitcast.1.me_ref, f32[8,16,128]{2,1,0:T(8,128)S(1)} %all-to-all-done.plans, bf16[384,1536]{1,0:T(8,128)(2,1)S(1)} %get-tuple-element.46.stored, ...), custom_call_target="tpu_custom_call" | custom-call | flops 1000000000 | bytes 10000000 | tf_op jit(solution)/shard_map/pallas_call | solution.py:586
  13.5 0.8 %shard_map.131 = (bf16[64,1536]{1,0:T(8,128)(2,1)S(1)}, bf16[64,1536]{1,0:T(8,128)(2,1)S(1)}, bf16[64,1536]{1,0:T(8,128)(2,1)S(1)}) custom-call(bf16[384,1536]{1,0:T(8,128)(2,1)S(1)} %get-tuple-element.46.stored, f32[4,64,384]{2,1,0:T(8,128)S(1)} %get-tuple-element.48.row_weights), custom_call_target="tpu_custom_call" | custom-call | flops 1000000000 | bytes 10000000 | tf_op jit(solution)/shard_map/pallas_call | solution.py:602
  14.3 2.4 %collective-permute-start.4 = (bf16[128,128]{1,0:T(8,128)(2,1)S(1)}, bf16[128,128]{1,0:T(8,128)(2,1)S(1)}, u32[]{:S(2)}, u32[]{:S(2)}) collective-permute-start(bf16[128,128]{1,0:T(8,128)(2,1)S(1)} %get-tuple-element.52), channel_id=1, source_target_pairs={{0,6},{1,7},{2,4},{3,5},{4,2},{5,3},{6,0},{7,1},{8,14},{9,15},{10,... | collective-permute-start | bytes 98312 | tf_op jit(solution)/shard_map/ppermute | solution.py:557
  16.7 0.3 collective-permute-start.5
  16.9 0.1 collective-permute-start.6
  17.0 0.4 shard_map.132.refs_3_
  17.4 2.3 %collective-permute-start.1 = (bf16[64,1536]{1,0:T(8,128)(2,1)S(1)}, bf16[64,1536]{1,0:T(8,128)(2,1)S(1)}, u32[]{:S(2)}, u32[]{:S(2)}) collective-permute-start(bf16[64,1536]{1,0:T(8,128)(2,1)S(1)} %get-tuple-element.49), channel_id=1, source_target_pairs={{0,6},{1,7},{2,4},{3,5},{4,2},{5,3},{6,0},{7,1},{8,14},{9,15},{10,... | collective-permute-start | bytes 589832 | tf_op jit(solution)/shard_map/ppermute | solution.py:557
  19.8 0.3 collective-permute-start.2
  20.0 0.0 collective-permute-done.4.refs_4_.refs_0_
  20.0 0.1 collective-permute-start.3
  20.1 0.2 shard_map.134
  20.3 3.2 %collective-permute-start.7 = (bf16[16,512]{1,0:T(8,128)(2,1)S(1)}, bf16[16,512]{1,0:T(8,128)(2,1)S(1)}, u32[]{:S(2)}, u32[]{:S(2)}) collective-permute-start(bf16[16,512]{1,0:T(8,128)(2,1)S(1)} %get-tuple-element.58), channel_id=1, source_target_pairs={{0,8},{8,16},{16,24},{1,9},{9,17},{17,25},{2,10},{10,18},{18,26},{... | collective-permute-start | bytes 49160 | tf_op jit(solution)/shard_map/ppermute | solution.py:624
  23.5 1.3 %collective-permute-start.8 = (bf16[16,512]{1,0:T(8,128)(2,1)S(1)}, bf16[16,512]{1,0:T(8,128)(2,1)S(1)}, u32[]{:S(2)}, u32[]{:S(2)}) collective-permute-start(bf16[16,512]{1,0:T(8,128)(2,1)S(1)} %get-tuple-element.59), channel_id=1, source_target_pairs={{8,0},{16,8},{24,16},{9,1},{17,9},{25,17},{10,2},{18,10},{26,18},{... | collective-permute-start | bytes 49160 | tf_op jit(solution)/shard_map/ppermute | solution.py:623
  24.8 4.7 %collective-permute-done.2.refs_1_ = bf16[64,1536]{1,0:T(8,128)(2,1)S(1)} collective-permute-done((bf16[64,1536]{1,0:T(8,128)(2,1)S(1)}, bf16[64,1536]{1,0:T(8,128)(2,1)S(1)}, u32[]{:S(2)}, u32[]{:S(2)}) %collective-permute-start.2) | collective-permute-done | bytes 196640 | tf_op jit(solution)/shard_map/ppermute | solution.py:557
  29.5 0.0 collective-permute-done.3.refs_2_
  29.5 0.7 %shard_map.133 = (bf16[16,8192]{1,0:T(8,128)(2,1)S(1)}, bf16[160,128]{1,0:T(8,128)(2,1)S(1)}) custom-call(s32[1]{0:T(128)} %bitcast.1.me_ref, f32[8,16,128]{2,1,0:T(8,128)S(1)} %all-to-all-done.plans, f32[64,128]{1,0:T(8,128)S(1)} %copy-done.4, bf16[64,1536]{1,0:T(8,128)(2,1)S(1)} %collective-permute-done.1.refs_0_, ...), custom_call_target="tpu_custom_call" | custom-call | flops 1000000000 | bytes 10000000 | tf_op jit(solution)/shard_map/pallas_call | solution.py:616
  30.2 7.2 %shard_map.136 = (bf16[64,8192]{1,0:T(8,128)(2,1)S(1)}, f32[96,256]{1,0:T(8,128)S(1)}, f32[96,256]{1,0:T(8,128)S(1)}) custom-call(s32[2]{0:T(128)S(1)} %pad_add_fusion.place, bf16[16,8192]{1,0:T(8,128)(2,1)S(1)} %get-tuple-element.56.main, bf16[160,128]{1,0:T(8,128)(2,1)S(1)} %get-tuple-element.57.strips, bf16[16,512]{1,0:T(8,128)(2,1)S(1)} %collective-permute-done.7.above, ...), custom_call_target="tpu_custom_call" | custom-call | tf_op jit(solution)/shard_map/pallas_call | solution.py:642
  37.4 1.6 %collective-permute-start.9 = (f32[96,256]{1,0:T(8,128)S(1)}, f32[96,256]{1,0:T(8,128)S(1)}, u32[]{:S(2)}, u32[]{:S(2)}) collective-permute-start(f32[96,256]{1,0:T(8,128)S(1)} %get-tuple-element.68), channel_id=1, source_target_pairs={{0,1},{1,0},{2,3},{3,2},{4,5},{5,4},{6,7},{7,6},{8,9},{9,8},{10,11... | collective-permute-start | bytes 294920 | tf_op jit(solution)/shard_map/ppermute | solution.py:557
  39.0 0.9 %collective-permute-done.9 = f32[96,256]{1,0:T(8,128)S(1)} collective-permute-done((f32[96,256]{1,0:T(8,128)S(1)}, f32[96,256]{1,0:T(8,128)S(1)}, u32[]{:S(2)}, u32[]{:S(2)}) %collective-permute-start.9) | collective-permute-done | bytes 98336 | tf_op jit(solution)/shard_map/ppermute | solution.py:557
  39.9 0.1 reduce-precision_subtract_fusion.1
  40.1 0.1 fusion.1
  40.2 2.1 %collective-permute-start.12 = (bf16[96,256]{1,0:T(8,128)(2,1)S(1)}, bf16[96,256]{1,0:T(8,128)(2,1)S(1)}, u32[]{:S(2)}, u32[]{:S(2)}) collective-permute-start(bf16[96,256]{1,0:T(8,128)(2,1)S(1)} %get-tuple-element.75), channel_id=1, source_target_pairs={{0,6},{1,7},{2,4},{3,5},{4,2},{5,3},{6,0},{7,1},{8,14},{9,15},{10,... | collective-permute-start | bytes 147464 | tf_op jit(solution)/shard_map/ppermute | solution.py:677
  42.2 0.3 collective-permute-start.11
  42.5 0.3 collective-permute-start.10
  42.9 1.2 %collective-permute-done.12 = bf16[96,256]{1,0:T(8,128)(2,1)S(1)} collective-permute-done((bf16[96,256]{1,0:T(8,128)(2,1)S(1)}, bf16[96,256]{1,0:T(8,128)(2,1)S(1)}, u32[]{:S(2)}, u32[]{:S(2)}) %collective-permute-start.12) | collective-permute-done | bytes 49184 | tf_op jit(solution)/shard_map/ppermute | solution.py:677
  44.1 1.3 %collective-permute-done.11 = bf16[96,256]{1,0:T(8,128)(2,1)S(1)} collective-permute-done((bf16[96,256]{1,0:T(8,128)(2,1)S(1)}, bf16[96,256]{1,0:T(8,128)(2,1)S(1)}, u32[]{:S(2)}, u32[]{:S(2)}) %collective-permute-start.11) | collective-permute-done | bytes 49184 | tf_op jit(solution)/shard_map/ppermute | solution.py:677
  45.4 0.1 collective-permute-done.10
  45.5 0.1 reduce-precision_subtract_fusion
  45.6 0.1 fusion
  45.8 2.9 %collective-permute-start.15 = (bf16[96,256]{1,0:T(8,128)(2,1)S(1)}, bf16[96,256]{1,0:T(8,128)(2,1)S(1)}, u32[]{:S(2)}, u32[]{:S(2)}) collective-permute-start(bf16[96,256]{1,0:T(8,128)(2,1)S(1)} %get-tuple-element.73), channel_id=1, source_target_pairs={{0,24},{8,16},{16,8},{24,0},{1,25},{9,17},{17,9},{25,1},{2,26},{10... | collective-permute-start | bytes 147464 | tf_op jit(solution)/shard_map/ppermute | solution.py:677
  48.7 0.7 %collective-permute-start.13 = (bf16[96,256]{1,0:T(8,128)(2,1)S(1)}, bf16[96,256]{1,0:T(8,128)(2,1)S(1)}, u32[]{:S(2)}, u32[]{:S(2)}) collective-permute-start(bf16[96,256]{1,0:T(8,128)(2,1)S(1)} %get-tuple-element.73), channel_id=1, source_target_pairs={{0,8},{8,0},{16,24},{24,16},{1,9},{9,1},{17,25},{25,17},{2,10},{10... | collective-permute-start | bytes 147464 | tf_op jit(solution)/shard_map/ppermute | solution.py:677
  49.4 1.2 %collective-permute-done.15 = bf16[96,256]{1,0:T(8,128)(2,1)S(1)} collective-permute-done((bf16[96,256]{1,0:T(8,128)(2,1)S(1)}, bf16[96,256]{1,0:T(8,128)(2,1)S(1)}, u32[]{:S(2)}, u32[]{:S(2)}) %collective-permute-start.15) | collective-permute-done | bytes 49184 | tf_op jit(solution)/shard_map/ppermute | solution.py:677
  50.6 3.0 %collective-permute-done.14 = bf16[96,256]{1,0:T(8,128)(2,1)S(1)} collective-permute-done((bf16[96,256]{1,0:T(8,128)(2,1)S(1)}, bf16[96,256]{1,0:T(8,128)(2,1)S(1)}, u32[]{:S(2)}, u32[]{:S(2)}) %collective-permute-start.14) | collective-permute-done | bytes 49184 | tf_op jit(solution)/shard_map/ppermute | solution.py:677
  53.6 2.5 %collective-permute-start.16 = (f32[96,256]{1,0:T(8,128)S(1)}, f32[96,256]{1,0:T(8,128)S(1)}, u32[]{:S(2)}, u32[]{:S(2)}) collective-permute-start(f32[96,256]{1,0:T(8,128)S(1)} %add_add_fusion.own), channel_id=1, source_target_pairs={{0,1},{1,0},{2,3},{3,2},{4,5},{5,4},{6,7},{7,6},{8,9},{9,8},{10,11... | collective-permute-start | bytes 294920 | tf_op jit(solution)/shard_map/ppermute | solution.py:557
  56.1 1.3 %copy.14 = bf16[8,8,64,128]{3,2,1,0:T(8,128)(2,1)} copy(bf16[8,8,64,128]{3,1,2,0:T(8,128)(2,1)S(1)} %bitcast.9) | data formatting | bytes 2097152
  57.3 1.0 %shard_map.137 = (f32[9,12,64]{2,1,0:T(8,128)}, f32[9,64,64]{2,1,0:T(8,128)}, f32[11,64]{1,0:T(8,128)}, f32[1,1]{1,0:T(1,128)}) custom-call(s32[1]{0:T(128)} %bitcast.1.me_ref, f32[96,256]{1,0:T(8,128)S(1)} %add_add_fusion.own, f32[96,256]{1,0:T(8,128)S(1)} %collective-permute-done.16.mate), custom_call_target="tpu_custom_call" | custom-call | tf_op jit(solution)/shard_map/pallas_call | solution.py:685
  (27 shorter events, 0.1 us)
Async XLA Ops:
  2.4 8.0 %collective-permute-start = (bf16[192,1536]{1,0:T(8,128)(2,1)}, bf16[192,1536]{1,0:T(8,128)(2,1)S(1)}, u32[]{:S(2)}, u32[]{:S(2)}) collective-permute-start(bf16[192,1536]{1,0:T(8,128)(2,1)} %own), channel_id=1, source_target_pairs={{0,1},{1,0},{2,3},{3,2},{4,5},{5,4},{6,7},{7,6},{8,9},{9,8},{10,11... | collective-permute-start | bytes 1769480 | tf_op jit(solution)/shard_map/ppermute | solution.py:557
  2.5 9.7 %all-to-all-start = ((f32[8,16,128]{2,1,0:T(8,128)}), f32[8,16,128]{2,1,0:T(8,128)S(1)}, u32[]{:S(2)}, u32[]{:S(2)}) async-start(f32[8,16,128]{2,1,0:T(8,128)} %get-tuple-element.40), calls=%async_computation | async-start | bytes 131072 | tf_op jit(solution)/shard_map/all_to_all | solution.py:576
  7.8 0.9 %copy-start = (bf16[9,64,64]{2,1,0:T(8,128)(2,1)S(1)}, bf16[9,64,64]{2,1,0:T(8,128)(2,1)}, u32[]{:S(2)}) copy-start(bf16[9,64,64]{2,1,0:T(8,128)(2,1)} %conv2.1) | copy-start | bytes 221188
  8.7 0.8 %copy-start.1 = (bf16[9,64,12]{1,2,0:T(8,128)(2,1)S(1)}, bf16[9,64,12]{1,2,0:T(8,128)(2,1)}, u32[]{:S(2)}) copy-start(bf16[9,64,12]{1,2,0:T(8,128)(2,1)} %param.15) | copy-start | bytes 41476
  9.5 0.7 %copy-start.2 = (bf16[11,64]{1,0:T(8,128)(2,1)S(1)}, bf16[11,64]{1,0:T(8,128)(2,1)}, u32[]{:S(2)}) copy-start(bf16[11,64]{1,0:T(8,128)(2,1)} %head.1) | copy-start | bytes 4228
  10.5 1.1 %copy-start.3 = (bf16[192,1536]{1,0:T(8,128)(2,1)S(1)}, bf16[192,1536]{1,0:T(8,128)(2,1)}, u32[]{:S(2)}) copy-start(bf16[192,1536]{1,0:T(8,128)(2,1)} %own) | copy-start | bytes 1769476
  14.3 5.7 %collective-permute-start.4 = (bf16[128,128]{1,0:T(8,128)(2,1)S(1)}, bf16[128,128]{1,0:T(8,128)(2,1)S(1)}, u32[]{:S(2)}, u32[]{:S(2)}) collective-permute-start(bf16[128,128]{1,0:T(8,128)(2,1)S(1)} %get-tuple-element.52), channel_id=1, source_target_pairs={{0,6},{1,7},{2,4},{3,5},{4,2},{5,3},{6,0},{7,1},{8,14},{9,15},{10,... | collective-permute-start | bytes 98312 | tf_op jit(solution)/shard_map/ppermute | solution.py:557
  16.7 3.5 %collective-permute-start.5 = (bf16[128,128]{1,0:T(8,128)(2,1)S(1)}, bf16[128,128]{1,0:T(8,128)(2,1)S(1)}, u32[]{:S(2)}, u32[]{:S(2)}) collective-permute-start(bf16[128,128]{1,0:T(8,128)(2,1)S(1)} %get-tuple-element.53), channel_id=1, source_target_pairs={{0,4},{1,5},{2,6},{3,7},{4,0},{5,1},{6,2},{7,3},{8,12},{9,13},{10,... | collective-permute-start | bytes 98312 | tf_op jit(solution)/shard_map/ppermute | solution.py:557
  16.9 3.2 %copy-start.4 = (f32[64,128]{1,0:T(8,128)S(1)}, f32[64,128]{1,0:T(8,128)}, u32[]{:S(2)}) copy-start(f32[64,128]{1,0:T(8,128)} %get-tuple-element.45.labels) | copy-start | bytes 98308
  16.9 3.2 %collective-permute-start.6 = (bf16[128,128]{1,0:T(8,128)(2,1)S(1)}, bf16[128,128]{1,0:T(8,128)(2,1)S(1)}, u32[]{:S(2)}, u32[]{:S(2)}) collective-permute-start(bf16[128,128]{1,0:T(8,128)(2,1)S(1)} %get-tuple-element.54), channel_id=1, source_target_pairs={{0,2},{1,3},{2,0},{3,1},{4,6},{5,7},{6,4},{7,5},{8,10},{9,11},{10,... | collective-permute-start | bytes 98312 | tf_op jit(solution)/shard_map/ppermute | solution.py:557
  17.4 7.4 %collective-permute-start.1 = (bf16[64,1536]{1,0:T(8,128)(2,1)S(1)}, bf16[64,1536]{1,0:T(8,128)(2,1)S(1)}, u32[]{:S(2)}, u32[]{:S(2)}) collective-permute-start(bf16[64,1536]{1,0:T(8,128)(2,1)S(1)} %get-tuple-element.49), channel_id=1, source_target_pairs={{0,6},{1,7},{2,4},{3,5},{4,2},{5,3},{6,0},{7,1},{8,14},{9,15},{10,... | collective-permute-start | bytes 589832 | tf_op jit(solution)/shard_map/ppermute | solution.py:557
  19.8 9.7 %collective-permute-start.2 = (bf16[64,1536]{1,0:T(8,128)(2,1)S(1)}, bf16[64,1536]{1,0:T(8,128)(2,1)S(1)}, u32[]{:S(2)}, u32[]{:S(2)}) collective-permute-start(bf16[64,1536]{1,0:T(8,128)(2,1)S(1)} %get-tuple-element.50), channel_id=1, source_target_pairs={{0,4},{1,5},{2,6},{3,7},{4,0},{5,1},{6,2},{7,3},{8,12},{9,13},{10,... | collective-permute-start | bytes 589832 | tf_op jit(solution)/shard_map/ppermute | solution.py:557
  20.0 9.5 %collective-permute-start.3 = (bf16[64,1536]{1,0:T(8,128)(2,1)S(1)}, bf16[64,1536]{1,0:T(8,128)(2,1)S(1)}, u32[]{:S(2)}, u32[]{:S(2)}) collective-permute-start(bf16[64,1536]{1,0:T(8,128)(2,1)S(1)} %get-tuple-element.51), channel_id=1, source_target_pairs={{0,2},{1,3},{2,0},{3,1},{4,6},{5,7},{6,4},{7,5},{8,10},{9,11},{10,... | collective-permute-start | bytes 589832 | tf_op jit(solution)/shard_map/ppermute | solution.py:557
  20.3 9.8 %collective-permute-start.7 = (bf16[16,512]{1,0:T(8,128)(2,1)S(1)}, bf16[16,512]{1,0:T(8,128)(2,1)S(1)}, u32[]{:S(2)}, u32[]{:S(2)}) collective-permute-start(bf16[16,512]{1,0:T(8,128)(2,1)S(1)} %get-tuple-element.58), channel_id=1, source_target_pairs={{0,8},{8,16},{16,24},{1,9},{9,17},{17,25},{2,10},{10,18},{18,26},{... | collective-permute-start | bytes 49160 | tf_op jit(solution)/shard_map/ppermute | solution.py:624
  23.5 6.6 %collective-permute-start.8 = (bf16[16,512]{1,0:T(8,128)(2,1)S(1)}, bf16[16,512]{1,0:T(8,128)(2,1)S(1)}, u32[]{:S(2)}, u32[]{:S(2)}) collective-permute-start(bf16[16,512]{1,0:T(8,128)(2,1)S(1)} %get-tuple-element.59), channel_id=1, source_target_pairs={{8,0},{16,8},{24,16},{9,1},{17,9},{25,17},{10,2},{18,10},{26,18},{... | collective-permute-start | bytes 49160 | tf_op jit(solution)/shard_map/ppermute | solution.py:623
  37.4 2.5 %collective-permute-start.9 = (f32[96,256]{1,0:T(8,128)S(1)}, f32[96,256]{1,0:T(8,128)S(1)}, u32[]{:S(2)}, u32[]{:S(2)}) collective-permute-start(f32[96,256]{1,0:T(8,128)S(1)} %get-tuple-element.68), channel_id=1, source_target_pairs={{0,1},{1,0},{2,3},{3,2},{4,5},{5,4},{6,7},{7,6},{8,9},{9,8},{10,11... | collective-permute-start | bytes 294920 | tf_op jit(solution)/shard_map/ppermute | solution.py:557
  40.2 3.9 %collective-permute-start.12 = (bf16[96,256]{1,0:T(8,128)(2,1)S(1)}, bf16[96,256]{1,0:T(8,128)(2,1)S(1)}, u32[]{:S(2)}, u32[]{:S(2)}) collective-permute-start(bf16[96,256]{1,0:T(8,128)(2,1)S(1)} %get-tuple-element.75), channel_id=1, source_target_pairs={{0,6},{1,7},{2,4},{3,5},{4,2},{5,3},{6,0},{7,1},{8,14},{9,15},{10,... | collective-permute-start | bytes 147464 | tf_op jit(solution)/shard_map/ppermute | solution.py:677
  42.2 3.2 %collective-permute-start.11 = (bf16[96,256]{1,0:T(8,128)(2,1)S(1)}, bf16[96,256]{1,0:T(8,128)(2,1)S(1)}, u32[]{:S(2)}, u32[]{:S(2)}) collective-permute-start(bf16[96,256]{1,0:T(8,128)(2,1)S(1)} %get-tuple-element.75), channel_id=1, source_target_pairs={{0,4},{1,5},{2,6},{3,7},{4,0},{5,1},{6,2},{7,3},{8,12},{9,13},{10,... | collective-permute-start | bytes 147464 | tf_op jit(solution)/shard_map/ppermute | solution.py:677
  42.5 2.9 %collective-permute-start.10 = (bf16[96,256]{1,0:T(8,128)(2,1)S(1)}, bf16[96,256]{1,0:T(8,128)(2,1)S(1)}, u32[]{:S(2)}, u32[]{:S(2)}) collective-permute-start(bf16[96,256]{1,0:T(8,128)(2,1)S(1)} %get-tuple-element.75), channel_id=1, source_target_pairs={{0,2},{1,3},{2,0},{3,1},{4,6},{5,7},{6,4},{7,5},{8,10},{9,11},{10,... | collective-permute-start | bytes 147464 | tf_op jit(solution)/shard_map/ppermute | solution.py:677
  45.8 4.8 %collective-permute-start.15 = (bf16[96,256]{1,0:T(8,128)(2,1)S(1)}, bf16[96,256]{1,0:T(8,128)(2,1)S(1)}, u32[]{:S(2)}, u32[]{:S(2)}) collective-permute-start(bf16[96,256]{1,0:T(8,128)(2,1)S(1)} %get-tuple-element.73), channel_id=1, source_target_pairs={{0,24},{8,16},{16,8},{24,0},{1,25},{9,17},{17,9},{25,1},{2,26},{10... | collective-permute-start | bytes 147464 | tf_op jit(solution)/shard_map/ppermute | solution.py:677
  48.7 4.9 %collective-permute-start.14 = (bf16[96,256]{1,0:T(8,128)(2,1)S(1)}, bf16[96,256]{1,0:T(8,128)(2,1)S(1)}, u32[]{:S(2)}, u32[]{:S(2)}) collective-permute-start(bf16[96,256]{1,0:T(8,128)(2,1)S(1)} %get-tuple-element.73), channel_id=1, source_target_pairs={{0,16},{8,24},{16,0},{24,8},{1,17},{9,25},{17,1},{25,9},{2,18},{10... | collective-permute-start | bytes 147464 | tf_op jit(solution)/shard_map/ppermute | solution.py:677
  48.7 4.9 %collective-permute-start.13 = (bf16[96,256]{1,0:T(8,128)(2,1)S(1)}, bf16[96,256]{1,0:T(8,128)(2,1)S(1)}, u32[]{:S(2)}, u32[]{:S(2)}) collective-permute-start(bf16[96,256]{1,0:T(8,128)(2,1)S(1)} %get-tuple-element.73), channel_id=1, source_target_pairs={{0,8},{8,0},{16,24},{24,16},{1,9},{9,1},{17,25},{25,17},{2,10},{10... | collective-permute-start | bytes 147464 | tf_op jit(solution)/shard_map/ppermute | solution.py:677
  53.6 3.8 %collective-permute-start.16 = (f32[96,256]{1,0:T(8,128)S(1)}, f32[96,256]{1,0:T(8,128)S(1)}, u32[]{:S(2)}, u32[]{:S(2)}) collective-permute-start(f32[96,256]{1,0:T(8,128)S(1)} %add_add_fusion.own), channel_id=1, source_target_pairs={{0,1},{1,0},{2,3},{3,2},{4,5},{5,4},{6,7},{7,6},{8,9},{9,8},{10,11... | collective-permute-start | bytes 294920 | tf_op jit(solution)/shard_map/ppermute | solution.py:557

commit v5 on v4

--- a/solution.py
+++ b/solution.py
@@ -93,12 +93,14 @@
         out[target, slots : 2 * slots, :] = weights
 
 
-def store_kernel(bands, me_ref, own, mate, stored, edge):
+def store_kernel(bands, me_ref, own, mate, stored, edge, sem):
     store, row_width = own.shape
     patch_cols = row_width // bands
     core = me_ref[0] % 2
-    stored[pl.ds(pl.multiple_of(core * store, 64), store), :] = own[...]
+    copy = pltpu.make_async_copy(own, stored.at[pl.ds(pl.multiple_of(core * store, 64), store)], sem)
+    copy.start()
     stored[pl.ds(pl.multiple_of((1 - core) * store, 64), store), :] = mate[...]
+    copy.wait()
     row_id = iota((6 * GROUP, patch_cols), 0)
     lane_id = iota((6 * GROUP, patch_cols), 1)
     column = row_id // GROUP
@@ -260,7 +262,18 @@
     strips[...] = side[...].astype(BF16)
 
 
-def weights_kernel(conv1, conv2, head, one_main, one_strip, two_main, two_back, head_pad, head_turn, wide, tall):
+def weights_kernel(
+    conv1_hbm, conv2_hbm, head_hbm, one_main, one_strip, two_main, two_back, head_pad, head_turn,
+    wide, tall, conv1, conv2, head, sems,
+):
+    copies = [
+        pltpu.make_async_copy(source, target, sems.at[i])
+        for i, (source, target) in enumerate(((conv1_hbm, conv1), (conv2_hbm, conv2), (head_hbm, head)))
+    ]
+    for copy in copies:
+        copy.start()
+    for copy in copies:
+        copy.wait()
     bands = conv1.shape[1]
     feat = conv2.shape[1]
     classes = head.shape[0]
@@ -557,6 +570,7 @@
         return lax.ppermute(value, "lon", [(i, i ^ move) for i in range(lon_count)])
 
     hbm = pl.BlockSpec(memory_space=pltpu.HBM)
+    in_hbm = lambda value: pltpu.with_memory_space_constraint(value, pltpu.HBM)
     plan, tile_labels = call(
         functools.partial(plan_kernel, store),
         [struct((lon_count, 16, 128), F32), struct((rows, cols), F32)],
@@ -577,9 +591,10 @@
     stored, edge = call(
         functools.partial(store_kernel, bands),
         [struct((2 * store, row_width), BF16), struct((6 * GROUP, 2 * store), BF16)],
-        in_specs=[smem, vmem, vmem],
+        [pltpu.SemaphoreType.DMA],
+        in_specs=[smem, hbm, vmem],
         cost_estimate=pl.CostEstimate(flops=10**9, bytes_accessed=10**7, transcendentals=0),
-    )(me, patches, mate_patches)
+    )(me, in_hbm(patches), mate_patches)
     plans, stored, edge = lax.optimization_barrier((plans, stored, edge))
     moves = list(range(chips - 1, -1, -1))
     cost = pl.CostEstimate(flops=10**9, bytes_accessed=10**7, transcendentals=0)
@@ -599,6 +614,8 @@
     smalls = [by_lon(small, 2 * move) if move else small for move, small in zip(moves, smalls)]
     parts = []
     for some in (moves[:-1], moves[-1:]):
+        if len(some) == 1:
+            row_weights, *smalls = lax.optimization_barrier((row_weights, *smalls))
         parts += call(
             functools.partial(part_kernel, [moves.index(move) for move in some]),
             [struct((rows, row_width), BF16 if move else F32) for move in some],
@@ -633,8 +650,16 @@
             struct((GROUP, feat), BF16),
             struct((feat, GROUP), BF16),
         ],
-        [pltpu.VMEM((9 * GROUP, feat), F32), pltpu.VMEM((128, 128), F32)],
-    )(conv1_weight.transpose(0, 2, 1), conv2_weight, head_weight)
+        [
+            pltpu.VMEM((9 * GROUP, feat), F32),
+            pltpu.VMEM((128, 128), F32),
+            pltpu.VMEM((9, bands, feat), BF16),
+            pltpu.VMEM(conv2_weight.shape, BF16),
+            pltpu.VMEM(head_weight.shape, BF16),
+            pltpu.SemaphoreType.DMA((3,)),
+        ],
+        in_specs=[hbm] * 3,
+    )(*[in_hbm(value) for value in (conv1_weight.transpose(0, 2, 1), conv2_weight, head_weight)])
 
     ext = rows + 6
     half = 3 * feat // 2

time: 58.9 us -> 57.5 us (0.976)
  local copies, waits for them, and re-layouts: 4.72 us -> 1.3 us
  Pallas kernels: 14.1 us -> 16.1 us
    unnamed x11 -> x3, local copies, waits for them, and re-layouts: 4.68 us -> 1.26 us
    all_to_all x1, waiting for transfers between devices: 0.01 us -> 1.21 us  [body(): plans = lax.all_to_all(plan, 'lon', split_axis=0, concat_axis=0, tiled=True)]
    pallas_call x1, Pallas kernels: 0.69 us -> 1.7 us  [body(): call(functools.partial(store_kernel, bands), [struct((2 * store, row_widt...]
    pallas_call x1, Pallas kernels: 0.18 us -> 1.14 us  [body(): call(weights_kernel, [struct((feat, 9 * GROUP), BF16), struct((feat, 9 *...]
  transfers between devices with their start and end apart: 18 -> 18, of which waited for: 7 -> 8; matrix products, arithmetic and copies ran while one was open for 2% -> 2% of each run, Pallas kernels for 4% -> 8%
where the time goes in v5:
time: 57.5 us; the launch traced here: 57.1 us
  starting transfers between devices  25.7 us (45%)
  Pallas kernels  16.1 us (28%)
  waiting for transfers between devices  12.6 us (22%)
  local copies, waits for them, and re-layouts  1.3 us (2%)
  between operations  0.85 us (1%)
    ppermute x9, starting transfers between devices, by_lon(): return lax.ppermute(value, 'lon', [(i, i ^ move) for i in range(lon_count)])  9.62 us
    pallas_call x1, Pallas kernels, body(): call(functools.partial(network_kernel, bands, classes, rows, cols, lat_co...  7.18 us
    ppermute x6, starting transfers between devices, sum_over(): lax.ppermute(sent, axis, [(i, i ^ move) for i in range(size)]).astype(F32)  6.33 us
    ppermute x6, waiting for transfers between devices, sum_over(): lax.ppermute(sent, axis, [(i, i ^ move) for i in range(size)]).astype(F32)  6.23 us
    all_to_all x1, starting transfers between devices, body(): plans = lax.all_to_all(plan, 'lon', split_axis=0, concat_axis=0, tiled=True)  5.28 us
    ppermute x9, waiting for transfers between devices, by_lon(): return lax.ppermute(value, 'lon', [(i, i ^ move) for i in range(lon_count)])  5.14 us
    ppermute x1, starting transfers between devices, body(): lax.ppermute(lower, 'lat', [(i, i + 1) for i in range(lat_count - 1)])  3.21 us
    pallas_call x1, Pallas kernels, body(): call(functools.partial(plan_kernel, store), [struct((lon_count, 16, 128),...  1.77 us
  transfers between devices with their start and end apart: 18, of which 8 were waited for; matrix products, arithmetic and copies ran while one was open for 2% of the time, Pallas kernels for 8%

profile of v5, /device:TPU:1, one launch (start us, length us, event | category | flops | bytes accessed | tf_op | source)
XLA Modules:
  0.0 57.1 jit_solution(5770642842093927509)
XLA Ops:
  0.6 1.8 %shard_map.128 = (f32[8,16,128]{2,1,0:T(8,128)}, f32[64,128]{1,0:T(8,128)}) custom-call(s32[1,512]{1,0:T(1,128)} %requests_hbm.1, s32[8,64]{1,0:T(8,128)} %bitcast.12, s32[8,64]{1,0:T(8,128)} %bitcast.13, f32[16]{0:T(128)} %levels_hbm.1, s32[64,128]{1,0:T(8,128)} %labels_hbm.1), custom_call_target="tpu_custom_call" | custom-call | tf_op jit(solution)/shard_map/pallas_call | solution.py:574
  2.4 0.1 collective-permute-start
  2.5 5.3 %all-to-all-start = ((f32[8,16,128]{2,1,0:T(8,128)}), f32[8,16,128]{2,1,0:T(8,128)S(1)}, u32[]{:S(2)}, u32[]{:S(2)}) async-start(f32[8,16,128]{2,1,0:T(8,128)} %get-tuple-element.45), calls=%async_computation | async-start | bytes 131072 | tf_op jit(solution)/shard_map/all_to_all | solution.py:590
  7.8 1.1 %shard_map.135 = (bf16[64,144]{1,0:T(8,128)(2,1)S(1)}, bf16[64,144]{1,0:T(8,128)(2,1)S(1)}, bf16[192,192]{1,0:T(8,128)(2,1)S(1)}, bf16[192,192]{1,0:T(8,128)(2,1...) custom-call(bf16[9,12,64]{2,1,0:T(8,128)(2,1)} %bitcast.11, bf16[9,64,64]{2,1,0:T(8,128)(2,1)} %conv2_hbm.1, ...), custom_call_target="tpu_custom_call" | custom-call | tf_op jit(solution)/shard_map/pallas_call | solution.py:643
  9.0 0.1 pad_add_fusion.place
  9.0 0.0 collective-permute-done.mate
  9.1 1.7 %shard_map.129 = (bf16[384,1536]{1,0:T(8,128)(2,1)S(1)}, bf16[96,384]{1,0:T(8,128)(2,1)S(1)}) custom-call(s32[1]{0:T(128)} %bitcast.1.me_ref, bf16[192,1536]{1,0:T(8,128)(2,1)} %own, bf16[192,1536]{1,0:T(8,128)(2,1)S(1)} %collective-permute-done.mate), custom_call_target="tpu_custom_call" | custom-call | flops 1000000000 | bytes 10000000 | tf_op jit(solution)/shard_map/pallas_call | solution.py:591
  10.8 1.2 %all-to-all-done.plans = f32[8,16,128]{2,1,0:T(8,128)S(1)} async-done(((f32[8,16,128]{2,1,0:T(8,128)}), f32[8,16,128]{2,1,0:T(8,128)S(1)}, u32[]{:S(2)}, u32[]{:S(2)}) %all-to-all-start) | async-done | bytes 65568 | tf_op jit(solution)/shard_map/all_to_all | solution.py:590
  12.0 1.3 %shard_map.130 = (f32[4,64,384]{2,1,0:T(8,128)S(1)}, bf16[128,128]{1,0:T(8,128)(2,1)S(1)}, bf16[128,128]{1,0:T(8,128)(2,1)S(1)}, bf16[128,128]{1,0:T(8,128)(2,1)S(1)}, f32[128,128]{1,0:T(8,128)S(1)}) custom-call(s32[1]{0:T(128)} %bitcast.1.me_ref, f32[8,16,128]{2,1,0:T(8,128)S(1)} %all-to-all-done.plans, bf16[384,1536]{1,0:T(8,128)(2,1)S(1)} %get-tuple-element.51.stored, ...), custom_call_target="tpu_custom_call" | custom-call | flops 1000000000 | bytes 10000000 | tf_op jit(solution)/shard_map/pallas_call | solution.py:601
  13.3 1.2 %collective-permute-start.4 = (bf16[128,128]{1,0:T(8,128)(2,1)S(1)}, bf16[128,128]{1,0:T(8,128)(2,1)S(1)}, u32[]{:S(2)}, u32[]{:S(2)}) collective-permute-start(bf16[128,128]{1,0:T(8,128)(2,1)S(1)} %get-tuple-element.57), channel_id=1, source_target_pairs={{0,6},{1,7},{2,4},{3,5},{4,2},{5,3},{6,0},{7,1},{8,14},{9,15},{10,... | collective-permute-start | bytes 98312 | tf_op jit(solution)/shard_map/ppermute | solution.py:570
  14.4 0.7 %collective-permute-start.5 = (bf16[128,128]{1,0:T(8,128)(2,1)S(1)}, bf16[128,128]{1,0:T(8,128)(2,1)S(1)}, u32[]{:S(2)}, u32[]{:S(2)}) collective-permute-start(bf16[128,128]{1,0:T(8,128)(2,1)S(1)} %get-tuple-element.58), channel_id=1, source_target_pairs={{0,4},{1,5},{2,6},{3,7},{4,0},{5,1},{6,2},{7,3},{8,12},{9,13},{10,... | collective-permute-start | bytes 98312 | tf_op jit(solution)/shard_map/ppermute | solution.py:570
  15.1 0.9 %collective-permute-start.6 = (bf16[128,128]{1,0:T(8,128)(2,1)S(1)}, bf16[128,128]{1,0:T(8,128)(2,1)S(1)}, u32[]{:S(2)}, u32[]{:S(2)}) collective-permute-start(bf16[128,128]{1,0:T(8,128)(2,1)S(1)} %get-tuple-element.59), channel_id=1, source_target_pairs={{0,2},{1,3},{2,0},{3,1},{4,6},{5,7},{6,4},{7,5},{8,10},{9,11},{10,... | collective-permute-start | bytes 98312 | tf_op jit(solution)/shard_map/ppermute | solution.py:570
  16.0 0.8 %shard_map.131 = (bf16[64,1536]{1,0:T(8,128)(2,1)S(1)}, bf16[64,1536]{1,0:T(8,128)(2,1)S(1)}, bf16[64,1536]{1,0:T(8,128)(2,1)S(1)}) custom-call(bf16[384,1536]{1,0:T(8,128)(2,1)S(1)} %get-tuple-element.51.stored, f32[4,64,384]{2,1,0:T(8,128)S(1)} %get-tuple-element.61.row_weights), custom_call_target="tpu_custom_call" | custom-call | flops 1000000000 | bytes 10000000 | tf_op jit(solution)/shard_map/pallas_call | solution.py:619
  16.8 1.2 %collective-permute-start.1 = (bf16[64,1536]{1,0:T(8,128)(2,1)S(1)}, bf16[64,1536]{1,0:T(8,128)(2,1)S(1)}, u32[]{:S(2)}, u32[]{:S(2)}) collective-permute-start(bf16[64,1536]{1,0:T(8,128)(2,1)S(1)} %get-tuple-element.54), channel_id=1, source_target_pairs={{0,6},{1,7},{2,4},{3,5},{4,2},{5,3},{6,0},{7,1},{8,14},{9,15},{10,... | collective-permute-start | bytes 589832 | tf_op jit(solution)/shard_map/ppermute | solution.py:570
  17.9 0.7 %collective-permute-start.2 = (bf16[64,1536]{1,0:T(8,128)(2,1)S(1)}, bf16[64,1536]{1,0:T(8,128)(2,1)S(1)}, u32[]{:S(2)}, u32[]{:S(2)}) collective-permute-start(bf16[64,1536]{1,0:T(8,128)(2,1)S(1)} %get-tuple-element.55), channel_id=1, source_target_pairs={{0,4},{1,5},{2,6},{3,7},{4,0},{5,1},{6,2},{7,3},{8,12},{9,13},{10,... | collective-permute-start | bytes 589832 | tf_op jit(solution)/shard_map/ppermute | solution.py:570
  18.6 0.0 collective-permute-done.4.refs_4_.refs_0_
  18.6 0.9 %collective-permute-start.3 = (bf16[64,1536]{1,0:T(8,128)(2,1)S(1)}, bf16[64,1536]{1,0:T(8,128)(2,1)S(1)}, u32[]{:S(2)}, u32[]{:S(2)}) collective-permute-start(bf16[64,1536]{1,0:T(8,128)(2,1)S(1)} %get-tuple-element.56), channel_id=1, source_target_pairs={{0,2},{1,3},{2,0},{3,1},{4,6},{5,7},{6,4},{7,5},{8,10},{9,11},{10,... | collective-permute-start | bytes 589832 | tf_op jit(solution)/shard_map/ppermute | solution.py:570
  19.5 0.0 collective-permute-done.5.refs_5_.refs_1_
  19.5 0.0 collective-permute-done.6.refs_6_.refs_2_
  19.5 0.2 shard_map.134
  19.7 3.2 %collective-permute-start.7 = (bf16[16,512]{1,0:T(8,128)(2,1)S(1)}, bf16[16,512]{1,0:T(8,128)(2,1)S(1)}, u32[]{:S(2)}, u32[]{:S(2)}) collective-permute-start(bf16[16,512]{1,0:T(8,128)(2,1)S(1)} %get-tuple-element.68), channel_id=1, source_target_pairs={{0,8},{8,16},{16,24},{1,9},{9,17},{17,25},{2,10},{10,18},{18,26},{... | collective-permute-start | bytes 49160 | tf_op jit(solution)/shard_map/ppermute | solution.py:641
  22.9 1.3 %collective-permute-start.8 = (bf16[16,512]{1,0:T(8,128)(2,1)S(1)}, bf16[16,512]{1,0:T(8,128)(2,1)S(1)}, u32[]{:S(2)}, u32[]{:S(2)}) collective-permute-start(bf16[16,512]{1,0:T(8,128)(2,1)S(1)} %get-tuple-element.69), channel_id=1, source_target_pairs={{8,0},{16,8},{24,16},{9,1},{17,9},{25,17},{10,2},{18,10},{26,18},{... | collective-permute-start | bytes 49160 | tf_op jit(solution)/shard_map/ppermute | solution.py:640
  24.2 0.4 shard_map.132.refs_3_
  24.6 4.2 %collective-permute-done.2.refs_1_ = bf16[64,1536]{1,0:T(8,128)(2,1)S(1)} collective-permute-done((bf16[64,1536]{1,0:T(8,128)(2,1)S(1)}, bf16[64,1536]{1,0:T(8,128)(2,1)S(1)}, u32[]{:S(2)}, u32[]{:S(2)}) %collective-permute-start.2) | collective-permute-done | bytes 196640 | tf_op jit(solution)/shard_map/ppermute | solution.py:570
  28.8 0.0 collective-permute-done.3.refs_2_
  28.8 0.7 %shard_map.133 = (bf16[16,8192]{1,0:T(8,128)(2,1)S(1)}, bf16[160,128]{1,0:T(8,128)(2,1)S(1)}) custom-call(s32[1]{0:T(128)} %bitcast.1.me_ref, f32[8,16,128]{2,1,0:T(8,128)S(1)} %all-to-all-done.plans, f32[64,128]{1,0:T(8,128)S(1)} %copy-done, bf16[64,1536]{1,0:T(8,128)(2,1)S(1)} %collective-permute-done.1.refs_0_, ...), custom_call_target="tpu_custom_call" | custom-call | flops 1000000000 | bytes 10000000 | tf_op jit(solution)/shard_map/pallas_call | solution.py:633
  29.4 0.0 collective-permute-done.8.below
  29.5 7.2 %shard_map.136 = (bf16[64,8192]{1,0:T(8,128)(2,1)S(1)}, f32[96,256]{1,0:T(8,128)S(1)}, f32[96,256]{1,0:T(8,128)S(1)}) custom-call(s32[2]{0:T(128)S(1)} %pad_add_fusion.place, bf16[16,8192]{1,0:T(8,128)(2,1)S(1)} %get-tuple-element.66.main, bf16[160,128]{1,0:T(8,128)(2,1)S(1)} %get-tuple-element.67.strips, bf16[16,512]{1,0:T(8,128)(2,1)S(1)} %collective-permute-done.7.above, ...), custom_call_target="tpu_custom_call" | custom-call | tf_op jit(solution)/shard_map/pallas_call | solution.py:667
  36.6 1.9 %collective-permute-start.9 = (f32[96,256]{1,0:T(8,128)S(1)}, f32[96,256]{1,0:T(8,128)S(1)}, u32[]{:S(2)}, u32[]{:S(2)}) collective-permute-start(f32[96,256]{1,0:T(8,128)S(1)} %get-tuple-element.78), channel_id=1, source_target_pairs={{0,1},{1,0},{2,3},{3,2},{4,5},{5,4},{6,7},{7,6},{8,9},{9,8},{10,11... | collective-permute-start | bytes 294920 | tf_op jit(solution)/shard_map/ppermute | solution.py:570
  38.6 0.9 %collective-permute-done.9 = f32[96,256]{1,0:T(8,128)S(1)} collective-permute-done((f32[96,256]{1,0:T(8,128)S(1)}, f32[96,256]{1,0:T(8,128)S(1)}, u32[]{:S(2)}, u32[]{:S(2)}) %collective-permute-start.9) | collective-permute-done | bytes 98336 | tf_op jit(solution)/shard_map/ppermute | solution.py:570
  39.5 0.1 reduce-precision_subtract_fusion.1
  39.7 0.1 fusion.1
  39.8 0.7 %collective-permute-start.12 = (bf16[96,256]{1,0:T(8,128)(2,1)S(1)}, bf16[96,256]{1,0:T(8,128)(2,1)S(1)}, u32[]{:S(2)}, u32[]{:S(2)}) collective-permute-start(bf16[96,256]{1,0:T(8,128)(2,1)S(1)} %get-tuple-element.85), channel_id=1, source_target_pairs={{0,6},{1,7},{2,4},{3,5},{4,2},{5,3},{6,0},{7,1},{8,14},{9,15},{10,... | collective-permute-start | bytes 147464 | tf_op jit(solution)/shard_map/ppermute | solution.py:702
  40.4 0.9 %collective-permute-start.11 = (bf16[96,256]{1,0:T(8,128)(2,1)S(1)}, bf16[96,256]{1,0:T(8,128)(2,1)S(1)}, u32[]{:S(2)}, u32[]{:S(2)}) collective-permute-start(bf16[96,256]{1,0:T(8,128)(2,1)S(1)} %get-tuple-element.85), channel_id=1, source_target_pairs={{0,4},{1,5},{2,6},{3,7},{4,0},{5,1},{6,2},{7,3},{8,12},{9,13},{10,... | collective-permute-start | bytes 147464 | tf_op jit(solution)/shard_map/ppermute | solution.py:702
  41.3 1.2 %collective-permute-start.10 = (bf16[96,256]{1,0:T(8,128)(2,1)S(1)}, bf16[96,256]{1,0:T(8,128)(2,1)S(1)}, u32[]{:S(2)}, u32[]{:S(2)}) collective-permute-start(bf16[96,256]{1,0:T(8,128)(2,1)S(1)} %get-tuple-element.85), channel_id=1, source_target_pairs={{0,2},{1,3},{2,0},{3,1},{4,6},{5,7},{6,4},{7,5},{8,10},{9,11},{10,... | collective-permute-start | bytes 147464 | tf_op jit(solution)/shard_map/ppermute | solution.py:702
  42.5 1.3 %collective-permute-done.12 = bf16[96,256]{1,0:T(8,128)(2,1)S(1)} collective-permute-done((bf16[96,256]{1,0:T(8,128)(2,1)S(1)}, bf16[96,256]{1,0:T(8,128)(2,1)S(1)}, u32[]{:S(2)}, u32[]{:S(2)}) %collective-permute-start.12) | collective-permute-done | bytes 49184 | tf_op jit(solution)/shard_map/ppermute | solution.py:702
  43.8 0.1 collective-permute-done.11
  43.9 0.6 %collective-permute-done.10 = bf16[96,256]{1,0:T(8,128)(2,1)S(1)} collective-permute-done((bf16[96,256]{1,0:T(8,128)(2,1)S(1)}, bf16[96,256]{1,0:T(8,128)(2,1)S(1)}, u32[]{:S(2)}, u32[]{:S(2)}) %collective-permute-start.10) | collective-permute-done | bytes 49184 | tf_op jit(solution)/shard_map/ppermute | solution.py:702
  44.6 0.1 reduce-precision_subtract_fusion
  44.7 0.1 fusion
  44.8 2.6 %collective-permute-start.15 = (bf16[96,256]{1,0:T(8,128)(2,1)S(1)}, bf16[96,256]{1,0:T(8,128)(2,1)S(1)}, u32[]{:S(2)}, u32[]{:S(2)}) collective-permute-start(bf16[96,256]{1,0:T(8,128)(2,1)S(1)} %get-tuple-element.83), channel_id=1, source_target_pairs={{0,24},{8,16},{16,8},{24,0},{1,25},{9,17},{17,9},{25,1},{2,26},{10... | collective-permute-start | bytes 147464 | tf_op jit(solution)/shard_map/ppermute | solution.py:702
  47.4 1.0 %collective-permute-start.13 = (bf16[96,256]{1,0:T(8,128)(2,1)S(1)}, bf16[96,256]{1,0:T(8,128)(2,1)S(1)}, u32[]{:S(2)}, u32[]{:S(2)}) collective-permute-start(bf16[96,256]{1,0:T(8,128)(2,1)S(1)} %get-tuple-element.83), channel_id=1, source_target_pairs={{0,8},{8,0},{16,24},{24,16},{1,9},{9,1},{17,25},{25,17},{2,10},{10... | collective-permute-start | bytes 147464 | tf_op jit(solution)/shard_map/ppermute | solution.py:702
  48.4 1.2 %collective-permute-done.15 = bf16[96,256]{1,0:T(8,128)(2,1)S(1)} collective-permute-done((bf16[96,256]{1,0:T(8,128)(2,1)S(1)}, bf16[96,256]{1,0:T(8,128)(2,1)S(1)}, u32[]{:S(2)}, u32[]{:S(2)}) %collective-permute-start.15) | collective-permute-done | bytes 49184 | tf_op jit(solution)/shard_map/ppermute | solution.py:702
  49.6 3.0 %collective-permute-done.14 = bf16[96,256]{1,0:T(8,128)(2,1)S(1)} collective-permute-done((bf16[96,256]{1,0:T(8,128)(2,1)S(1)}, bf16[96,256]{1,0:T(8,128)(2,1)S(1)}, u32[]{:S(2)}, u32[]{:S(2)}) %collective-permute-start.14) | collective-permute-done | bytes 49184 | tf_op jit(solution)/shard_map/ppermute | solution.py:702
  52.6 0.0 collective-permute-done.13
  52.6 2.1 %collective-permute-start.16 = (f32[96,256]{1,0:T(8,128)S(1)}, f32[96,256]{1,0:T(8,128)S(1)}, u32[]{:S(2)}, u32[]{:S(2)}) collective-permute-start(f32[96,256]{1,0:T(8,128)S(1)} %add_add_fusion.own), channel_id=1, source_target_pairs={{0,1},{1,0},{2,3},{3,2},{4,5},{5,4},{6,7},{7,6},{8,9},{9,8},{10,11... | collective-permute-start | bytes 294920 | tf_op jit(solution)/shard_map/ppermute | solution.py:570
  54.8 1.3 %copy.14 = bf16[8,8,64,128]{3,2,1,0:T(8,128)(2,1)} copy(bf16[8,8,64,128]{3,1,2,0:T(8,128)(2,1)S(1)} %bitcast.9) | data formatting | bytes 2097152
  56.1 1.0 %shard_map.137 = (f32[9,12,64]{2,1,0:T(8,128)}, f32[9,64,64]{2,1,0:T(8,128)}, f32[11,64]{1,0:T(8,128)}, f32[1,1]{1,0:T(1,128)}) custom-call(s32[1]{0:T(128)} %bitcast.1.me_ref, f32[96,256]{1,0:T(8,128)S(1)} %add_add_fusion.own, f32[96,256]{1,0:T(8,128)S(1)} %collective-permute-done.16.mate), custom_call_target="tpu_custom_call" | custom-call | tf_op jit(solution)/shard_map/pallas_call | solution.py:710
  (19 shorter events, 0.1 us)
Async XLA Ops:
  2.4 6.6 %collective-permute-start = (bf16[192,1536]{1,0:T(8,128)(2,1)}, bf16[192,1536]{1,0:T(8,128)(2,1)S(1)}, u32[]{:S(2)}, u32[]{:S(2)}) collective-permute-start(bf16[192,1536]{1,0:T(8,128)(2,1)} %own), channel_id=1, source_target_pairs={{0,1},{1,0},{2,3},{3,2},{4,5},{5,4},{6,7},{7,6},{8,9},{9,8},{10,11... | collective-permute-start | bytes 1769480 | tf_op jit(solution)/shard_map/ppermute | solution.py:570
  2.5 9.4 %all-to-all-start = ((f32[8,16,128]{2,1,0:T(8,128)}), f32[8,16,128]{2,1,0:T(8,128)S(1)}, u32[]{:S(2)}, u32[]{:S(2)}) async-start(f32[8,16,128]{2,1,0:T(8,128)} %get-tuple-element.45), calls=%async_computation | async-start | bytes 131072 | tf_op jit(solution)/shard_map/all_to_all | solution.py:590
  13.3 5.3 %collective-permute-start.4 = (bf16[128,128]{1,0:T(8,128)(2,1)S(1)}, bf16[128,128]{1,0:T(8,128)(2,1)S(1)}, u32[]{:S(2)}, u32[]{:S(2)}) collective-permute-start(bf16[128,128]{1,0:T(8,128)(2,1)S(1)} %get-tuple-element.57), channel_id=1, source_target_pairs={{0,6},{1,7},{2,4},{3,5},{4,2},{5,3},{6,0},{7,1},{8,14},{9,15},{10,... | collective-permute-start | bytes 98312 | tf_op jit(solution)/shard_map/ppermute | solution.py:570
  14.4 5.1 %collective-permute-start.5 = (bf16[128,128]{1,0:T(8,128)(2,1)S(1)}, bf16[128,128]{1,0:T(8,128)(2,1)S(1)}, u32[]{:S(2)}, u32[]{:S(2)}) collective-permute-start(bf16[128,128]{1,0:T(8,128)(2,1)S(1)} %get-tuple-element.58), channel_id=1, source_target_pairs={{0,4},{1,5},{2,6},{3,7},{4,0},{5,1},{6,2},{7,3},{8,12},{9,13},{10,... | collective-permute-start | bytes 98312 | tf_op jit(solution)/shard_map/ppermute | solution.py:570
  15.1 4.4 %collective-permute-start.6 = (bf16[128,128]{1,0:T(8,128)(2,1)S(1)}, bf16[128,128]{1,0:T(8,128)(2,1)S(1)}, u32[]{:S(2)}, u32[]{:S(2)}) collective-permute-start(bf16[128,128]{1,0:T(8,128)(2,1)S(1)} %get-tuple-element.59), channel_id=1, source_target_pairs={{0,2},{1,3},{2,0},{3,1},{4,6},{5,7},{6,4},{7,5},{8,10},{9,11},{10,... | collective-permute-start | bytes 98312 | tf_op jit(solution)/shard_map/ppermute | solution.py:570
  16.0 3.5 %copy-start = (f32[64,128]{1,0:T(8,128)S(1)}, f32[64,128]{1,0:T(8,128)}, u32[]{:S(2)}) copy-start(f32[64,128]{1,0:T(8,128)} %get-tuple-element.50.labels) | copy-start | bytes 98308
  16.8 7.8 %collective-permute-start.1 = (bf16[64,1536]{1,0:T(8,128)(2,1)S(1)}, bf16[64,1536]{1,0:T(8,128)(2,1)S(1)}, u32[]{:S(2)}, u32[]{:S(2)}) collective-permute-start(bf16[64,1536]{1,0:T(8,128)(2,1)S(1)} %get-tuple-element.54), channel_id=1, source_target_pairs={{0,6},{1,7},{2,4},{3,5},{4,2},{5,3},{6,0},{7,1},{8,14},{9,15},{10,... | collective-permute-start | bytes 589832 | tf_op jit(solution)/shard_map/ppermute | solution.py:570
  17.9 10.8 %collective-permute-start.2 = (bf16[64,1536]{1,0:T(8,128)(2,1)S(1)}, bf16[64,1536]{1,0:T(8,128)(2,1)S(1)}, u32[]{:S(2)}, u32[]{:S(2)}) collective-permute-start(bf16[64,1536]{1,0:T(8,128)(2,1)S(1)} %get-tuple-element.55), channel_id=1, source_target_pairs={{0,4},{1,5},{2,6},{3,7},{4,0},{5,1},{6,2},{7,3},{8,12},{9,13},{10,... | collective-permute-start | bytes 589832 | tf_op jit(solution)/shard_map/ppermute | solution.py:570
  18.6 10.2 %collective-permute-start.3 = (bf16[64,1536]{1,0:T(8,128)(2,1)S(1)}, bf16[64,1536]{1,0:T(8,128)(2,1)S(1)}, u32[]{:S(2)}, u32[]{:S(2)}) collective-permute-start(bf16[64,1536]{1,0:T(8,128)(2,1)S(1)} %get-tuple-element.56), channel_id=1, source_target_pairs={{0,2},{1,3},{2,0},{3,1},{4,6},{5,7},{6,4},{7,5},{8,10},{9,11},{10,... | collective-permute-start | bytes 589832 | tf_op jit(solution)/shard_map/ppermute | solution.py:570
  19.7 9.8 %collective-permute-start.7 = (bf16[16,512]{1,0:T(8,128)(2,1)S(1)}, bf16[16,512]{1,0:T(8,128)(2,1)S(1)}, u32[]{:S(2)}, u32[]{:S(2)}) collective-permute-start(bf16[16,512]{1,0:T(8,128)(2,1)S(1)} %get-tuple-element.68), channel_id=1, source_target_pairs={{0,8},{8,16},{16,24},{1,9},{9,17},{17,25},{2,10},{10,18},{18,26},{... | collective-permute-start | bytes 49160 | tf_op jit(solution)/shard_map/ppermute | solution.py:641
  22.9 6.6 %collective-permute-start.8 = (bf16[16,512]{1,0:T(8,128)(2,1)S(1)}, bf16[16,512]{1,0:T(8,128)(2,1)S(1)}, u32[]{:S(2)}, u32[]{:S(2)}) collective-permute-start(bf16[16,512]{1,0:T(8,128)(2,1)S(1)} %get-tuple-element.69), channel_id=1, source_target_pairs={{8,0},{16,8},{24,16},{9,1},{17,9},{25,17},{10,2},{18,10},{26,18},{... | collective-permute-start | bytes 49160 | tf_op jit(solution)/shard_map/ppermute | solution.py:640
  36.6 2.9 %collective-permute-start.9 = (f32[96,256]{1,0:T(8,128)S(1)}, f32[96,256]{1,0:T(8,128)S(1)}, u32[]{:S(2)}, u32[]{:S(2)}) collective-permute-start(f32[96,256]{1,0:T(8,128)S(1)} %get-tuple-element.78), channel_id=1, source_target_pairs={{0,1},{1,0},{2,3},{3,2},{4,5},{5,4},{6,7},{7,6},{8,9},{9,8},{10,11... | collective-permute-start | bytes 294920 | tf_op jit(solution)/shard_map/ppermute | solution.py:570
  39.8 4.0 %collective-permute-start.12 = (bf16[96,256]{1,0:T(8,128)(2,1)S(1)}, bf16[96,256]{1,0:T(8,128)(2,1)S(1)}, u32[]{:S(2)}, u32[]{:S(2)}) collective-permute-start(bf16[96,256]{1,0:T(8,128)(2,1)S(1)} %get-tuple-element.85), channel_id=1, source_target_pairs={{0,6},{1,7},{2,4},{3,5},{4,2},{5,3},{6,0},{7,1},{8,14},{9,15},{10,... | collective-permute-start | bytes 147464 | tf_op jit(solution)/shard_map/ppermute | solution.py:702
  40.4 3.5 %collective-permute-start.11 = (bf16[96,256]{1,0:T(8,128)(2,1)S(1)}, bf16[96,256]{1,0:T(8,128)(2,1)S(1)}, u32[]{:S(2)}, u32[]{:S(2)}) collective-permute-start(bf16[96,256]{1,0:T(8,128)(2,1)S(1)} %get-tuple-element.85), channel_id=1, source_target_pairs={{0,4},{1,5},{2,6},{3,7},{4,0},{5,1},{6,2},{7,3},{8,12},{9,13},{10,... | collective-permute-start | bytes 147464 | tf_op jit(solution)/shard_map/ppermute | solution.py:702
  41.3 3.2 %collective-permute-start.10 = (bf16[96,256]{1,0:T(8,128)(2,1)S(1)}, bf16[96,256]{1,0:T(8,128)(2,1)S(1)}, u32[]{:S(2)}, u32[]{:S(2)}) collective-permute-start(bf16[96,256]{1,0:T(8,128)(2,1)S(1)} %get-tuple-element.85), channel_id=1, source_target_pairs={{0,2},{1,3},{2,0},{3,1},{4,6},{5,7},{6,4},{7,5},{8,10},{9,11},{10,... | collective-permute-start | bytes 147464 | tf_op jit(solution)/shard_map/ppermute | solution.py:702
  44.8 4.8 %collective-permute-start.15 = (bf16[96,256]{1,0:T(8,128)(2,1)S(1)}, bf16[96,256]{1,0:T(8,128)(2,1)S(1)}, u32[]{:S(2)}, u32[]{:S(2)}) collective-permute-start(bf16[96,256]{1,0:T(8,128)(2,1)S(1)} %get-tuple-element.83), channel_id=1, source_target_pairs={{0,24},{8,16},{16,8},{24,0},{1,25},{9,17},{17,9},{25,1},{2,26},{10... | collective-permute-start | bytes 147464 | tf_op jit(solution)/shard_map/ppermute | solution.py:702
  47.4 5.2 %collective-permute-start.14 = (bf16[96,256]{1,0:T(8,128)(2,1)S(1)}, bf16[96,256]{1,0:T(8,128)(2,1)S(1)}, u32[]{:S(2)}, u32[]{:S(2)}) collective-permute-start(bf16[96,256]{1,0:T(8,128)(2,1)S(1)} %get-tuple-element.83), channel_id=1, source_target_pairs={{0,16},{8,24},{16,0},{24,8},{1,17},{9,25},{17,1},{25,9},{2,18},{10... | collective-permute-start | bytes 147464 | tf_op jit(solution)/shard_map/ppermute | solution.py:702
  47.4 5.2 %collective-permute-start.13 = (bf16[96,256]{1,0:T(8,128)(2,1)S(1)}, bf16[96,256]{1,0:T(8,128)(2,1)S(1)}, u32[]{:S(2)}, u32[]{:S(2)}) collective-permute-start(bf16[96,256]{1,0:T(8,128)(2,1)S(1)} %get-tuple-element.83), channel_id=1, source_target_pairs={{0,8},{8,0},{16,24},{24,16},{1,9},{9,1},{17,25},{25,17},{2,10},{10... | collective-permute-start | bytes 147464 | tf_op jit(solution)/shard_map/ppermute | solution.py:702
  52.6 3.4 %collective-permute-start.16 = (f32[96,256]{1,0:T(8,128)S(1)}, f32[96,256]{1,0:T(8,128)S(1)}, u32[]{:S(2)}, u32[]{:S(2)}) collective-permute-start(f32[96,256]{1,0:T(8,128)S(1)} %add_add_fusion.own), channel_id=1, source_target_pairs={{0,1},{1,0},{2,3},{3,2},{4,5},{5,4},{6,7},{7,6},{8,9},{9,8},{10,11... | collective-permute-start | bytes 294920 | tf_op jit(solution)/shard_map/ppermute | solution.py:570

commit v6 on v5

--- a/solution.py
+++ b/solution.py
@@ -132,7 +132,7 @@
     return high, (value - high.astype(F32)).astype(BF16)
 
 
-END_LINES = 80
+ENDS = 8
 
 
 def ends_part_kernel(moves, bands, me_ref, plans, stored, edge, row_weights, *refs):
@@ -154,28 +154,28 @@
         both = jnp.transpose(over[jnp.bitwise_xor(here, move)])
         weights = jnp.where(core == 0, both[0:rows], both[rows:])
         row_weights[i] = weights
-        ends += [weights[0:3], weights[rows - 3 : rows]]
+        ends += [weights[0:ENDS], weights[rows - ENDS : rows]]
     high, low = high_low(jnp.concatenate(ends, axis=0))
     count = high.shape[0]
     both = dot(jnp.concatenate([high, low], axis=0), stored[...])
     product[...] = both[0:count] + both[count:]
     for i, (move, small) in enumerate(zip(moves, smalls, strict=True)):
-        lines[...] = jnp.zeros_like(lines)
+        pair = slice(2 * ENDS * i, 2 * ENDS * (i + 1))
         for band in range(bands):
-            lines[6 * band : 6 * band + 6, :] = product[6 * i : 6 * i + 6, band * cols : (band + 1) * cols]
-        small[0:END_LINES, :] = lines[...].astype(small.dtype)
+            lines[2 * ENDS * band : 2 * ENDS * (band + 1), :] = product[pair, band * cols : (band + 1) * cols]
+        small[0 : lines.shape[0], :] = lines[...].astype(small.dtype)
         chip = jnp.bitwise_xor(here, move)
         near, before, after = sides[chip + 1], sides[chip], sides[chip + 2]
         left = jnp.where(core == 1, near[0 : 3 * GROUP, 0:rows], before[0 : 3 * GROUP, rows:])
         right = jnp.where(core == 0, near[3 * GROUP :, rows:], after[3 * GROUP :, 0:rows])
-        small[END_LINES:, :] = jnp.concatenate([left, right], axis=1).astype(small.dtype)
+        small[lines.shape[0] :, :] = jnp.concatenate([left, right], axis=1).astype(small.dtype)
 
 
 def part_kernel(indices, stored, row_weights, *outs):
     rows = outs[0].shape[0]
     row_width = stored.shape[1]
     for index, out in zip(indices, outs, strict=True):
-        high, low = high_low(row_weights[index])
+        high, low = high_low(row_weights[index][ENDS : ENDS + rows])
         both = jnp.concatenate([high, low], axis=0)
         for start in range(0, row_width, 512):
             stop = min(start + 512, row_width)
@@ -194,12 +194,13 @@
     total[...] = value
     before = plans[jnp.maximum(me - 1, 0), 1:2, rows : 2 * rows]
     after = plans[jnp.minimum(me + 1, count - 1), 0:1, rows : 2 * rows]
-    for target, start, end in ((upper, 0, 0), (lower, rows - 3, 3)):
+    lines = 2 * ENDS * bands
+    for target, start, end in ((upper, 0, 0), (lower, rows - 3, 2 * ENDS - 3)):
         bundle[...] = jnp.zeros_like(bundle)
         for i in range(3):
             line = jnp.concatenate(
                 [
-                    total[pl.ds(end + i, bands, stride=6), :],
+                    total[pl.ds(end + i, bands, stride=2 * ENDS), :],
                     labels[start + i : start + i + 1, :],
                     jnp.zeros((GROUP - bands - 1, cols), F32),
                 ],
@@ -209,7 +210,7 @@
             for column, at in ((3, 0), (4, 1), (5, cols - 2), (6, cols - 1)):
                 bundle[:, column * 3 + i : column * 3 + i + 1] = line[:, at : at + 1]
         for column in range(3):
-            group = total[END_LINES + column * GROUP : END_LINES + (column + 1) * GROUP, :]
+            group = total[lines + column * GROUP : lines + (column + 1) * GROUP, :]
             bundle[:, column * 3 : column * 3 + 3] = group[:, start : start + 3]
             at = (column + 7) * 3
             bundle[:, at : at + 3] = group[:, rows + start : rows + start + 3]
@@ -224,11 +225,16 @@
     inputs, (main, strips, bank, side) = refs[:-4], refs[-4:]
     parts, smalls = inputs[: len(inputs) // 2], inputs[len(inputs) // 2 :]
     me = me_ref[0]
+    small_sum = smalls[0][...].astype(F32)
+    for small in smalls[1:]:
+        small_sum = small_sum + small[...].astype(F32)
     for band in range(bands):
         columns = slice(band * patch_cols, (band + 1) * patch_cols)
         total = parts[0][:, columns].astype(F32)
         for part in parts[1:]:
             total = total + part[:, columns].astype(F32)
+        ends = small_sum[2 * ENDS * band : 2 * ENDS * (band + 1)]
+        total = jnp.concatenate([ends[0:ENDS], total, ends[ENDS:]], axis=0)
         bank[band * tile_rows : (band + 1) * tile_rows, :] = total
     bank[bands * tile_rows : (bands + 1) * tile_rows, :] = labels[...]
     bank[(bands + 1) * tile_rows : GROUP * tile_rows, :] = jnp.zeros(
@@ -239,9 +245,7 @@
             pl.ds(row, GROUP, stride=tile_rows), :
         ].astype(BF16)
 
-    far = smalls[0][END_LINES:, :].astype(F32)
-    for small in smalls[1:]:
-        far = far + small[END_LINES:, :].astype(F32)
+    far = small_sum[2 * ENDS * bands :]
     side[...] = jnp.zeros_like(side)
     side[0 : 3 * GROUP, 3 : 3 + tile_rows] = far[:, :tile_rows]
     side[7 * GROUP : 10 * GROUP, 3 : 3 + tile_rows] = far[:, tile_rows:]
@@ -597,16 +601,17 @@
     )(me, in_hbm(patches), mate_patches)
     plans, stored, edge = lax.optimization_barrier((plans, stored, edge))
     moves = list(range(chips - 1, -1, -1))
+    small_lines = 2 * ENDS * bands + 3 * GROUP
     cost = pl.CostEstimate(flops=10**9, bytes_accessed=10**7, transcendentals=0)
     row_weights, *smalls = call(
         functools.partial(ends_part_kernel, moves, bands),
         [struct((chips, rows, 2 * store), F32)]
-        + [struct((END_LINES + 3 * GROUP, cols), BF16 if move else F32) for move in moves],
+        + [struct((small_lines, cols), BF16 if move else F32) for move in moves],
         [
             pltpu.VMEM((chips, 2 * store, 2 * rows), F32),
             pltpu.VMEM((chips + 2, 6 * GROUP, 2 * rows), F32),
-            pltpu.VMEM((6 * chips, row_width), F32),
-            pltpu.VMEM((END_LINES, cols), F32),
+            pltpu.VMEM((2 * ENDS * chips, row_width), F32),
+            pltpu.VMEM((2 * ENDS * bands, cols), F32),
         ],
         in_specs=[smem, vmem, vmem, vmem],
         cost_estimate=cost,
@@ -618,7 +623,7 @@
             row_weights, *smalls = lax.optimization_barrier((row_weights, *smalls))
         parts += call(
             functools.partial(part_kernel, [moves.index(move) for move in some]),
-            [struct((rows, row_width), BF16 if move else F32) for move in some],
+            [struct((rows - 2 * ENDS, row_width), BF16 if move else F32) for move in some],
             in_specs=[vmem, vmem],
             cost_estimate=cost,
         )(stored, row_weights)
@@ -626,7 +631,7 @@
     upper, lower = call(
         functools.partial(ends_kernel, bands),
         [struct((GROUP, 3 * cols + 128), BF16)] * 2,
-        [pltpu.VMEM((END_LINES + 3 * GROUP, cols), F32), pltpu.VMEM((GROUP, 128), F32)],
+        [pltpu.VMEM((small_lines, cols), F32), pltpu.VMEM((GROUP, 128), F32)],
         in_specs=[smem] + [vmem] * (2 + chips),
         cost_estimate=pl.CostEstimate(flops=3 * 10**10, bytes_accessed=10**7, transcendentals=0),
     )(me, plans, tile_labels, *smalls)

time: 57.5 us -> 56.7 us (0.986)
  waiting for transfers between devices: 12.6 us -> 8.65 us
  starting transfers between devices: 25.7 us -> 28.9 us
    ppermute x9, starting transfers between devices: 9.62 us -> 12.8 us  [by_lon(): return lax.ppermute(value, 'lon', [(i, i ^ move) for i in range(lon_count)])]
    ppermute x9, waiting for transfers between devices: 5.14 us -> 2.58 us  [by_lon(): return lax.ppermute(value, 'lon', [(i, i ^ move) for i in range(lon_count)])]
    ppermute x6, waiting for transfers between devices: 6.23 us -> 4.36 us  [sum_over(): lax.ppermute(sent, axis, [(i, i ^ move) for i in range(size)]).astype(F32)]
  transfers between devices with their start and end apart: 18 -> 18, of which waited for: 8 -> 10; matrix products, arithmetic and copies ran while one was open for 2% -> 2% of each run, Pallas kernels for 8% -> 9%
where the time goes in v6:
time: 56.7 us; the launch traced here: 56.3 us
  starting transfers between devices  28.9 us (51%)
  Pallas kernels  16.1 us (28%)
  waiting for transfers between devices  8.65 us (15%)
  local copies, waits for them, and re-layouts  1.3 us (2%)
  between operations  0.84 us (1%)
    ppermute x9, starting transfers between devices, by_lon(): return lax.ppermute(value, 'lon', [(i, i ^ move) for i in range(lon_count)])  12.8 us
    pallas_call x1, Pallas kernels, body(): call(functools.partial(network_kernel, bands, classes, rows, cols, lat_co...  7.18 us
    ppermute x6, starting transfers between devices, sum_over(): lax.ppermute(sent, axis, [(i, i ^ move) for i in range(size)]).astype(F32)  6.33 us
    all_to_all x1, starting transfers between devices, body(): plans = lax.all_to_all(plan, 'lon', split_axis=0, concat_axis=0, tiled=True)  5.28 us
    ppermute x6, waiting for transfers between devices, sum_over(): lax.ppermute(sent, axis, [(i, i ^ move) for i in range(size)]).astype(F32)  4.36 us
    ppermute x1, starting transfers between devices, body(): lax.ppermute(lower, 'lat', [(i, i + 1) for i in range(lat_count - 1)])  3.19 us
    ppermute x9, waiting for transfers between devices, by_lon(): return lax.ppermute(value, 'lon', [(i, i ^ move) for i in range(lon_count)])  2.58 us
    pallas_call x1, Pallas kernels, body(): call(functools.partial(plan_kernel, store), [struct((lon_count, 16, 128),...  1.77 us
  transfers between devices with their start and end apart: 18, of which 10 were waited for; matrix products, arithmetic and copies ran while one was open for 2% of the time, Pallas kernels for 9%

profile of v6, /device:TPU:1, one launch (start us, length us, event | category | flops | bytes accessed | tf_op | source)
XLA Modules:
  0.0 56.3 jit_solution(12745820912795488659)
XLA Ops:
  0.6 1.8 %shard_map.128 = (f32[8,16,128]{2,1,0:T(8,128)}, f32[64,128]{1,0:T(8,128)}) custom-call(s32[1,512]{1,0:T(1,128)} %requests_hbm.1, s32[8,64]{1,0:T(8,128)} %bitcast.12, s32[8,64]{1,0:T(8,128)} %bitcast.13, f32[16]{0:T(128)} %levels_hbm.1, s32[64,128]{1,0:T(8,128)} %labels_hbm.1), custom_call_target="tpu_custom_call" | custom-call | tf_op jit(solution)/shard_map/pallas_call | solution.py:578
  2.4 0.1 collective-permute-start
  2.5 5.3 %all-to-all-start = ((f32[8,16,128]{2,1,0:T(8,128)}), f32[8,16,128]{2,1,0:T(8,128)S(1)}, u32[]{:S(2)}, u32[]{:S(2)}) async-start(f32[8,16,128]{2,1,0:T(8,128)} %get-tuple-element.45), calls=%async_computation | async-start | bytes 131072 | tf_op jit(solution)/shard_map/all_to_all | solution.py:594
  7.8 1.1 %shard_map.135 = (bf16[64,144]{1,0:T(8,128)(2,1)S(1)}, bf16[64,144]{1,0:T(8,128)(2,1)S(1)}, bf16[192,192]{1,0:T(8,128)(2,1)S(1)}, bf16[192,192]{1,0:T(8,128)(2,1...) custom-call(bf16[9,12,64]{2,1,0:T(8,128)(2,1)} %bitcast.11, bf16[9,64,64]{2,1,0:T(8,128)(2,1)} %conv2_hbm.1, ...), custom_call_target="tpu_custom_call" | custom-call | tf_op jit(solution)/shard_map/pallas_call | solution.py:648
  9.0 0.1 pad_add_fusion.place
  9.0 0.0 collective-permute-done.mate
  9.1 1.7 %shard_map.129 = (bf16[384,1536]{1,0:T(8,128)(2,1)S(1)}, bf16[96,384]{1,0:T(8,128)(2,1)S(1)}) custom-call(s32[1]{0:T(128)} %bitcast.1.me_ref, bf16[192,1536]{1,0:T(8,128)(2,1)} %own, bf16[192,1536]{1,0:T(8,128)(2,1)S(1)} %collective-permute-done.mate), custom_call_target="tpu_custom_call" | custom-call | flops 1000000000 | bytes 10000000 | tf_op jit(solution)/shard_map/pallas_call | solution.py:595
  10.8 1.2 %all-to-all-done.plans = f32[8,16,128]{2,1,0:T(8,128)S(1)} async-done(((f32[8,16,128]{2,1,0:T(8,128)}), f32[8,16,128]{2,1,0:T(8,128)S(1)}, u32[]{:S(2)}, u32[]{:S(2)}) %all-to-all-start) | async-done | bytes 65568 | tf_op jit(solution)/shard_map/all_to_all | solution.py:594
  12.0 1.3 %shard_map.130 = (f32[4,64,384]{2,1,0:T(8,128)S(1)}, bf16[240,128]{1,0:T(8,128)(2,1)S(1)}, bf16[240,128]{1,0:T(8,128)(2,1)S(1)}, bf16[240,128]{1,0:T(8,128)(2,1)S(1)}, f32[240,128]{1,0:T(8,128)S(1)}) custom-call(s32[1]{0:T(128)} %bitcast.1.me_ref, f32[8,16,128]{2,1,0:T(8,128)S(1)} %all-to-all-done.plans, bf16[384,1536]{1,0:T(8,128)(2,1)S(1)} %get-tuple-element.51.stored, ...), custom_call_target="tpu_custom_call" | custom-call | flops 1000000000 | bytes 10000000 | tf_op jit(solution)/shard_map/pallas_call | solution.py:606
  13.3 1.2 %collective-permute-start.4 = (bf16[240,128]{1,0:T(8,128)(2,1)S(1)}, bf16[240,128]{1,0:T(8,128)(2,1)S(1)}, u32[]{:S(2)}, u32[]{:S(2)}) collective-permute-start(bf16[240,128]{1,0:T(8,128)(2,1)S(1)} %get-tuple-element.57), channel_id=1, source_target_pairs={{0,6},{1,7},{2,4},{3,5},{4,2},{5,3},{6,0},{7,1},{8,14},{9,15},{10,... | collective-permute-start | bytes 184328 | tf_op jit(solution)/shard_map/ppermute | solution.py:574
  14.4 0.7 %collective-permute-start.5 = (bf16[240,128]{1,0:T(8,128)(2,1)S(1)}, bf16[240,128]{1,0:T(8,128)(2,1)S(1)}, u32[]{:S(2)}, u32[]{:S(2)}) collective-permute-start(bf16[240,128]{1,0:T(8,128)(2,1)S(1)} %get-tuple-element.58), channel_id=1, source_target_pairs={{0,4},{1,5},{2,6},{3,7},{4,0},{5,1},{6,2},{7,3},{8,12},{9,13},{10,... | collective-permute-start | bytes 184328 | tf_op jit(solution)/shard_map/ppermute | solution.py:574
  15.1 0.9 %collective-permute-start.6 = (bf16[240,128]{1,0:T(8,128)(2,1)S(1)}, bf16[240,128]{1,0:T(8,128)(2,1)S(1)}, u32[]{:S(2)}, u32[]{:S(2)}) collective-permute-start(bf16[240,128]{1,0:T(8,128)(2,1)S(1)} %get-tuple-element.59), channel_id=1, source_target_pairs={{0,2},{1,3},{2,0},{3,1},{4,6},{5,7},{6,4},{7,5},{8,10},{9,11},{10,... | collective-permute-start | bytes 184328 | tf_op jit(solution)/shard_map/ppermute | solution.py:574
  16.0 0.8 %shard_map.131 = (bf16[48,1536]{1,0:T(8,128)(2,1)S(1)}, bf16[48,1536]{1,0:T(8,128)(2,1)S(1)}, bf16[48,1536]{1,0:T(8,128)(2,1)S(1)}) custom-call(bf16[384,1536]{1,0:T(8,128)(2,1)S(1)} %get-tuple-element.51.stored, f32[4,64,384]{2,1,0:T(8,128)S(1)} %get-tuple-element.61.row_weights), custom_call_target="tpu_custom_call" | custom-call | flops 1000000000 | bytes 10000000 | tf_op jit(solution)/shard_map/pallas_call | solution.py:624
  16.8 1.2 %collective-permute-start.1 = (bf16[48,1536]{1,0:T(8,128)(2,1)S(1)}, bf16[48,1536]{1,0:T(8,128)(2,1)S(1)}, u32[]{:S(2)}, u32[]{:S(2)}) collective-permute-start(bf16[48,1536]{1,0:T(8,128)(2,1)S(1)} %get-tuple-element.54), channel_id=1, source_target_pairs={{0,6},{1,7},{2,4},{3,5},{4,2},{5,3},{6,0},{7,1},{8,14},{9,15},{10,... | collective-permute-start | bytes 442376 | tf_op jit(solution)/shard_map/ppermute | solution.py:574
  17.9 0.7 %collective-permute-start.2 = (bf16[48,1536]{1,0:T(8,128)(2,1)S(1)}, bf16[48,1536]{1,0:T(8,128)(2,1)S(1)}, u32[]{:S(2)}, u32[]{:S(2)}) collective-permute-start(bf16[48,1536]{1,0:T(8,128)(2,1)S(1)} %get-tuple-element.55), channel_id=1, source_target_pairs={{0,4},{1,5},{2,6},{3,7},{4,0},{5,1},{6,2},{7,3},{8,12},{9,13},{10,... | collective-permute-start | bytes 442376 | tf_op jit(solution)/shard_map/ppermute | solution.py:574
  18.6 0.0 collective-permute-done.4.refs_4_.refs_0_
  18.6 0.9 %collective-permute-start.3 = (bf16[48,1536]{1,0:T(8,128)(2,1)S(1)}, bf16[48,1536]{1,0:T(8,128)(2,1)S(1)}, u32[]{:S(2)}, u32[]{:S(2)}) collective-permute-start(bf16[48,1536]{1,0:T(8,128)(2,1)S(1)} %get-tuple-element.56), channel_id=1, source_target_pairs={{0,2},{1,3},{2,0},{3,1},{4,6},{5,7},{6,4},{7,5},{8,10},{9,11},{10,... | collective-permute-start | bytes 442376 | tf_op jit(solution)/shard_map/ppermute | solution.py:574
  19.5 0.0 collective-permute-done.5.refs_5_.refs_1_
  19.5 0.2 shard_map.134
  19.7 3.2 %collective-permute-start.7 = (bf16[16,512]{1,0:T(8,128)(2,1)S(1)}, bf16[16,512]{1,0:T(8,128)(2,1)S(1)}, u32[]{:S(2)}, u32[]{:S(2)}) collective-permute-start(bf16[16,512]{1,0:T(8,128)(2,1)S(1)} %get-tuple-element.68), channel_id=1, source_target_pairs={{0,8},{8,16},{16,24},{1,9},{9,17},{17,25},{2,10},{10,18},{18,26},{... | collective-permute-start | bytes 49160 | tf_op jit(solution)/shard_map/ppermute | solution.py:646
  22.9 1.3 %collective-permute-start.8 = (bf16[16,512]{1,0:T(8,128)(2,1)S(1)}, bf16[16,512]{1,0:T(8,128)(2,1)S(1)}, u32[]{:S(2)}, u32[]{:S(2)}) collective-permute-start(bf16[16,512]{1,0:T(8,128)(2,1)S(1)} %get-tuple-element.69), channel_id=1, source_target_pairs={{8,0},{16,8},{24,16},{9,1},{17,9},{25,17},{10,2},{18,10},{26,18},{... | collective-permute-start | bytes 49160 | tf_op jit(solution)/shard_map/ppermute | solution.py:645
  24.2 0.3 shard_map.132.refs_3_
  24.5 0.0 collective-permute-done.1.refs_0_
  24.5 1.6 %collective-permute-done.2.refs_1_ = bf16[48,1536]{1,0:T(8,128)(2,1)S(1)} collective-permute-done((bf16[48,1536]{1,0:T(8,128)(2,1)S(1)}, bf16[48,1536]{1,0:T(8,128)(2,1)S(1)}, u32[]{:S(2)}, u32[]{:S(2)}) %collective-permute-start.2) | collective-permute-done | bytes 147488 | tf_op jit(solution)/shard_map/ppermute | solution.py:574
  26.1 0.7 %shard_map.133 = (bf16[16,8192]{1,0:T(8,128)(2,1)S(1)}, bf16[160,128]{1,0:T(8,128)(2,1)S(1)}) custom-call(s32[1]{0:T(128)} %bitcast.1.me_ref, f32[8,16,128]{2,1,0:T(8,128)S(1)} %all-to-all-done.plans, f32[64,128]{1,0:T(8,128)S(1)} %copy-done, bf16[48,1536]{1,0:T(8,128)(2,1)S(1)} %collective-permute-done.1.refs_0_, ...), custom_call_target="tpu_custom_call" | custom-call | flops 1000000000 | bytes 10000000 | tf_op jit(solution)/shard_map/pallas_call | solution.py:638
  26.8 0.5 collective-permute-done.8.below
  27.3 7.2 %shard_map.136 = (bf16[64,8192]{1,0:T(8,128)(2,1)S(1)}, f32[96,256]{1,0:T(8,128)S(1)}, f32[96,256]{1,0:T(8,128)S(1)}) custom-call(s32[2]{0:T(128)S(1)} %pad_add_fusion.place, bf16[16,8192]{1,0:T(8,128)(2,1)S(1)} %get-tuple-element.66.main, bf16[160,128]{1,0:T(8,128)(2,1)S(1)} %get-tuple-element.67.strips, bf16[16,512]{1,0:T(8,128)(2,1)S(1)} %collective-permute-done.7.above, ...), custom_call_target="tpu_custom_call" | custom-call | tf_op jit(solution)/shard_map/pallas_call | solution.py:672
  34.5 4.0 %collective-permute-start.9 = (f32[96,256]{1,0:T(8,128)S(1)}, f32[96,256]{1,0:T(8,128)S(1)}, u32[]{:S(2)}, u32[]{:S(2)}) collective-permute-start(f32[96,256]{1,0:T(8,128)S(1)} %get-tuple-element.78), channel_id=1, source_target_pairs={{0,1},{1,0},{2,3},{3,2},{4,5},{5,4},{6,7},{7,6},{8,9},{9,8},{10,11... | collective-permute-start | bytes 294920 | tf_op jit(solution)/shard_map/ppermute | solution.py:574
  38.6 0.9 %collective-permute-done.9 = f32[96,256]{1,0:T(8,128)S(1)} collective-permute-done((f32[96,256]{1,0:T(8,128)S(1)}, f32[96,256]{1,0:T(8,128)S(1)}, u32[]{:S(2)}, u32[]{:S(2)}) %collective-permute-start.9) | collective-permute-done | bytes 98336 | tf_op jit(solution)/shard_map/ppermute | solution.py:574
  39.5 0.1 reduce-precision_subtract_fusion.1
  39.7 0.1 fusion.1
  39.8 0.7 %collective-permute-start.12 = (bf16[96,256]{1,0:T(8,128)(2,1)S(1)}, bf16[96,256]{1,0:T(8,128)(2,1)S(1)}, u32[]{:S(2)}, u32[]{:S(2)}) collective-permute-start(bf16[96,256]{1,0:T(8,128)(2,1)S(1)} %get-tuple-element.85), channel_id=1, source_target_pairs={{0,6},{1,7},{2,4},{3,5},{4,2},{5,3},{6,0},{7,1},{8,14},{9,15},{10,... | collective-permute-start | bytes 147464 | tf_op jit(solution)/shard_map/ppermute | solution.py:707
  40.4 0.9 %collective-permute-start.11 = (bf16[96,256]{1,0:T(8,128)(2,1)S(1)}, bf16[96,256]{1,0:T(8,128)(2,1)S(1)}, u32[]{:S(2)}, u32[]{:S(2)}) collective-permute-start(bf16[96,256]{1,0:T(8,128)(2,1)S(1)} %get-tuple-element.85), channel_id=1, source_target_pairs={{0,4},{1,5},{2,6},{3,7},{4,0},{5,1},{6,2},{7,3},{8,12},{9,13},{10,... | collective-permute-start | bytes 147464 | tf_op jit(solution)/shard_map/ppermute | solution.py:707
  41.3 1.2 %collective-permute-start.10 = (bf16[96,256]{1,0:T(8,128)(2,1)S(1)}, bf16[96,256]{1,0:T(8,128)(2,1)S(1)}, u32[]{:S(2)}, u32[]{:S(2)}) collective-permute-start(bf16[96,256]{1,0:T(8,128)(2,1)S(1)} %get-tuple-element.85), channel_id=1, source_target_pairs={{0,2},{1,3},{2,0},{3,1},{4,6},{5,7},{6,4},{7,5},{8,10},{9,11},{10,... | collective-permute-start | bytes 147464 | tf_op jit(solution)/shard_map/ppermute | solution.py:707
  42.5 1.3 %collective-permute-done.12 = bf16[96,256]{1,0:T(8,128)(2,1)S(1)} collective-permute-done((bf16[96,256]{1,0:T(8,128)(2,1)S(1)}, bf16[96,256]{1,0:T(8,128)(2,1)S(1)}, u32[]{:S(2)}, u32[]{:S(2)}) %collective-permute-start.12) | collective-permute-done | bytes 49184 | tf_op jit(solution)/shard_map/ppermute | solution.py:707
  43.8 0.1 collective-permute-done.11
  43.9 0.7 %collective-permute-done.10 = bf16[96,256]{1,0:T(8,128)(2,1)S(1)} collective-permute-done((bf16[96,256]{1,0:T(8,128)(2,1)S(1)}, bf16[96,256]{1,0:T(8,128)(2,1)S(1)}, u32[]{:S(2)}, u32[]{:S(2)}) %collective-permute-start.10) | collective-permute-done | bytes 49184 | tf_op jit(solution)/shard_map/ppermute | solution.py:707
  44.6 0.1 reduce-precision_subtract_fusion
  44.7 0.1 fusion
  44.8 1.5 %collective-permute-start.15 = (bf16[96,256]{1,0:T(8,128)(2,1)S(1)}, bf16[96,256]{1,0:T(8,128)(2,1)S(1)}, u32[]{:S(2)}, u32[]{:S(2)}) collective-permute-start(bf16[96,256]{1,0:T(8,128)(2,1)S(1)} %get-tuple-element.83), channel_id=1, source_target_pairs={{0,24},{8,16},{16,8},{24,0},{1,25},{9,17},{17,9},{25,1},{2,26},{10... | collective-permute-start | bytes 147464 | tf_op jit(solution)/shard_map/ppermute | solution.py:707
  46.4 1.0 %collective-permute-start.14 = (bf16[96,256]{1,0:T(8,128)(2,1)S(1)}, bf16[96,256]{1,0:T(8,128)(2,1)S(1)}, u32[]{:S(2)}, u32[]{:S(2)}) collective-permute-start(bf16[96,256]{1,0:T(8,128)(2,1)S(1)} %get-tuple-element.83), channel_id=1, source_target_pairs={{0,16},{8,24},{16,0},{24,8},{1,17},{9,25},{17,1},{25,9},{2,18},{10... | collective-permute-start | bytes 147464 | tf_op jit(solution)/shard_map/ppermute | solution.py:707
  47.4 1.1 %collective-permute-start.13 = (bf16[96,256]{1,0:T(8,128)(2,1)S(1)}, bf16[96,256]{1,0:T(8,128)(2,1)S(1)}, u32[]{:S(2)}, u32[]{:S(2)}) collective-permute-start(bf16[96,256]{1,0:T(8,128)(2,1)S(1)} %get-tuple-element.83), channel_id=1, source_target_pairs={{0,8},{8,0},{16,24},{24,16},{1,9},{9,1},{17,25},{25,17},{2,10},{10... | collective-permute-start | bytes 147464 | tf_op jit(solution)/shard_map/ppermute | solution.py:707
  48.4 1.2 %collective-permute-done.15 = bf16[96,256]{1,0:T(8,128)(2,1)S(1)} collective-permute-done((bf16[96,256]{1,0:T(8,128)(2,1)S(1)}, bf16[96,256]{1,0:T(8,128)(2,1)S(1)}, u32[]{:S(2)}, u32[]{:S(2)}) %collective-permute-start.15) | collective-permute-done | bytes 49184 | tf_op jit(solution)/shard_map/ppermute | solution.py:707
  49.6 0.6 %collective-permute-done.14 = bf16[96,256]{1,0:T(8,128)(2,1)S(1)} collective-permute-done((bf16[96,256]{1,0:T(8,128)(2,1)S(1)}, bf16[96,256]{1,0:T(8,128)(2,1)S(1)}, u32[]{:S(2)}, u32[]{:S(2)}) %collective-permute-start.14) | collective-permute-done | bytes 49184 | tf_op jit(solution)/shard_map/ppermute | solution.py:707
  50.2 0.5 collective-permute-done.13
  50.8 3.3 %collective-permute-start.16 = (f32[96,256]{1,0:T(8,128)S(1)}, f32[96,256]{1,0:T(8,128)S(1)}, u32[]{:S(2)}, u32[]{:S(2)}) collective-permute-start(f32[96,256]{1,0:T(8,128)S(1)} %add_add_fusion.own), channel_id=1, source_target_pairs={{0,1},{1,0},{2,3},{3,2},{4,5},{5,4},{6,7},{7,6},{8,9},{9,8},{10,11... | collective-permute-start | bytes 294920 | tf_op jit(solution)/shard_map/ppermute | solution.py:574
  54.0 1.3 %copy.14 = bf16[8,8,64,128]{3,2,1,0:T(8,128)(2,1)} copy(bf16[8,8,64,128]{3,1,2,0:T(8,128)(2,1)S(1)} %bitcast.9) | data formatting | bytes 2097152
  55.3 1.0 %shard_map.137 = (f32[9,12,64]{2,1,0:T(8,128)}, f32[9,64,64]{2,1,0:T(8,128)}, f32[11,64]{1,0:T(8,128)}, f32[1,1]{1,0:T(1,128)}) custom-call(s32[1]{0:T(128)} %bitcast.1.me_ref, f32[96,256]{1,0:T(8,128)S(1)} %add_add_fusion.own, f32[96,256]{1,0:T(8,128)S(1)} %collective-permute-done.16.mate), custom_call_target="tpu_custom_call" | custom-call | tf_op jit(solution)/shard_map/pallas_call | solution.py:715
  (19 shorter events, 0.1 us)
Async XLA Ops:
  2.4 6.6 %collective-permute-start = (bf16[192,1536]{1,0:T(8,128)(2,1)}, bf16[192,1536]{1,0:T(8,128)(2,1)S(1)}, u32[]{:S(2)}, u32[]{:S(2)}) collective-permute-start(bf16[192,1536]{1,0:T(8,128)(2,1)} %own), channel_id=1, source_target_pairs={{0,1},{1,0},{2,3},{3,2},{4,5},{5,4},{6,7},{7,6},{8,9},{9,8},{10,11... | collective-permute-start | bytes 1769480 | tf_op jit(solution)/shard_map/ppermute | solution.py:574
  2.5 9.4 %all-to-all-start = ((f32[8,16,128]{2,1,0:T(8,128)}), f32[8,16,128]{2,1,0:T(8,128)S(1)}, u32[]{:S(2)}, u32[]{:S(2)}) async-start(f32[8,16,128]{2,1,0:T(8,128)} %get-tuple-element.45), calls=%async_computation | async-start | bytes 131072 | tf_op jit(solution)/shard_map/all_to_all | solution.py:594
  13.3 5.3 %collective-permute-start.4 = (bf16[240,128]{1,0:T(8,128)(2,1)S(1)}, bf16[240,128]{1,0:T(8,128)(2,1)S(1)}, u32[]{:S(2)}, u32[]{:S(2)}) collective-permute-start(bf16[240,128]{1,0:T(8,128)(2,1)S(1)} %get-tuple-element.57), channel_id=1, source_target_pairs={{0,6},{1,7},{2,4},{3,5},{4,2},{5,3},{6,0},{7,1},{8,14},{9,15},{10,... | collective-permute-start | bytes 184328 | tf_op jit(solution)/shard_map/ppermute | solution.py:574
  14.4 5.0 %collective-permute-start.5 = (bf16[240,128]{1,0:T(8,128)(2,1)S(1)}, bf16[240,128]{1,0:T(8,128)(2,1)S(1)}, u32[]{:S(2)}, u32[]{:S(2)}) collective-permute-start(bf16[240,128]{1,0:T(8,128)(2,1)S(1)} %get-tuple-element.58), channel_id=1, source_target_pairs={{0,4},{1,5},{2,6},{3,7},{4,0},{5,1},{6,2},{7,3},{8,12},{9,13},{10,... | collective-permute-start | bytes 184328 | tf_op jit(solution)/shard_map/ppermute | solution.py:574
  15.1 4.4 %collective-permute-start.6 = (bf16[240,128]{1,0:T(8,128)(2,1)S(1)}, bf16[240,128]{1,0:T(8,128)(2,1)S(1)}, u32[]{:S(2)}, u32[]{:S(2)}) collective-permute-start(bf16[240,128]{1,0:T(8,128)(2,1)S(1)} %get-tuple-element.59), channel_id=1, source_target_pairs={{0,2},{1,3},{2,0},{3,1},{4,6},{5,7},{6,4},{7,5},{8,10},{9,11},{10,... | collective-permute-start | bytes 184328 | tf_op jit(solution)/shard_map/ppermute | solution.py:574
  16.0 3.5 %copy-start = (f32[64,128]{1,0:T(8,128)S(1)}, f32[64,128]{1,0:T(8,128)}, u32[]{:S(2)}) copy-start(f32[64,128]{1,0:T(8,128)} %get-tuple-element.50.labels) | copy-start | bytes 98308
  16.8 7.7 %collective-permute-start.1 = (bf16[48,1536]{1,0:T(8,128)(2,1)S(1)}, bf16[48,1536]{1,0:T(8,128)(2,1)S(1)}, u32[]{:S(2)}, u32[]{:S(2)}) collective-permute-start(bf16[48,1536]{1,0:T(8,128)(2,1)S(1)} %get-tuple-element.54), channel_id=1, source_target_pairs={{0,6},{1,7},{2,4},{3,5},{4,2},{5,3},{6,0},{7,1},{8,14},{9,15},{10,... | collective-permute-start | bytes 442376 | tf_op jit(solution)/shard_map/ppermute | solution.py:574
  17.9 8.2 %collective-permute-start.2 = (bf16[48,1536]{1,0:T(8,128)(2,1)S(1)}, bf16[48,1536]{1,0:T(8,128)(2,1)S(1)}, u32[]{:S(2)}, u32[]{:S(2)}) collective-permute-start(bf16[48,1536]{1,0:T(8,128)(2,1)S(1)} %get-tuple-element.55), channel_id=1, source_target_pairs={{0,4},{1,5},{2,6},{3,7},{4,0},{5,1},{6,2},{7,3},{8,12},{9,13},{10,... | collective-permute-start | bytes 442376 | tf_op jit(solution)/shard_map/ppermute | solution.py:574
  18.6 7.6 %collective-permute-start.3 = (bf16[48,1536]{1,0:T(8,128)(2,1)S(1)}, bf16[48,1536]{1,0:T(8,128)(2,1)S(1)}, u32[]{:S(2)}, u32[]{:S(2)}) collective-permute-start(bf16[48,1536]{1,0:T(8,128)(2,1)S(1)} %get-tuple-element.56), channel_id=1, source_target_pairs={{0,2},{1,3},{2,0},{3,1},{4,6},{5,7},{6,4},{7,5},{8,10},{9,11},{10,... | collective-permute-start | bytes 442376 | tf_op jit(solution)/shard_map/ppermute | solution.py:574
  19.7 7.2 %collective-permute-start.7 = (bf16[16,512]{1,0:T(8,128)(2,1)S(1)}, bf16[16,512]{1,0:T(8,128)(2,1)S(1)}, u32[]{:S(2)}, u32[]{:S(2)}) collective-permute-start(bf16[16,512]{1,0:T(8,128)(2,1)S(1)} %get-tuple-element.68), channel_id=1, source_target_pairs={{0,8},{8,16},{16,24},{1,9},{9,17},{17,25},{2,10},{10,18},{18,26},{... | collective-permute-start | bytes 49160 | tf_op jit(solution)/shard_map/ppermute | solution.py:646
  22.9 4.5 %collective-permute-start.8 = (bf16[16,512]{1,0:T(8,128)(2,1)S(1)}, bf16[16,512]{1,0:T(8,128)(2,1)S(1)}, u32[]{:S(2)}, u32[]{:S(2)}) collective-permute-start(bf16[16,512]{1,0:T(8,128)(2,1)S(1)} %get-tuple-element.69), channel_id=1, source_target_pairs={{8,0},{16,8},{24,16},{9,1},{17,9},{25,17},{10,2},{18,10},{26,18},{... | collective-permute-start | bytes 49160 | tf_op jit(solution)/shard_map/ppermute | solution.py:645
  34.5 5.0 %collective-permute-start.9 = (f32[96,256]{1,0:T(8,128)S(1)}, f32[96,256]{1,0:T(8,128)S(1)}, u32[]{:S(2)}, u32[]{:S(2)}) collective-permute-start(f32[96,256]{1,0:T(8,128)S(1)} %get-tuple-element.78), channel_id=1, source_target_pairs={{0,1},{1,0},{2,3},{3,2},{4,5},{5,4},{6,7},{7,6},{8,9},{9,8},{10,11... | collective-permute-start | bytes 294920 | tf_op jit(solution)/shard_map/ppermute | solution.py:574
  39.8 4.0 %collective-permute-start.12 = (bf16[96,256]{1,0:T(8,128)(2,1)S(1)}, bf16[96,256]{1,0:T(8,128)(2,1)S(1)}, u32[]{:S(2)}, u32[]{:S(2)}) collective-permute-start(bf16[96,256]{1,0:T(8,128)(2,1)S(1)} %get-tuple-element.85), channel_id=1, source_target_pairs={{0,6},{1,7},{2,4},{3,5},{4,2},{5,3},{6,0},{7,1},{8,14},{9,15},{10,... | collective-permute-start | bytes 147464 | tf_op jit(solution)/shard_map/ppermute | solution.py:707
  40.4 3.5 %collective-permute-start.11 = (bf16[96,256]{1,0:T(8,128)(2,1)S(1)}, bf16[96,256]{1,0:T(8,128)(2,1)S(1)}, u32[]{:S(2)}, u32[]{:S(2)}) collective-permute-start(bf16[96,256]{1,0:T(8,128)(2,1)S(1)} %get-tuple-element.85), channel_id=1, source_target_pairs={{0,4},{1,5},{2,6},{3,7},{4,0},{5,1},{6,2},{7,3},{8,12},{9,13},{10,... | collective-permute-start | bytes 147464 | tf_op jit(solution)/shard_map/ppermute | solution.py:707
  41.3 3.2 %collective-permute-start.10 = (bf16[96,256]{1,0:T(8,128)(2,1)S(1)}, bf16[96,256]{1,0:T(8,128)(2,1)S(1)}, u32[]{:S(2)}, u32[]{:S(2)}) collective-permute-start(bf16[96,256]{1,0:T(8,128)(2,1)S(1)} %get-tuple-element.85), channel_id=1, source_target_pairs={{0,2},{1,3},{2,0},{3,1},{4,6},{5,7},{6,4},{7,5},{8,10},{9,11},{10,... | collective-permute-start | bytes 147464 | tf_op jit(solution)/shard_map/ppermute | solution.py:707
  44.8 4.8 %collective-permute-start.15 = (bf16[96,256]{1,0:T(8,128)(2,1)S(1)}, bf16[96,256]{1,0:T(8,128)(2,1)S(1)}, u32[]{:S(2)}, u32[]{:S(2)}) collective-permute-start(bf16[96,256]{1,0:T(8,128)(2,1)S(1)} %get-tuple-element.83), channel_id=1, source_target_pairs={{0,24},{8,16},{16,8},{24,0},{1,25},{9,17},{17,9},{25,1},{2,26},{10... | collective-permute-start | bytes 147464 | tf_op jit(solution)/shard_map/ppermute | solution.py:707
  46.4 3.9 %collective-permute-start.14 = (bf16[96,256]{1,0:T(8,128)(2,1)S(1)}, bf16[96,256]{1,0:T(8,128)(2,1)S(1)}, u32[]{:S(2)}, u32[]{:S(2)}) collective-permute-start(bf16[96,256]{1,0:T(8,128)(2,1)S(1)} %get-tuple-element.83), channel_id=1, source_target_pairs={{0,16},{8,24},{16,0},{24,8},{1,17},{9,25},{17,1},{25,9},{2,18},{10... | collective-permute-start | bytes 147464 | tf_op jit(solution)/shard_map/ppermute | solution.py:707
  47.4 3.4 %collective-permute-start.13 = (bf16[96,256]{1,0:T(8,128)(2,1)S(1)}, bf16[96,256]{1,0:T(8,128)(2,1)S(1)}, u32[]{:S(2)}, u32[]{:S(2)}) collective-permute-start(bf16[96,256]{1,0:T(8,128)(2,1)S(1)} %get-tuple-element.83), channel_id=1, source_target_pairs={{0,8},{8,0},{16,24},{24,16},{1,9},{9,1},{17,25},{25,17},{2,10},{10... | collective-permute-start | bytes 147464 | tf_op jit(solution)/shard_map/ppermute | solution.py:707
  50.8 4.5 %collective-permute-start.16 = (f32[96,256]{1,0:T(8,128)S(1)}, f32[96,256]{1,0:T(8,128)S(1)}, u32[]{:S(2)}, u32[]{:S(2)}) collective-permute-start(f32[96,256]{1,0:T(8,128)S(1)} %add_add_fusion.own), channel_id=1, source_target_pairs={{0,1},{1,0},{2,3},{3,2},{4,5},{5,4},{6,7},{7,6},{8,9},{9,8},{10,11... | collective-permute-start | bytes 294920 | tf_op jit(solution)/shard_map/ppermute | solution.py:574

commit v7 on v6

--- a/solution.py
+++ b/solution.py
@@ -638,7 +638,7 @@
     main, strips = call(
         functools.partial(composite_kernel, bands),
         [struct((GROUP, rows * cols), BF16), struct((10 * GROUP, 128), BF16)],
-        [pltpu.VMEM((GROUP * rows, cols), F32), pltpu.VMEM((10 * GROUP, 128), F32)],
+        [pltpu.VMEM(((GROUP + 1) * rows, cols), F32), pltpu.VMEM((10 * GROUP, 128), F32)],
         in_specs=[smem] + [vmem] * (2 + 2 * chips),
         cost_estimate=cost,
     )(me, plans, tile_labels, *parts, *smalls)
@@ -691,15 +691,17 @@
         one_main, one_strip, two_main, two_back, head_pad, head_turn,
     )
 
-    row_id, lane_id = iota((half, sum_width), 0), iota((half, sum_width), 1)
-    at_loss = lane_id == 3 * feat + 3 * GROUP
-    at_loss, at_rest = at_loss & (row_id == feat), at_loss & (row_id == feat + GROUP)
+    last = sum_width - 128
+    row_id, lane_id = iota((2 * GROUP, 128), 0), iota((2 * GROUP, 128), 1)
+    at_loss = lane_id == 3 * feat + 3 * GROUP - last
+    at_loss, at_rest = at_loss & (row_id == 0), at_loss & (row_id == GROUP)
 
     def sum_over(value, axis, moves):
-        value = jnp.where(at_loss, value + jnp.roll(value, -GROUP, axis=0), value)
-        rounded = lax.reduce_precision(value, 8, 7)
-        rest = lax.reduce_precision(jnp.roll(value - rounded, GROUP, axis=0), 8, 7)
-        rounded = jnp.where(at_rest, rest, rounded)
+        tile = value[feat : feat + 2 * GROUP, last:]
+        tile = jnp.where(at_loss, tile + jnp.roll(tile, GROUP, axis=0), tile)
+        rest = jnp.roll(tile - lax.reduce_precision(tile, 8, 7), GROUP, axis=0)
+        tile = jnp.where(at_rest, rest, tile)
+        rounded = lax.reduce_precision(lax.dynamic_update_slice(value, tile, (feat, last)), 8, 7)
         sent = rounded.astype(BF16)
         size = lax.axis_size(axis)
         terms = [rounded]

time: 56.7 us -> 56.6 us (level)
  no operation moved by 1% of the time
where the time goes in v7:
time: 56.6 us; the launch traced here: 56.2 us
  starting transfers between devices  28.9 us (51%)
  Pallas kernels  16.1 us (28%)
  waiting for transfers between devices  8.65 us (15%)
  local copies, waits for them, and re-layouts  1.28 us (2%)
  between operations  0.78 us (1%)
    ppermute x9, starting transfers between devices, by_lon(): return lax.ppermute(value, 'lon', [(i, i ^ move) for i in range(lon_count)])  12.8 us
    pallas_call x1, Pallas kernels, body(): call(functools.partial(network_kernel, bands, classes, rows, cols, lat_co...  7.18 us
    ppermute x6, starting transfers between devices, sum_over(): lax.ppermute(sent, axis, [(i, i ^ move) for i in range(size)]).astype(F32)  6.33 us
    all_to_all x1, starting transfers between devices, body(): plans = lax.all_to_all(plan, 'lon', split_axis=0, concat_axis=0, tiled=True)  5.28 us
    ppermute x6, waiting for transfers between devices, sum_over(): lax.ppermute(sent, axis, [(i, i ^ move) for i in range(size)]).astype(F32)  4.36 us
    ppermute x1, starting transfers between devices, body(): lax.ppermute(lower, 'lat', [(i, i + 1) for i in range(lat_count - 1)])  3.19 us
    ppermute x9, waiting for transfers between devices, by_lon(): return lax.ppermute(value, 'lon', [(i, i ^ move) for i in range(lon_count)])  2.58 us
    pallas_call x1, Pallas kernels, body(): call(functools.partial(plan_kernel, store), [struct((lon_count, 16, 128),...  1.77 us
  transfers between devices with their start and end apart: 18, of which 10 were waited for; matrix products, arithmetic and copies ran while one was open for 2% of the time, Pallas kernels for 9%

profile of v7, /device:TPU:1, one launch (start us, length us, event | category | flops | bytes accessed | tf_op | source)
XLA Modules:
  0.0 56.2 jit_solution(10630487530091605868)
XLA Ops:
  0.6 1.8 %shard_map.128 = (f32[8,16,128]{2,1,0:T(8,128)}, f32[64,128]{1,0:T(8,128)}) custom-call(s32[1,512]{1,0:T(1,128)} %requests_hbm.1, s32[8,64]{1,0:T(8,128)} %bitcast.12, s32[8,64]{1,0:T(8,128)} %bitcast.13, f32[16]{0:T(128)} %levels_hbm.1, s32[64,128]{1,0:T(8,128)} %labels_hbm.1), custom_call_target="tpu_custom_call" | custom-call | tf_op jit(solution)/shard_map/pallas_call | solution.py:578
  2.4 0.1 collective-permute-start
  2.5 5.3 %all-to-all-start = ((f32[8,16,128]{2,1,0:T(8,128)}), f32[8,16,128]{2,1,0:T(8,128)S(1)}, u32[]{:S(2)}, u32[]{:S(2)}) async-start(f32[8,16,128]{2,1,0:T(8,128)} %get-tuple-element.45), calls=%async_computation | async-start | bytes 131072 | tf_op jit(solution)/shard_map/all_to_all | solution.py:594
  7.8 1.1 %shard_map.135 = (bf16[64,144]{1,0:T(8,128)(2,1)S(1)}, bf16[64,144]{1,0:T(8,128)(2,1)S(1)}, bf16[192,192]{1,0:T(8,128)(2,1)S(1)}, bf16[192,192]{1,0:T(8,128)(2,1...) custom-call(bf16[9,12,64]{2,1,0:T(8,128)(2,1)} %bitcast.11, bf16[9,64,64]{2,1,0:T(8,128)(2,1)} %conv2_hbm.1, ...), custom_call_target="tpu_custom_call" | custom-call | tf_op jit(solution)/shard_map/pallas_call | solution.py:648
  9.0 0.1 pad_add_fusion.place
  9.0 0.0 collective-permute-done.mate
  9.1 1.7 %shard_map.129 = (bf16[384,1536]{1,0:T(8,128)(2,1)S(1)}, bf16[96,384]{1,0:T(8,128)(2,1)S(1)}) custom-call(s32[1]{0:T(128)} %bitcast.1.me_ref, bf16[192,1536]{1,0:T(8,128)(2,1)} %own, bf16[192,1536]{1,0:T(8,128)(2,1)S(1)} %collective-permute-done.mate), custom_call_target="tpu_custom_call" | custom-call | flops 1000000000 | bytes 10000000 | tf_op jit(solution)/shard_map/pallas_call | solution.py:595
  10.8 1.2 %all-to-all-done.plans = f32[8,16,128]{2,1,0:T(8,128)S(1)} async-done(((f32[8,16,128]{2,1,0:T(8,128)}), f32[8,16,128]{2,1,0:T(8,128)S(1)}, u32[]{:S(2)}, u32[]{:S(2)}) %all-to-all-start) | async-done | bytes 65568 | tf_op jit(solution)/shard_map/all_to_all | solution.py:594
  12.0 1.3 %shard_map.130 = (f32[4,64,384]{2,1,0:T(8,128)S(1)}, bf16[240,128]{1,0:T(8,128)(2,1)S(1)}, bf16[240,128]{1,0:T(8,128)(2,1)S(1)}, bf16[240,128]{1,0:T(8,128)(2,1)S(1)}, f32[240,128]{1,0:T(8,128)S(1)}) custom-call(s32[1]{0:T(128)} %bitcast.1.me_ref, f32[8,16,128]{2,1,0:T(8,128)S(1)} %all-to-all-done.plans, bf16[384,1536]{1,0:T(8,128)(2,1)S(1)} %get-tuple-element.51.stored, ...), custom_call_target="tpu_custom_call" | custom-call | flops 1000000000 | bytes 10000000 | tf_op jit(solution)/shard_map/pallas_call | solution.py:606
  13.3 1.2 %collective-permute-start.4 = (bf16[240,128]{1,0:T(8,128)(2,1)S(1)}, bf16[240,128]{1,0:T(8,128)(2,1)S(1)}, u32[]{:S(2)}, u32[]{:S(2)}) collective-permute-start(bf16[240,128]{1,0:T(8,128)(2,1)S(1)} %get-tuple-element.57), channel_id=1, source_target_pairs={{0,6},{1,7},{2,4},{3,5},{4,2},{5,3},{6,0},{7,1},{8,14},{9,15},{10,... | collective-permute-start | bytes 184328 | tf_op jit(solution)/shard_map/ppermute | solution.py:574
  14.4 0.7 %collective-permute-start.5 = (bf16[240,128]{1,0:T(8,128)(2,1)S(1)}, bf16[240,128]{1,0:T(8,128)(2,1)S(1)}, u32[]{:S(2)}, u32[]{:S(2)}) collective-permute-start(bf16[240,128]{1,0:T(8,128)(2,1)S(1)} %get-tuple-element.58), channel_id=1, source_target_pairs={{0,4},{1,5},{2,6},{3,7},{4,0},{5,1},{6,2},{7,3},{8,12},{9,13},{10,... | collective-permute-start | bytes 184328 | tf_op jit(solution)/shard_map/ppermute | solution.py:574
  15.1 0.9 %collective-permute-start.6 = (bf16[240,128]{1,0:T(8,128)(2,1)S(1)}, bf16[240,128]{1,0:T(8,128)(2,1)S(1)}, u32[]{:S(2)}, u32[]{:S(2)}) collective-permute-start(bf16[240,128]{1,0:T(8,128)(2,1)S(1)} %get-tuple-element.59), channel_id=1, source_target_pairs={{0,2},{1,3},{2,0},{3,1},{4,6},{5,7},{6,4},{7,5},{8,10},{9,11},{10,... | collective-permute-start | bytes 184328 | tf_op jit(solution)/shard_map/ppermute | solution.py:574
  16.0 0.8 %shard_map.131 = (bf16[48,1536]{1,0:T(8,128)(2,1)S(1)}, bf16[48,1536]{1,0:T(8,128)(2,1)S(1)}, bf16[48,1536]{1,0:T(8,128)(2,1)S(1)}) custom-call(bf16[384,1536]{1,0:T(8,128)(2,1)S(1)} %get-tuple-element.51.stored, f32[4,64,384]{2,1,0:T(8,128)S(1)} %get-tuple-element.61.row_weights), custom_call_target="tpu_custom_call" | custom-call | flops 1000000000 | bytes 10000000 | tf_op jit(solution)/shard_map/pallas_call | solution.py:624
  16.8 1.2 %collective-permute-start.1 = (bf16[48,1536]{1,0:T(8,128)(2,1)S(1)}, bf16[48,1536]{1,0:T(8,128)(2,1)S(1)}, u32[]{:S(2)}, u32[]{:S(2)}) collective-permute-start(bf16[48,1536]{1,0:T(8,128)(2,1)S(1)} %get-tuple-element.54), channel_id=1, source_target_pairs={{0,6},{1,7},{2,4},{3,5},{4,2},{5,3},{6,0},{7,1},{8,14},{9,15},{10,... | collective-permute-start | bytes 442376 | tf_op jit(solution)/shard_map/ppermute | solution.py:574
  17.9 0.7 %collective-permute-start.2 = (bf16[48,1536]{1,0:T(8,128)(2,1)S(1)}, bf16[48,1536]{1,0:T(8,128)(2,1)S(1)}, u32[]{:S(2)}, u32[]{:S(2)}) collective-permute-start(bf16[48,1536]{1,0:T(8,128)(2,1)S(1)} %get-tuple-element.55), channel_id=1, source_target_pairs={{0,4},{1,5},{2,6},{3,7},{4,0},{5,1},{6,2},{7,3},{8,12},{9,13},{10,... | collective-permute-start | bytes 442376 | tf_op jit(solution)/shard_map/ppermute | solution.py:574
  18.6 0.0 collective-permute-done.4.refs_4_.refs_0_
  18.6 0.9 %collective-permute-start.3 = (bf16[48,1536]{1,0:T(8,128)(2,1)S(1)}, bf16[48,1536]{1,0:T(8,128)(2,1)S(1)}, u32[]{:S(2)}, u32[]{:S(2)}) collective-permute-start(bf16[48,1536]{1,0:T(8,128)(2,1)S(1)} %get-tuple-element.56), channel_id=1, source_target_pairs={{0,2},{1,3},{2,0},{3,1},{4,6},{5,7},{6,4},{7,5},{8,10},{9,11},{10,... | collective-permute-start | bytes 442376 | tf_op jit(solution)/shard_map/ppermute | solution.py:574
  19.5 0.2 shard_map.134
  19.7 3.2 %collective-permute-start.7 = (bf16[16,512]{1,0:T(8,128)(2,1)S(1)}, bf16[16,512]{1,0:T(8,128)(2,1)S(1)}, u32[]{:S(2)}, u32[]{:S(2)}) collective-permute-start(bf16[16,512]{1,0:T(8,128)(2,1)S(1)} %get-tuple-element.68), channel_id=1, source_target_pairs={{0,8},{8,16},{16,24},{1,9},{9,17},{17,25},{2,10},{10,18},{18,26},{... | collective-permute-start | bytes 49160 | tf_op jit(solution)/shard_map/ppermute | solution.py:646
  22.9 1.3 %collective-permute-start.8 = (bf16[16,512]{1,0:T(8,128)(2,1)S(1)}, bf16[16,512]{1,0:T(8,128)(2,1)S(1)}, u32[]{:S(2)}, u32[]{:S(2)}) collective-permute-start(bf16[16,512]{1,0:T(8,128)(2,1)S(1)} %get-tuple-element.69), channel_id=1, source_target_pairs={{8,0},{16,8},{24,16},{9,1},{17,9},{25,17},{10,2},{18,10},{26,18},{... | collective-permute-start | bytes 49160 | tf_op jit(solution)/shard_map/ppermute | solution.py:645
  24.2 0.3 shard_map.132.refs_3_
  24.5 0.0 collective-permute-done.1.refs_0_
  24.5 1.6 %collective-permute-done.2.refs_1_ = bf16[48,1536]{1,0:T(8,128)(2,1)S(1)} collective-permute-done((bf16[48,1536]{1,0:T(8,128)(2,1)S(1)}, bf16[48,1536]{1,0:T(8,128)(2,1)S(1)}, u32[]{:S(2)}, u32[]{:S(2)}) %collective-permute-start.2) | collective-permute-done | bytes 147488 | tf_op jit(solution)/shard_map/ppermute | solution.py:574
  26.1 0.7 %shard_map.133 = (bf16[16,8192]{1,0:T(8,128)(2,1)S(1)}, bf16[160,128]{1,0:T(8,128)(2,1)S(1)}) custom-call(s32[1]{0:T(128)} %bitcast.1.me_ref, f32[8,16,128]{2,1,0:T(8,128)S(1)} %all-to-all-done.plans, f32[64,128]{1,0:T(8,128)S(1)} %copy-done, bf16[48,1536]{1,0:T(8,128)(2,1)S(1)} %collective-permute-done.1.refs_0_, ...), custom_call_target="tpu_custom_call" | custom-call | flops 1000000000 | bytes 10000000 | tf_op jit(solution)/shard_map/pallas_call | solution.py:638
  26.8 0.5 collective-permute-done.8.below
  27.3 7.2 %shard_map.136 = (bf16[64,8192]{1,0:T(8,128)(2,1)S(1)}, f32[96,256]{1,0:T(8,128)S(1)}, f32[96,256]{1,0:T(8,128)S(1)}) custom-call(s32[2]{0:T(128)S(1)} %pad_add_fusion.place, bf16[16,8192]{1,0:T(8,128)(2,1)S(1)} %get-tuple-element.66.main, bf16[160,128]{1,0:T(8,128)(2,1)S(1)} %get-tuple-element.67.strips, bf16[16,512]{1,0:T(8,128)(2,1)S(1)} %collective-permute-done.7.above, ...), custom_call_target="tpu_custom_call" | custom-call | tf_op jit(solution)/shard_map/pallas_call | solution.py:672
  34.5 4.0 %collective-permute-start.9 = (f32[96,256]{1,0:T(8,128)S(1)}, f32[96,256]{1,0:T(8,128)S(1)}, u32[]{:S(2)}, u32[]{:S(2)}) collective-permute-start(f32[96,256]{1,0:T(8,128)S(1)} %get-tuple-element.78), channel_id=1, source_target_pairs={{0,1},{1,0},{2,3},{3,2},{4,5},{5,4},{6,7},{7,6},{8,9},{9,8},{10,11... | collective-permute-start | bytes 294920 | tf_op jit(solution)/shard_map/ppermute | solution.py:574
  38.6 0.9 %collective-permute-done.9 = f32[96,256]{1,0:T(8,128)S(1)} collective-permute-done((f32[96,256]{1,0:T(8,128)S(1)}, f32[96,256]{1,0:T(8,128)S(1)}, u32[]{:S(2)}, u32[]{:S(2)}) %collective-permute-start.9) | collective-permute-done | bytes 98336 | tf_op jit(solution)/shard_map/ppermute | solution.py:574
  39.5 0.1 reduce-precision_subtract_fusion.1
  39.6 0.1 fusion
  39.7 0.7 %collective-permute-start.12 = (bf16[96,256]{1,0:T(8,128)(2,1)S(1)}, bf16[96,256]{1,0:T(8,128)(2,1)S(1)}, u32[]{:S(2)}, u32[]{:S(2)}) collective-permute-start(bf16[96,256]{1,0:T(8,128)(2,1)S(1)} %reduce-precision_convert_fusion.1), channel_id=1, source_target_pairs={{0,6},{1,7},{2,4},{3,5},{4,2},{5,3},{6,0},{7,1},{8,14},{9,15},{10,... | collective-permute-start | bytes 147464 | tf_op jit(solution)/shard_map/ppermute | solution.py:709
  40.4 0.9 %collective-permute-start.11 = (bf16[96,256]{1,0:T(8,128)(2,1)S(1)}, bf16[96,256]{1,0:T(8,128)(2,1)S(1)}, u32[]{:S(2)}, u32[]{:S(2)}) collective-permute-start(bf16[96,256]{1,0:T(8,128)(2,1)S(1)} %reduce-precision_convert_fusion.1), channel_id=1, source_target_pairs={{0,4},{1,5},{2,6},{3,7},{4,0},{5,1},{6,2},{7,3},{8,12},{9,13},{10,... | collective-permute-start | bytes 147464 | tf_op jit(solution)/shard_map/ppermute | solution.py:709
  41.2 1.2 %collective-permute-start.10 = (bf16[96,256]{1,0:T(8,128)(2,1)S(1)}, bf16[96,256]{1,0:T(8,128)(2,1)S(1)}, u32[]{:S(2)}, u32[]{:S(2)}) collective-permute-start(bf16[96,256]{1,0:T(8,128)(2,1)S(1)} %reduce-precision_convert_fusion.1), channel_id=1, source_target_pairs={{0,2},{1,3},{2,0},{3,1},{4,6},{5,7},{6,4},{7,5},{8,10},{9,11},{10,... | collective-permute-start | bytes 147464 | tf_op jit(solution)/shard_map/ppermute | solution.py:709
  42.4 1.3 %collective-permute-done.12 = bf16[96,256]{1,0:T(8,128)(2,1)S(1)} collective-permute-done((bf16[96,256]{1,0:T(8,128)(2,1)S(1)}, bf16[96,256]{1,0:T(8,128)(2,1)S(1)}, u32[]{:S(2)}, u32[]{:S(2)}) %collective-permute-start.12) | collective-permute-done | bytes 49184 | tf_op jit(solution)/shard_map/ppermute | solution.py:709
  43.7 0.1 collective-permute-done.11
  43.8 0.7 %collective-permute-done.10 = bf16[96,256]{1,0:T(8,128)(2,1)S(1)} collective-permute-done((bf16[96,256]{1,0:T(8,128)(2,1)S(1)}, bf16[96,256]{1,0:T(8,128)(2,1)S(1)}, u32[]{:S(2)}, u32[]{:S(2)}) %collective-permute-start.10) | collective-permute-done | bytes 49184 | tf_op jit(solution)/shard_map/ppermute | solution.py:709
  44.5 0.1 reduce-precision_subtract_fusion
  44.6 0.1 fusion.1
  44.7 1.5 %collective-permute-start.15 = (bf16[96,256]{1,0:T(8,128)(2,1)S(1)}, bf16[96,256]{1,0:T(8,128)(2,1)S(1)}, u32[]{:S(2)}, u32[]{:S(2)}) collective-permute-start(bf16[96,256]{1,0:T(8,128)(2,1)S(1)} %reduce-precision_convert_fusion), channel_id=1, source_target_pairs={{0,24},{8,16},{16,8},{24,0},{1,25},{9,17},{17,9},{25,1},{2,26},{10... | collective-permute-start | bytes 147464 | tf_op jit(solution)/shard_map/ppermute | solution.py:709
  46.2 1.0 %collective-permute-start.14 = (bf16[96,256]{1,0:T(8,128)(2,1)S(1)}, bf16[96,256]{1,0:T(8,128)(2,1)S(1)}, u32[]{:S(2)}, u32[]{:S(2)}) collective-permute-start(bf16[96,256]{1,0:T(8,128)(2,1)S(1)} %reduce-precision_convert_fusion), channel_id=1, source_target_pairs={{0,16},{8,24},{16,0},{24,8},{1,17},{9,25},{17,1},{25,9},{2,18},{10... | collective-permute-start | bytes 147464 | tf_op jit(solution)/shard_map/ppermute | solution.py:709
  47.3 1.1 %collective-permute-start.13 = (bf16[96,256]{1,0:T(8,128)(2,1)S(1)}, bf16[96,256]{1,0:T(8,128)(2,1)S(1)}, u32[]{:S(2)}, u32[]{:S(2)}) collective-permute-start(bf16[96,256]{1,0:T(8,128)(2,1)S(1)} %reduce-precision_convert_fusion), channel_id=1, source_target_pairs={{0,8},{8,0},{16,24},{24,16},{1,9},{9,1},{17,25},{25,17},{2,10},{10... | collective-permute-start | bytes 147464 | tf_op jit(solution)/shard_map/ppermute | solution.py:709
  48.3 1.2 %collective-permute-done.15 = bf16[96,256]{1,0:T(8,128)(2,1)S(1)} collective-permute-done((bf16[96,256]{1,0:T(8,128)(2,1)S(1)}, bf16[96,256]{1,0:T(8,128)(2,1)S(1)}, u32[]{:S(2)}, u32[]{:S(2)}) %collective-permute-start.15) | collective-permute-done | bytes 49184 | tf_op jit(solution)/shard_map/ppermute | solution.py:709
  49.5 0.6 %collective-permute-done.14 = bf16[96,256]{1,0:T(8,128)(2,1)S(1)} collective-permute-done((bf16[96,256]{1,0:T(8,128)(2,1)S(1)}, bf16[96,256]{1,0:T(8,128)(2,1)S(1)}, u32[]{:S(2)}, u32[]{:S(2)}) %collective-permute-start.14) | collective-permute-done | bytes 49184 | tf_op jit(solution)/shard_map/ppermute | solution.py:709
  50.1 0.5 collective-permute-done.13
  50.6 3.3 %collective-permute-start.16 = (f32[96,256]{1,0:T(8,128)S(1)}, f32[96,256]{1,0:T(8,128)S(1)}, u32[]{:S(2)}, u32[]{:S(2)}) collective-permute-start(f32[96,256]{1,0:T(8,128)S(1)} %add_add_fusion.own), channel_id=1, source_target_pairs={{0,1},{1,0},{2,3},{3,2},{4,5},{5,4},{6,7},{7,6},{8,9},{9,8},{10,11... | collective-permute-start | bytes 294920 | tf_op jit(solution)/shard_map/ppermute | solution.py:574
  53.9 1.3 %copy.14 = bf16[8,8,64,128]{3,2,1,0:T(8,128)(2,1)} copy(bf16[8,8,64,128]{3,1,2,0:T(8,128)(2,1)S(1)} %bitcast.9) | data formatting | bytes 2097152
  55.2 0.0 collective-permute-done.16.mate
  55.2 1.0 %shard_map.137 = (f32[9,12,64]{2,1,0:T(8,128)}, f32[9,64,64]{2,1,0:T(8,128)}, f32[11,64]{1,0:T(8,128)}, f32[1,1]{1,0:T(1,128)}) custom-call(s32[1]{0:T(128)} %bitcast.1.me_ref, f32[96,256]{1,0:T(8,128)S(1)} %add_add_fusion.own, f32[96,256]{1,0:T(8,128)S(1)} %collective-permute-done.16.mate), custom_call_target="tpu_custom_call" | custom-call | tf_op jit(solution)/shard_map/pallas_call | solution.py:717
  (17 shorter events, 0.1 us)
Async XLA Ops:
  2.4 6.6 %collective-permute-start = (bf16[192,1536]{1,0:T(8,128)(2,1)}, bf16[192,1536]{1,0:T(8,128)(2,1)S(1)}, u32[]{:S(2)}, u32[]{:S(2)}) collective-permute-start(bf16[192,1536]{1,0:T(8,128)(2,1)} %own), channel_id=1, source_target_pairs={{0,1},{1,0},{2,3},{3,2},{4,5},{5,4},{6,7},{7,6},{8,9},{9,8},{10,11... | collective-permute-start | bytes 1769480 | tf_op jit(solution)/shard_map/ppermute | solution.py:574
  2.5 9.4 %all-to-all-start = ((f32[8,16,128]{2,1,0:T(8,128)}), f32[8,16,128]{2,1,0:T(8,128)S(1)}, u32[]{:S(2)}, u32[]{:S(2)}) async-start(f32[8,16,128]{2,1,0:T(8,128)} %get-tuple-element.45), calls=%async_computation | async-start | bytes 131072 | tf_op jit(solution)/shard_map/all_to_all | solution.py:594
  13.3 5.3 %collective-permute-start.4 = (bf16[240,128]{1,0:T(8,128)(2,1)S(1)}, bf16[240,128]{1,0:T(8,128)(2,1)S(1)}, u32[]{:S(2)}, u32[]{:S(2)}) collective-permute-start(bf16[240,128]{1,0:T(8,128)(2,1)S(1)} %get-tuple-element.57), channel_id=1, source_target_pairs={{0,6},{1,7},{2,4},{3,5},{4,2},{5,3},{6,0},{7,1},{8,14},{9,15},{10,... | collective-permute-start | bytes 184328 | tf_op jit(solution)/shard_map/ppermute | solution.py:574
  14.4 5.0 %collective-permute-start.5 = (bf16[240,128]{1,0:T(8,128)(2,1)S(1)}, bf16[240,128]{1,0:T(8,128)(2,1)S(1)}, u32[]{:S(2)}, u32[]{:S(2)}) collective-permute-start(bf16[240,128]{1,0:T(8,128)(2,1)S(1)} %get-tuple-element.58), channel_id=1, source_target_pairs={{0,4},{1,5},{2,6},{3,7},{4,0},{5,1},{6,2},{7,3},{8,12},{9,13},{10,... | collective-permute-start | bytes 184328 | tf_op jit(solution)/shard_map/ppermute | solution.py:574
  15.1 4.4 %collective-permute-start.6 = (bf16[240,128]{1,0:T(8,128)(2,1)S(1)}, bf16[240,128]{1,0:T(8,128)(2,1)S(1)}, u32[]{:S(2)}, u32[]{:S(2)}) collective-permute-start(bf16[240,128]{1,0:T(8,128)(2,1)S(1)} %get-tuple-element.59), channel_id=1, source_target_pairs={{0,2},{1,3},{2,0},{3,1},{4,6},{5,7},{6,4},{7,5},{8,10},{9,11},{10,... | collective-permute-start | bytes 184328 | tf_op jit(solution)/shard_map/ppermute | solution.py:574
  16.0 3.5 %copy-start = (f32[64,128]{1,0:T(8,128)S(1)}, f32[64,128]{1,0:T(8,128)}, u32[]{:S(2)}) copy-start(f32[64,128]{1,0:T(8,128)} %get-tuple-element.50.labels) | copy-start | bytes 98308
  16.8 7.7 %collective-permute-start.1 = (bf16[48,1536]{1,0:T(8,128)(2,1)S(1)}, bf16[48,1536]{1,0:T(8,128)(2,1)S(1)}, u32[]{:S(2)}, u32[]{:S(2)}) collective-permute-start(bf16[48,1536]{1,0:T(8,128)(2,1)S(1)} %get-tuple-element.54), channel_id=1, source_target_pairs={{0,6},{1,7},{2,4},{3,5},{4,2},{5,3},{6,0},{7,1},{8,14},{9,15},{10,... | collective-permute-start | bytes 442376 | tf_op jit(solution)/shard_map/ppermute | solution.py:574
  17.9 8.2 %collective-permute-start.2 = (bf16[48,1536]{1,0:T(8,128)(2,1)S(1)}, bf16[48,1536]{1,0:T(8,128)(2,1)S(1)}, u32[]{:S(2)}, u32[]{:S(2)}) collective-permute-start(bf16[48,1536]{1,0:T(8,128)(2,1)S(1)} %get-tuple-element.55), channel_id=1, source_target_pairs={{0,4},{1,5},{2,6},{3,7},{4,0},{5,1},{6,2},{7,3},{8,12},{9,13},{10,... | collective-permute-start | bytes 442376 | tf_op jit(solution)/shard_map/ppermute | solution.py:574
  18.6 7.6 %collective-permute-start.3 = (bf16[48,1536]{1,0:T(8,128)(2,1)S(1)}, bf16[48,1536]{1,0:T(8,128)(2,1)S(1)}, u32[]{:S(2)}, u32[]{:S(2)}) collective-permute-start(bf16[48,1536]{1,0:T(8,128)(2,1)S(1)} %get-tuple-element.56), channel_id=1, source_target_pairs={{0,2},{1,3},{2,0},{3,1},{4,6},{5,7},{6,4},{7,5},{8,10},{9,11},{10,... | collective-permute-start | bytes 442376 | tf_op jit(solution)/shard_map/ppermute | solution.py:574
  19.7 7.2 %collective-permute-start.7 = (bf16[16,512]{1,0:T(8,128)(2,1)S(1)}, bf16[16,512]{1,0:T(8,128)(2,1)S(1)}, u32[]{:S(2)}, u32[]{:S(2)}) collective-permute-start(bf16[16,512]{1,0:T(8,128)(2,1)S(1)} %get-tuple-element.68), channel_id=1, source_target_pairs={{0,8},{8,16},{16,24},{1,9},{9,17},{17,25},{2,10},{10,18},{18,26},{... | collective-permute-start | bytes 49160 | tf_op jit(solution)/shard_map/ppermute | solution.py:646
  22.9 4.5 %collective-permute-start.8 = (bf16[16,512]{1,0:T(8,128)(2,1)S(1)}, bf16[16,512]{1,0:T(8,128)(2,1)S(1)}, u32[]{:S(2)}, u32[]{:S(2)}) collective-permute-start(bf16[16,512]{1,0:T(8,128)(2,1)S(1)} %get-tuple-element.69), channel_id=1, source_target_pairs={{8,0},{16,8},{24,16},{9,1},{17,9},{25,17},{10,2},{18,10},{26,18},{... | collective-permute-start | bytes 49160 | tf_op jit(solution)/shard_map/ppermute | solution.py:645
  34.5 5.0 %collective-permute-start.9 = (f32[96,256]{1,0:T(8,128)S(1)}, f32[96,256]{1,0:T(8,128)S(1)}, u32[]{:S(2)}, u32[]{:S(2)}) collective-permute-start(f32[96,256]{1,0:T(8,128)S(1)} %get-tuple-element.78), channel_id=1, source_target_pairs={{0,1},{1,0},{2,3},{3,2},{4,5},{5,4},{6,7},{7,6},{8,9},{9,8},{10,11... | collective-permute-start | bytes 294920 | tf_op jit(solution)/shard_map/ppermute | solution.py:574
  39.7 4.0 %collective-permute-start.12 = (bf16[96,256]{1,0:T(8,128)(2,1)S(1)}, bf16[96,256]{1,0:T(8,128)(2,1)S(1)}, u32[]{:S(2)}, u32[]{:S(2)}) collective-permute-start(bf16[96,256]{1,0:T(8,128)(2,1)S(1)} %reduce-precision_convert_fusion.1), channel_id=1, source_target_pairs={{0,6},{1,7},{2,4},{3,5},{4,2},{5,3},{6,0},{7,1},{8,14},{9,15},{10,... | collective-permute-start | bytes 147464 | tf_op jit(solution)/shard_map/ppermute | solution.py:709
  40.4 3.5 %collective-permute-start.11 = (bf16[96,256]{1,0:T(8,128)(2,1)S(1)}, bf16[96,256]{1,0:T(8,128)(2,1)S(1)}, u32[]{:S(2)}, u32[]{:S(2)}) collective-permute-start(bf16[96,256]{1,0:T(8,128)(2,1)S(1)} %reduce-precision_convert_fusion.1), channel_id=1, source_target_pairs={{0,4},{1,5},{2,6},{3,7},{4,0},{5,1},{6,2},{7,3},{8,12},{9,13},{10,... | collective-permute-start | bytes 147464 | tf_op jit(solution)/shard_map/ppermute | solution.py:709
  41.2 3.2 %collective-permute-start.10 = (bf16[96,256]{1,0:T(8,128)(2,1)S(1)}, bf16[96,256]{1,0:T(8,128)(2,1)S(1)}, u32[]{:S(2)}, u32[]{:S(2)}) collective-permute-start(bf16[96,256]{1,0:T(8,128)(2,1)S(1)} %reduce-precision_convert_fusion.1), channel_id=1, source_target_pairs={{0,2},{1,3},{2,0},{3,1},{4,6},{5,7},{6,4},{7,5},{8,10},{9,11},{10,... | collective-permute-start | bytes 147464 | tf_op jit(solution)/shard_map/ppermute | solution.py:709
  44.7 4.8 %collective-permute-start.15 = (bf16[96,256]{1,0:T(8,128)(2,1)S(1)}, bf16[96,256]{1,0:T(8,128)(2,1)S(1)}, u32[]{:S(2)}, u32[]{:S(2)}) collective-permute-start(bf16[96,256]{1,0:T(8,128)(2,1)S(1)} %reduce-precision_convert_fusion), channel_id=1, source_target_pairs={{0,24},{8,16},{16,8},{24,0},{1,25},{9,17},{17,9},{25,1},{2,26},{10... | collective-permute-start | bytes 147464 | tf_op jit(solution)/shard_map/ppermute | solution.py:709
  46.2 3.9 %collective-permute-start.14 = (bf16[96,256]{1,0:T(8,128)(2,1)S(1)}, bf16[96,256]{1,0:T(8,128)(2,1)S(1)}, u32[]{:S(2)}, u32[]{:S(2)}) collective-permute-start(bf16[96,256]{1,0:T(8,128)(2,1)S(1)} %reduce-precision_convert_fusion), channel_id=1, source_target_pairs={{0,16},{8,24},{16,0},{24,8},{1,17},{9,25},{17,1},{25,9},{2,18},{10... | collective-permute-start | bytes 147464 | tf_op jit(solution)/shard_map/ppermute | solution.py:709
  47.3 3.4 %collective-permute-start.13 = (bf16[96,256]{1,0:T(8,128)(2,1)S(1)}, bf16[96,256]{1,0:T(8,128)(2,1)S(1)}, u32[]{:S(2)}, u32[]{:S(2)}) collective-permute-start(bf16[96,256]{1,0:T(8,128)(2,1)S(1)} %reduce-precision_convert_fusion), channel_id=1, source_target_pairs={{0,8},{8,0},{16,24},{24,16},{1,9},{9,1},{17,25},{25,17},{2,10},{10... | collective-permute-start | bytes 147464 | tf_op jit(solution)/shard_map/ppermute | solution.py:709
  50.6 4.5 %collective-permute-start.16 = (f32[96,256]{1,0:T(8,128)S(1)}, f32[96,256]{1,0:T(8,128)S(1)}, u32[]{:S(2)}, u32[]{:S(2)}) collective-permute-start(f32[96,256]{1,0:T(8,128)S(1)} %add_add_fusion.own), channel_id=1, source_target_pairs={{0,1},{1,0},{2,3},{3,2},{4,5},{5,4},{6,7},{7,6},{8,9},{9,8},{10,11... | collective-permute-start | bytes 294920 | tf_op jit(solution)/shard_map/ppermute | solution.py:574

commit v8 on v7

--- a/solution.py
+++ b/solution.py
@@ -267,17 +267,12 @@
 
 
 def weights_kernel(
-    conv1_hbm, conv2_hbm, head_hbm, one_main, one_strip, two_main, two_back, head_pad, head_turn,
-    wide, tall, conv1, conv2, head, sems,
+    conv1, conv2_hbm, head, one_main, one_strip, two_main, two_back, head_pad, head_turn,
+    wide, tall, conv2, sem,
 ):
-    copies = [
-        pltpu.make_async_copy(source, target, sems.at[i])
-        for i, (source, target) in enumerate(((conv1_hbm, conv1), (conv2_hbm, conv2), (head_hbm, head)))
-    ]
-    for copy in copies:
-        copy.start()
-    for copy in copies:
-        copy.wait()
+    copy = pltpu.make_async_copy(conv2_hbm, conv2, sem)
+    copy.start()
+    copy.wait()
     bands = conv1.shape[1]
     feat = conv2.shape[1]
     classes = head.shape[0]
@@ -658,13 +653,11 @@
         [
             pltpu.VMEM((9 * GROUP, feat), F32),
             pltpu.VMEM((128, 128), F32),
-            pltpu.VMEM((9, bands, feat), BF16),
             pltpu.VMEM(conv2_weight.shape, BF16),
-            pltpu.VMEM(head_weight.shape, BF16),
-            pltpu.SemaphoreType.DMA((3,)),
+            pltpu.SemaphoreType.DMA,
         ],
-        in_specs=[hbm] * 3,
-    )(*[in_hbm(value) for value in (conv1_weight.transpose(0, 2, 1), conv2_weight, head_weight)])
+        in_specs=[vmem, hbm, vmem],
+    )(conv1_weight.transpose(0, 2, 1), in_hbm(conv2_weight), head_weight)
 
     ext = rows + 6
     half = 3 * feat // 2

time: 56.6 us -> 57.5 us (1.016)
  local copies, waits for them, and re-layouts: 1.28 us -> 2.73 us
  waiting for transfers between devices: 8.65 us -> 7.98 us
    unnamed x3 -> x7, local copies, waits for them, and re-layouts: 1.26 us -> 2.71 us
    all_to_all x1, waiting for transfers between devices: 1.21 us -> 0.01 us  [body(): plans = lax.all_to_all(plan, 'lon', split_axis=0, concat_axis=0, tiled=True)]
  transfers between devices with their start and end apart: 18 -> 18, of which waited for: 10 -> 8; matrix products, arithmetic and copies ran while one was open for 2% -> 2% of each run, Pallas kernels for 9% -> 8%
where the time goes in v8:
time: 57.5 us; the launch traced here: 57 us
  starting transfers between devices  29 us (50%)
  Pallas kernels  16.1 us (28%)
  waiting for transfers between devices  7.98 us (14%)
  local copies, waits for them, and re-layouts  2.73 us (5%)
  between operations  0.79 us (1%)
    ppermute x9, starting transfers between devices, by_lon(): return lax.ppermute(value, 'lon', [(i, i ^ move) for i in range(lon_count)])  12.9 us
    pallas_call x1, Pallas kernels, body(): call(functools.partial(network_kernel, bands, classes, rows, cols, lat_co...  7.18 us
    ppermute x6, starting transfers between devices, sum_over(): lax.ppermute(sent, axis, [(i, i ^ move) for i in range(size)]).astype(F32)  6.33 us
    all_to_all x1, starting transfers between devices, body(): plans = lax.all_to_all(plan, 'lon', split_axis=0, concat_axis=0, tiled=True)  5.28 us
    ppermute x6, waiting for transfers between devices, sum_over(): lax.ppermute(sent, axis, [(i, i ^ move) for i in range(size)]).astype(F32)  4.89 us
    ppermute x1, starting transfers between devices, body(): lax.ppermute(lower, 'lat', [(i, i + 1) for i in range(lat_count - 1)])  3.2 us
    ppermute x9, waiting for transfers between devices, by_lon(): return lax.ppermute(value, 'lon', [(i, i ^ move) for i in range(lon_count)])  3.06 us
    unnamed x7, local copies, waits for them, and re-layouts  2.71 us
  transfers between devices with their start and end apart: 18, of which 8 were waited for; matrix products, arithmetic and copies ran while one was open for 2% of the time, Pallas kernels for 8%

profile of v8, /device:TPU:1, one launch (start us, length us, event | category | flops | bytes accessed | tf_op | source)
XLA Modules:
  0.0 57.0 jit_solution(16851607191805867539)
XLA Ops:
  0.6 1.8 %shard_map.128 = (f32[8,16,128]{2,1,0:T(8,128)}, f32[64,128]{1,0:T(8,128)}) custom-call(s32[1,512]{1,0:T(1,128)} %requests_hbm.1, s32[8,64]{1,0:T(8,128)} %bitcast.12, s32[8,64]{1,0:T(8,128)} %bitcast.13, f32[16]{0:T(128)} %levels_hbm.1, s32[64,128]{1,0:T(8,128)} %labels_hbm.1), custom_call_target="tpu_custom_call" | custom-call | tf_op jit(solution)/shard_map/pallas_call | solution.py:573
  2.4 0.1 collective-permute-start
  2.5 5.3 %all-to-all-start = ((f32[8,16,128]{2,1,0:T(8,128)}), f32[8,16,128]{2,1,0:T(8,128)S(1)}, u32[]{:S(2)}, u32[]{:S(2)}) async-start(f32[8,16,128]{2,1,0:T(8,128)} %get-tuple-element.45), calls=%async_computation | async-start | bytes 131072 | tf_op jit(solution)/shard_map/all_to_all | solution.py:589
  7.8 0.8 %copy-done = bf16[9,64,12]{1,2,0:T(8,128)(2,1)S(1)} copy-done((bf16[9,64,12]{1,2,0:T(8,128)(2,1)S(1)}, bf16[9,64,12]{1,2,0:T(8,128)(2,1)}, u32[]{:S(2)}) %copy-start) | copy-done | bytes 13848
  8.6 0.7 %copy-done.1 = bf16[11,64]{1,0:T(8,128)(2,1)S(1)} copy-done((bf16[11,64]{1,0:T(8,128)(2,1)S(1)}, bf16[11,64]{1,0:T(8,128)(2,1)}, u32[]{:S(2)}) %copy-start.1) | copy-done | bytes 1432
  9.3 1.1 %shard_map.135 = (bf16[64,144]{1,0:T(8,128)(2,1)S(1)}, bf16[64,144]{1,0:T(8,128)(2,1)S(1)}, bf16[192,192]{1,0:T(8,128)(2,1)S(1)}, bf16[192,192]{1,0:T(8,128)(2,1...) custom-call(bf16[9,12,64]{2,1,0:T(8,128)(2,1)S(1)} %bitcast.10, bf16[9,64,64]{2,1,0:T(8,128)(2,1)} %conv2_hbm.1, ...), custom_call_target="tpu_custom_call" | custom-call | tf_op jit(solution)/shard_map/pallas_call | solution.py:643
  10.4 0.1 pad_add_fusion.place
  10.5 0.0 collective-permute-done.mate
  10.5 1.7 %shard_map.129 = (bf16[384,1536]{1,0:T(8,128)(2,1)S(1)}, bf16[96,384]{1,0:T(8,128)(2,1)S(1)}) custom-call(s32[1]{0:T(128)} %bitcast.1.me_ref, bf16[192,1536]{1,0:T(8,128)(2,1)} %own, bf16[192,1536]{1,0:T(8,128)(2,1)S(1)} %collective-permute-done.mate), custom_call_target="tpu_custom_call" | custom-call | flops 1000000000 | bytes 10000000 | tf_op jit(solution)/shard_map/pallas_call | solution.py:590
  12.2 1.3 %shard_map.130 = (f32[4,64,384]{2,1,0:T(8,128)S(1)}, bf16[240,128]{1,0:T(8,128)(2,1)S(1)}, bf16[240,128]{1,0:T(8,128)(2,1)S(1)}, bf16[240,128]{1,0:T(8,128)(2,1)S(1)}, f32[240,128]{1,0:T(8,128)S(1)}) custom-call(s32[1]{0:T(128)} %bitcast.1.me_ref, f32[8,16,128]{2,1,0:T(8,128)S(1)} %all-to-all-done.plans, bf16[384,1536]{1,0:T(8,128)(2,1)S(1)} %get-tuple-element.51.stored, ...), custom_call_target="tpu_custom_call" | custom-call | flops 1000000000 | bytes 10000000 | tf_op jit(solution)/shard_map/pallas_call | solution.py:601
  13.5 2.4 %collective-permute-start.4 = (bf16[240,128]{1,0:T(8,128)(2,1)S(1)}, bf16[240,128]{1,0:T(8,128)(2,1)S(1)}, u32[]{:S(2)}, u32[]{:S(2)}) collective-permute-start(bf16[240,128]{1,0:T(8,128)(2,1)S(1)} %get-tuple-element.57), channel_id=1, source_target_pairs={{0,6},{1,7},{2,4},{3,5},{4,2},{5,3},{6,0},{7,1},{8,14},{9,15},{10,... | collective-permute-start | bytes 184328 | tf_op jit(solution)/shard_map/ppermute | solution.py:569
  15.9 0.3 collective-permute-start.5
  16.1 0.1 collective-permute-start.6
  16.2 0.8 %shard_map.131 = (bf16[48,1536]{1,0:T(8,128)(2,1)S(1)}, bf16[48,1536]{1,0:T(8,128)(2,1)S(1)}, bf16[48,1536]{1,0:T(8,128)(2,1)S(1)}) custom-call(bf16[384,1536]{1,0:T(8,128)(2,1)S(1)} %get-tuple-element.51.stored, f32[4,64,384]{2,1,0:T(8,128)S(1)} %get-tuple-element.61.row_weights), custom_call_target="tpu_custom_call" | custom-call | flops 1000000000 | bytes 10000000 | tf_op jit(solution)/shard_map/pallas_call | solution.py:619
  17.0 2.3 %collective-permute-start.1 = (bf16[48,1536]{1,0:T(8,128)(2,1)S(1)}, bf16[48,1536]{1,0:T(8,128)(2,1)S(1)}, u32[]{:S(2)}, u32[]{:S(2)}) collective-permute-start(bf16[48,1536]{1,0:T(8,128)(2,1)S(1)} %get-tuple-element.54), channel_id=1, source_target_pairs={{0,6},{1,7},{2,4},{3,5},{4,2},{5,3},{6,0},{7,1},{8,14},{9,15},{10,... | collective-permute-start | bytes 442376 | tf_op jit(solution)/shard_map/ppermute | solution.py:569
  19.3 0.3 collective-permute-start.2
  19.6 0.0 collective-permute-done.4.refs_4_.refs_0_
  19.6 0.1 collective-permute-start.3
  19.7 0.2 shard_map.134
  19.9 3.2 %collective-permute-start.7 = (bf16[16,512]{1,0:T(8,128)(2,1)S(1)}, bf16[16,512]{1,0:T(8,128)(2,1)S(1)}, u32[]{:S(2)}, u32[]{:S(2)}) collective-permute-start(bf16[16,512]{1,0:T(8,128)(2,1)S(1)} %get-tuple-element.68), channel_id=1, source_target_pairs={{0,8},{8,16},{16,24},{1,9},{9,17},{17,25},{2,10},{10,18},{18,26},{... | collective-permute-start | bytes 49160 | tf_op jit(solution)/shard_map/ppermute | solution.py:641
  23.1 1.3 %collective-permute-start.8 = (bf16[16,512]{1,0:T(8,128)(2,1)S(1)}, bf16[16,512]{1,0:T(8,128)(2,1)S(1)}, u32[]{:S(2)}, u32[]{:S(2)}) collective-permute-start(bf16[16,512]{1,0:T(8,128)(2,1)S(1)} %get-tuple-element.69), channel_id=1, source_target_pairs={{8,0},{16,8},{24,16},{9,1},{17,9},{25,17},{10,2},{18,10},{26,18},{... | collective-permute-start | bytes 49160 | tf_op jit(solution)/shard_map/ppermute | solution.py:640
  24.4 0.3 shard_map.132.refs_3_
  24.7 0.0 collective-permute-done.1.refs_0_
  24.8 2.1 %collective-permute-done.2.refs_1_ = bf16[48,1536]{1,0:T(8,128)(2,1)S(1)} collective-permute-done((bf16[48,1536]{1,0:T(8,128)(2,1)S(1)}, bf16[48,1536]{1,0:T(8,128)(2,1)S(1)}, u32[]{:S(2)}, u32[]{:S(2)}) %collective-permute-start.2) | collective-permute-done | bytes 147488 | tf_op jit(solution)/shard_map/ppermute | solution.py:569
  26.9 0.7 %shard_map.133 = (bf16[16,8192]{1,0:T(8,128)(2,1)S(1)}, bf16[160,128]{1,0:T(8,128)(2,1)S(1)}) custom-call(s32[1]{0:T(128)} %bitcast.1.me_ref, f32[8,16,128]{2,1,0:T(8,128)S(1)} %all-to-all-done.plans, f32[64,128]{1,0:T(8,128)S(1)} %copy-done.2, bf16[48,1536]{1,0:T(8,128)(2,1)S(1)} %collective-permute-done.1.refs_0_, ...), custom_call_target="tpu_custom_call" | custom-call | flops 1000000000 | bytes 10000000 | tf_op jit(solution)/shard_map/pallas_call | solution.py:633
  27.6 0.0 collective-permute-done.8.below
  27.6 7.2 %shard_map.136 = (bf16[64,8192]{1,0:T(8,128)(2,1)S(1)}, f32[96,256]{1,0:T(8,128)S(1)}, f32[96,256]{1,0:T(8,128)S(1)}) custom-call(s32[2]{0:T(128)S(1)} %pad_add_fusion.place, bf16[16,8192]{1,0:T(8,128)(2,1)S(1)} %get-tuple-element.66.main, bf16[160,128]{1,0:T(8,128)(2,1)S(1)} %get-tuple-element.67.strips, bf16[16,512]{1,0:T(8,128)(2,1)S(1)} %collective-permute-done.7.above, ...), custom_call_target="tpu_custom_call" | custom-call | tf_op jit(solution)/shard_map/pallas_call | solution.py:665
  34.8 3.8 %collective-permute-start.9 = (f32[96,256]{1,0:T(8,128)S(1)}, f32[96,256]{1,0:T(8,128)S(1)}, u32[]{:S(2)}, u32[]{:S(2)}) collective-permute-start(f32[96,256]{1,0:T(8,128)S(1)} %get-tuple-element.78), channel_id=1, source_target_pairs={{0,1},{1,0},{2,3},{3,2},{4,5},{5,4},{6,7},{7,6},{8,9},{9,8},{10,11... | collective-permute-start | bytes 294920 | tf_op jit(solution)/shard_map/ppermute | solution.py:569
  38.6 0.9 %collective-permute-done.9 = f32[96,256]{1,0:T(8,128)S(1)} collective-permute-done((f32[96,256]{1,0:T(8,128)S(1)}, f32[96,256]{1,0:T(8,128)S(1)}, u32[]{:S(2)}, u32[]{:S(2)}) %collective-permute-start.9) | collective-permute-done | bytes 98336 | tf_op jit(solution)/shard_map/ppermute | solution.py:569
  39.5 0.1 reduce-precision_subtract_fusion.1
  39.6 0.1 fusion
  39.7 2.1 %collective-permute-start.12 = (bf16[96,256]{1,0:T(8,128)(2,1)S(1)}, bf16[96,256]{1,0:T(8,128)(2,1)S(1)}, u32[]{:S(2)}, u32[]{:S(2)}) collective-permute-start(bf16[96,256]{1,0:T(8,128)(2,1)S(1)} %reduce-precision_convert_fusion.1), channel_id=1, source_target_pairs={{0,6},{1,7},{2,4},{3,5},{4,2},{5,3},{6,0},{7,1},{8,14},{9,15},{10,... | collective-permute-start | bytes 147464 | tf_op jit(solution)/shard_map/ppermute | solution.py:702
  41.8 0.3 collective-permute-start.11
  42.1 0.3 collective-permute-start.10
  42.4 1.2 %collective-permute-done.12 = bf16[96,256]{1,0:T(8,128)(2,1)S(1)} collective-permute-done((bf16[96,256]{1,0:T(8,128)(2,1)S(1)}, bf16[96,256]{1,0:T(8,128)(2,1)S(1)}, u32[]{:S(2)}, u32[]{:S(2)}) %collective-permute-start.12) | collective-permute-done | bytes 49184 | tf_op jit(solution)/shard_map/ppermute | solution.py:702
  43.6 1.3 %collective-permute-done.11 = bf16[96,256]{1,0:T(8,128)(2,1)S(1)} collective-permute-done((bf16[96,256]{1,0:T(8,128)(2,1)S(1)}, bf16[96,256]{1,0:T(8,128)(2,1)S(1)}, u32[]{:S(2)}, u32[]{:S(2)}) %collective-permute-start.11) | collective-permute-done | bytes 49184 | tf_op jit(solution)/shard_map/ppermute | solution.py:702
  45.0 0.1 collective-permute-done.10
  45.0 0.1 reduce-precision_subtract_fusion
  45.1 0.1 fusion.1
  45.2 1.6 %collective-permute-start.15 = (bf16[96,256]{1,0:T(8,128)(2,1)S(1)}, bf16[96,256]{1,0:T(8,128)(2,1)S(1)}, u32[]{:S(2)}, u32[]{:S(2)}) collective-permute-start(bf16[96,256]{1,0:T(8,128)(2,1)S(1)} %reduce-precision_convert_fusion), channel_id=1, source_target_pairs={{0,24},{8,16},{16,8},{24,0},{1,25},{9,17},{17,9},{25,1},{2,26},{10... | collective-permute-start | bytes 147464 | tf_op jit(solution)/shard_map/ppermute | solution.py:702
  46.8 1.0 %collective-permute-start.14 = (bf16[96,256]{1,0:T(8,128)(2,1)S(1)}, bf16[96,256]{1,0:T(8,128)(2,1)S(1)}, u32[]{:S(2)}, u32[]{:S(2)}) collective-permute-start(bf16[96,256]{1,0:T(8,128)(2,1)S(1)} %reduce-precision_convert_fusion), channel_id=1, source_target_pairs={{0,16},{8,24},{16,0},{24,8},{1,17},{9,25},{17,1},{25,9},{2,18},{10... | collective-permute-start | bytes 147464 | tf_op jit(solution)/shard_map/ppermute | solution.py:702
  47.8 1.1 %collective-permute-start.13 = (bf16[96,256]{1,0:T(8,128)(2,1)S(1)}, bf16[96,256]{1,0:T(8,128)(2,1)S(1)}, u32[]{:S(2)}, u32[]{:S(2)}) collective-permute-start(bf16[96,256]{1,0:T(8,128)(2,1)S(1)} %reduce-precision_convert_fusion), channel_id=1, source_target_pairs={{0,8},{8,0},{16,24},{24,16},{1,9},{9,1},{17,25},{25,17},{2,10},{10... | collective-permute-start | bytes 147464 | tf_op jit(solution)/shard_map/ppermute | solution.py:702
  48.8 1.2 %collective-permute-done.15 = bf16[96,256]{1,0:T(8,128)(2,1)S(1)} collective-permute-done((bf16[96,256]{1,0:T(8,128)(2,1)S(1)}, bf16[96,256]{1,0:T(8,128)(2,1)S(1)}, u32[]{:S(2)}, u32[]{:S(2)}) %collective-permute-start.15) | collective-permute-done | bytes 49184 | tf_op jit(solution)/shard_map/ppermute | solution.py:702
  50.0 0.6 %collective-permute-done.14 = bf16[96,256]{1,0:T(8,128)(2,1)S(1)} collective-permute-done((bf16[96,256]{1,0:T(8,128)(2,1)S(1)}, bf16[96,256]{1,0:T(8,128)(2,1)S(1)}, u32[]{:S(2)}, u32[]{:S(2)}) %collective-permute-start.14) | collective-permute-done | bytes 49184 | tf_op jit(solution)/shard_map/ppermute | solution.py:702
  50.7 0.5 collective-permute-done.13
  51.2 3.6 %collective-permute-start.16 = (f32[96,256]{1,0:T(8,128)S(1)}, f32[96,256]{1,0:T(8,128)S(1)}, u32[]{:S(2)}, u32[]{:S(2)}) collective-permute-start(f32[96,256]{1,0:T(8,128)S(1)} %add_add_fusion.own), channel_id=1, source_target_pairs={{0,1},{1,0},{2,3},{3,2},{4,5},{5,4},{6,7},{7,6},{8,9},{9,8},{10,11... | collective-permute-start | bytes 294920 | tf_op jit(solution)/shard_map/ppermute | solution.py:569
  54.7 1.3 %copy.14 = bf16[8,8,64,128]{3,2,1,0:T(8,128)(2,1)} copy(bf16[8,8,64,128]{3,1,2,0:T(8,128)(2,1)S(1)} %bitcast.9) | data formatting | bytes 2097152
  56.0 1.0 %shard_map.137 = (f32[9,12,64]{2,1,0:T(8,128)}, f32[9,64,64]{2,1,0:T(8,128)}, f32[11,64]{1,0:T(8,128)}, f32[1,1]{1,0:T(1,128)}) custom-call(s32[1]{0:T(128)} %bitcast.1.me_ref, f32[96,256]{1,0:T(8,128)S(1)} %add_add_fusion.own, f32[96,256]{1,0:T(8,128)S(1)} %collective-permute-done.16.mate), custom_call_target="tpu_custom_call" | custom-call | tf_op jit(solution)/shard_map/pallas_call | solution.py:710
  (21 shorter events, 0.1 us)
Async XLA Ops:
  2.4 8.1 %collective-permute-start = (bf16[192,1536]{1,0:T(8,128)(2,1)}, bf16[192,1536]{1,0:T(8,128)(2,1)S(1)}, u32[]{:S(2)}, u32[]{:S(2)}) collective-permute-start(bf16[192,1536]{1,0:T(8,128)(2,1)} %own), channel_id=1, source_target_pairs={{0,1},{1,0},{2,3},{3,2},{4,5},{5,4},{6,7},{7,6},{8,9},{9,8},{10,11... | collective-permute-start | bytes 1769480 | tf_op jit(solution)/shard_map/ppermute | solution.py:569
  2.5 9.6 %all-to-all-start = ((f32[8,16,128]{2,1,0:T(8,128)}), f32[8,16,128]{2,1,0:T(8,128)S(1)}, u32[]{:S(2)}, u32[]{:S(2)}) async-start(f32[8,16,128]{2,1,0:T(8,128)} %get-tuple-element.45), calls=%async_computation | async-start | bytes 131072 | tf_op jit(solution)/shard_map/all_to_all | solution.py:589
  7.8 0.8 %copy-start = (bf16[9,64,12]{1,2,0:T(8,128)(2,1)S(1)}, bf16[9,64,12]{1,2,0:T(8,128)(2,1)}, u32[]{:S(2)}) copy-start(bf16[9,64,12]{1,2,0:T(8,128)(2,1)} %param.15) | copy-start | bytes 41476
  8.6 0.7 %copy-start.1 = (bf16[11,64]{1,0:T(8,128)(2,1)S(1)}, bf16[11,64]{1,0:T(8,128)(2,1)}, u32[]{:S(2)}) copy-start(bf16[11,64]{1,0:T(8,128)(2,1)} %head.1) | copy-start | bytes 4228
  13.5 6.1 %collective-permute-start.4 = (bf16[240,128]{1,0:T(8,128)(2,1)S(1)}, bf16[240,128]{1,0:T(8,128)(2,1)S(1)}, u32[]{:S(2)}, u32[]{:S(2)}) collective-permute-start(bf16[240,128]{1,0:T(8,128)(2,1)S(1)} %get-tuple-element.57), channel_id=1, source_target_pairs={{0,6},{1,7},{2,4},{3,5},{4,2},{5,3},{6,0},{7,1},{8,14},{9,15},{10,... | collective-permute-start | bytes 184328 | tf_op jit(solution)/shard_map/ppermute | solution.py:569
  15.9 3.8 %collective-permute-start.5 = (bf16[240,128]{1,0:T(8,128)(2,1)S(1)}, bf16[240,128]{1,0:T(8,128)(2,1)S(1)}, u32[]{:S(2)}, u32[]{:S(2)}) collective-permute-start(bf16[240,128]{1,0:T(8,128)(2,1)S(1)} %get-tuple-element.58), channel_id=1, source_target_pairs={{0,4},{1,5},{2,6},{3,7},{4,0},{5,1},{6,2},{7,3},{8,12},{9,13},{10,... | collective-permute-start | bytes 184328 | tf_op jit(solution)/shard_map/ppermute | solution.py:569
  16.1 3.6 %collective-permute-start.6 = (bf16[240,128]{1,0:T(8,128)(2,1)S(1)}, bf16[240,128]{1,0:T(8,128)(2,1)S(1)}, u32[]{:S(2)}, u32[]{:S(2)}) collective-permute-start(bf16[240,128]{1,0:T(8,128)(2,1)S(1)} %get-tuple-element.59), channel_id=1, source_target_pairs={{0,2},{1,3},{2,0},{3,1},{4,6},{5,7},{6,4},{7,5},{8,10},{9,11},{10,... | collective-permute-start | bytes 184328 | tf_op jit(solution)/shard_map/ppermute | solution.py:569
  16.2 3.5 %copy-start.2 = (f32[64,128]{1,0:T(8,128)S(1)}, f32[64,128]{1,0:T(8,128)}, u32[]{:S(2)}) copy-start(f32[64,128]{1,0:T(8,128)} %get-tuple-element.50.labels) | copy-start | bytes 98308
  17.0 7.8 %collective-permute-start.1 = (bf16[48,1536]{1,0:T(8,128)(2,1)S(1)}, bf16[48,1536]{1,0:T(8,128)(2,1)S(1)}, u32[]{:S(2)}, u32[]{:S(2)}) collective-permute-start(bf16[48,1536]{1,0:T(8,128)(2,1)S(1)} %get-tuple-element.54), channel_id=1, source_target_pairs={{0,6},{1,7},{2,4},{3,5},{4,2},{5,3},{6,0},{7,1},{8,14},{9,15},{10,... | collective-permute-start | bytes 442376 | tf_op jit(solution)/shard_map/ppermute | solution.py:569
  19.3 7.5 %collective-permute-start.2 = (bf16[48,1536]{1,0:T(8,128)(2,1)S(1)}, bf16[48,1536]{1,0:T(8,128)(2,1)S(1)}, u32[]{:S(2)}, u32[]{:S(2)}) collective-permute-start(bf16[48,1536]{1,0:T(8,128)(2,1)S(1)} %get-tuple-element.55), channel_id=1, source_target_pairs={{0,4},{1,5},{2,6},{3,7},{4,0},{5,1},{6,2},{7,3},{8,12},{9,13},{10,... | collective-permute-start | bytes 442376 | tf_op jit(solution)/shard_map/ppermute | solution.py:569
  19.6 7.2 %collective-permute-start.3 = (bf16[48,1536]{1,0:T(8,128)(2,1)S(1)}, bf16[48,1536]{1,0:T(8,128)(2,1)S(1)}, u32[]{:S(2)}, u32[]{:S(2)}) collective-permute-start(bf16[48,1536]{1,0:T(8,128)(2,1)S(1)} %get-tuple-element.56), channel_id=1, source_target_pairs={{0,2},{1,3},{2,0},{3,1},{4,6},{5,7},{6,4},{7,5},{8,10},{9,11},{10,... | collective-permute-start | bytes 442376 | tf_op jit(solution)/shard_map/ppermute | solution.py:569
  19.9 7.7 %collective-permute-start.7 = (bf16[16,512]{1,0:T(8,128)(2,1)S(1)}, bf16[16,512]{1,0:T(8,128)(2,1)S(1)}, u32[]{:S(2)}, u32[]{:S(2)}) collective-permute-start(bf16[16,512]{1,0:T(8,128)(2,1)S(1)} %get-tuple-element.68), channel_id=1, source_target_pairs={{0,8},{8,16},{16,24},{1,9},{9,17},{17,25},{2,10},{10,18},{18,26},{... | collective-permute-start | bytes 49160 | tf_op jit(solution)/shard_map/ppermute | solution.py:641
  23.1 4.5 %collective-permute-start.8 = (bf16[16,512]{1,0:T(8,128)(2,1)S(1)}, bf16[16,512]{1,0:T(8,128)(2,1)S(1)}, u32[]{:S(2)}, u32[]{:S(2)}) collective-permute-start(bf16[16,512]{1,0:T(8,128)(2,1)S(1)} %get-tuple-element.69), channel_id=1, source_target_pairs={{8,0},{16,8},{24,16},{9,1},{17,9},{25,17},{10,2},{18,10},{26,18},{... | collective-permute-start | bytes 49160 | tf_op jit(solution)/shard_map/ppermute | solution.py:640
  34.8 4.7 %collective-permute-start.9 = (f32[96,256]{1,0:T(8,128)S(1)}, f32[96,256]{1,0:T(8,128)S(1)}, u32[]{:S(2)}, u32[]{:S(2)}) collective-permute-start(f32[96,256]{1,0:T(8,128)S(1)} %get-tuple-element.78), channel_id=1, source_target_pairs={{0,1},{1,0},{2,3},{3,2},{4,5},{5,4},{6,7},{7,6},{8,9},{9,8},{10,11... | collective-permute-start | bytes 294920 | tf_op jit(solution)/shard_map/ppermute | solution.py:569
  39.7 3.9 %collective-permute-start.12 = (bf16[96,256]{1,0:T(8,128)(2,1)S(1)}, bf16[96,256]{1,0:T(8,128)(2,1)S(1)}, u32[]{:S(2)}, u32[]{:S(2)}) collective-permute-start(bf16[96,256]{1,0:T(8,128)(2,1)S(1)} %reduce-precision_convert_fusion.1), channel_id=1, source_target_pairs={{0,6},{1,7},{2,4},{3,5},{4,2},{5,3},{6,0},{7,1},{8,14},{9,15},{10,... | collective-permute-start | bytes 147464 | tf_op jit(solution)/shard_map/ppermute | solution.py:702
  41.8 3.2 %collective-permute-start.11 = (bf16[96,256]{1,0:T(8,128)(2,1)S(1)}, bf16[96,256]{1,0:T(8,128)(2,1)S(1)}, u32[]{:S(2)}, u32[]{:S(2)}) collective-permute-start(bf16[96,256]{1,0:T(8,128)(2,1)S(1)} %reduce-precision_convert_fusion.1), channel_id=1, source_target_pairs={{0,4},{1,5},{2,6},{3,7},{4,0},{5,1},{6,2},{7,3},{8,12},{9,13},{10,... | collective-permute-start | bytes 147464 | tf_op jit(solution)/shard_map/ppermute | solution.py:702
  42.1 2.9 %collective-permute-start.10 = (bf16[96,256]{1,0:T(8,128)(2,1)S(1)}, bf16[96,256]{1,0:T(8,128)(2,1)S(1)}, u32[]{:S(2)}, u32[]{:S(2)}) collective-permute-start(bf16[96,256]{1,0:T(8,128)(2,1)S(1)} %reduce-precision_convert_fusion.1), channel_id=1, source_target_pairs={{0,2},{1,3},{2,0},{3,1},{4,6},{5,7},{6,4},{7,5},{8,10},{9,11},{10,... | collective-permute-start | bytes 147464 | tf_op jit(solution)/shard_map/ppermute | solution.py:702
  45.2 4.8 %collective-permute-start.15 = (bf16[96,256]{1,0:T(8,128)(2,1)S(1)}, bf16[96,256]{1,0:T(8,128)(2,1)S(1)}, u32[]{:S(2)}, u32[]{:S(2)}) collective-permute-start(bf16[96,256]{1,0:T(8,128)(2,1)S(1)} %reduce-precision_convert_fusion), channel_id=1, source_target_pairs={{0,24},{8,16},{16,8},{24,0},{1,25},{9,17},{17,9},{25,1},{2,26},{10... | collective-permute-start | bytes 147464 | tf_op jit(solution)/shard_map/ppermute | solution.py:702
  46.8 3.9 %collective-permute-start.14 = (bf16[96,256]{1,0:T(8,128)(2,1)S(1)}, bf16[96,256]{1,0:T(8,128)(2,1)S(1)}, u32[]{:S(2)}, u32[]{:S(2)}) collective-permute-start(bf16[96,256]{1,0:T(8,128)(2,1)S(1)} %reduce-precision_convert_fusion), channel_id=1, source_target_pairs={{0,16},{8,24},{16,0},{24,8},{1,17},{9,25},{17,1},{25,9},{2,18},{10... | collective-permute-start | bytes 147464 | tf_op jit(solution)/shard_map/ppermute | solution.py:702
  47.8 3.4 %collective-permute-start.13 = (bf16[96,256]{1,0:T(8,128)(2,1)S(1)}, bf16[96,256]{1,0:T(8,128)(2,1)S(1)}, u32[]{:S(2)}, u32[]{:S(2)}) collective-permute-start(bf16[96,256]{1,0:T(8,128)(2,1)S(1)} %reduce-precision_convert_fusion), channel_id=1, source_target_pairs={{0,8},{8,0},{16,24},{24,16},{1,9},{9,1},{17,25},{25,17},{2,10},{10... | collective-permute-start | bytes 147464 | tf_op jit(solution)/shard_map/ppermute | solution.py:702
  51.2 4.8 %collective-permute-start.16 = (f32[96,256]{1,0:T(8,128)S(1)}, f32[96,256]{1,0:T(8,128)S(1)}, u32[]{:S(2)}, u32[]{:S(2)}) collective-permute-start(f32[96,256]{1,0:T(8,128)S(1)} %add_add_fusion.own), channel_id=1, source_target_pairs={{0,1},{1,0},{2,3},{3,2},{4,5},{5,4},{6,7},{7,6},{8,9},{9,8},{10,11... | collective-permute-start | bytes 294920 | tf_op jit(solution)/shard_map/ppermute | solution.py:569
